TPU v7x, 32 devices: a whole 2x2x4 slice. The times are simulated.
32 devices in a mesh: seq: 4 (over y, core), batch: 8 (over z, x).
Axes of the slice: x: 2, y: 2, z: 4, core: 2. Of those that a mesh axis runs over, the one named last changes fastest.
Arguments:
- layer_input: bfloat16 [8, 2048, 1024], P('batch', 'seq'), may hold values from -6 to 6
- lengths: int32 [8], P('batch'), may hold values from 1537 to 2048, as said below
- first_gain: bfloat16 [1024], P('batch'), may hold values from 0.5 to 1.5
- first_shift: bfloat16 [1024], P('batch'), may hold values from -1.25 to 1.25
- joined_weight: bfloat16 [1024, 3072], P('batch'), may hold values from -1 to 1
- joined_bias: bfloat16 [2048], P('batch'), may hold values from -4 to 4
- output_weight: bfloat16 [1024, 1024], P('batch'), may hold values from -0.375 to 0.375
- output_bias: bfloat16 [1024], P('batch'), may hold values from -1.25 to 1.25
- second_gain: bfloat16 [1024], P('batch'), may hold values from 0.5 to 1.5
- second_shift: bfloat16 [1024], P('batch'), may hold values from -1.25 to 1.25
- expand_weight: bfloat16 [1024, 4096], P('batch'), may hold values from -0.1875 to 0.1875
- expand_bias: bfloat16 [4096], P('batch'), may hold values from -1.75 to 1.75
- shrink_weight: bfloat16 [4096, 1024], P('batch'), may hold values from -0.1875 to 0.1875
- shrink_bias: bfloat16 [1024], P('batch'), may hold values from -1.25 to 1.25
- out_grad: bfloat16 [8, 2048, 1024], P('batch', 'seq'), may hold values from -6 to 6
Outputs:
- layer_output: bfloat16 [8, 2048, 1024], P('batch', 'seq')
- input_grad: float32 [8, 2048, 1024], P('batch', 'seq')
- first_gain_grad: float32 [1024], P('batch')
- first_shift_grad: float32 [1024], P('batch')
- joined_weight_grad: float32 [1024, 3072], P('batch')
- joined_bias_grad: float32 [2048], P('batch')
- output_weight_grad: float32 [1024, 1024], P('batch')
- output_bias_grad: float32 [1024], P('batch')
- second_gain_grad: float32 [1024], P('batch')
- second_shift_grad: float32 [1024], P('batch')
- expand_weight_grad: float32 [1024, 4096], P('batch')
- expand_bias_grad: float32 [4096], P('batch')
- shrink_weight_grad: float32 [4096, 1024], P('batch')
- shrink_bias_grad: float32 [1024], P('batch')
Inputs may be any that keep to these rules, and one draw needn't show every extreme that they name: `lengths`: among the 1 row of each index of batch, one row drawn from the seed reaches the last index of seq (its length exceeds 2048 - 512); exactly one row in all has length 2048; with more than one row to an index of batch, one row has length 200.
All inputs are finite; a program needn't handle non-finite values.
Results may differ from a plain program's by a relative error of at most 0.018.
Values may be sent and summed in bfloat16 or wider, within the bound.
No kernel may reach another device: no remote copies, remote signals or barrier semaphores. Data moves between devices by JAX's collectives and lax.ppermute only.
A program may use at most 256 MiB of HBM per device.

v0:
```python
import jax
import jax.numpy as jnp
from jax import lax
from jax.sharding import PartitionSpec as P

H = 16
HD = 64


EPSILON = 1e-05


def layer_norm(values, norm_gain, norm_shift):
    mean_val = jnp.mean(values, axis=-1, keepdims=True)
    centered = values - mean_val
    variance = jnp.mean(centered * centered, axis=-1, keepdims=True)
    return centered * lax.rsqrt(variance + EPSILON) * norm_gain + norm_shift


def gelu_tanh(values):
    return jax.nn.gelu(values, approximate=True)


def block_scores(query_block, key_block, lengths, slopes, block_start):
    block_size = query_block.shape[1]
    key_count = key_block.shape[1]
    query_pos = block_start + jnp.arange(block_size, dtype=jnp.int32)
    key_pos = jnp.arange(key_count, dtype=jnp.int32)
    scores = (
        jnp.einsum("rqhd,rkhd->rhqk", query_block, key_block, preferred_element_type=jnp.float32)
        * 0.125
    )
    offset = (key_pos[None, :] - query_pos[:, None]).astype(jnp.float32)
    scores = scores + slopes[None, :, None, None] * offset[None, None]
    live_mask = (key_pos[None, :] <= query_pos[:, None])[None, None] & (
        key_pos[None, :] < lengths[:, None]
    )[:, None, None, :]
    return jnp.where(live_mask, scores, -1e30)


def attend(packed, lengths, slopes):
    row_count, seq_len, packed_width = packed.shape
    head_count = packed_width // (3 * HD)
    grid = packed.reshape(row_count, seq_len, head_count, 3, HD)
    queries = grid[:, :, :, 0]
    key_rows = grid[:, :, :, 1]
    value_rows = grid[:, :, :, 2]
    block_size = min(512, seq_len)
    outputs = []
    log_sums = []
    for block_index in range(seq_len // block_size):
        block_start = block_index * block_size
        block_end = block_start + block_size
        scores = block_scores(
            queries[:, block_start:block_end], key_rows[:, :block_end], lengths, slopes, block_start
        )
        row_max = jnp.max(scores, axis=-1, keepdims=True)
        exp_scores = jnp.exp(scores - row_max)
        row_sum = jnp.sum(exp_scores, axis=-1, keepdims=True)
        attn_probs = (exp_scores / row_sum).astype(jnp.bfloat16)
        block_out = jnp.einsum(
            "rhqk,rkhd->rqhd",
            attn_probs,
            value_rows[:, :block_end],
            preferred_element_type=jnp.float32,
        )
        outputs.append(block_out.astype(jnp.bfloat16))
        log_sums.append((row_max + jnp.log(row_sum))[..., 0])
    mixed = jnp.concatenate(outputs, axis=1).reshape(row_count, seq_len, head_count * HD)
    return (mixed, jnp.concatenate(log_sums, axis=2))


def attend_back(packed, grad_heads, log_sums, lengths, slopes):
    row_count, seq_len, packed_width = packed.shape
    head_count = packed_width // (3 * HD)
    grid = packed.reshape(row_count, seq_len, head_count, 3, HD)
    queries = grid[:, :, :, 0]
    key_rows = grid[:, :, :, 1]
    value_rows = grid[:, :, :, 2]
    grad_grid = grad_heads.reshape(row_count, seq_len, head_count, HD)
    key_grad = jnp.zeros((row_count, seq_len, head_count, HD), jnp.float32)
    value_grad = jnp.zeros((row_count, seq_len, head_count, HD), jnp.float32)
    query_grads = []
    block_size = min(512, seq_len)
    for block_index in range(seq_len // block_size):
        block_start = block_index * block_size
        block_end = block_start + block_size
        query_block = queries[:, block_start:block_end]
        scores = block_scores(query_block, key_rows[:, :block_end], lengths, slopes, block_start)
        attn_probs = jnp.exp(scores - log_sums[:, :, block_start:block_end, None])
        grad_block = grad_grid[:, block_start:block_end]
        prob_grad = jnp.einsum(
            "rqhd,rkhd->rhqk",
            grad_block,
            value_rows[:, :block_end],
            preferred_element_type=jnp.float32,
        )
        inner = jnp.sum(attn_probs * prob_grad, axis=-1, keepdims=True)
        score_grad = (attn_probs * (prob_grad - inner)).astype(jnp.bfloat16)
        query_grads.append(
            jnp.einsum(
                "rhqk,rkhd->rqhd",
                score_grad,
                key_rows[:, :block_end],
                preferred_element_type=jnp.float32,
            )
            * 0.125
        )
        key_part = (
            jnp.einsum(
                "rhqk,rqhd->rkhd", score_grad, query_block, preferred_element_type=jnp.float32
            )
            * 0.125
        )
        key_grad = key_grad.at[:, :block_end].add(key_part)
        value_part = jnp.einsum(
            "rhqk,rqhd->rkhd",
            attn_probs.astype(jnp.bfloat16),
            grad_block,
            preferred_element_type=jnp.float32,
        )
        value_grad = value_grad.at[:, :block_end].add(value_part)
    query_grad = jnp.concatenate(query_grads, axis=1)
    stacked = jnp.stack([query_grad, key_grad, value_grad], axis=3).astype(jnp.bfloat16)
    return stacked.reshape(row_count, seq_len, head_count * 3 * HD)


def body(
    layer_input,
    lengths,
    first_gain,
    first_shift,
    joined_weight,
    joined_bias,
    output_weight,
    output_bias,
    second_gain,
    second_shift,
    expand_weight,
    expand_bias,
    shrink_weight,
    shrink_bias,
    out_grad,
):
    params = (
        lax.all_gather(first_gain, "batch", axis=0, tiled=True),
        lax.all_gather(first_shift, "batch", axis=0, tiled=True),
        lax.all_gather(joined_weight, "batch", axis=0, tiled=True),
        lax.all_gather(joined_bias, "batch", axis=0, tiled=True),
        lax.all_gather(output_weight, "batch", axis=0, tiled=True),
        lax.all_gather(output_bias, "batch", axis=0, tiled=True),
        lax.all_gather(second_gain, "batch", axis=0, tiled=True),
        lax.all_gather(second_shift, "batch", axis=0, tiled=True),
        lax.all_gather(expand_weight, "batch", axis=0, tiled=True),
        lax.all_gather(expand_bias, "batch", axis=0, tiled=True),
        lax.all_gather(shrink_weight, "batch", axis=0, tiled=True),
        lax.all_gather(shrink_bias, "batch", axis=0, tiled=True),
    )
    (
        gain_one,
        shift_one,
        joined_full,
        fbias_full,
        outw_full,
        obias_full,
        gain_two,
        shift_two,
        expand_full,
        ebias_full,
        shrink_full,
        sbias_full,
    ) = params
    row_count, local_len, feat_count = layer_input.shape
    tok_count = row_count * local_len
    head_local = H // lax.axis_size("seq")
    head_ids = lax.axis_index("seq") * head_local + jnp.arange(head_local, dtype=jnp.int32) + 1
    slopes = 2.0 ** (-8.0 * head_ids.astype(jnp.float32) / H)
    inputs = layer_input.astype(jnp.float32).reshape(tok_count, feat_count)
    normed, first_back = jax.vjp(
        layer_norm, inputs, gain_one.astype(jnp.float32), shift_one.astype(jnp.float32)
    )
    normed16 = normed.astype(jnp.bfloat16)
    joined = jnp.dot(normed16, joined_full, preferred_element_type=jnp.float32).reshape(
        tok_count, H, 3, HD
    )
    bias_grid = fbias_full.astype(jnp.float32).reshape(H, 2, HD)
    packed = jnp.stack(
        [joined[:, :, 0] + bias_grid[:, 0], joined[:, :, 1], joined[:, :, 2] + bias_grid[:, 1]],
        axis=2,
    )
    packed = packed.astype(jnp.bfloat16).reshape(row_count, local_len, 3 * feat_count)
    heads = lax.all_to_all(packed, "seq", split_axis=2, concat_axis=1, tiled=True)
    head_out, log_sums = attend(heads, lengths, slopes)
    merged = lax.all_to_all(head_out, "seq", split_axis=1, concat_axis=2, tiled=True).reshape(
        tok_count, feat_count
    )
    resid = (
        inputs
        + jnp.dot(merged, outw_full, preferred_element_type=jnp.float32)
        + obias_full.astype(jnp.float32)
    )
    second, second_back = jax.vjp(
        layer_norm, resid, gain_two.astype(jnp.float32), shift_two.astype(jnp.float32)
    )
    second16 = second.astype(jnp.bfloat16)
    pre_act = jnp.dot(
        second16, expand_full, preferred_element_type=jnp.float32
    ) + ebias_full.astype(jnp.float32)
    activ, gelu_back = jax.vjp(gelu_tanh, pre_act)
    activ16 = activ.astype(jnp.bfloat16)
    result = (
        resid
        + jnp.dot(activ16, shrink_full, preferred_element_type=jnp.float32)
        + sbias_full.astype(jnp.float32)
    )
    layer_output = result.astype(jnp.bfloat16).reshape(row_count, local_len, feat_count)
    cotan16 = out_grad.reshape(tok_count, feat_count)
    cotan = cotan16.astype(jnp.float32)
    shrink_wgrad = jnp.einsum("tf,td->fd", activ16, cotan16, preferred_element_type=jnp.float32)
    shrink_bgrad = jnp.sum(cotan, axis=0)
    activ_grad = jnp.einsum("td,fd->tf", cotan16, shrink_full, preferred_element_type=jnp.float32)
    pre_grad = gelu_back(activ_grad)[0].astype(jnp.bfloat16)
    expand_wgrad = jnp.einsum("td,tf->df", second16, pre_grad, preferred_element_type=jnp.float32)
    expand_bgrad = jnp.sum(pre_grad, axis=0, dtype=jnp.float32)
    second_grad = jnp.einsum("tf,df->td", pre_grad, expand_full, preferred_element_type=jnp.float32)
    resid_part, gain_two_grad, shift_two_grad = second_back(second_grad)
    resid_grad = cotan + resid_part
    branch_grad = resid_grad.astype(jnp.bfloat16)
    outw_grad = jnp.einsum("td,te->de", merged, branch_grad, preferred_element_type=jnp.float32)
    obias_grad = jnp.sum(branch_grad, axis=0, dtype=jnp.float32)
    mixed_grad = jnp.einsum(
        "te,de->td", branch_grad, outw_full, preferred_element_type=jnp.float32
    ).astype(jnp.bfloat16)
    grad_heads = lax.all_to_all(
        mixed_grad.reshape(row_count, local_len, feat_count),
        "seq",
        split_axis=2,
        concat_axis=1,
        tiled=True,
    )
    packed_grad = attend_back(heads, grad_heads, log_sums, lengths, slopes)
    joined_grad = lax.all_to_all(
        packed_grad, "seq", split_axis=1, concat_axis=2, tiled=True
    ).reshape(tok_count, 3 * feat_count)
    grad_grid = joined_grad.reshape(tok_count, H, 3, HD)
    fbias_grad = jnp.stack(
        [
            jnp.sum(grad_grid[:, :, 0], axis=0, dtype=jnp.float32),
            jnp.sum(grad_grid[:, :, 2], axis=0, dtype=jnp.float32),
        ],
        axis=1,
    ).reshape(2 * feat_count)
    joined_wgrad = jnp.einsum(
        "td,te->de", normed16, joined_grad, preferred_element_type=jnp.float32
    )
    normed_grad = jnp.einsum(
        "te,de->td", joined_grad, joined_full, preferred_element_type=jnp.float32
    )
    input_part, gain_one_grad, shift_one_grad = first_back(normed_grad)
    input_grad = (resid_grad + input_part).reshape(row_count, local_len, feat_count)
    shares = (
        lax.psum_scatter(
            gain_one_grad.astype(jnp.bfloat16), "batch", scatter_dimension=0, tiled=True
        ).astype(jnp.float32),
        lax.psum_scatter(
            shift_one_grad.astype(jnp.bfloat16), "batch", scatter_dimension=0, tiled=True
        ).astype(jnp.float32),
        lax.psum_scatter(
            joined_wgrad.astype(jnp.bfloat16), "batch", scatter_dimension=0, tiled=True
        ).astype(jnp.float32),
        lax.psum_scatter(
            fbias_grad.astype(jnp.bfloat16), "batch", scatter_dimension=0, tiled=True
        ).astype(jnp.float32),
        lax.psum_scatter(
            outw_grad.astype(jnp.bfloat16), "batch", scatter_dimension=0, tiled=True
        ).astype(jnp.float32),
        lax.psum_scatter(
            obias_grad.astype(jnp.bfloat16), "batch", scatter_dimension=0, tiled=True
        ).astype(jnp.float32),
        lax.psum_scatter(
            gain_two_grad.astype(jnp.bfloat16), "batch", scatter_dimension=0, tiled=True
        ).astype(jnp.float32),
        lax.psum_scatter(
            shift_two_grad.astype(jnp.bfloat16), "batch", scatter_dimension=0, tiled=True
        ).astype(jnp.float32),
        lax.psum_scatter(
            expand_wgrad.astype(jnp.bfloat16), "batch", scatter_dimension=0, tiled=True
        ).astype(jnp.float32),
        lax.psum_scatter(
            expand_bgrad.astype(jnp.bfloat16), "batch", scatter_dimension=0, tiled=True
        ).astype(jnp.float32),
        lax.psum_scatter(
            shrink_wgrad.astype(jnp.bfloat16), "batch", scatter_dimension=0, tiled=True
        ).astype(jnp.float32),
        lax.psum_scatter(
            shrink_bgrad.astype(jnp.bfloat16), "batch", scatter_dimension=0, tiled=True
        ).astype(jnp.float32),
    )
    totals = (
        lax.psum(shares[0].astype(jnp.bfloat16), "seq").astype(jnp.float32),
        lax.psum(shares[1].astype(jnp.bfloat16), "seq").astype(jnp.float32),
        lax.psum(shares[2].astype(jnp.bfloat16), "seq").astype(jnp.float32),
        lax.psum(shares[3].astype(jnp.bfloat16), "seq").astype(jnp.float32),
        lax.psum(shares[4].astype(jnp.bfloat16), "seq").astype(jnp.float32),
        lax.psum(shares[5].astype(jnp.bfloat16), "seq").astype(jnp.float32),
        lax.psum(shares[6].astype(jnp.bfloat16), "seq").astype(jnp.float32),
        lax.psum(shares[7].astype(jnp.bfloat16), "seq").astype(jnp.float32),
        lax.psum(shares[8].astype(jnp.bfloat16), "seq").astype(jnp.float32),
        lax.psum(shares[9].astype(jnp.bfloat16), "seq").astype(jnp.float32),
        lax.psum(shares[10].astype(jnp.bfloat16), "seq").astype(jnp.float32),
        lax.psum(shares[11].astype(jnp.bfloat16), "seq").astype(jnp.float32),
    )
    return (
        layer_output,
        input_grad,
        totals[0],
        totals[1],
        totals[2],
        totals[3],
        totals[4],
        totals[5],
        totals[6],
        totals[7],
        totals[8],
        totals[9],
        totals[10],
        totals[11],
    )


def solution(mesh):
    in_specs = (
        P("batch", "seq", None),
        P("batch"),
        P("batch"),
        P("batch"),
        P("batch", None),
        P("batch"),
        P("batch", None),
        P("batch"),
        P("batch"),
        P("batch"),
        P("batch", None),
        P("batch"),
        P("batch", None),
        P("batch"),
        P("batch", "seq", None),
    )
    out_specs = (
        P("batch", "seq", None),
        P("batch", "seq", None),
        P("batch"),
        P("batch"),
        P("batch", None),
        P("batch"),
        P("batch", None),
        P("batch"),
        P("batch"),
        P("batch"),
        P("batch", None),
        P("batch"),
        P("batch", None),
        P("batch"),
    )
    return jax.shard_map(body, mesh=mesh, in_specs=in_specs, out_specs=out_specs, check_vma=False)
```

profile of v0, /device:TPU:0, one launch (start us, length us, event | category | flops | bytes accessed | tf_op | source)
XLA Modules:
  0.0 1194.4 jit_solution(9337650903999033201)
XLA Ops:
  12.6 22.4 %all-gather = bf16[8,1,128]{2,1,0:T(2,128)(2,1)S(1)} all-gather(bf16[1,1,128]{2,1,0:T(2,128)(2,1)S(1)} %bitcast.402), channel_id=1, replica_groups=mesh['seq'=4,'batch'=8] {'batch'}, dimensions={0}, use_global_device_ids=true | all-gather | bytes 2304 | tf_op jit(solution)/shard_map/all_gather | solution.py:146
  35.0 16.5 %all-gather.1 = bf16[8,1,128]{2,1,0:T(2,128)(2,1)S(1)} all-gather(bf16[1,1,128]{2,1,0:T(2,128)(2,1)S(1)} %bitcast.403), channel_id=1, replica_groups=mesh['seq'=4,'batch'=8] {'batch'}, dimensions={0}, use_global_device_ids=true | all-gather | bytes 2304 | tf_op jit(solution)/shard_map/all_gather | solution.py:147
  51.5 18.3 %all-gather.2 = bf16[8,1,256]{2,1,0:T(2,128)(2,1)S(1)} all-gather(bf16[1,1,256]{2,1,0:T(2,128)(2,1)S(1)} %reshape.1175), channel_id=1, replica_groups=mesh['seq'=4,'batch'=8] {'batch'}, dimensions={0}, use_global_device_ids=true | all-gather | bytes 4608 | tf_op jit(solution)/shard_map/all_gather | solution.py:149
  71.3 40.8 %all-gather.13.cloned.1.call-done = bf16[1024,3072]{1,0:T(8,128)(2,1)} async-done(((bf16[128,3072]{1,0:T(8,128)(2,1)}), bf16[1024,3072]{1,0:T(8,128)(2,1)}) %all-gather.13.cloned.1.call-update) | async-done | bytes 6291472 | tf_op jit(solution)/shard_map/all_gather | solution.py:148
  112.1 8.7 copy.78
  120.8 6.3 fusion.119
  128.0 27.5 %copy.110 = bf16[1,512,3072]{1,0,2:T(2,128)(2,1)} copy(bf16[1,512,3072]{1,2,0:T(8,128)(2,1)S(1)} %bitcast.362) | data formatting | bytes 6291456 | tf_op jit(solution)/shard_map/convert_element_type | solution.py:191
  156.0 21.9 %reduce.53 = bf16[3072,512]{1,0:T(8,128)(2,1)} reduce(bf16[3072,1,512]{2,1,0:T(2,128)(2,1)} %bitcast.358, bf16[]{:T(256)} %broadcast.690), dimensions={1}, to_apply=%bitcast.343.reduce_sub_computation | reduce | bytes 6291458
  177.8 5.3 reshape.1208
  197.2 28.0 %all-to-all-done = bf16[4,2,196608]{2,1,0:T(2,128)(2,1)} async-done(((bf16[4,2,196608]{2,1,0:T(2,128)(2,1)}), bf16[4,2,196608]{2,1,0:T(2,128)(2,1)}, u32[]{:S(2)}, u32[]{:S(2)}) %all-to-all-start) | async-done | bytes 3145760 | tf_op jit(solution)/shard_map/all_to_all | solution.py:192
  225.2 6.2 reshape.1209
  239.1 6.1 reshape.1141
  267.2 10.5 fusion.146
  277.6 8.1 fusion
  291.0 6.6 fusion.109
  309.4 11.6 reduce.54
  328.7 16.8 %all-gather.3 = bf16[8,1,128]{2,1,0:T(2,128)(2,1)S(1)} all-gather(bf16[1,1,128]{2,1,0:T(2,128)(2,1)S(1)} %bitcast.404), channel_id=1, replica_groups=mesh['seq'=4,'batch'=8] {'batch'}, dimensions={0}, use_global_device_ids=true | all-gather | bytes 2304 | tf_op jit(solution)/shard_map/all_gather | solution.py:151
  345.6 17.9 %all-gather.4 = bf16[8,1,128]{2,1,0:T(2,128)(2,1)S(1)} all-gather(bf16[1,1,128]{2,1,0:T(2,128)(2,1)S(1)} %bitcast.405), channel_id=1, replica_groups=mesh['seq'=4,'batch'=8] {'batch'}, dimensions={0}, use_global_device_ids=true | all-gather | bytes 2304 | tf_op jit(solution)/shard_map/all_gather | solution.py:152
  363.4 17.0 %all-gather.5 = bf16[8,1,128]{2,1,0:T(2,128)(2,1)S(1)} all-gather(bf16[1,1,128]{2,1,0:T(2,128)(2,1)S(1)} %bitcast.406), channel_id=1, replica_groups=mesh['seq'=4,'batch'=8] {'batch'}, dimensions={0}, use_global_device_ids=true | all-gather | bytes 2304 | tf_op jit(solution)/shard_map/all_gather | solution.py:153
  380.5 26.5 %all-gather.6 = bf16[8,1,512]{2,1,0:T(2,128)(2,1)S(1)} all-gather(bf16[1,1,512]{2,1,0:T(2,128)(2,1)S(1)} %reshape.1183), channel_id=1, replica_groups=mesh['seq'=4,'batch'=8] {'batch'}, dimensions={0}, use_global_device_ids=true | all-gather | bytes 9216 | tf_op jit(solution)/shard_map/all_gather | solution.py:155
  417.0 10.7 fusion.140
  427.7 14.3 %fusion.151 = (bf16[4096]{0:T(1024)(128)(2,1)}, bf16[512,4096]{1,0:T(8,128)(2,1)S(1)}) fusion(f32[512,4096]{1,0:T(8,128)} %fusion.140, f32[4096]{0:T(1024)S(1)} %bitcast.390, bf16[4096,1024]{1,0:T(8,128)(2,1)} %all-gather.19.cloned.1.call-done, bf16[1,512,1024]{2,1,0:T(8,128)(2,1)S(1)} %copy-done.13), kind=kOutput, calls=%fused_computation.228 | convolution fusion | flops 4341100544 | bytes 22044672 | tf_op jit(solution)/shard_map/td,fd->tf/dot_general | solution.py:221
  442.0 5.5 multiply_reduce_fusion.4
  454.9 7.0 reduce.55
  470.3 11.7 all-to-all-done.2
  495.7 5.7 multiply_reduce_fusion.2
  504.0 6.5 multiply_reduce_fusion.1
  522.6 10.6 multiply_convert_fusion.1
  542.3 9.2 multiply_reduce_fusion
  551.6 10.3 multiply_convert_fusion
  561.9 6.4 fusion.112
  568.3 5.2 fusion.59
  578.0 11.4 copy.93
  589.4 33.2 %reduce.56 = bf16[2048,768]{1,0:T(8,128)(2,1)} reduce(bf16[2048,1,768]{2,1,0:T(2,128)(2,1)} %bitcast.359, bf16[]{:T(256)} %broadcast.690), dimensions={1}, to_apply=%bitcast.281.reduce_sub_computation | reduce | bytes 6291458
  625.6 40.3 %all_to_all.60 = bf16[4,2,196608]{2,1,0:T(2,128)(2,1)} all-to-all(bf16[4,2,196608]{2,1,0:T(2,128)(2,1)S(1)} %reshape.1214), channel_id=1, replica_groups=mesh['seq'=4,'batch'=8] {'seq'}, dimensions={0} | all-to-all | bytes 6291456 | tf_op jit(solution)/shard_map/all_to_all | solution.py:242
  665.9 6.1 reshape.1215
  681.8 7.8 convolution_convert_fusion.2
  690.7 13.6 %convolution_convert_fusion = bf16[4096,1024]{1,0:T(8,128)(2,1)} fusion(bf16[1,512,1024]{2,1,0:T(8,128)(2,1)S(1)} %copy-done.14, f32[512,4096]{1,0:T(8,128)} %fusion.140, f32[4096]{0:T(1024)S(1)} %bitcast.391), kind=kOutput, calls=%fused_computation.35 | convolution fusion | flops 4320133120 | bytes 17842176 | tf_op jit(solution)/shard_map/tf,td->fd/dot_general | solution.py:219
  706.0 9.2 convolution_convert_fusion.1
  719.8 17.0 %all-gather.7 = bf16[8,1,128]{2,1,0:T(2,128)(2,1)S(1)} all-gather(bf16[1,1,128]{2,1,0:T(2,128)(2,1)S(1)} %bitcast.407), channel_id=1, replica_groups=mesh['seq'=4,'batch'=8] {'batch'}, dimensions={0}, use_global_device_ids=true | all-gather | bytes 2304 | tf_op jit(solution)/shard_map/all_gather | solution.py:157
  736.8 12.4 %fusion.86 = bf16[1,512,1024]{2,1,0:T(8,128)(2,1)} fusion(f32[512,1024]{1,0:T(8,128)S(1)} %copy-done.11, bf16[4096,1024]{1,0:T(8,128)(2,1)} %all-gather.19.cloned.1.call-done, f32[1024]{0:T(1024)S(1)} %bitcast.401, f32[512,4096]{1,0:T(8,128)} %fusion.140, f32[4096]{0:T(1024)S(1)} %bitcast.392), kind=kOutput, calls=%fused_computation.124 | convolution fusion | flops 4317511680 | bytes 19943424 | tf_op jit(solution)/shard_map/dot_general | solution.py:213
  749.2 54.7 %reduce-scatter.5.cloned.1.call-done = bf16[128,3072]{1,0:T(8,128)(2,1)} async-done(((bf16[1024,3072]{1,0:T(8,128)(2,1)}), bf16[128,3072]{1,0:T(8,128)(2,1)}) %reduce-scatter.5.cloned.1.call-update) | async-done | bytes 786448 | tf_op jit(solution)/shard_map/reduce_scatter | solution.py:268
  804.0 151.8 %reduce-scatter.11.cloned.1.call-done = bf16[512,1024]{1,0:T(8,128)(2,1)} async-done(((bf16[4096,1024]{1,0:T(8,128)(2,1)}), bf16[512,1024]{1,0:T(8,128)(2,1)}) %reduce-scatter.11.cloned.1.call-update) | async-done | bytes 1048592 | tf_op jit(solution)/shard_map/reduce_scatter | solution.py:292
  955.8 152.1 %reduce-scatter.9.cloned.1.call-done = bf16[128,4096]{1,0:T(8,128)(2,1)} async-done(((bf16[1024,4096]{1,0:T(8,128)(2,1)}), bf16[128,4096]{1,0:T(8,128)(2,1)}) %reduce-scatter.9.cloned.1.call-update) | async-done | bytes 1048592 | tf_op jit(solution)/shard_map/reduce_scatter | solution.py:286
  1107.9 8.9 fusion.141
  1120.1 35.5 %all-reduce.10 = (bf16[1024]{0:T(1024)(128)(2,1)S(1)}, bf16[1024]{0:T(1024)(128)(2,1)S(1)}, bf16[2048]{0:T(1024)(128)(2,1)S(1)}, bf16[1024]{0:T(1024)(128)(2,1)S...) all-reduce(bf16[1024]{0:T(1024)(128)(2,1)S(1)} %get-tuple-element.1, ...), channel_id=2, replica_groups=mesh['seq'=4,'batch'=8] {'batch'}, use_global_device_ids=true, to_apply=%region_21.22.clone | all-reduce | flops 12288 | bytes 49152
  1156.1 6.4 all-reduce.11
  1170.9 7.9 all-reduce.15.cloned.1.call-done
  (330 shorter events, 181.9 us)
Async XLA Ops:
  7.2 27.8 %copy-start.62 = (bf16[128]{0:T(256)(128)(2,1)S(1)}, bf16[128]{0:T(256)(128)(2,1)}, u32[]{:S(2)}) copy-start(bf16[128]{0:T(256)(128)(2,1)} %param.38) | copy-start | bytes 772
  7.2 104.9 %all-gather.13.cloned.1.call-start = ((), (), s32[]{:S(2)}) async-start(), calls=%async_computation.8 | async-start | bytes 7077888 | tf_op jit(solution)/shard_map/all_gather | solution.py:148
  8.0 405.3 %all-gather.15.cloned.1.call-start = ((), (), s32[]{:S(2)}) async-start(), calls=%async_computation.9 | async-start | bytes 2359296 | tf_op jit(solution)/shard_map/all_gather | solution.py:150
  8.7 408.3 %all-gather.17.cloned.1.call-start = ((), (), s32[]{:S(2)}) async-start(), calls=%async_computation.10 | async-start | bytes 9437184 | tf_op jit(solution)/shard_map/all_gather | solution.py:154
  9.4 418.2 %all-gather.19.cloned.1.call-start = ((), (), s32[]{:S(2)}) async-start(), calls=%async_computation.11 | async-start | bytes 9437184 | tf_op jit(solution)/shard_map/all_gather | solution.py:156
  12.1 108.7 %copy-start.36 = (f32[512]{0:T(512)}, f32[512]{0:T(512)S(1)}, u32[]{:S(2)}) copy-start(f32[512]{0:T(512)S(1)} %broadcast_multiply_fusion.1) | copy-start | bytes 6148
  12.5 39.0 %copy-start.40 = (f32[512]{0:T(512)}, f32[512]{0:T(512)S(1)}, u32[]{:S(2)}) copy-start(f32[512]{0:T(512)S(1)} %fusion.63) | copy-start | bytes 6148
  12.5 108.3 %copy-start.42 = (f32[512]{0:T(512)}, f32[512]{0:T(512)S(1)}, u32[]{:S(2)}) copy-start(f32[512]{0:T(512)S(1)} %fusion.135) | copy-start | bytes 6148
  35.0 85.8 %copy-start.33 = (f32[8,1,128]{2,1,0:T(1,128)}, f32[8,1,128]{2,1,0:T(1,128)S(1)}, u32[]{:S(2)}) copy-start(f32[8,1,128]{2,1,0:T(1,128)S(1)} %convert_element_type.372) | copy-start | bytes 12292
  51.5 69.3 %copy-start.54 = (f32[8,1,128]{2,1,0:T(1,128)}, f32[8,1,128]{2,1,0:T(1,128)S(1)}, u32[]{:S(2)}) copy-start(f32[8,1,128]{2,1,0:T(1,128)S(1)} %convert_element_type.373) | copy-start | bytes 12292
  183.1 42.1 %all-to-all-start = ((bf16[4,2,196608]{2,1,0:T(2,128)(2,1)}), bf16[4,2,196608]{2,1,0:T(2,128)(2,1)}, u32[]{:S(2)}, u32[]{:S(2)}) async-start(bf16[4,2,196608]{2,1,0:T(2,128)(2,1)} %reshape.1208), calls=%async_computation | async-start | bytes 6291456 | tf_op jit(solution)/shard_map/all_to_all | solution.py:192
  247.5 10.3 copy-start.18
  247.5 17.0 %copy-start.21 = (bf16[1,2048,4,64]{1,3,2,0:T(8,128)(2,1)}, bf16[1,2048,4,64]{1,3,2,0:T(8,128)(2,1)S(1)}, u32[]{:S(2)}) copy-start(bf16[1,2048,4,64]{1,3,2,0:T(8,128)(2,1)S(1)} %get-tuple-element.163) | copy-start | bytes 3145732
  247.5 43.5 %copy-start.16 = (bf16[1,2048,4,64]{1,3,2,0:T(8,128)(2,1)}, bf16[1,2048,4,64]{1,3,2,0:T(8,128)(2,1)S(1)}, u32[]{:S(2)}) copy-start(bf16[1,2048,4,64]{1,3,2,0:T(8,128)(2,1)S(1)} %get-tuple-element.161) | copy-start | bytes 3145732
  285.8 11.9 slice-start
  285.8 11.9 slice-start.1
  291.0 8.2 slice-start.3
  309.4 19.4 %copy-start.60 = (bf16[512]{0:T(512)(128)(2,1)S(1)}, bf16[512]{0:T(512)(128)(2,1)}, u32[]{:S(2)}) copy-start(bf16[512]{0:T(512)(128)(2,1)} %param.46) | copy-start | bytes 3076
  309.4 19.4 %copy-start.63 = (bf16[128]{0:T(256)(128)(2,1)S(1)}, bf16[128]{0:T(256)(128)(2,1)}, u32[]{:S(2)}) copy-start(bf16[128]{0:T(256)(128)(2,1)} %param.42) | copy-start | bytes 772
  309.4 36.2 %copy-start.64 = (bf16[128]{0:T(256)(128)(2,1)S(1)}, bf16[128]{0:T(256)(128)(2,1)}, u32[]{:S(2)}) copy-start(bf16[128]{0:T(256)(128)(2,1)} %param.43) | copy-start | bytes 772
  309.4 54.0 %copy-start.65 = (bf16[128]{0:T(256)(128)(2,1)S(1)}, bf16[128]{0:T(256)(128)(2,1)}, u32[]{:S(2)}) copy-start(bf16[128]{0:T(256)(128)(2,1)} %param.44) | copy-start | bytes 772
  324.5 82.5 %all-to-all-start.1 = ((bf16[4,2,65536]{2,1,0:T(2,128)(2,1)}), bf16[4,2,65536]{2,1,0:T(2,128)(2,1)}, u32[]{:S(2)}, u32[]{:S(2)}) async-start(bf16[4,2,65536]{2,1,0:T(2,128)(2,1)} %reshape.1210), calls=%async_computation.1 | async-start | bytes 2097152 | tf_op jit(solution)/shard_map/all_to_all | solution.py:194
  363.4 84.1 %copy-start.48 = (f32[8,1,128]{2,1,0:T(1,128)}, f32[8,1,128]{2,1,0:T(1,128)S(1)}, u32[]{:S(2)}) copy-start(f32[8,1,128]{2,1,0:T(1,128)S(1)} %convert_element_type.375) | copy-start | bytes 12292
  380.5 36.5 %copy-start.56 = (f32[8,1,128]{2,1,0:T(1,128)}, f32[8,1,128]{2,1,0:T(1,128)S(1)}, u32[]{:S(2)}) copy-start(f32[8,1,128]{2,1,0:T(1,128)S(1)} %convert_element_type.376) | copy-start | bytes 12292
  406.9 20.8 %copy-start.46 = (f32[8,1,512]{2,1,0:T(1,128)}, f32[8,1,512]{2,1,0:T(1,128)S(1)}, u32[]{:S(2)}) copy-start(f32[8,1,512]{2,1,0:T(1,128)S(1)} %convert_element_type.377) | copy-start | bytes 49156
  416.6 30.9 %copy-start.10 = (f32[512,1024]{1,0:T(8,128)}, f32[512,1024]{1,0:T(8,128)S(1)}, u32[]{:S(2)}) copy-start(f32[512,1024]{1,0:T(8,128)S(1)} %get-tuple-element.175) | copy-start | bytes 6291460
  416.6 30.9 %copy-start.44 = (f32[512]{0:T(512)}, f32[512]{0:T(512)S(1)}, u32[]{:S(2)}) copy-start(f32[512]{0:T(512)S(1)} %broadcast_multiply_fusion) | copy-start | bytes 6148
  417.0 30.6 %copy-start.51 = (f32[512]{0:T(512)}, f32[512]{0:T(512)S(1)}, u32[]{:S(2)}) copy-start(f32[512]{0:T(512)S(1)} %fusion.136) | copy-start | bytes 6148
  417.0 10.7 copy-start.13
  427.7 14.3 %copy-start.67 = (bf16[1024,4096]{1,0:T(8,128)(2,1)S(1)}, bf16[1024,4096]{1,0:T(8,128)(2,1)}, u32[]{:S(2)}) copy-start(bf16[1024,4096]{1,0:T(8,128)(2,1)} %all-gather.17.cloned.1.call-done) | copy-start | bytes 25165828
  464.0 18.0 %all-to-all-start.2 = ((bf16[4,2,65536]{2,1,0:T(2,128)(2,1)}), bf16[4,2,65536]{2,1,0:T(2,128)(2,1)S(1)}, u32[]{:S(2)}, u32[]{:S(2)}) async-start(bf16[4,2,65536]{2,1,0:T(2,128)(2,1)} %reshape.1212), calls=%async_computation.2 | async-start | bytes 2097152 | tf_op jit(solution)/shard_map/all_to_all | solution.py:234
  467.5 281.8 %reduce-scatter.7.cloned.1.call-start = ((), (), s32[]{:S(2)}) async-start(), calls=%async_computation.13 | async-start | bytes 2359296 | tf_op jit(solution)/shard_map/reduce_scatter | solution.py:274
  470.2 333.7 %reduce-scatter.5.cloned.1.call-start = ((), (), s32[]{:S(2)}) async-start(), calls=%async_computation.12 | async-start | bytes 7077888 | tf_op jit(solution)/shard_map/reduce_scatter | solution.py:268
  485.0 25.5 %copy-start.12 = (bf16[1,2048,4,64]{1,3,2,0:T(8,128)(2,1)}, bf16[1,2048,4,64]{1,3,2,0:T(8,128)(2,1)S(1)}, u32[]{:S(2)}) copy-start(bf16[1,2048,4,64]{1,3,2,0:T(8,128)(2,1)S(1)} %reshape.1159) | copy-start | bytes 3145732
  513.5 9.0 slice-start.11
  513.5 9.0 slice-start.12
  522.5 10.7 copy-start.20
  522.5 19.8 %slice-start.4 = ((s8[16777216]{0:T(1024)(128)(4,1)}), s8[4194304]{0:T(1024)(128)(4,1)S(1)}, s32[]{:S(2)}) async-start(s8[16777216]{0:T(1024)(128)(4,1)} %bitcast.350), calls=%async_computation.21 | async-start | bytes 8388608
  522.5 19.8 %slice-start.5 = ((s8[16777216]{0:T(1024)(128)(4,1)}), s8[4194304]{0:T(1024)(128)(4,1)S(1)}, s32[]{:S(2)}) async-start(s8[16777216]{0:T(1024)(128)(4,1)} %bitcast.350), calls=%async_computation.22 | async-start | bytes 8388608
  522.5 19.8 %slice-start.6 = ((s8[16777216]{0:T(1024)(128)(4,1)}), s8[4194304]{0:T(1024)(128)(4,1)S(1)}, s32[]{:S(2)}) async-start(s8[16777216]{0:T(1024)(128)(4,1)} %bitcast.350), calls=%async_computation.23 | async-start | bytes 8388608
  533.2 9.1 slice-start.7
  689.5 266.2 %reduce-scatter.11.cloned.1.call-start = ((), (), s32[]{:S(2)}) async-start(), calls=%async_computation.15 | async-start | bytes 9437184 | tf_op jit(solution)/shard_map/reduce_scatter | solution.py:292
  704.4 403.5 %reduce-scatter.9.cloned.1.call-start = ((), (), s32[]{:S(2)}) async-start(), calls=%async_computation.14 | async-start | bytes 9437184 | tf_op jit(solution)/shard_map/reduce_scatter | solution.py:286
  715.2 463.6 %all-reduce.15.cloned.1.call-start = ((), (), s32[]{:S(2)}) async-start(), calls=%async_computation.16 | async-start | bytes 6291456 | tf_op jit(solution)/shard_map/psum | solution.py:302
  1107.9 9.0 copy-start.15
  1107.9 9.4 copy-start.41
  1116.8 49.9 %copy-start.9 = (f32[512,1024]{1,0:T(8,128)S(1)}, f32[512,1024]{1,0:T(8,128)}, u32[]{:S(2)}) copy-start(f32[512,1024]{1,0:T(8,128)} %copy-done.8) | copy-start | bytes 6291460
  1116.8 49.9 %copy-start.39 = (f32[512]{0:T(512)S(1)}, f32[512]{0:T(512)}, u32[]{:S(2)}) copy-start(f32[512]{0:T(512)} %copy-done.38) | copy-start | bytes 6148
  (51 other events, 203.4 us)
Sparse Core Ops, SparseCore 0:
  10.2 101.8 all-gather.12
  114.2 47.4 all-gather.14
  163.9 123.4 all-gather.16
  289.3 123.8 all-gather.18
  471.5 65.5 reduce-scatter.6
  689.7 114.2 reduce-scatter.4
  807.6 148.1 reduce-scatter.10
  959.8 148.0 reduce-scatter.8
  1110.5 68.2 all-reduce.14
where the time goes:
time: 1200 us; the launch traced here: 1190 us
  waiting for transfers between devices  450 us (38%)
  blocking collectives  234 us (20%)
  matrix products  194 us (16%)
  other arithmetic  151 us (13%)
  local copies, waits for them, and re-layouts  133 us (11%)
  between operations  18.3 us (2%)
  starting transfers between devices  13.5 us (1%)
    reduce_scatter x1, waiting for transfers between devices, body(): lax.psum_scatter(expand_wgrad.astype(jnp.bfloat16), 'batch', scatter_dime...  152 us
    reduce_scatter x1, waiting for transfers between devices, body(): lax.psum_scatter(shrink_wgrad.astype(jnp.bfloat16), 'batch', scatter_dime...  152 us
    unnamed x9, other arithmetic  73.8 us
    unnamed x198, local copies, waits for them, and re-layouts  56.9 us
    reduce_scatter x1, waiting for transfers between devices, body(): lax.psum_scatter(joined_wgrad.astype(jnp.bfloat16), 'batch', scatter_dime...  54.7 us
    all_gather x1, waiting for transfers between devices, body(): lax.all_gather(joined_weight, 'batch', axis=0, tiled=True)  40.8 us
    all_to_all x1, blocking collectives, body(): lax.all_to_all(packed_grad, 'seq', split_axis=1, concat_axis=2, tiled=True)  40.3 us
    unnamed x1, blocking collectives  35.5 us
  transfers between devices with their start and end apart: 12, of which 7 were waited for; matrix products, arithmetic and copies ran while one was open for 35% of the time, Pallas kernels for 0%

commit v1 on v0

v1 whole, which is shorter than its diff:
```python
import functools

import jax
import jax.numpy as jnp
from jax import lax
from jax.experimental import pallas as pl
from jax.experimental.pallas import tpu as pltpu
from jax.sharding import PartitionSpec as P

H = 16
HD = 64
EPSILON = 1e-05
F32 = jnp.float32
BF = jnp.bfloat16
NT = (((1,), (1,)), ((), ()))
NN = (((1,), (0,)), ((), ()))
TN = (((0,), (0,)), ((), ()))
MIB = 2**20


def dg(left, right, dims):
    return lax.dot_general(left, right, dims, preferred_element_type=F32)


def params(limit=56):
    return pltpu.CompilerParams(vmem_limit_bytes=limit * MIB)


def cost(flops, moved, exps=0):
    return pl.CostEstimate(flops=flops, bytes_accessed=moved, transcendentals=exps)


def norm_parts(values):
    mean = jnp.mean(values, axis=-1, keepdims=True)
    centered = values - mean
    scale = lax.rsqrt(jnp.mean(centered * centered, axis=-1, keepdims=True) + EPSILON)
    return centered * scale, scale


def norm_back(grad, unit, scale, gain):
    scaled = grad * gain
    return scale * (
        scaled
        - jnp.mean(scaled, axis=-1, keepdims=True)
        - unit * jnp.mean(scaled * unit, axis=-1, keepdims=True)
    )


def pairs(size, bit):
    return [(i, i ^ bit) for i in range(size)]


def bits_low_last(size):
    bits = []
    bit = 2
    while bit < size:
        bits.append(bit)
        bit *= 2
    if size > 1:
        bits.append(1)
    return bits


def place_of(rel, size):
    place = 0
    for at, bit in enumerate(bits_low_last(size)):
        place |= (1 << at) if rel & bit else 0
    return place


def place_table(me, size):
    index = jnp.arange(size, dtype=jnp.int32) ^ me
    place = jnp.zeros_like(index)
    for at, bit in enumerate(bits_low_last(size)):
        place = place | jnp.where(index & bit, 1 << at, 0)
    return place


def gather_stack(block, axis, size):
    out = block[None]
    for bit in bits_low_last(size):
        out = jnp.concatenate([out, lax.ppermute(out, axis, pairs(size, bit))], 0)
    return out


def add16(left, right):
    return (left.astype(F32) + right.astype(F32)).astype(BF)


def scatter_stack(stack, axis, size):
    for bit in bits_low_last(size)[::-1]:
        half = stack.shape[0] // 2
        stack = add16(stack[:half], lax.ppermute(stack[half:], axis, pairs(size, bit)))
    return stack[0]


def gather_rel(block, axis, size):
    out = {0: block}
    for bit in bits_low_last(size):
        for rel in list(out):
            out[rel | bit] = lax.ppermute(out[rel], axis, pairs(size, bit))
    return out


def scatter_rel(parts, axis, size, last=True):
    parts = dict(parts)
    order = bits_low_last(size)[::-1]
    for bit in order:
        for rel in sorted(parts, reverse=True):
            if rel & bit:
                other = lax.ppermute(parts.pop(rel), axis, pairs(size, bit))
                if bit == order[-1] and not last:
                    return parts[0], other
                parts[rel ^ bit] = add16(parts[rel ^ bit], other)
    return parts[0]


def first_kernel(nt, nb, rows, info, xa, xb, weight, vecs, jbias, *rest):
    normed, joined, full = rest[-3:]
    step = pl.program_id(0)

    @pl.when(step == 0)
    def _():
        for k in range(nb):
            full[k * rows : (k + 1) * rows] = weight[info[2 + k], :rows]

    gain = vecs[0:1]
    shift = vecs[1:2]

    def work(x):
        unit, _ = norm_parts(x[...].astype(F32))
        value = (unit * gain + shift).astype(BF)
        normed[...] = value
        joined[...] = (dg(value, full[...], NN) + jbias[...]).astype(BF)

    @pl.when(step < nt)
    def _():
        work(xa)

    @pl.when(step >= nt)
    def _():
        work(xb)


def first_call(rel, xa, xb, info, weight, vecs, jbias, before, ns):
    tok, dim = xa.shape
    nb, padded, cols = weight.shape
    rows = dim // nb
    tile = min(256, tok)
    nt = tok // tile
    whole = lambda shape: pl.BlockSpec(shape, lambda i, info: (0,) * len(shape), pipeline_mode=pl.Buffered(1))
    place = lambda i, info: ((info[0] ^ (rel + lax.div(i, nt))) * nt + lax.rem(i, nt), 0)
    outs = [jax.ShapeDtypeStruct((ns * tok, dim), BF), jax.ShapeDtypeStruct((ns * tok, cols), BF)]
    extra = [] if before is None else list(before)
    return pl.pallas_call(
        functools.partial(first_kernel, nt, nb, rows),
        grid_spec=pltpu.PrefetchScalarGridSpec(
            num_scalar_prefetch=1,
            grid=(2 * nt,),
            in_specs=[
                pl.BlockSpec((tile, dim), lambda i, info: (jnp.minimum(i, nt - 1), 0)),
                pl.BlockSpec((tile, dim), lambda i, info: (jnp.maximum(i - nt, 0), 0)),
                whole(weight.shape),
                whole(vecs.shape),
                whole(jbias.shape),
            ]
            + [pl.BlockSpec(memory_space=pl.ANY)] * len(extra),
            out_specs=[pl.BlockSpec((tile, dim), place), pl.BlockSpec((tile, cols), place)],
            scratch_shapes=[pltpu.VMEM((dim, cols), BF)],
        ),
        out_shape=outs,
        input_output_aliases={6: 0, 7: 1} if extra else {},
        compiler_params=params(40),
        cost_estimate=cost(4 * tok * dim * cols, 4 * tok * (2 * dim + cols)),
        name="first",
    )(info, xa, xb, weight, vecs, jbias, *extra)


def three(value):
    high = value.astype(BF)
    rest = value - high.astype(F32)
    mid = rest.astype(BF)
    return high, mid, (rest - mid.astype(F32)).astype(BF)


def spread(lane, base, columns):
    for at, column in columns:
        base = jnp.where(lane == at, column.astype(F32), base)
    return base.astype(BF)


def key_extra(count, slope, length):
    lane = lax.broadcasted_iota(jnp.int32, (count, HD), 1)
    pos = lax.broadcasted_iota(jnp.int32, (count, HD), 0)
    high, mid, low = three(slope * pos.astype(F32))
    dead = jnp.where(pos < length, 0.0, -1e30)
    return spread(lane, jnp.where(lane < 7, 1.0, 0.0), [(0, high), (1, mid), (2, low), (3, dead)])


def attend_kernel(count, size, info, slopes, joined, mixed, sums, keys):
    pair = pl.program_id(0)
    lane = lax.broadcasted_iota(jnp.int32, (size, HD), 1)
    ones = jnp.where(lane < 4, 1.0, 0.0).astype(BF)
    for hh in range(2):
        base = 3 * HD * hh
        extra = key_extra(count, slopes[2 * pair + hh], info[1])
        keys[hh] = jnp.concatenate([joined[:, base + HD : base + 2 * HD], extra], 1)
    query_at = lax.broadcasted_iota(jnp.int32, (size, size), 0)
    key_at = lax.broadcasted_iota(jnp.int32, (size, size), 1)
    for block in range(count // size):
        low = block * size
        high = low + size
        outs = []
        logs = []
        for hh in range(2):
            base = 3 * HD * hh
            query = (joined[low:high, base : base + HD].astype(F32) * 0.125).astype(BF)
            query = jnp.concatenate([query, ones], 1)
            near = jnp.where(key_at <= query_at, dg(query, keys[hh, low:high], NT), -1e30)
            top = jnp.max(near, axis=1, keepdims=True)
            if block:
                far = dg(query, keys[hh, 0:low], NT)
                top = jnp.maximum(top, jnp.max(far, axis=1, keepdims=True))
            near = jnp.exp(near - top)
            total = jnp.sum(near, axis=1, keepdims=True)
            acc = dg(near.astype(BF), joined[low:high, base + 2 * HD : base + 3 * HD], NN)
            if block:
                far = jnp.exp(far - top)
                total += jnp.sum(far, axis=1, keepdims=True)
                acc += dg(far.astype(BF), joined[0:low, base + 2 * HD : base + 3 * HD], NN)
            outs.append(acc / total)
            logs.append(jnp.broadcast_to(top + jnp.log(total), (size, HD)))
        mixed[low:high] = jnp.concatenate(outs, 1).astype(BF)
        sums[low:high] = jnp.concatenate(logs, 1)


def attend(joined, info, slopes):
    count, width = joined.shape
    groups = width // (6 * HD)
    smem = pl.BlockSpec(memory_space=pltpu.SMEM)
    area = count * count * groups
    return pl.pallas_call(
        functools.partial(attend_kernel, count, min(512, count)),
        grid=(groups,),
        in_specs=[smem, smem, pl.BlockSpec((count, 6 * HD), lambda p: (0, p))],
        out_specs=[pl.BlockSpec((count, 2 * HD), lambda p: (0, p))] * 2,
        out_shape=[
            jax.ShapeDtypeStruct((count, groups * 2 * HD), BF),
            jax.ShapeDtypeStruct((count, groups * 2 * HD), F32),
        ],
        scratch_shapes=[pltpu.VMEM((2, count, 2 * HD), BF)],
        compiler_params=params(),
        cost_estimate=cost(area * 1024, 4 * joined.size, area),
        name="attend",
    )(info, slopes, joined)


def attend_back_kernel(
    count, size, info, slopes, joined, grad, mixed, sums, out, keys, queries, values, grads, query_grad
):
    pair = pl.program_id(0)
    lane = lax.broadcasted_iota(jnp.int32, (count, HD), 1)
    for hh in range(2):
        base = 3 * HD * hh
        half = slice(hh * HD, (hh + 1) * HD)
        extra = key_extra(count, slopes[2 * pair + hh], info[1])
        keys[hh] = jnp.concatenate([joined[:, base + HD : base + 2 * HD], extra], 1)
        query = (joined[:, base : base + HD].astype(F32) * 0.125).astype(BF)
        high, mid, low = three(-sums[:, half])
        extra = spread(lane, jnp.where(lane < 4, 1.0, 0.0), [(4, high), (5, mid), (6, low)])
        queries[hh] = jnp.concatenate([query, extra], 1)
        part = grad[:, half]
        inner = jnp.sum(part.astype(F32) * mixed[:, half].astype(F32), axis=1, keepdims=True)
        high, mid, low = three(jnp.broadcast_to(-inner, (count, HD)))
        extra = spread(lane, jnp.zeros((count, HD), F32), [(0, high), (1, mid), (2, low)])
        grads[hh] = jnp.concatenate([part, extra], 1)
        ones = jnp.where(lane < 3, 1.0, 0.0).astype(BF)
        values[hh] = jnp.concatenate([joined[:, base + 2 * HD : base + 3 * HD], ones], 1)
    key_at = lax.broadcasted_iota(jnp.int32, (size, size), 0)
    query_at = lax.broadcasted_iota(jnp.int32, (size, size), 1)
    blocks = count // size
    for j in range(blocks):
        ks = slice(j * size, (j + 1) * size)
        pieces = []
        for hh in range(2):
            key_sum = None
            for i in range(j, blocks):
                qs = slice(i * size, (i + 1) * size)
                probs = jnp.exp(dg(keys[hh, ks], queries[hh, qs], NT))
                if i == j:
                    probs = jnp.where(key_at <= query_at, probs, 0.0)
                slope = (probs * dg(values[hh, ks], grads[hh, qs], NT)).astype(BF)
                value_part = dg(probs.astype(BF), grads[hh, qs], NN)
                key_part = dg(slope, queries[hh, qs], NN)
                query_part = dg(keys[hh, ks], slope, TN)
                value_sum = value_part if key_sum is None else value_sum + value_part
                key_sum = key_part if key_sum is None else key_sum + key_part
                query_grad[hh, :, qs] = query_part if j == 0 else query_grad[hh, :, qs] + query_part
            pieces += [jnp.zeros((size, HD), F32), key_sum[:, :HD], value_sum[:, :HD]]
        out[ks] = jnp.concatenate(pieces, 1).astype(BF)
    for hh in range(2):
        base = 3 * HD * hh
        out[:, base : base + HD] = (query_grad[hh].T[:, :HD] * 0.125).astype(BF)


def attend_back(joined, grad, mixed, sums, info, slopes):
    count, width = joined.shape
    groups = width // (6 * HD)
    smem = pl.BlockSpec(memory_space=pltpu.SMEM)
    wide = pl.BlockSpec((count, 6 * HD), lambda p: (0, p))
    narrow = pl.BlockSpec((count, 2 * HD), lambda p: (0, p))
    area = count * count * groups
    return pl.pallas_call(
        functools.partial(attend_back_kernel, count, min(512, count)),
        grid=(groups,),
        in_specs=[smem, smem, wide, narrow, narrow, narrow],
        out_specs=wide,
        out_shape=jax.ShapeDtypeStruct((count, width), BF),
        scratch_shapes=[pltpu.VMEM((2, count, 2 * HD), BF)] * 4 + [pltpu.VMEM((2, 2 * HD, count), F32)],
        compiler_params=params(),
        cost_estimate=cost(area * 2560, 8 * joined.size, area),
        name="attend_back",
    )(info, slopes, joined, grad, mixed, sums)


def middle_kernel(ns, nb, rows, cw, info, x, vecs, *refs):
    mixed = refs[:ns]
    weights = refs[ns : 2 * ns]
    merged, resid, second, full = refs[2 * ns :]

    @pl.when(pl.program_id(0) == 0)
    def _():
        for rel in range(ns):
            col = pl.ds(pl.multiple_of((info[0] ^ rel) * cw, cw), cw)
            for k in range(nb):
                full[k * rows : (k + 1) * rows, col] = weights[rel][info[2 + k]]

    for rel in range(ns):
        col = pl.ds(pl.multiple_of((info[0] ^ rel) * cw, cw), cw)
        merged[:, col] = mixed[rel][...]
    value = x[...].astype(F32) + dg(merged[...], full[...], NN) + vecs[4:5]
    resid[...] = value
    unit, _ = norm_parts(value)
    second[...] = (unit * vecs[5:6] + vecs[6:7]).astype(BF)


def middle_call(info, x, vecs, mixed, weights):
    tok, dim = x.shape
    ns = len(mixed)
    nb, rows, cw = weights[0].shape
    tile = min(256, tok)
    whole = lambda shape: pl.BlockSpec(shape, lambda i, info: (0,) * len(shape), pipeline_mode=pl.Buffered(1))
    part = lambda width: pl.BlockSpec((tile, width), lambda i, info: (i, 0))
    return pl.pallas_call(
        functools.partial(middle_kernel, ns, nb, rows, cw),
        grid_spec=pltpu.PrefetchScalarGridSpec(
            num_scalar_prefetch=1,
            grid=(tok // tile,),
            in_specs=[part(dim), whole(vecs.shape)] + [part(cw)] * ns + [whole((nb, rows, cw))] * ns,
            out_specs=[part(dim), part(dim), part(dim), whole((dim, dim))],
        ),
        out_shape=[
            jax.ShapeDtypeStruct((tok, dim), BF),
            jax.ShapeDtypeStruct((tok, dim), F32),
            jax.ShapeDtypeStruct((tok, dim), BF),
            jax.ShapeDtypeStruct((dim, dim), BF),
        ],
        compiler_params=params(40),
        cost_estimate=cost(2 * tok * dim * dim, 12 * tok * dim + 4 * dim * dim),
        name="middle",
    )(info, x, vecs, *mixed, *weights)


def feed_kernel(nt, nb, rows, units, info, sa, sb, ca, cb, expand, shrink, ebias, activ, pre_grad, out, back, bgrad, wide, tall):
    step = pl.program_id(0)

    @pl.when(step == 0)
    def _():
        for k in range(nb):
            wide[k * rows : (k + 1) * rows] = expand[info[2 + k]]
            tall[k * units : (k + 1) * units] = shrink[info[2 + k]]
        bgrad[...] = jnp.zeros_like(bgrad)

    def work(second, cot):
        pre = dg(second[...], wide[...], NN) + ebias[...]
        square = pre * pre
        bend = jnp.tanh(0.7978845608028654 * pre * (1.0 + 0.044715 * square))
        half = 0.5 + 0.5 * bend
        act = (pre * half).astype(BF)
        activ[...] = act
        out[0] = dg(act, tall[...], NN).astype(BF)
        steep = half + pre * (0.5 - 0.5 * bend * bend) * (0.7978845608028654 + 0.10703222440890037 * square)
        grad = (dg(cot[...], tall[...], NT) * steep).astype(BF)
        pre_grad[...] = grad
        bgrad[...] += jnp.sum(grad.astype(F32), axis=0, keepdims=True)
        back[0] = dg(grad, wide[...], NT).astype(BF)

    @pl.when(step < nt)
    def _():
        work(sa, ca)

    @pl.when(step >= nt)
    def _():
        work(sb, cb)


def feed_call(info, sa, sb, ca, cb, expand, shrink, ebias):
    tok, dim = sa.shape
    nb, rows, ff = expand.shape
    units = shrink.shape[1]
    tile = min(256, tok)
    nt = tok // tile
    whole = lambda shape: pl.BlockSpec(shape, lambda i, info: (0,) * len(shape), pipeline_mode=pl.Buffered(1))
    left = pl.BlockSpec((tile, dim), lambda i, info: (jnp.minimum(i, nt - 1), 0))
    right = pl.BlockSpec((tile, dim), lambda i, info: (jnp.maximum(i - nt, 0), 0))
    flat = pl.BlockSpec((tile, ff), lambda i, info: (i, 0))
    part = pl.BlockSpec((1, tile, dim), lambda i, info: (lax.div(i, nt), lax.rem(i, nt), 0))

    return pl.pallas_call(
        functools.partial(feed_kernel, nt, nb, rows, units),
        grid_spec=pltpu.PrefetchScalarGridSpec(
            num_scalar_prefetch=1,
            grid=(2 * nt,),
            in_specs=[left, right, left, right, whole(expand.shape), whole(shrink.shape), whole(ebias.shape)],
            out_specs=[flat, flat, part, part, pl.BlockSpec((1, ff), lambda i, info: (0, 0))],
            scratch_shapes=[pltpu.VMEM((dim, ff), BF), pltpu.VMEM((ff, dim), BF)],
        ),
        out_shape=[
            jax.ShapeDtypeStruct((2 * tok, ff), BF),
            jax.ShapeDtypeStruct((2 * tok, ff), BF),
            jax.ShapeDtypeStruct((2, tok, dim), BF),
            jax.ShapeDtypeStruct((2, tok, dim), BF),
            jax.ShapeDtypeStruct((1, ff), F32),
        ],
        compiler_params=params(),
        cost_estimate=cost(16 * tok * dim * ff, 16 * tok * dim + 8 * dim * ff, 2 * tok * ff),
        name="feed",
    )(info, sa, sb, ca, cb, expand, shrink, ebias)


def wgrad_kernel(count, nb, rows, tile, split, info, *refs):
    lefts = refs[:count]
    rights = refs[count : 2 * count]
    out = refs[2 * count]
    total = dg(lefts[0][...], rights[0][...], TN)
    for at in range(1, count):
        total += dg(lefts[at][...], rights[at][...], TN)
    first = pl.program_id(0) * (tile // rows)
    if split == 1:
        total = total.astype(BF)
        for k in range(tile // rows):
            out[info[2 + first + k]] = total[k * rows : (k + 1) * rows]
    else:
        held = refs[2 * count + 1]
        held[...] = total
        cw = total.shape[1] // split
        for rel in range(split):
            col = pl.ds(pl.multiple_of((info[0] ^ rel) * cw, cw), cw)
            value = held[:, col].astype(BF)
            for k in range(tile // rows):
                out[rel, info[2 + first + k]] = value[k * rows : (k + 1) * rows]


def wgrad_call(info, lefts, rights, nb, split=1):
    dim = lefts[0].shape[1]
    width = rights[0].shape[1]
    rows = dim // nb
    tile = 256
    tok = sum(a.shape[0] for a in lefts)
    shape = (nb, rows, width) if split == 1 else (split, nb, rows, width // split)
    whole = lambda shape: pl.BlockSpec(shape, lambda i, info: (0,) * len(shape), pipeline_mode=pl.Buffered(1))
    return pl.pallas_call(
        functools.partial(wgrad_kernel, len(lefts), nb, rows, tile, split),
        grid_spec=pltpu.PrefetchScalarGridSpec(
            num_scalar_prefetch=1,
            grid=(dim // tile,),
            in_specs=[pl.BlockSpec((a.shape[0], tile), lambda i, info: (0, i)) for a in lefts]
            + [whole(b.shape) for b in rights],
            out_specs=pl.BlockSpec(shape, lambda i, info: (0,) * len(shape)),
            scratch_shapes=[] if split == 1 else [pltpu.VMEM((tile, width), F32)],
        ),
        out_shape=jax.ShapeDtypeStruct(shape, BF),
        compiler_params=params(),
        cost_estimate=cost(2 * tok * dim * width, 2 * tok * (dim + width) + 2 * dim * width),
        name="weight_grad",
    )(info, *lefts, *rights)


def turn_kernel(ns, cw, info, ga, gb, resid, cot, vecs, full, resid_grad, branch, mixed_grad, sums, held):
    @pl.when(pl.program_id(0) == 0)
    def _():
        sums[...] = jnp.zeros_like(sums)

    grad = ga[...].astype(F32) + gb[...].astype(F32)
    unit, scale = norm_parts(resid[...])
    outer = cot[...].astype(F32)
    value = outer + norm_back(grad, unit, scale, vecs[5:6])
    resid_grad[...] = value
    low = value.astype(BF)
    branch[...] = low
    held[...] = dg(low, full[...], NT).astype(BF)
    for rel in range(ns):
        col = pl.ds(pl.multiple_of((info[0] ^ rel) * cw, cw), cw)
        mixed_grad[rel] = held[:, col]
    for at, term in enumerate((grad * unit, grad, low.astype(F32), outer)):
        sums[at : at + 1] += jnp.sum(term, axis=0, keepdims=True)


def turn_call(info, ga, gb, resid, cot, vecs, full, ns):
    tok, dim = resid.shape
    cw = dim // ns
    tile = min(256, tok)
    whole = lambda shape: pl.BlockSpec(shape, lambda i, info: (0,) * len(shape), pipeline_mode=pl.Buffered(1))
    part = pl.BlockSpec((tile, dim), lambda i, info: (i, 0))
    return pl.pallas_call(
        functools.partial(turn_kernel, ns, cw),
        grid_spec=pltpu.PrefetchScalarGridSpec(
            num_scalar_prefetch=1,
            grid=(tok // tile,),
            in_specs=[part, part, part, part, whole(vecs.shape), whole(full.shape)],
            out_specs=[
                part,
                part,
                pl.BlockSpec((ns, tile, cw), lambda i, info: (0, i, 0)),
                pl.BlockSpec((8, dim), lambda i, info: (0, 0)),
            ],
            scratch_shapes=[pltpu.VMEM((tile, dim), BF)],
        ),
        out_shape=[
            jax.ShapeDtypeStruct((tok, dim), F32),
            jax.ShapeDtypeStruct((tok, dim), BF),
            jax.ShapeDtypeStruct((ns, tok, cw), BF),
            jax.ShapeDtypeStruct((8, dim), F32),
        ],
        compiler_params=params(40),
        cost_estimate=cost(2 * tok * dim * dim, 16 * tok * dim + 2 * dim * dim),
        name="turn",
    )(info, ga, gb, resid, cot, vecs, full)


def last_kernel(nb, rows, tok_tiles, info, joined_grad, normed, weight, out, sums, sides, full):
    @pl.when(pl.program_id(0) == 0)
    def _():
        for k in range(nb):
            full[k * rows : (k + 1) * rows] = weight[info[2 + k], :rows]
        sums[...] = jnp.zeros_like(sums)
        sides[...] = jnp.zeros_like(sides)

    grad = dg(joined_grad[...], full[...], NT)
    out[0] = grad.astype(BF)
    sums[0:1] += jnp.sum(grad * normed[...].astype(F32), axis=0, keepdims=True)
    sums[1:2] += jnp.sum(grad, axis=0, keepdims=True)
    sides[...] += jnp.sum(joined_grad[...].astype(F32), axis=0, keepdims=True)


def last_call(info, joined_grad, normed, weight, ns):
    count, cols = joined_grad.shape
    dim = normed.shape[1]
    nb = weight.shape[0]
    rows = dim // nb
    tok = count // ns
    tile = min(256, tok)
    nt = tok // tile
    whole = lambda shape: pl.BlockSpec(shape, lambda i, info: (0,) * len(shape), pipeline_mode=pl.Buffered(1))
    return pl.pallas_call(
        functools.partial(last_kernel, nb, rows, nt),
        grid_spec=pltpu.PrefetchScalarGridSpec(
            num_scalar_prefetch=1,
            grid=(ns * nt,),
            in_specs=[
                pl.BlockSpec((tile, cols), lambda i, info: (i, 0)),
                pl.BlockSpec((tile, dim), lambda i, info: (i, 0)),
                whole(weight.shape),
            ],
            out_specs=[
                pl.BlockSpec((1, tile, dim), lambda i, info: (info[0] ^ lax.div(i, nt), lax.rem(i, nt), 0)),
                pl.BlockSpec((8, dim), lambda i, info: (0, 0)),
                pl.BlockSpec((1, cols), lambda i, info: (0, 0)),
            ],
            scratch_shapes=[pltpu.VMEM((dim, cols), BF)],
        ),
        out_shape=[
            jax.ShapeDtypeStruct((ns, tok, dim), BF),
            jax.ShapeDtypeStruct((8, dim), F32),
            jax.ShapeDtypeStruct((1, cols), F32),
        ],
        compiler_params=params(40),
        cost_estimate=cost(2 * count * dim * cols, 2 * count * (2 * dim + cols)),
        name="last",
    )(info, joined_grad, normed, weight)


def end_kernel(ga, gb, x, resid_grad, vecs, out):
    grad = ga[...].astype(F32) + gb[...].astype(F32)
    unit, scale = norm_parts(x[...].astype(F32))
    out[...] = resid_grad[...] + norm_back(grad, unit, scale, vecs[0:1])


def end_call(ga, gb, x, resid_grad, vecs):
    tok, dim = x.shape
    tile = min(128, tok)
    part = pl.BlockSpec((tile, dim), lambda i: (i, 0))
    return pl.pallas_call(
        end_kernel,
        grid=(tok // tile,),
        in_specs=[part, part, part, part, pl.BlockSpec(vecs.shape, lambda i: (0, 0))],
        out_specs=part,
        out_shape=jax.ShapeDtypeStruct((tok, dim), F32),
        compiler_params=params(40),
        cost_estimate=cost(20 * tok * dim, 14 * tok * dim),
        name="end",
    )(ga, gb, x, resid_grad, vecs)


def body(
    layer_input,
    lengths,
    first_gain,
    first_shift,
    joined_weight,
    joined_bias,
    output_weight,
    output_bias,
    second_gain,
    second_shift,
    expand_weight,
    expand_bias,
    shrink_weight,
    shrink_bias,
    out_grad,
):
    ns = lax.axis_size("seq")
    nb = lax.axis_size("batch")
    si = lax.axis_index("seq")
    bi = lax.axis_index("batch")
    tok = layer_input.shape[1]
    dim = layer_input.shape[2]
    count = ns * tok
    heads = H // ns
    cols = 3 * HD * heads
    cw = HD * heads
    rows = dim // nb
    ff = expand_weight.shape[1] // ns
    units = ff // nb
    x = layer_input[0]
    cot = out_grad[0]
    info = jnp.concatenate([jnp.stack([si, lengths[0]]), place_table(bi, nb)]).astype(jnp.int32)
    head_ids = si * heads + jnp.arange(heads, dtype=jnp.int32) + 1
    slopes = 2.0 ** (-8.0 * head_ids.astype(F32) / H)

    smalls = jnp.concatenate(
        [first_gain, first_shift, joined_bias, output_bias, second_gain, second_shift, expand_bias, shrink_bias]
    )
    wide = -(-smalls.shape[0] // cols)
    pad = -(-wide // 16) * 16
    small_rows = jnp.pad(smalls, (0, pad * cols - smalls.shape[0])).reshape(pad, cols)
    joined_part = lax.dynamic_slice(joined_weight, (0, si * cols), (rows, cols))
    group_one = gather_stack(jnp.concatenate([joined_part, small_rows], 0), "batch", nb)
    xs = gather_rel(x, "seq", ns)
    cots = gather_rel(cot, "seq", ns)
    expand_part = lax.dynamic_slice(
        expand_weight.reshape(rows, nb, ns, units), (0, 0, si, 0), (rows, nb, 1, units)
    ).reshape(rows, ff)
    shrink_part = lax.dynamic_slice(shrink_weight, (si * units, 0), (units, dim))
    outw_part = lax.dynamic_slice(output_weight, (0, si * cw), (rows, cw))
    expand_all = gather_stack(expand_part, "batch", nb)
    shrink_all = gather_stack(shrink_part, "batch", nb)
    outw_all = gather_rel(gather_stack(outw_part, "batch", nb), "seq", ns)

    places = place_table(bi, nb)
    flat = group_one[:, rows : rows + wide].reshape(nb, wide * cols)[:, : smalls.shape[0]]
    flat = jnp.take(flat, places, axis=0).astype(F32)
    vecs = flat.reshape(nb, 12, rows).transpose(1, 0, 2).reshape(12, dim)
    low = vecs[2:4].reshape(2, nb, rows).transpose(1, 0, 2).reshape(2 * dim)
    low = lax.dynamic_slice(low, (si * 2 * cw,), (2 * cw,)).reshape(heads, 2, HD)
    jbias = jnp.stack([low[:, 0], jnp.zeros_like(low[:, 0]), low[:, 1]], 1).reshape(1, cols)
    ebias = vecs[7:11].reshape(4, nb, rows).transpose(1, 0, 2).reshape(nb, ns, units)
    ebias = lax.dynamic_slice(ebias, (0, si, 0), (nb, 1, units)).reshape(1, ff)
    held = None
    for rel in range(0, ns, 2):
        held = first_call(rel, xs[rel], xs[rel + 1], info, group_one, vecs, jbias, held, ns)
    normed, joined = held
    mixed, log_sums = attend(joined, info, slopes)

    def to_tokens(values):
        out = []
        for rel in range(ns):
            block = lax.dynamic_slice(values, ((si ^ rel) * tok, 0), (tok, values.shape[1]))
            out.append(lax.ppermute(block, "seq", pairs(ns, rel)) if rel else block)
        return out

    merged, resid, second, outw_full = middle_call(
        info, x, vecs, to_tokens(mixed), [outw_all[rel] for rel in range(ns)]
    )
    seconds = gather_rel(second, "seq", ns)
    out_parts = {}
    back_parts = {}
    activs = []
    pre_grads = []
    bias_sum = 0.0
    for rel in range(0, ns, 2):
        activ, pre_grad, out, back, bgrad = feed_call(
            info, seconds[rel], seconds[rel + 1], cots[rel], cots[rel + 1], expand_all, shrink_all, ebias
        )
        activs.append(activ)
        pre_grads.append(pre_grad)
        bias_sum = bias_sum + bgrad
        for at in range(2):
            out_parts[rel + at] = out[at]
            back_parts[rel + at] = back[at]
    back_a, back_b = scatter_rel(back_parts, "seq", ns, last=False)
    resid_grad, branch, mixed_grad, turn_sums = turn_call(info, back_a, back_b, resid, cot, vecs, outw_full, ns)
    out_a, out_b = scatter_rel(out_parts, "seq", ns, last=False)
    layer_output = (resid + out_a.astype(F32) + out_b.astype(F32) + vecs[11:12]).astype(BF)

    pair_of = lambda values: [jnp.concatenate([values[r], values[r + 1]], 0) for r in range(0, ns, 2)]
    shrink_stack = wgrad_call(info, activs, pair_of(cots), nb)
    expand_stack = wgrad_call(info, pair_of(seconds), pre_grads, nb)
    outw_stack = wgrad_call(info, [merged], [branch], nb, split=ns)

    heads_grad = jnp.zeros((count, cw), BF)
    for rel in range(ns):
        block = mixed_grad[rel]
        block = lax.ppermute(block, "seq", pairs(ns, rel)) if rel else block
        heads_grad = lax.dynamic_update_slice(heads_grad, block, ((si ^ rel) * tok, 0))
    joined_grad = attend_back(joined, heads_grad, mixed, log_sums, info, slopes)
    normed_parts, last_sums, sides = last_call(info, joined_grad, normed, group_one, ns)
    norm_a, norm_b = scatter_rel({rel: normed_parts[rel] for rel in range(ns)}, "seq", ns, last=False)
    joined_stack = wgrad_call(info, [normed], [joined_grad], nb)
    input_grad = end_call(norm_a, norm_b, x, resid_grad, vecs)

    shift_one = last_sums[1]
    gain_one = (last_sums[0] - vecs[1] * shift_one) / vecs[0]
    side = sides.reshape(heads, 3, HD)
    side = jnp.stack([side[:, 0], side[:, 2]], 1).reshape(2 * cw)
    side = lax.dynamic_update_slice(jnp.zeros((2 * dim,), F32), side, (si * 2 * cw,))
    spread_bias = lax.dynamic_update_slice(
        jnp.zeros((nb, ns, units), F32), bias_sum.reshape(nb, 1, units), (0, si, 0)
    )
    pieces = [gain_one, shift_one, side, turn_sums[2], turn_sums[0], turn_sums[1], spread_bias, turn_sums[3]]
    shares = jnp.concatenate([piece.reshape(nb, -1) for piece in pieces], 1).astype(BF)
    owners = bi ^ jnp.array(sorted(range(nb), key=lambda rel: place_of(rel, nb)), jnp.int32)
    shares = scatter_stack(jnp.take(shares, owners, axis=0), "batch", nb)
    for bit in bits_low_last(ns)[::-1]:
        shares = add16(shares, lax.ppermute(shares, "seq", pairs(ns, bit)))
    shares = shares.astype(F32)

    def collect(block):
        parts = gather_rel(block, "seq", ns)
        stack = jnp.stack([parts[rel] for rel in range(ns)])
        return jnp.take(stack, jnp.arange(ns, dtype=jnp.int32) ^ si, axis=0).astype(F32)

    shrink_grad = collect(scatter_stack(shrink_stack, "batch", nb)).reshape(ns * units, dim)
    expand_grad = collect(scatter_stack(expand_stack, "batch", nb).reshape(rows, nb, units))
    expand_grad = expand_grad.transpose(1, 2, 0, 3).reshape(rows, ns * ff)
    outw_share = scatter_rel({rel: outw_stack[rel] for rel in range(ns)}, "seq", ns)
    outw_grad = collect(scatter_stack(outw_share, "batch", nb)).transpose(1, 0, 2).reshape(rows, dim)
    joined_wgrad = collect(scatter_stack(joined_stack, "batch", nb)).transpose(1, 0, 2).reshape(rows, ns * cols)
    small = []
    at = 0
    for size in (1, 1, 2, 1, 1, 1, 4, 1):
        small.append(shares[at * rows : (at + size) * rows])
        at += size
    return (
        layer_output[None],
        input_grad[None],
        small[0],
        small[1],
        joined_wgrad,
        small[2],
        outw_grad,
        small[3],
        small[4],
        small[5],
        expand_grad,
        small[6],
        shrink_grad,
        small[7],
    )


def solution(mesh):
    row = P("batch")
    mat = P("batch", None)
    act = P("batch", "seq", None)
    return jax.shard_map(
        body,
        mesh=mesh,
        in_specs=(act, row, row, row, mat, row, mat, row, row, row, mat, row, mat, row, act),
        out_specs=(act, act, row, row, mat, row, mat, row, row, row, mat, row, mat, row),
        check_vma=False,
    )
```

time: 1200 us -> 543 us (0.45)
  waiting for transfers between devices: 450 us -> 194 us
  blocking collectives: 234 us -> 0 us
  matrix products: 194 us -> 0 us
  Pallas kernels: 0 us -> 149 us
  other arithmetic: 151 us -> 53 us
  local copies, waits for them, and re-layouts: 133 us -> 79.7 us
  starting transfers between devices: 13.5 us -> 56.3 us
  between operations: 18.3 us -> 2.96 us
    reduce_scatter x4 -> x0, waiting for transfers between devices: 359 us -> none  [the longest x1 152 us: body(): lax.psum_scatter(expand_wgrad.astype(jnp.bfloat16), 'batch', scatter_dime...]
    dot_general x36 -> x0, matrix products: 194 us -> none  [the longest x4 22.4 us: attend_back(): jnp.einsum('rqhd,rkhd->rhqk', grad_block, value_rows[:, :block_end], pref...]
    ppermute x0 -> x71, waiting for transfers between devices: none -> 194 us  [the longest x15 84.3 us: scatter_stack(): lax.ppermute(stack[half:], axis, pairs(size, bit))]
    all_gather x8 -> x0, blocking collectives: 152 us -> none  [the longest x1 26.5 us: body(): lax.all_gather(expand_bias, 'batch', axis=0, tiled=True)]
    pallas_call x0 -> x14, Pallas kernels: none -> 149 us  [the longest x1 34.1 us: attend_back(): pl.pallas_call(functools.partial(attend_back_kernel, count, min(512, coun...]
    unnamed x9 -> x4, other arithmetic: 73.8 us -> 0.09 us
    ppermute x0 -> x71, starting transfers between devices: none -> 56.3 us  [the longest x12 19.5 us: gather_stack(): out = jnp.concatenate([out, lax.ppermute(out, axis, pairs(size, bit))], 0)]
    all_gather x4 -> x0, waiting for transfers between devices: 40.8 us -> none  [the longest x1 40.8 us: body(): lax.all_gather(joined_weight, 'batch', axis=0, tiled=True)]
  transfers between devices with their start and end apart: 12 -> 71, of which waited for: 7 -> 21; matrix products, arithmetic and copies ran while one was open for 35% -> 20% of each run, Pallas kernels for 0% -> 27%
where the time goes in v1:
time: 543 us; the launch traced here: 535 us
  waiting for transfers between devices  194 us (36%)
  Pallas kernels  149 us (27%)
  local copies, waits for them, and re-layouts  79.7 us (15%)
  starting transfers between devices  56.3 us (10%)
  other arithmetic  53 us (10%)
    ppermute x15, waiting for transfers between devices, scatter_stack(): lax.ppermute(stack[half:], axis, pairs(size, bit))  84.3 us
    ppermute x12, waiting for transfers between devices, gather_stack(): out = jnp.concatenate([out, lax.ppermute(out, axis, pairs(size, bit))], 0)  65.6 us
    pallas_call x1, Pallas kernels, attend_back(): pl.pallas_call(functools.partial(attend_back_kernel, count, min(512, coun...  34.1 us
    pallas_call x4, Pallas kernels, wgrad_call(): pl.pallas_call(functools.partial(wgrad_kernel, len(lefts), nb, rows, tile...  34 us
    unnamed x138, local copies, waits for them, and re-layouts  33.7 us
    pallas_call x2, Pallas kernels, feed_call(): pl.pallas_call(functools.partial(feed_kernel, nt, nb, rows, units), grid_...  32 us
    ppermute x24, waiting for transfers between devices, gather_rel(): out[rel | bit] = lax.ppermute(out[rel], axis, pairs(size, bit))  22.2 us
    pallas_call x1, Pallas kernels, attend(): pl.pallas_call(functools.partial(attend_kernel, count, min(512, count)),...  20.2 us
  transfers between devices with their start and end apart: 71, of which 21 were waited for; matrix products, arithmetic and copies ran while one was open for 20% of the time, Pallas kernels for 27%

profile of v1, /device:TPU:0, one launch (start us, length us, event | category | flops | bytes accessed | tf_op | source)
XLA Modules:
  0.0 534.7 jit_solution(10779372933247052586)
XLA Ops:
  8.5 3.1 collective-permute-start
  21.2 2.7 collective-permute-start.1
  24.6 14.8 %collective-permute-done.1 = bf16[2,144,768]{2,1,0:T(8,128)(2,1)S(1)} collective-permute-done((bf16[2,144,768]{2,1,0:T(8,128)(2,1)S(1)}, bf16[2,144,768]{2,1,0:T(8,128)(2,1)S(1)}, u32[]{:S(2)}, u32[]{:S(2)}) %collective-permute-start.1) | collective-permute-done | bytes 442400 | tf_op jit(solution)/shard_map/ppermute | solution.py:82
  43.0 3.5 collective-permute-start.10
  54.3 12.7 %collective-permute-done.11 = bf16[4,128,256]{2,1,0:T(8,128)(2,1)} collective-permute-done((bf16[4,128,256]{2,1,0:T(8,128)(2,1)S(1)}, bf16[4,128,256]{2,1,0:T(8,128)(2,1)}, u32[]{:S(2)}, u32[]{:S(2)}) %collective-permute-start.11) | collective-permute-done | bytes 262176 | tf_op jit(solution)/shard_map/ppermute | solution.py:82
  67.1 3.4 collective-permute-start.18
  76.1 5.3 first.2
  81.6 5.5 %first.3 = (bf16[2048,1024]{1,0:T(8,128)(2,1)S(1)}, bf16[2048,768]{1,0:T(8,128)(2,1)S(1)}) custom-call(s32[10]{0:T(128)S(1)} %pad_add_fusion.info, bf16[512,1024]{1,0:T(8,128)(2,1)} %collective-permute-done.3.xa, bf16[512,1024]{1,0:T(8,128)(2,1)} %collective-permute-done.4.xb, ...), custom_call_target="tpu_custom_call", output_to_operand_aliasing={{0}: (6, {}), {1}: (7, {})} | custom-call | flops 1610612736 | bytes 5767168 | tf_op jit(solution)/shard_map/first/pallas_call | solution.py:155
  90.8 13.8 %collective-permute-done.18 = bf16[2,128,1024]{2,1,0:T(8,128)(2,1)} collective-permute-done((bf16[2,128,1024]{2,1,0:T(8,128)(2,1)}, bf16[2,128,1024]{2,1,0:T(8,128)(2,1)}, u32[]{:S(2)}, u32[]{:S(2)}) %collective-permute-start.18) | collective-permute-done | bytes 524320 | tf_op jit(solution)/shard_map/ppermute | solution.py:82
  105.2 20.2 %attend.1 = (bf16[2048,256]{1,0:T(8,128)(2,1)}, f32[2048,256]{1,0:T(8,128)}) custom-call(s32[10]{0:T(128)} %copy-done.20, f32[4]{0:T(128)} %multiply_power_fusion.slopes, bf16[2048,768]{1,0:T(8,128)(2,1)} %copy-done.8), custom_call_target="tpu_custom_call" | custom-call | flops 8589934592 | bytes 6291456 | tf_op jit(solution)/shard_map/attend/pallas_call | solution.py:242
  133.1 5.8 %collective-permute-done.7.refs_2_ = bf16[512,256]{1,0:T(8,128)(2,1)S(1)} collective-permute-done((bf16[512,256]{1,0:T(8,128)(2,1)S(1)}, bf16[512,256]{1,0:T(8,128)(2,1)S(1)}, u32[]{:S(2)}, u32[]{:S(2)}) %collective-permute-start.7) | collective-permute-done | bytes 262176 | tf_op jit(solution)/shard_map/ppermute | solution.py:689
  139.0 4.2 collective-permute-done.8.refs_3_
  144.2 4.0 middle.1
  150.8 3.0 pad_maximum_fusion.3.refs_2_
  154.5 21.9 %collective-permute-done.22 = bf16[4,128,1024]{2,1,0:T(8,128)(2,1)S(1)} collective-permute-done((bf16[4,128,1024]{2,1,0:T(8,128)(2,1)S(1)}, bf16[4,128,1024]{2,1,0:T(8,128)(2,1)S(1)}, u32[]{:S(2)}, u32[]{:S(2)}) %collective-permute-start.22) | collective-permute-done | bytes 1048608 | tf_op jit(solution)/shard_map/ppermute | solution.py:82
  177.9 3.2 pad_maximum_fusion.4.refs_3_
  182.1 16.2 %feed.2 = (bf16[1024,1024]{1,0:T(8,128)(2,1)}, bf16[1024,1024]{1,0:T(8,128)(2,1)}, bf16[2,512,1024]{2,1,0:T(8,128)(2,1)}, bf16[2,512,1024]{2,1,0:T(8,128)(2,1)}, f32[1,1024]{1,0:T(1,128)}) custom-call(s32[10]{0:T(128)} %copy-done.20, bf16[512,1024]{1,0:T(8,128)(2,1)} %copy-done.16, bf16[512,1024]{1,0:T(8,128)(2,1)} %copy-done.49, ...), custom_call_target="tpu_custom_call" | custom-call | flops 8589934592 | bytes 16777216 | tf_op jit(solution)/shard_map/feed/pallas_call | solution.py:419
  203.8 15.9 %feed.3 = (bf16[1024,1024]{1,0:T(8,128)(2,1)}, bf16[1024,1024]{1,0:T(8,128)(2,1)}, bf16[2,512,1024]{2,1,0:T(8,128)(2,1)}, bf16[2,512,1024]{2,1,0:T(8,128)(2,1)}, f32[1,1024]{1,0:T(1,128)}) custom-call(s32[10]{0:T(128)} %copy-done.20, bf16[512,1024]{1,0:T(8,128)(2,1)} %collective-permute-done.24.sa, bf16[512,1024]{1,0:T(8,128)(2,1)} %collective-permute-done.25.sb, ...), custom_call_target="tpu_custom_call" | custom-call | flops 8589934592 | bytes 16777216 | tf_op jit(solution)/shard_map/feed/pallas_call | solution.py:419
  219.6 3.0 pad_maximum_fusion.2.refs_1_
  222.7 9.8 %weight_grad.6 = bf16[8,128,1024]{2,1,0:T(8,128)(2,1)} custom-call(s32[10]{0:T(128)} %copy-done.20, bf16[1024,1024]{1,0:T(8,128)(2,1)} %pad_maximum_fusion.1.refs_0_, bf16[1024,1024]{1,0:T(8,128)(2,1)} %pad_maximum_fusion.2.refs_1_, bf16[1024,1024]{1,0:T(8,128)(2,1)} %get-tuple-element.65.refs_2_, bf16[1024,1024]{1,0:T(8,128)(2,1)} %get-tuple-element.66.refs_3_), custom_call_target="tpu_custom_call" | custom-call | flops 4294967296 | bytes 10485760 | tf_op jit(solution)/shard_map/weight_grad/pallas_call | solution.py:472
  236.2 9.9 %weight_grad.7 = bf16[8,128,1024]{2,1,0:T(8,128)(2,1)} custom-call(s32[10]{0:T(128)} %copy-done.20, bf16[1024,1024]{1,0:T(8,128)(2,1)} %get-tuple-element.67.refs_0_, bf16[1024,1024]{1,0:T(8,128)(2,1)} %get-tuple-element.68.refs_1_, bf16[1024,1024]{1,0:T(8,128)(2,1)} %pad_maximum_fusion.3.refs_2_, bf16[1024,1024]{1,0:T(8,128)(2,1)} %pad_maximum_fusion.4.refs_3_), custom_call_target="tpu_custom_call" | custom-call | flops 4294967296 | bytes 10485760 | tf_op jit(solution)/shard_map/weight_grad/pallas_call | solution.py:472
  252.1 8.9 %collective-permute-done.59 = bf16[4,128,1024]{2,1,0:T(8,128)(2,1)} collective-permute-done((bf16[4,128,1024]{2,1,0:T(8,128)(2,1)}, bf16[4,128,1024]{2,1,0:T(8,128)(2,1)}, u32[]{:S(2)}, u32[]{:S(2)}) %collective-permute-start.59) | collective-permute-done | bytes 1048608 | tf_op jit(solution)/shard_map/ppermute | solution.py:93
  262.7 20.2 %collective-permute-done.65 = bf16[4,128,1024]{2,1,0:T(8,128)(2,1)S(1)} collective-permute-done((bf16[4,128,1024]{2,1,0:T(8,128)(2,1)S(1)}, bf16[4,128,1024]{2,1,0:T(8,128)(2,1)S(1)}, u32[]{:S(2)}, u32[]{:S(2)}) %collective-permute-start.65) | collective-permute-done | bytes 1048608 | tf_op jit(solution)/shard_map/ppermute | solution.py:93
  284.8 13.4 %collective-permute-done.60 = bf16[2,128,1024]{2,1,0:T(8,128)(2,1)S(1)} collective-permute-done((bf16[2,128,1024]{2,1,0:T(8,128)(2,1)S(1)}, bf16[2,128,1024]{2,1,0:T(8,128)(2,1)S(1)}, u32[]{:S(2)}, u32[]{:S(2)}) %collective-permute-start.60) | collective-permute-done | bytes 524320 | tf_op jit(solution)/shard_map/ppermute | solution.py:93
  298.4 10.9 %collective-permute-done.66 = bf16[2,128,1024]{2,1,0:T(8,128)(2,1)S(1)} collective-permute-done((bf16[2,128,1024]{2,1,0:T(8,128)(2,1)S(1)}, bf16[2,128,1024]{2,1,0:T(8,128)(2,1)S(1)}, u32[]{:S(2)}, u32[]{:S(2)}) %collective-permute-start.66) | collective-permute-done | bytes 524320 | tf_op jit(solution)/shard_map/ppermute | solution.py:93
  311.8 3.2 collective-permute-done.61
  316.6 4.0 collective-permute-done.67
  320.7 4.9 turn.1
  330.3 5.9 %weight_grad.5 = bf16[4,8,128,256]{3,2,1,0:T(8,128)(2,1)} custom-call(s32[10]{0:T(128)} %copy-done.20, bf16[512,1024]{1,0:T(8,128)(2,1)} %copy-done.11, bf16[512,1024]{1,0:T(8,128)(2,1)} %copy-done.14), custom_call_target="tpu_custom_call" | custom-call | flops 1073741824 | bytes 4194304 | tf_op jit(solution)/shard_map/weight_grad/pallas_call | solution.py:472
  340.1 3.3 fusion.6
  345.3 2.7 collective-permute-done.34
  348.6 4.2 collective-permute-done.35
  354.4 34.1 %attend_back.1.joined_grad.refs_1_ = bf16[2048,768]{1,0:T(8,128)(2,1)} custom-call(s32[10]{0:T(128)} %copy-done.20, f32[4]{0:T(128)} %multiply_power_fusion.slopes, bf16[2048,768]{1,0:T(8,128)(2,1)} %copy-done.8, bf16[2048,256]{1,0:T(8,128)(2,1)} %copy-done.46, bf16[2048,256]{1,0:T(8,128)(2,1)} %get-tuple-element.45.mixed, f32[2048,256]{1,0:T(8,128)} %get-tuple-element.54.sums), custom_call_target="tpu_custom_call" | custom-call | flops 21474836480 | bytes 12582912 | tf_op jit(solution)/shard_map/attend_back/pallas_call | solution.py:313
  390.4 6.1 %last.1 = (bf16[4,512,1024]{2,1,0:T(8,128)(2,1)S(1)}, f32[8,1024]{1,0:T(8,128)S(1)}, f32[1,768]{1,0:T(1,128)S(1)}) custom-call(s32[10]{0:T(128)S(1)} %copy-done.23, bf16[2048,768]{1,0:T(8,128)(2,1)S(1)} %copy-done.24, bf16[2048,1024]{1,0:T(8,128)(2,1)S(1)} %copy-done.6, bf16[8,144,768]{2,1,0:T(8,128)(2,1)S(1)} %pad_maximum_fusion.5.weight), custom_call_target="tpu_custom_call" | custom-call | flops 3221225472 | bytes 11534336 | tf_op jit(solution)/shard_map/last/pallas_call | solution.py:565
  404.7 2.8 convert_bitcast_fusion
  407.5 3.0 slice_bitcast_fusion
  410.6 3.6 collective-permute-start.40
  414.2 8.4 %weight_grad.4 = bf16[8,128,768]{2,1,0:T(8,128)(2,1)} custom-call(s32[10]{0:T(128)} %copy-done.20, bf16[2048,1024]{1,0:T(8,128)(2,1)} %copy-done.5, bf16[2048,768]{1,0:T(8,128)(2,1)} %attend_back.1.joined_grad.refs_1_), custom_call_target="tpu_custom_call" | custom-call | flops 3221225472 | bytes 8912896 | tf_op jit(solution)/shard_map/weight_grad/pallas_call | solution.py:472
  433.7 2.6 copy.38
  436.3 3.1 reshape.188
  440.9 4.7 collective-permute-done.52
  452.0 2.8 collective-permute-done.53
  456.8 18.5 %collective-permute-done.54 = bf16[2,128,256]{2,1,0:T(8,128)(2,1)S(1)} collective-permute-done((bf16[2,128,256]{2,1,0:T(8,128)(2,1)S(1)}, bf16[2,128,256]{2,1,0:T(8,128)(2,1)S(1)}, u32[]{:S(2)}, u32[]{:S(2)}) %collective-permute-start.54) | collective-permute-done | bytes 131104 | tf_op jit(solution)/shard_map/ppermute | solution.py:93
  481.0 3.6 fusion
  489.6 21.7 %collective-permute-done.48 = bf16[128,768]{1,0:T(8,128)(2,1)} collective-permute-done((bf16[128,768]{1,0:T(8,128)(2,1)S(1)}, bf16[128,768]{1,0:T(8,128)(2,1)}, u32[]{:S(2)}, u32[]{:S(2)}) %collective-permute-start.48) | collective-permute-done | bytes 196640 | tf_op jit(solution)/shard_map/ppermute | solution.py:101
  520.3 3.0 copy.36
  523.3 3.0 copy.39
  531.4 2.9 end.1
  (387 shorter events, 144.5 us)
Async XLA Ops:
  11.6 59.8 %collective-permute-start.3 = (bf16[512,1024]{1,0:T(8,128)(2,1)}, bf16[512,1024]{1,0:T(8,128)(2,1)}, u32[]{:S(2)}, u32[]{:S(2)}) collective-permute-start(bf16[512,1024]{1,0:T(8,128)(2,1)} %bitcast.152), channel_id=1, source_target_pairs={{0,16},{8,24},{16,0},{24,8},{1,17},{9,25},{17,1},{25,9},{2,18},{10... | collective-permute-start | bytes 3145736 | tf_op jit(solution)/shard_map/ppermute | solution.py:101
  14.0 29.0 %collective-permute-start.9 = (bf16[1,128,256]{2,1,0:T(8,128)(2,1)S(1)}, bf16[1,128,256]{2,1,0:T(8,128)(2,1)S(1)}, u32[]{:S(2)}, u32[]{:S(2)}) collective-permute-start(bf16[1,128,256]{2,1,0:T(8,128)(2,1)S(1)} %dynamic-slice_bitcast_fusion.1), channel_id=1, source_target_pairs={{0,2},{1,3},{2,0},{3,1},{4,6},{5,7},{6,4},{7,5},{8,10},{9,11},{10,... | collective-permute-start | bytes 196616 | tf_op jit(solution)/shard_map/ppermute | solution.py:82
  17.9 33.0 %collective-permute-start.17 = (bf16[1,128,1024]{2,1,0:T(8,128)(2,1)S(1)}, bf16[1,128,1024]{2,1,0:T(8,128)(2,1)}, u32[]{:S(2)}, u32[]{:S(2)}) collective-permute-start(bf16[1,128,1024]{2,1,0:T(8,128)(2,1)S(1)} %broadcast_in_dim_reshape.3), channel_id=1, source_target_pairs={{0,2},{1,3},{2,0},{3,1},{4,6},{5,7},{6,4},{7,5},{8,10},{9,11},{10,... | collective-permute-start | bytes 786440 | tf_op jit(solution)/shard_map/ppermute | solution.py:82
  19.6 33.3 %collective-permute-start.20 = (bf16[1,128,1024]{2,1,0:T(8,128)(2,1)S(1)}, bf16[1,128,1024]{2,1,0:T(8,128)(2,1)S(1)}, u32[]{:S(2)}, u32[]{:S(2)}) collective-permute-start(bf16[1,128,1024]{2,1,0:T(8,128)(2,1)S(1)} %dynamic-slice_bitcast_fusion), channel_id=1, source_target_pairs={{0,2},{1,3},{2,0},{3,1},{4,6},{5,7},{6,4},{7,5},{8,10},{9,11},{10,... | collective-permute-start | bytes 786440 | tf_op jit(solution)/shard_map/ppermute | solution.py:82
  21.2 18.2 %collective-permute-start.1 = (bf16[2,144,768]{2,1,0:T(8,128)(2,1)S(1)}, bf16[2,144,768]{2,1,0:T(8,128)(2,1)S(1)}, u32[]{:S(2)}, u32[]{:S(2)}) collective-permute-start(bf16[2,144,768]{2,1,0:T(8,128)(2,1)S(1)} %pad_maximum_fusion.15), channel_id=1, source_target_pairs={{0,4},{1,5},{2,6},{3,7},{4,0},{5,1},{6,2},{7,3},{8,12},{9,13},{10,... | collective-permute-start | bytes 1327112 | tf_op jit(solution)/shard_map/ppermute | solution.py:82
  41.5 30.7 %collective-permute-start.2 = (bf16[4,144,768]{2,1,0:T(8,128)(2,1)}, bf16[4,144,768]{2,1,0:T(8,128)(2,1)S(1)}, u32[]{:S(2)}, u32[]{:S(2)}) collective-permute-start(bf16[4,144,768]{2,1,0:T(8,128)(2,1)} %pad_maximum_fusion.10), channel_id=1, source_target_pairs={{0,1},{1,0},{2,3},{3,2},{4,5},{5,4},{6,7},{7,6},{8,9},{9,8},{10,11... | collective-permute-start | bytes 2654216 | tf_op jit(solution)/shard_map/ppermute | solution.py:82
  50.1 17.0 %collective-permute-start.11 = (bf16[4,128,256]{2,1,0:T(8,128)(2,1)S(1)}, bf16[4,128,256]{2,1,0:T(8,128)(2,1)}, u32[]{:S(2)}, u32[]{:S(2)}) collective-permute-start(bf16[4,128,256]{2,1,0:T(8,128)(2,1)S(1)} %pad_maximum_fusion.16), channel_id=1, source_target_pairs={{0,1},{1,0},{2,3},{3,2},{4,5},{5,4},{6,7},{7,6},{8,9},{9,8},{10,11... | collective-permute-start | bytes 786440 | tf_op jit(solution)/shard_map/ppermute | solution.py:82
  50.9 24.7 %collective-permute-start.5 = (bf16[512,1024]{1,0:T(8,128)(2,1)S(1)}, bf16[512,1024]{1,0:T(8,128)(2,1)}, u32[]{:S(2)}, u32[]{:S(2)}) collective-permute-start(bf16[512,1024]{1,0:T(8,128)(2,1)S(1)} %bitcast.153), channel_id=1, source_target_pairs={{0,8},{8,0},{16,24},{24,16},{1,9},{9,1},{17,25},{25,17},{2,10},{10... | collective-permute-start | bytes 3145736 | tf_op jit(solution)/shard_map/ppermute | solution.py:101
  52.8 77.0 %collective-permute-start.26 = (bf16[512,1024]{1,0:T(8,128)(2,1)}, bf16[512,1024]{1,0:T(8,128)(2,1)}, u32[]{:S(2)}, u32[]{:S(2)}) collective-permute-start(bf16[512,1024]{1,0:T(8,128)(2,1)} %bitcast.9.ca.cot), channel_id=1, source_target_pairs={{0,16},{8,24},{16,0},{24,8},{1,17},{9,25},{17,1},{25,9},{2,18},{10... | collective-permute-start | bytes 3145736 | tf_op jit(solution)/shard_map/ppermute | solution.py:101
  67.1 37.6 %collective-permute-start.18 = (bf16[2,128,1024]{2,1,0:T(8,128)(2,1)}, bf16[2,128,1024]{2,1,0:T(8,128)(2,1)}, u32[]{:S(2)}, u32[]{:S(2)}) collective-permute-start(bf16[2,128,1024]{2,1,0:T(8,128)(2,1)} %pad_maximum_fusion.13), channel_id=1, source_target_pairs={{0,4},{1,5},{2,6},{3,7},{4,0},{5,1},{6,2},{7,3},{8,12},{9,13},{10,... | collective-permute-start | bytes 1572872 | tf_op jit(solution)/shard_map/ppermute | solution.py:82
  71.5 33.2 %collective-permute-start.13 = (bf16[8,128,256]{2,1,0:T(8,128)(2,1)S(1)}, bf16[8,128,256]{2,1,0:T(8,128)(2,1)}, u32[]{:S(2)}, u32[]{:S(2)}) collective-permute-start(bf16[8,128,256]{2,1,0:T(8,128)(2,1)S(1)} %pad_maximum_fusion.12.refs_4_), channel_id=1, source_target_pairs={{0,16},{8,24},{16,0},{24,8},{1,17},{9,25},{17,1},{25,9},{2,18},{10... | collective-permute-start | bytes 1572872 | tf_op jit(solution)/shard_map/ppermute | solution.py:101
  75.6 73.6 %collective-permute-start.16 = (bf16[512,1024]{1,0:T(8,128)(2,1)}, bf16[512,1024]{1,0:T(8,128)(2,1)}, u32[]{:S(2)}, u32[]{:S(2)}) collective-permute-start(bf16[512,1024]{1,0:T(8,128)(2,1)} %bitcast.9.ca.cot), channel_id=1, source_target_pairs={{0,8},{8,0},{16,24},{24,16},{1,9},{9,1},{17,25},{25,17},{2,10},{10... | collective-permute-start | bytes 3145736 | tf_op jit(solution)/shard_map/ppermute | solution.py:101
  81.5 45.2 %collective-permute-start.21 = (bf16[2,128,1024]{2,1,0:T(8,128)(2,1)S(1)}, bf16[2,128,1024]{2,1,0:T(8,128)(2,1)S(1)}, u32[]{:S(2)}, u32[]{:S(2)}) collective-permute-start(bf16[2,128,1024]{2,1,0:T(8,128)(2,1)S(1)} %copy-done.52), channel_id=1, source_target_pairs={{0,4},{1,5},{2,6},{3,7},{4,0},{5,1},{6,2},{7,3},{8,12},{9,13},{10,... | collective-permute-start | bytes 1572872 | tf_op jit(solution)/shard_map/ppermute | solution.py:82
  104.7 23.6 %collective-permute-start.12 = (bf16[8,128,256]{2,1,0:T(8,128)(2,1)S(1)}, bf16[8,128,256]{2,1,0:T(8,128)(2,1)S(1)}, u32[]{:S(2)}, u32[]{:S(2)}) collective-permute-start(bf16[8,128,256]{2,1,0:T(8,128)(2,1)S(1)} %pad_maximum_fusion.12.refs_4_), channel_id=1, source_target_pairs={{0,8},{8,0},{16,24},{24,16},{1,9},{9,1},{17,25},{25,17},{2,10},{10... | collective-permute-start | bytes 1572872 | tf_op jit(solution)/shard_map/ppermute | solution.py:101
  104.7 26.0 %collective-permute-start.14 = (bf16[8,128,256]{2,1,0:T(8,128)(2,1)}, bf16[8,128,256]{2,1,0:T(8,128)(2,1)S(1)}, u32[]{:S(2)}, u32[]{:S(2)}) collective-permute-start(bf16[8,128,256]{2,1,0:T(8,128)(2,1)} %collective-permute-done.13.refs_6_), channel_id=1, source_target_pairs={{0,8},{8,0},{16,24},{24,16},{1,9},{9,1},{17,25},{25,17},{2,10},{10... | collective-permute-start | bytes 1572872 | tf_op jit(solution)/shard_map/ppermute | solution.py:101
  128.3 26.1 %collective-permute-start.19 = (bf16[4,128,1024]{2,1,0:T(8,128)(2,1)S(1)}, bf16[4,128,1024]{2,1,0:T(8,128)(2,1)S(1)}, u32[]{:S(2)}, u32[]{:S(2)}) collective-permute-start(bf16[4,128,1024]{2,1,0:T(8,128)(2,1)S(1)} %pad_maximum_fusion.6), channel_id=1, source_target_pairs={{0,1},{1,0},{2,3},{3,2},{4,5},{5,4},{6,7},{7,6},{8,9},{9,8},{10,11... | collective-permute-start | bytes 3145736 | tf_op jit(solution)/shard_map/ppermute | solution.py:82
  131.6 44.8 %collective-permute-start.22 = (bf16[4,128,1024]{2,1,0:T(8,128)(2,1)S(1)}, bf16[4,128,1024]{2,1,0:T(8,128)(2,1)S(1)}, u32[]{:S(2)}, u32[]{:S(2)}) collective-permute-start(bf16[4,128,1024]{2,1,0:T(8,128)(2,1)S(1)} %pad_maximum_fusion.7), channel_id=1, source_target_pairs={{0,1},{1,0},{2,3},{3,2},{4,5},{5,4},{6,7},{7,6},{8,9},{9,8},{10,11... | collective-permute-start | bytes 3145736 | tf_op jit(solution)/shard_map/ppermute | solution.py:82
  139.0 38.9 %collective-permute-start.27 = (bf16[512,1024]{1,0:T(8,128)(2,1)}, bf16[512,1024]{1,0:T(8,128)(2,1)S(1)}, u32[]{:S(2)}, u32[]{:S(2)}) collective-permute-start(bf16[512,1024]{1,0:T(8,128)(2,1)} %collective-permute-done.26.ca), channel_id=1, source_target_pairs={{0,8},{8,0},{16,24},{24,16},{1,9},{9,1},{17,25},{25,17},{2,10},{10... | collective-permute-start | bytes 3145736 | tf_op jit(solution)/shard_map/ppermute | solution.py:101
  148.3 32.8 %collective-permute-start.24 = (bf16[512,1024]{1,0:T(8,128)(2,1)S(1)}, bf16[512,1024]{1,0:T(8,128)(2,1)}, u32[]{:S(2)}, u32[]{:S(2)}) collective-permute-start(bf16[512,1024]{1,0:T(8,128)(2,1)S(1)} %get-tuple-element.47.sa), channel_id=1, source_target_pairs={{0,16},{8,24},{16,0},{24,8},{1,17},{9,25},{17,1},{25,9},{2,18},{10... | collective-permute-start | bytes 3145736 | tf_op jit(solution)/shard_map/ppermute | solution.py:101
  149.2 32.0 %collective-permute-start.15 = (bf16[512,1024]{1,0:T(8,128)(2,1)S(1)}, bf16[512,1024]{1,0:T(8,128)(2,1)S(1)}, u32[]{:S(2)}, u32[]{:S(2)}) collective-permute-start(bf16[512,1024]{1,0:T(8,128)(2,1)S(1)} %get-tuple-element.47.sa), channel_id=1, source_target_pairs={{0,8},{8,0},{16,24},{24,16},{1,9},{9,1},{17,25},{25,17},{2,10},{10... | collective-permute-start | bytes 3145736 | tf_op jit(solution)/shard_map/ppermute | solution.py:101
  181.1 22.7 %collective-permute-start.25 = (bf16[512,1024]{1,0:T(8,128)(2,1)}, bf16[512,1024]{1,0:T(8,128)(2,1)}, u32[]{:S(2)}, u32[]{:S(2)}) collective-permute-start(bf16[512,1024]{1,0:T(8,128)(2,1)} %collective-permute-done.24.sa), channel_id=1, source_target_pairs={{0,8},{8,0},{16,24},{24,16},{1,9},{9,1},{17,25},{25,17},{2,10},{10... | collective-permute-start | bytes 3145736 | tf_op jit(solution)/shard_map/ppermute | solution.py:101
  200.8 137.8 %collective-permute-start.23 = (bf16[512,1024]{1,0:T(8,128)(2,1)}, bf16[512,1024]{1,0:T(8,128)(2,1)}, u32[]{:S(2)}, u32[]{:S(2)}) collective-permute-start(bf16[512,1024]{1,0:T(8,128)(2,1)} %slice_bitcast_fusion.5), channel_id=1, source_target_pairs={{0,8},{8,0},{16,24},{24,16},{1,9},{9,1},{17,25},{25,17},{2,10},{10... | collective-permute-start | bytes 3145736 | tf_op jit(solution)/shard_map/ppermute | solution.py:111
  202.3 47.6 %collective-permute-start.30 = (bf16[512,1024]{1,0:T(8,128)(2,1)}, bf16[512,1024]{1,0:T(8,128)(2,1)}, u32[]{:S(2)}, u32[]{:S(2)}) collective-permute-start(bf16[512,1024]{1,0:T(8,128)(2,1)} %slice_bitcast_fusion.3), channel_id=1, source_target_pairs={{0,8},{8,0},{16,24},{24,16},{1,9},{9,1},{17,25},{25,17},{2,10},{10... | collective-permute-start | bytes 3145736 | tf_op jit(solution)/shard_map/ppermute | solution.py:111
  234.7 26.3 %collective-permute-start.59 = (bf16[4,128,1024]{2,1,0:T(8,128)(2,1)}, bf16[4,128,1024]{2,1,0:T(8,128)(2,1)}, u32[]{:S(2)}, u32[]{:S(2)}) collective-permute-start(bf16[4,128,1024]{2,1,0:T(8,128)(2,1)} %slice.360), channel_id=1, source_target_pairs={{0,1},{1,0},{2,3},{3,2},{4,5},{5,4},{6,7},{7,6},{8,9},{9,8},{10,11... | collective-permute-start | bytes 3145736 | tf_op jit(solution)/shard_map/ppermute | solution.py:93
  247.6 35.4 %collective-permute-start.65 = (bf16[4,128,1024]{2,1,0:T(8,128)(2,1)S(1)}, bf16[4,128,1024]{2,1,0:T(8,128)(2,1)S(1)}, u32[]{:S(2)}, u32[]{:S(2)}) collective-permute-start(bf16[4,128,1024]{2,1,0:T(8,128)(2,1)S(1)} %slice.367), channel_id=1, source_target_pairs={{0,1},{1,0},{2,3},{3,2},{4,5},{5,4},{6,7},{7,6},{8,9},{9,8},{10,11... | collective-permute-start | bytes 3145736 | tf_op jit(solution)/shard_map/ppermute | solution.py:93
  249.6 33.8 %collective-permute-start.31 = (bf16[512,1024]{1,0:T(8,128)(2,1)S(1)}, bf16[512,1024]{1,0:T(8,128)(2,1)S(1)}, u32[]{:S(2)}, u32[]{:S(2)}) collective-permute-start(bf16[512,1024]{1,0:T(8,128)(2,1)S(1)} %slice_bitcast_fusion.2), channel_id=1, source_target_pairs={{0,8},{8,0},{16,24},{24,16},{1,9},{9,1},{17,25},{25,17},{2,10},{10... | collective-permute-start | bytes 3145736 | tf_op jit(solution)/shard_map/ppermute | solution.py:111
  249.9 59.8 %collective-permute-start.28 = (bf16[512,1024]{1,0:T(8,128)(2,1)S(1)}, bf16[512,1024]{1,0:T(8,128)(2,1)S(1)}, u32[]{:S(2)}, u32[]{:S(2)}) collective-permute-start(bf16[512,1024]{1,0:T(8,128)(2,1)S(1)} %slice_bitcast_fusion.4), channel_id=1, source_target_pairs={{0,8},{8,0},{16,24},{24,16},{1,9},{9,1},{17,25},{25,17},{2,10},{10... | collective-permute-start | bytes 3145736 | tf_op jit(solution)/shard_map/ppermute | solution.py:111
  262.6 35.5 %collective-permute-start.60 = (bf16[2,128,1024]{2,1,0:T(8,128)(2,1)S(1)}, bf16[2,128,1024]{2,1,0:T(8,128)(2,1)S(1)}, u32[]{:S(2)}, u32[]{:S(2)}) collective-permute-start(bf16[2,128,1024]{2,1,0:T(8,128)(2,1)S(1)} %slice.362), channel_id=1, source_target_pairs={{0,4},{1,5},{2,6},{3,7},{4,0},{5,1},{6,2},{7,3},{8,12},{9,13},{10,... | collective-permute-start | bytes 1572872 | tf_op jit(solution)/shard_map/ppermute | solution.py:93
  283.4 26.0 %collective-permute-start.66 = (bf16[2,128,1024]{2,1,0:T(8,128)(2,1)S(1)}, bf16[2,128,1024]{2,1,0:T(8,128)(2,1)S(1)}, u32[]{:S(2)}, u32[]{:S(2)}) collective-permute-start(bf16[2,128,1024]{2,1,0:T(8,128)(2,1)S(1)} %slice.369), channel_id=1, source_target_pairs={{0,4},{1,5},{2,6},{3,7},{4,0},{5,1},{6,2},{7,3},{8,12},{9,13},{10,... | collective-permute-start | bytes 1572872 | tf_op jit(solution)/shard_map/ppermute | solution.py:93
  283.9 36.8 %collective-permute-start.32 = (bf16[512,1024]{1,0:T(8,128)(2,1)S(1)}, bf16[512,1024]{1,0:T(8,128)(2,1)S(1)}, u32[]{:S(2)}, u32[]{:S(2)}) collective-permute-start(bf16[512,1024]{1,0:T(8,128)(2,1)S(1)} %fusion.2), channel_id=1, source_target_pairs={{0,16},{8,24},{16,0},{24,8},{1,17},{9,25},{17,1},{25,9},{2,18},{10... | collective-permute-start | bytes 3145736 | tf_op jit(solution)/shard_map/ppermute | solution.py:111
  311.1 28.2 %collective-permute-start.29 = (bf16[512,1024]{1,0:T(8,128)(2,1)}, bf16[512,1024]{1,0:T(8,128)(2,1)}, u32[]{:S(2)}, u32[]{:S(2)}) collective-permute-start(bf16[512,1024]{1,0:T(8,128)(2,1)} %fusion.4), channel_id=1, source_target_pairs={{0,16},{8,24},{16,0},{24,8},{1,17},{9,25},{17,1},{25,9},{2,18},{10... | collective-permute-start | bytes 3145736 | tf_op jit(solution)/shard_map/ppermute | solution.py:111
  315.8 32.2 %collective-permute-start.63 = (bf16[128,8,128]{2,1,0:T(8,128)(2,1)}, bf16[128,8,128]{2,1,0:T(8,128)(2,1)}, u32[]{:S(2)}, u32[]{:S(2)}) collective-permute-start(bf16[128,8,128]{2,1,0:T(8,128)(2,1)} %bitcast.88), channel_id=1, source_target_pairs={{0,16},{8,24},{16,0},{24,8},{1,17},{9,25},{17,1},{25,9},{2,18},{10... | collective-permute-start | bytes 786440 | tf_op jit(solution)/shard_map/ppermute | solution.py:101
  320.5 79.2 %collective-permute-start.62 = (bf16[128,8,128]{2,1,0:T(8,128)(2,1)}, bf16[128,8,128]{2,1,0:T(8,128)(2,1)}, u32[]{:S(2)}, u32[]{:S(2)}) collective-permute-start(bf16[128,8,128]{2,1,0:T(8,128)(2,1)} %bitcast.88), channel_id=1, source_target_pairs={{0,8},{8,0},{16,24},{24,16},{1,9},{9,1},{17,25},{25,17},{2,10},{10... | collective-permute-start | bytes 786440 | tf_op jit(solution)/shard_map/ppermute | solution.py:101
  344.5 55.3 %collective-permute-start.69 = (bf16[128,1024]{1,0:T(8,128)(2,1)S(1)}, bf16[128,1024]{1,0:T(8,128)(2,1)}, u32[]{:S(2)}, u32[]{:S(2)}) collective-permute-start(bf16[128,1024]{1,0:T(8,128)(2,1)S(1)} %bitcast.166), channel_id=1, source_target_pairs={{0,16},{8,24},{16,0},{24,8},{1,17},{9,25},{17,1},{25,9},{2,18},{10... | collective-permute-start | bytes 786440 | tf_op jit(solution)/shard_map/ppermute | solution.py:101
  348.0 76.8 %collective-permute-start.68 = (bf16[128,1024]{1,0:T(8,128)(2,1)S(1)}, bf16[128,1024]{1,0:T(8,128)(2,1)}, u32[]{:S(2)}, u32[]{:S(2)}) collective-permute-start(bf16[128,1024]{1,0:T(8,128)(2,1)S(1)} %bitcast.167), channel_id=1, source_target_pairs={{0,8},{8,0},{16,24},{24,16},{1,9},{9,1},{17,25},{25,17},{2,10},{10... | collective-permute-start | bytes 786440 | tf_op jit(solution)/shard_map/ppermute | solution.py:101
  348.0 81.8 %collective-permute-start.51 = (bf16[8,128,256]{2,1,0:T(8,128)(2,1)}, bf16[8,128,256]{2,1,0:T(8,128)(2,1)}, u32[]{:S(2)}, u32[]{:S(2)}) collective-permute-start(bf16[8,128,256]{2,1,0:T(8,128)(2,1)} %get-tuple-element.94), channel_id=1, source_target_pairs={{0,8},{8,0},{16,24},{24,16},{1,9},{9,1},{17,25},{25,17},{2,10},{10... | collective-permute-start | bytes 1572872 | tf_op jit(solution)/shard_map/ppermute | solution.py:111
  352.8 47.5 %collective-permute-start.64 = (bf16[128,8,128]{2,1,0:T(8,128)(2,1)}, bf16[128,8,128]{2,1,0:T(8,128)(2,1)}, u32[]{:S(2)}, u32[]{:S(2)}) collective-permute-start(bf16[128,8,128]{2,1,0:T(8,128)(2,1)} %collective-permute-done.63), channel_id=1, source_target_pairs={{0,8},{8,0},{16,24},{24,16},{1,9},{9,1},{17,25},{25,17},{2,10},{10... | collective-permute-start | bytes 786440 | tf_op jit(solution)/shard_map/ppermute | solution.py:101
  399.7 39.9 %collective-permute-start.50 = (bf16[8,128,256]{2,1,0:T(8,128)(2,1)}, bf16[8,128,256]{2,1,0:T(8,128)(2,1)S(1)}, u32[]{:S(2)}, u32[]{:S(2)}) collective-permute-start(bf16[8,128,256]{2,1,0:T(8,128)(2,1)} %get-tuple-element.93), channel_id=1, source_target_pairs={{0,8},{8,0},{16,24},{24,16},{1,9},{9,1},{17,25},{25,17},{2,10},{10... | collective-permute-start | bytes 1572872 | tf_op jit(solution)/shard_map/ppermute | solution.py:111
  399.8 25.6 %collective-permute-start.70 = (bf16[128,1024]{1,0:T(8,128)(2,1)}, bf16[128,1024]{1,0:T(8,128)(2,1)}, u32[]{:S(2)}, u32[]{:S(2)}) collective-permute-start(bf16[128,1024]{1,0:T(8,128)(2,1)} %collective-permute-done.69), channel_id=1, source_target_pairs={{0,8},{8,0},{16,24},{24,16},{1,9},{9,1},{17,25},{25,17},{2,10},{10... | collective-permute-start | bytes 786440 | tf_op jit(solution)/shard_map/ppermute | solution.py:101
  424.7 56.3 %collective-permute-start.37 = (bf16[512,1024]{1,0:T(8,128)(2,1)}, bf16[512,1024]{1,0:T(8,128)(2,1)}, u32[]{:S(2)}, u32[]{:S(2)}) collective-permute-start(bf16[512,1024]{1,0:T(8,128)(2,1)} %get-tuple-element.91), channel_id=1, source_target_pairs={{0,8},{8,0},{16,24},{24,16},{1,9},{9,1},{17,25},{25,17},{2,10},{10... | collective-permute-start | bytes 3145736 | tf_op jit(solution)/shard_map/ppermute | solution.py:111
  424.7 23.8 %collective-permute-start.44 = (bf16[4,128,768]{2,1,0:T(8,128)(2,1)}, bf16[4,128,768]{2,1,0:T(8,128)(2,1)}, u32[]{:S(2)}, u32[]{:S(2)}) collective-permute-start(bf16[4,128,768]{2,1,0:T(8,128)(2,1)} %slice.340), channel_id=1, source_target_pairs={{0,1},{1,0},{2,3},{3,2},{4,5},{5,4},{6,7},{7,6},{8,9},{9,8},{10,11... | collective-permute-start | bytes 2359304 | tf_op jit(solution)/shard_map/ppermute | solution.py:93
  439.5 41.5 %collective-permute-start.36 = (bf16[512,1024]{1,0:T(8,128)(2,1)S(1)}, bf16[512,1024]{1,0:T(8,128)(2,1)S(1)}, u32[]{:S(2)}, u32[]{:S(2)}) collective-permute-start(bf16[512,1024]{1,0:T(8,128)(2,1)S(1)} %copy-done.47), channel_id=1, source_target_pairs={{0,8},{8,0},{16,24},{24,16},{1,9},{9,1},{17,25},{25,17},{2,10},{10... | collective-permute-start | bytes 3145736 | tf_op jit(solution)/shard_map/ppermute | solution.py:111
  439.6 17.2 %collective-permute-start.43 = (bf16[1536]{0:T(1024)(128)(2,1)S(1)}, bf16[1536]{0:T(1024)(128)(2,1)S(1)}, u32[]{:S(2)}, u32[]{:S(2)}) collective-permute-start(bf16[1536]{0:T(1024)(128)(2,1)S(1)} %add_convert_fusion.17), channel_id=1, source_target_pairs={{0,16},{8,24},{16,0},{24,8},{1,17},{9,25},{17,1},{25,9},{2,18},{10... | collective-permute-start | bytes 9224 | tf_op jit(solution)/shard_map/ppermute | solution.py:745
  450.1 25.3 %collective-permute-start.45 = (bf16[2,128,768]{2,1,0:T(8,128)(2,1)S(1)}, bf16[2,128,768]{2,1,0:T(8,128)(2,1)S(1)}, u32[]{:S(2)}, u32[]{:S(2)}) collective-permute-start(bf16[2,128,768]{2,1,0:T(8,128)(2,1)S(1)} %slice.342), channel_id=1, source_target_pairs={{0,4},{1,5},{2,6},{3,7},{4,0},{5,1},{6,2},{7,3},{8,12},{9,13},{10,... | collective-permute-start | bytes 1179656 | tf_op jit(solution)/shard_map/ppermute | solution.py:93
  454.8 20.5 %collective-permute-start.54 = (bf16[2,128,256]{2,1,0:T(8,128)(2,1)S(1)}, bf16[2,128,256]{2,1,0:T(8,128)(2,1)S(1)}, u32[]{:S(2)}, u32[]{:S(2)}) collective-permute-start(bf16[2,128,256]{2,1,0:T(8,128)(2,1)S(1)} %slice.353), channel_id=1, source_target_pairs={{0,4},{1,5},{2,6},{3,7},{4,0},{5,1},{6,2},{7,3},{8,12},{9,13},{10,... | collective-permute-start | bytes 393224 | tf_op jit(solution)/shard_map/ppermute | solution.py:93
  484.6 41.7 %collective-permute-start.38 = (bf16[512,1024]{1,0:T(8,128)(2,1)}, bf16[512,1024]{1,0:T(8,128)(2,1)S(1)}, u32[]{:S(2)}, u32[]{:S(2)}) collective-permute-start(bf16[512,1024]{1,0:T(8,128)(2,1)} %get-tuple-element.89), channel_id=1, source_target_pairs={{0,16},{8,24},{16,0},{24,8},{1,17},{9,25},{17,1},{25,9},{2,18},{10... | collective-permute-start | bytes 3145736 | tf_op jit(solution)/shard_map/ppermute | solution.py:111
  486.4 24.9 %collective-permute-start.48 = (bf16[128,768]{1,0:T(8,128)(2,1)S(1)}, bf16[128,768]{1,0:T(8,128)(2,1)}, u32[]{:S(2)}, u32[]{:S(2)}) collective-permute-start(bf16[128,768]{1,0:T(8,128)(2,1)S(1)} %bitcast.168), channel_id=1, source_target_pairs={{0,16},{8,24},{16,0},{24,8},{1,17},{9,25},{17,1},{25,9},{2,18},{10... | collective-permute-start | bytes 589832 | tf_op jit(solution)/shard_map/ppermute | solution.py:101
  489.0 23.6 %collective-permute-start.47 = (bf16[128,768]{1,0:T(8,128)(2,1)S(1)}, bf16[128,768]{1,0:T(8,128)(2,1)}, u32[]{:S(2)}, u32[]{:S(2)}) collective-permute-start(bf16[128,768]{1,0:T(8,128)(2,1)S(1)} %bitcast.169), channel_id=1, source_target_pairs={{0,8},{8,0},{16,24},{24,16},{1,9},{9,1},{17,25},{25,17},{2,10},{10... | collective-permute-start | bytes 589832 | tf_op jit(solution)/shard_map/ppermute | solution.py:101
  (81 other events, 825.4 us)

commit v2 on v1

v2 whole, which is shorter than its diff:
```python
import functools

import jax
import jax.numpy as jnp
from jax import lax
from jax.experimental import pallas as pl
from jax.experimental.pallas import tpu as pltpu
from jax.sharding import PartitionSpec as P

H = 16
HD = 64
EPSILON = 1e-05
F32 = jnp.float32
BF = jnp.bfloat16
NT = (((1,), (1,)), ((), ()))
NN = (((1,), (0,)), ((), ()))
TN = (((0,), (0,)), ((), ()))
MIB = 2**20
SHRINK = 1000


def dg(left, right, dims):
    return lax.dot_general(left, right, dims, preferred_element_type=F32)


def params(limit=56):
    return pltpu.CompilerParams(vmem_limit_bytes=limit * MIB)


def cost(flops, moved, exps=0):
    return pl.CostEstimate(flops=flops // SHRINK, bytes_accessed=moved // SHRINK, transcendentals=exps // SHRINK)


def norm_parts(values):
    mean = jnp.mean(values, axis=-1, keepdims=True)
    centered = values - mean
    scale = lax.rsqrt(jnp.mean(centered * centered, axis=-1, keepdims=True) + EPSILON)
    return centered * scale, scale


def norm_back(grad, unit, scale, gain):
    scaled = grad * gain
    return scale * (
        scaled
        - jnp.mean(scaled, axis=-1, keepdims=True)
        - unit * jnp.mean(scaled * unit, axis=-1, keepdims=True)
    )


def pairs(size, bit):
    return [(i, i ^ bit) for i in range(size)]


def bits_low_last(size):
    bits = []
    bit = 2
    while bit < size:
        bits.append(bit)
        bit *= 2
    if size > 1:
        bits.append(1)
    return bits


def add16(left, right):
    return (left.astype(F32) + right.astype(F32)).astype(BF)


def gather_rel(block, axis, size):
    out = {0: block}
    for bit in bits_low_last(size):
        for rel in list(out):
            out[rel | bit] = lax.ppermute(out[rel], axis, pairs(size, bit))
    return out


def scatter_rel(parts, axis, size, last=True):
    parts = dict(parts)
    order = bits_low_last(size)[::-1]
    for bit in order:
        for rel in sorted(parts, reverse=True):
            if rel & bit:
                other = lax.ppermute(parts.pop(rel), axis, pairs(size, bit))
                if bit == order[-1] and not last:
                    return parts[0], other
                parts[rel ^ bit] = add16(parts[rel ^ bit], other)
    return parts[0]


def tie(*values):
    return lax.optimization_barrier(values)


def place_table(me, size):
    index = jnp.arange(size, dtype=jnp.int32) ^ me
    place = jnp.zeros_like(index)
    for at, bit in enumerate(bits_low_last(size)):
        place = place | jnp.where(index & bit, 1 << at, 0)
    return place


def owner_table(me, size):
    place = jnp.arange(size, dtype=jnp.int32)
    rel = jnp.zeros_like(place)
    for at, bit in enumerate(bits_low_last(size)):
        rel = rel | jnp.where(place & (1 << at), bit, 0)
    return rel ^ me


def gather_all(block, axis, size, me):
    order = bits_low_last(size)
    out = block[None]
    for bit in order:
        out = jnp.concatenate([out, lax.ppermute(out, axis, pairs(size, bit))], 0)
    return jnp.take(out, place_table(me, size), axis=0)


def scatter_all(blocks, axis, size, me):
    stack = jnp.take(blocks, owner_table(me, size), axis=0)
    for bit in bits_low_last(size)[::-1]:
        half = stack.shape[0] // 2
        stack = add16(stack[:half], lax.ppermute(stack[half:], axis, pairs(size, bit)))
    return stack[0]


class Ring:
    def __init__(self, size, index, live):
        self.size = size
        self.live = live
        order = list(range(0, size, 2)) + list(range(size - 1, 0, -2))
        self.forward = [(order[i], order[(i + 1) % size]) for i in range(size)]
        self.backward = [(b, a) for a, b in self.forward]
        count = jnp.arange(size, dtype=jnp.int32)
        place = lambda k: jnp.where(k % 2 == 0, k // 2, size - (k + 1) // 2)
        if self.live:
            self.slots = (place(count) - place(index) + size) % size
            seat = (place(index) + count) % size
            self.owners = jnp.where(seat < size // 2, 2 * seat, 2 * (size - seat) - 1)
        else:
            self.slots = count
            self.owners = count
        self.half = size // 2

    def table(self):
        return jnp.concatenate([self.slots, self.owners])

    def ahead(self, value):
        return lax.ppermute(value, "batch", self.forward)

    def back(self, value):
        return lax.ppermute(value, "batch", self.backward)


def owner_at(info, live, nb, slot):
    return info[2 + nb + slot] if live else slot


def put(outs, slot, value):
    if len(outs) == 1:
        outs[0][slot] = value
        return
    for at, out in enumerate(outs):

        @pl.when(slot == at)
        def _():
            out[0] = value


def blocks_of(refs):
    out = []
    for ref in refs:
        out += [(ref, at) for at in range(ref.shape[0])]
    return out


def once(shape):
    return pl.BlockSpec(shape, lambda i, *_: (0,) * len(shape), pipeline_mode=pl.Buffered(1))


def first_pack_kernel(info, joined, outw, out):
    cols = joined.shape[1]
    out[:, :cols] = joined[...]
    out[:, cols:] = outw[...]


def first_pack(info, joined, outw, cols, cw):
    rows = joined.shape[0]
    return pl.pallas_call(
        first_pack_kernel,
        grid_spec=pltpu.PrefetchScalarGridSpec(
            num_scalar_prefetch=1,
            grid=(1,),
            in_specs=[
                pl.BlockSpec((rows, cols), lambda i, info: (0, info[0])),
                pl.BlockSpec((rows, cw), lambda i, info: (0, info[0])),
            ],
            out_specs=pl.BlockSpec((rows, cols + cw), lambda i, info: (0, 0)),
        ),
        out_shape=jax.ShapeDtypeStruct((rows, cols + cw), BF),
        compiler_params=params(40),
        name="first_pack",
    )(info, joined, outw)


def second_pack_kernel(nb, ns, units, info, expand, shrink, out):
    rows = expand.shape[0]
    for k in range(nb):
        col = pl.ds(pl.multiple_of((k * ns + info[0]) * units, units), units)
        out[:rows, k * units : (k + 1) * units] = expand[:, col]
    out[rows:] = shrink[...]


def second_pack(info, expand, shrink, nb, ns):
    rows, wide = expand.shape
    dim = shrink.shape[1]
    units = shrink.shape[0] // ns
    return pl.pallas_call(
        functools.partial(second_pack_kernel, nb, ns, units),
        grid_spec=pltpu.PrefetchScalarGridSpec(
            num_scalar_prefetch=1,
            grid=(1,),
            in_specs=[
                pl.BlockSpec((rows, wide), lambda i, info: (0, 0)),
                pl.BlockSpec((units, dim), lambda i, info: (info[0], 0)),
            ],
            out_specs=pl.BlockSpec((rows + units, dim), lambda i, info: (0, 0)),
        ),
        out_shape=jax.ShapeDtypeStruct((rows + units, dim), BF),
        compiler_params=params(40),
        name="second_pack",
    )(info, expand, shrink)


def first_kernel(ns, nt, nb, rows, cols, live, info, vecs, jbias, *refs):
    xs, weights = refs[:ns], refs[ns:-4]
    normed, joined, full, outw = refs[-4:]
    step = pl.program_id(0)

    @pl.when(step == 0)
    def _():
        for slot, (ref, at) in enumerate(blocks_of(weights)):
            high = owner_at(info, live, nb, slot) * rows
            high = pl.multiple_of(high, rows) if live else high
            full[pl.ds(high, rows)] = ref[at, :, :cols]
            outw[pl.ds(high, rows)] = ref[at, :, cols:]

    for rel in range(ns):

        @pl.when(lax.div(step, nt) == rel)
        def _():
            unit, _ = norm_parts(xs[rel][...].astype(F32))
            value = (unit * vecs[0:1] + vecs[1:2]).astype(BF)
            normed[...] = value
            joined[...] = (dg(value, full[...], NN) + jbias[...]).astype(BF)


def first_call(info, vecs, jbias, xs, weights, live):
    ns = len(xs)
    tok, dim = xs[0].shape
    nb = sum(weight.shape[0] for weight in weights)
    rows = dim // nb
    cols = jbias.shape[1]
    cw = weights[0].shape[2] - cols
    tile = min(256, tok)
    nt = tok // tile
    place = lambda i, info: ((info[0] ^ lax.div(i, nt)) * nt + lax.rem(i, nt), 0)

    def source(rel):
        return pl.BlockSpec((tile, dim), lambda i, info: (jnp.clip(i - rel * nt, 0, nt - 1), 0))

    return pl.pallas_call(
        functools.partial(first_kernel, ns, nt, nb, rows, cols, live),
        grid_spec=pltpu.PrefetchScalarGridSpec(
            num_scalar_prefetch=1,
            grid=(ns * nt,),
            in_specs=[once(vecs.shape), once(jbias.shape)]
            + [source(rel) for rel in range(ns)]
            + [once(weight.shape) for weight in weights],
            out_specs=[
                pl.BlockSpec((tile, dim), place),
                pl.BlockSpec((tile, cols), place),
                once((dim, cols)),
                once((dim, cw)),
            ],
        ),
        out_shape=[
            jax.ShapeDtypeStruct((ns * tok, dim), BF),
            jax.ShapeDtypeStruct((ns * tok, cols), BF),
            jax.ShapeDtypeStruct((dim, cols), BF),
            jax.ShapeDtypeStruct((dim, cw), BF),
        ],
        compiler_params=params(40),
        cost_estimate=cost(2 * ns * tok * dim * cols, 2 * ns * tok * (2 * dim + cols)),
        name="first",
    )(info, vecs, jbias, *xs, *weights)


def three(value):
    high = value.astype(BF)
    rest = value - high.astype(F32)
    mid = rest.astype(BF)
    return high, mid, (rest - mid.astype(F32)).astype(BF)


def spread(lane, base, columns):
    for at, column in columns:
        base = jnp.where(lane == at, column.astype(F32), base)
    return base.astype(BF)


def key_extra(count, slope, length):
    lane = lax.broadcasted_iota(jnp.int32, (count, HD), 1)
    pos = lax.broadcasted_iota(jnp.int32, (count, HD), 0)
    high, mid, low = three(slope * pos.astype(F32))
    dead = jnp.where(pos < length, 0.0, -1e30)
    return spread(lane, jnp.where(lane < 7, 1.0, 0.0), [(0, high), (1, mid), (2, low), (3, dead)])


def attend_kernel(count, size, pair, info, slopes, joined, mixed, sums, keys):
    lane = lax.broadcasted_iota(jnp.int32, (size, HD), 1)
    ones = jnp.where(lane < 4, 1.0, 0.0).astype(BF)
    for hh in range(2):
        base = 3 * HD * hh
        extra = key_extra(count, slopes[2 * pair + hh], info[1])
        keys[hh] = jnp.concatenate([joined[:, base + HD : base + 2 * HD], extra], 1)
    query_at = lax.broadcasted_iota(jnp.int32, (size, size), 0)
    key_at = lax.broadcasted_iota(jnp.int32, (size, size), 1)
    for block in range(count // size):
        low = block * size
        high = low + size
        outs = []
        logs = []
        for hh in range(2):
            base = 3 * HD * hh
            query = (joined[low:high, base : base + HD].astype(F32) * 0.125).astype(BF)
            query = jnp.concatenate([query, ones], 1)
            near = jnp.where(key_at <= query_at, dg(query, keys[hh, low:high], NT), -1e30)
            top = jnp.max(near, axis=1, keepdims=True)
            if block:
                far = dg(query, keys[hh, 0:low], NT)
                top = jnp.maximum(top, jnp.max(far, axis=1, keepdims=True))
            near = jnp.exp(near - top)
            total = jnp.sum(near, axis=1, keepdims=True)
            acc = dg(near.astype(BF), joined[low:high, base + 2 * HD : base + 3 * HD], NN)
            if block:
                far = jnp.exp(far - top)
                total += jnp.sum(far, axis=1, keepdims=True)
                acc += dg(far.astype(BF), joined[0:low, base + 2 * HD : base + 3 * HD], NN)
            outs.append(acc / total)
            logs.append(jnp.broadcast_to(top + jnp.log(total), (size, HD)))
        mixed[low:high] = jnp.concatenate(outs, 1).astype(BF)
        sums[low:high] = jnp.concatenate(logs, 1)


def attend(joined, info, slopes, pair):
    count = joined.shape[0]
    smem = pl.BlockSpec(memory_space=pltpu.SMEM)
    area = count * count
    return pl.pallas_call(
        functools.partial(attend_kernel, count, min(512, count), pair),
        grid=(1,),
        in_specs=[smem, smem, pl.BlockSpec((count, 6 * HD), lambda i: (0, pair))],
        out_specs=[pl.BlockSpec((count, 2 * HD), lambda i: (0, 0))] * 2,
        out_shape=[
            jax.ShapeDtypeStruct((count, 2 * HD), BF),
            jax.ShapeDtypeStruct((count, 2 * HD), F32),
        ],
        scratch_shapes=[pltpu.VMEM((2, count, 2 * HD), BF)],
        compiler_params=params(),
        cost_estimate=cost(area * 1024, 20 * count * HD, area),
        name="attend",
    )(info, slopes, joined)


def attend_back_kernel(count, size, ns, pair, info, slopes, joined, mixed, sums, *refs):
    pieces_in = refs[:ns]
    out, sides, keys, queries, values, grads, query_grad = refs[ns:]
    tok = count // ns
    lane = lax.broadcasted_iota(jnp.int32, (count, HD), 1)
    near_lane = lax.broadcasted_iota(jnp.int32, (tok, HD), 1)
    for hh in range(2):
        base = 3 * HD * hh
        half = slice(hh * HD, (hh + 1) * HD)
        extra = key_extra(count, slopes[2 * pair + hh], info[1])
        keys[hh] = jnp.concatenate([joined[:, base + HD : base + 2 * HD], extra], 1)
        query = (joined[:, base : base + HD].astype(F32) * 0.125).astype(BF)
        high, mid, low = three(-sums[:, half])
        extra = spread(lane, jnp.where(lane < 4, 1.0, 0.0), [(4, high), (5, mid), (6, low)])
        queries[hh] = jnp.concatenate([query, extra], 1)
        ones = jnp.where(lane < 3, 1.0, 0.0).astype(BF)
        values[hh] = jnp.concatenate([joined[:, base + 2 * HD : base + 3 * HD], ones], 1)
        for rel in range(ns):
            at = pl.ds(pl.multiple_of((info[0] ^ rel) * tok, tok), tok)
            part = pieces_in[rel][:, half]
            inner = jnp.sum(part.astype(F32) * mixed[at, half].astype(F32), axis=1, keepdims=True)
            high, mid, low = three(jnp.broadcast_to(-inner, (tok, HD)))
            extra = spread(near_lane, jnp.zeros((tok, HD), F32), [(0, high), (1, mid), (2, low)])
            grads[hh, at] = jnp.concatenate([part, extra], 1)
    key_at = lax.broadcasted_iota(jnp.int32, (size, size), 0)
    query_at = lax.broadcasted_iota(jnp.int32, (size, size), 1)
    blocks = count // size
    for j in range(blocks):
        ks = slice(j * size, (j + 1) * size)
        pieces = []
        for hh in range(2):
            key_sum = None
            for i in range(j, blocks):
                qs = slice(i * size, (i + 1) * size)
                probs = jnp.exp(dg(keys[hh, ks], queries[hh, qs], NT))
                if i == j:
                    probs = jnp.where(key_at <= query_at, probs, 0.0)
                slope = (probs * dg(values[hh, ks], grads[hh, qs], NT)).astype(BF)
                value_part = dg(probs.astype(BF), grads[hh, qs], NN)
                key_part = dg(slope, queries[hh, qs], NN)
                query_part = dg(keys[hh, ks], slope, TN)
                value_sum = value_part if key_sum is None else value_sum + value_part
                key_sum = key_part if key_sum is None else key_sum + key_part
                query_grad[hh, :, qs] = query_part if j == 0 else query_grad[hh, :, qs] + query_part
            pieces += [jnp.zeros((size, HD), F32), key_sum[:, :HD], value_sum[:, :HD]]
        out[ks] = jnp.concatenate(pieces, 1).astype(BF)
    for hh in range(2):
        base = 3 * HD * hh
        out[:, base : base + HD] = (query_grad[hh].T[:, :HD] * 0.125).astype(BF)
    sides[...] = jnp.sum(out[...].astype(F32), axis=0, keepdims=True)


def attend_back(joined, grads, mixed, sums, info, slopes, pair):
    count = joined.shape[0]
    ns = len(grads)
    smem = pl.BlockSpec(memory_space=pltpu.SMEM)
    wide = pl.BlockSpec((count, 6 * HD), lambda i: (0, pair))
    narrow = pl.BlockSpec((count, 2 * HD), lambda i: (0, 0))
    piece = pl.BlockSpec((count // ns, 2 * HD), lambda i: (0, 0))
    area = count * count
    return pl.pallas_call(
        functools.partial(attend_back_kernel, count, min(512, count), ns, pair),
        grid=(1,),
        in_specs=[smem, smem, wide, narrow, narrow] + [piece] * ns,
        out_specs=[pl.BlockSpec((count, 6 * HD), lambda i: (0, 0)), pl.BlockSpec((1, 6 * HD), lambda i: (0, 0))],
        out_shape=[jax.ShapeDtypeStruct((count, 6 * HD), BF), jax.ShapeDtypeStruct((1, 6 * HD), F32)],
        scratch_shapes=[pltpu.VMEM((2, count, 2 * HD), BF)] * 4 + [pltpu.VMEM((2, 2 * HD, count), F32)],
        compiler_params=params(),
        cost_estimate=cost(area * 2560, 40 * count * HD, area),
        name="attend_back",
    )(info, slopes, joined, mixed, sums, *grads)


def middle_kernel(ns, np, info, x, vecs, *refs):
    mixed, weights = refs[: ns * np], refs[ns * np : ns * np + ns]
    merged, resid, second, full = refs[ns * np + ns :]
    cw = weights[0].shape[1]
    pw = cw // np

    @pl.when(pl.program_id(0) == 0)
    def _():
        for rel in range(ns):
            full[:, pl.ds(pl.multiple_of((info[0] ^ rel) * cw, cw), cw)] = weights[rel][...]

    for pair in range(np):
        for rel in range(ns):
            col = pl.ds(pl.multiple_of((info[0] ^ rel) * cw + pair * pw, pw), pw)
            merged[:, col] = mixed[pair * ns + rel][...]
    value = x[...].astype(F32) + dg(merged[...], full[...], NN) + vecs[4:5]
    resid[...] = value
    unit, _ = norm_parts(value)
    second[...] = (unit * vecs[5:6] + vecs[6:7]).astype(BF)


def middle_call(info, x, vecs, mixed, weights):
    tok, dim = x.shape
    ns = len(weights)
    np = len(mixed) // ns
    tile = min(256, tok)
    part = lambda width: pl.BlockSpec((tile, width), lambda i, info: (i, 0))
    return pl.pallas_call(
        functools.partial(middle_kernel, ns, np),
        grid_spec=pltpu.PrefetchScalarGridSpec(
            num_scalar_prefetch=1,
            grid=(tok // tile,),
            in_specs=[part(dim), once(vecs.shape)]
            + [part(block.shape[1]) for block in mixed]
            + [once(weight.shape) for weight in weights],
            out_specs=[part(dim), part(dim), part(dim), once((dim, dim))],
        ),
        out_shape=[
            jax.ShapeDtypeStruct((tok, dim), BF),
            jax.ShapeDtypeStruct((tok, dim), F32),
            jax.ShapeDtypeStruct((tok, dim), BF),
            jax.ShapeDtypeStruct((dim, dim), BF),
        ],
        compiler_params=params(40),
        cost_estimate=cost(2 * tok * dim * dim, 12 * tok * dim + 4 * dim * dim),
        name="middle",
    )(info, x, vecs, *mixed, *weights)


def feed_kernel(nt, nb, rows, units, live, info, sa, sb, ca, cb, ebias, *refs):
    weights = refs[:-9]
    activ, pre_grad, oa, ob, ba, bb, bgrad, wide, tall = refs[-9:]
    step = pl.program_id(0)

    @pl.when(step == 0)
    def _():
        blocks = blocks_of(weights)
        for slot in range(nb):
            owner = owner_at(info, live, nb, slot)
            high = pl.multiple_of(owner * rows, rows) if live else owner * rows
            deep = pl.multiple_of(owner * units, units) if live else owner * units
            if len(blocks) == nb:
                ref, at = blocks[slot]
                wide[pl.ds(high, rows)] = ref[at, :rows]
                tall[pl.ds(deep, units)] = ref[at, rows:]
            else:
                wide[pl.ds(high, rows)] = weights[0][slot]
                tall[pl.ds(deep, units)] = weights[1][slot]
        bgrad[...] = jnp.zeros_like(bgrad)

    def work(second, cot, out, back):
        pre = dg(second[...], wide[...], NN) + ebias[...]
        square = pre * pre
        bend = jnp.tanh(0.7978845608028654 * pre * (1.0 + 0.044715 * square))
        half = 0.5 + 0.5 * bend
        act = (pre * half).astype(BF)
        activ[...] = act
        out[...] = dg(act, tall[...], NN).astype(BF)
        steep = half + pre * (0.5 - 0.5 * bend * bend) * (0.7978845608028654 + 0.10703222440890037 * square)
        grad = (dg(cot[...], tall[...], NT) * steep).astype(BF)
        pre_grad[...] = grad
        bgrad[...] += jnp.sum(grad.astype(F32), axis=0, keepdims=True)
        back[...] = dg(grad, wide[...], NT).astype(BF)

    @pl.when(step < nt)
    def _():
        work(sa, ca, oa, ba)

    @pl.when(step >= nt)
    def _():
        work(sb, cb, ob, bb)


def feed_call(info, sa, sb, ca, cb, ebias, weights, rows, units, nb, live):
    tok, dim = sa.shape
    ff = ebias.shape[1]
    tile = min(256, tok)
    nt = tok // tile
    left = pl.BlockSpec((tile, dim), lambda i, info: (jnp.minimum(i, nt - 1), 0))
    right = pl.BlockSpec((tile, dim), lambda i, info: (jnp.maximum(i - nt, 0), 0))
    flat = pl.BlockSpec((tile, ff), lambda i, info: (i, 0))
    shape = jax.ShapeDtypeStruct((tok, dim), BF)
    return pl.pallas_call(
        functools.partial(feed_kernel, nt, nb, rows, units, live),
        grid_spec=pltpu.PrefetchScalarGridSpec(
            num_scalar_prefetch=1,
            grid=(2 * nt,),
            in_specs=[left, right, left, right, once(ebias.shape)] + [once(weight.shape) for weight in weights],
            out_specs=[flat, flat, left, right, left, right, pl.BlockSpec((1, ff), lambda i, info: (0, 0))],
            scratch_shapes=[pltpu.VMEM((dim, ff), BF), pltpu.VMEM((ff, dim), BF)],
        ),
        out_shape=[jax.ShapeDtypeStruct((2 * tok, ff), BF)] * 2
        + [shape] * 4
        + [jax.ShapeDtypeStruct((1, ff), F32)],
        compiler_params=params(),
        cost_estimate=cost(16 * tok * dim * ff, 16 * tok * dim + 8 * dim * ff, 2 * tok * ff),
        name="feed",
    )(info, sa, sb, ca, cb, ebias, *weights)


def feed_grad_kernel(ns, nb, rows, units, steps, info, *refs):
    half = ns // 2
    activs, cots, seconds, grads = refs[:half], refs[half : half + ns], refs[half + ns : half + 2 * ns], refs[half + 2 * ns : 2 * half + 2 * ns]
    outs = refs[2 * half + 2 * ns :]
    step = pl.program_id(0)

    def total(wides, thins, wide_left):
        out = None
        for rel in range(ns):
            thin = thins[rel]
            tok = thin.shape[0]
            wide = wides[rel // 2][(rel % 2) * tok : (rel % 2 + 1) * tok]
            term = dg(wide, thin[...], TN) if wide_left else dg(thin[...], wide, TN)
            out = term if out is None else out + term
        return out.astype(BF)

    def store(value, high, count, at, low):
        for k in range(value.shape[0] // count):
            slot = info[2 + at * (value.shape[0] // count) + k]
            piece = value[k * count : (k + 1) * count]
            if len(outs) == nb:
                for mine, out in enumerate(outs):

                    @pl.when(slot == mine)
                    def _():
                        out[0, low : low + count] = piece

            else:
                outs[0 if high else 1][slot] = piece

    @pl.when(step < steps)
    def _():
        store(total(activs, cots, True), False, units, step, rows)

    @pl.when(step >= steps)
    def _():
        store(total(grads, seconds, False), True, rows, step - steps, 0)


def feed_grad_call(info, activs, cots, seconds, grads, nb, live):
    ns = len(cots)
    dim = cots[0].shape[1]
    ff = activs[0].shape[1]
    rows, units = dim // nb, ff // nb
    tile = 256
    steps = ff // tile
    tok = ns * cots[0].shape[0]
    left = lambda a: pl.BlockSpec((a.shape[0], tile), lambda i, info: (0, jnp.minimum(i, steps - 1)))
    right = lambda a: pl.BlockSpec((a.shape[0], tile), lambda i, info: (0, jnp.maximum(i - steps, 0)))
    fixed = lambda a: once(a.shape)
    shapes = [(1, rows + units, dim)] * nb if live else [(nb, rows, ff), (nb, units, dim)]
    return pl.pallas_call(
        functools.partial(feed_grad_kernel, ns, nb, rows, units, steps),
        grid_spec=pltpu.PrefetchScalarGridSpec(
            num_scalar_prefetch=1,
            grid=(steps + dim // tile,),
            in_specs=[left(a) for a in activs]
            + [fixed(a) for a in cots]
            + [right(a) for a in seconds]
            + [fixed(a) for a in grads],
            out_specs=[once(shape) for shape in shapes],
        ),
        out_shape=[jax.ShapeDtypeStruct(shape, BF) for shape in shapes],
        compiler_params=params(),
        cost_estimate=cost(4 * tok * dim * ff, 4 * tok * (dim + ff) + 4 * dim * ff),
        name="feed_grad",
    )(info, *activs, *cots, *seconds, *grads)


def split_grad_kernel(ns, info, left, right, *refs):
    outs, held = refs[:ns], refs[ns]
    held[...] = dg(left[...], right[...], TN)
    cw = held.shape[1] // ns
    for rel in range(ns):
        col = pl.ds(pl.multiple_of((info[0] ^ rel) * cw, cw), cw)
        outs[rel][...] = held[:, col].astype(BF)


def split_grad(info, left, right, ns):
    tok, dim = left.shape
    tile = 256
    cw = dim // ns
    return pl.pallas_call(
        functools.partial(split_grad_kernel, ns),
        grid_spec=pltpu.PrefetchScalarGridSpec(
            num_scalar_prefetch=1,
            grid=(dim // tile,),
            in_specs=[pl.BlockSpec((tok, tile), lambda i, info: (0, i)), once((tok, dim))],
            out_specs=[pl.BlockSpec((tile, cw), lambda i, info: (i, 0))] * ns,
            scratch_shapes=[pltpu.VMEM((tile, dim), F32)],
        ),
        out_shape=[jax.ShapeDtypeStruct((dim, cw), BF)] * ns,
        compiler_params=params(40),
        cost_estimate=cost(2 * tok * dim * dim, 6 * dim * dim),
        name="split_grad",
    )(info, left, right)


def joined_grad_kernel(nb, rows, np, info, left, other, *refs):
    rights, outs = refs[:np], refs[np:]
    totals = [dg(left[...], right[...], TN).astype(BF) for right in rights]
    value = jnp.concatenate(totals + [other[...]], 1)
    tile = value.shape[0]
    first = pl.program_id(0) * (tile // rows)
    for k in range(tile // rows):
        put(outs, info[2 + first + k], value[k * rows : (k + 1) * rows])


def joined_grad_call(info, left, rights, other, nb, live):
    count, dim = left.shape
    cols = sum(right.shape[1] for right in rights)
    cw = other.shape[1]
    rows = dim // nb
    tile = 256
    shapes = [(1, rows, cols + cw)] * nb if live else [(nb, rows, cols + cw)]
    return pl.pallas_call(
        functools.partial(joined_grad_kernel, nb, rows, len(rights)),
        grid_spec=pltpu.PrefetchScalarGridSpec(
            num_scalar_prefetch=1,
            grid=(dim // tile,),
            in_specs=[
                pl.BlockSpec((count, tile), lambda i, info: (0, i)),
                pl.BlockSpec((tile, cw), lambda i, info: (i, 0)),
            ]
            + [once(right.shape) for right in rights],
            out_specs=[once(shape) for shape in shapes],
        ),
        out_shape=[jax.ShapeDtypeStruct(shape, BF) for shape in shapes],
        compiler_params=params(),
        cost_estimate=cost(2 * count * dim * cols, 2 * count * (dim + cols) + 4 * dim * dim),
        name="joined_grad",
    )(info, left, other, *rights)


def turn_kernel(ns, np, cw, info, ga, gb, resid, cot, vecs, full, resid_grad, branch, *refs):
    mixed_grads, sums, held = refs[: ns * np], refs[ns * np], refs[ns * np + 1]

    @pl.when(pl.program_id(0) == 0)
    def _():
        sums[...] = jnp.zeros_like(sums)

    grad = ga[...].astype(F32) + gb[...].astype(F32)
    unit, scale = norm_parts(resid[...])
    outer = cot[...].astype(F32)
    value = outer + norm_back(grad, unit, scale, vecs[5:6])
    resid_grad[...] = value
    low = value.astype(BF)
    branch[...] = low
    held[...] = dg(low, full[...], NT).astype(BF)
    pw = cw // np
    for pair in range(np):
        for rel in range(ns):
            col = pl.ds(pl.multiple_of((info[0] ^ rel) * cw + pair * pw, pw), pw)
            mixed_grads[pair * ns + rel][...] = held[:, col]
    for at, term in enumerate((grad * unit, grad, low.astype(F32), outer)):
        sums[at : at + 1] += jnp.sum(term, axis=0, keepdims=True)


def turn_call(info, ga, gb, resid, cot, vecs, full, ns, np):
    tok, dim = resid.shape
    cw = dim // ns
    tile = min(256, tok)
    part = pl.BlockSpec((tile, dim), lambda i, info: (i, 0))
    return pl.pallas_call(
        functools.partial(turn_kernel, ns, np, cw),
        grid_spec=pltpu.PrefetchScalarGridSpec(
            num_scalar_prefetch=1,
            grid=(tok // tile,),
            in_specs=[part, part, part, part, once(vecs.shape), once(full.shape)],
            out_specs=[part, part]
            + [pl.BlockSpec((tile, cw // np), lambda i, info: (i, 0))] * (ns * np)
            + [pl.BlockSpec((8, dim), lambda i, info: (0, 0))],
            scratch_shapes=[pltpu.VMEM((tile, dim), BF)],
        ),
        out_shape=[
            jax.ShapeDtypeStruct((tok, dim), F32),
            jax.ShapeDtypeStruct((tok, dim), BF),
        ]
        + [jax.ShapeDtypeStruct((tok, cw // np), BF)] * (ns * np)
        + [jax.ShapeDtypeStruct((8, dim), F32)],
        compiler_params=params(40),
        cost_estimate=cost(2 * tok * dim * dim, 16 * tok * dim + 2 * dim * dim),
        name="turn",
    )(info, ga, gb, resid, cot, vecs, full)


def last_kernel(ns, nt, np, info, normed, weight, *refs):
    rights, outs, sums = refs[:np], refs[np:-1], refs[-1]
    step = pl.program_id(0)

    @pl.when(step == 0)
    def _():
        sums[...] = jnp.zeros_like(sums)

    grad = None
    at = 0
    for right in rights:
        width = right.shape[1]
        term = dg(right[...], weight[:, at : at + width], NT)
        grad = term if grad is None else grad + term
        at += width
    low = grad.astype(BF)
    rel = ns - 1 - lax.div(step, nt)
    tile = low.shape[0]
    row = pl.multiple_of(lax.rem(step, nt) * tile, tile)
    for mine in range(ns):

        @pl.when(rel == mine)
        def _():
            if ns == 4 and mine % 2:
                outs[2][mine // 2, pl.ds(row, tile)] = low
            elif ns == 4:
                outs[mine // 2][pl.ds(row, tile)] = low
            else:
                outs[mine][pl.ds(row, tile)] = low

    sums[0:1] += jnp.sum(grad * normed[...].astype(F32), axis=0, keepdims=True)
    sums[1:2] += jnp.sum(grad, axis=0, keepdims=True)


def last_call(info, rights, normed, weight, ns):
    count, dim = normed.shape
    cols = weight.shape[1]
    tok = count // ns
    tile = min(256, tok)
    nt = tok // tile
    source = lambda i, info: ((info[0] ^ (ns - 1 - lax.div(i, nt))) * nt + lax.rem(i, nt), 0)
    shapes = [(tok, dim)] * 2 + [(2, tok, dim)] if ns == 4 else [(tok, dim)] * ns
    return pl.pallas_call(
        functools.partial(last_kernel, ns, nt, len(rights)),
        grid_spec=pltpu.PrefetchScalarGridSpec(
            num_scalar_prefetch=1,
            grid=(ns * nt,),
            in_specs=[pl.BlockSpec((tile, dim), source), once(weight.shape)]
            + [pl.BlockSpec((tile, right.shape[1]), source) for right in rights],
            out_specs=[once(shape) for shape in shapes] + [pl.BlockSpec((8, dim), lambda i, info: (0, 0))],
        ),
        out_shape=[jax.ShapeDtypeStruct(shape, BF) for shape in shapes] + [jax.ShapeDtypeStruct((8, dim), F32)],
        compiler_params=params(40),
        cost_estimate=cost(2 * count * dim * cols, 2 * count * (2 * dim + cols)),
        name="last",
    )(info, normed, weight, *rights)


def end_kernel(ga, gb, x, resid_grad, vecs, out):
    grad = ga[...].astype(F32) + gb[...].astype(F32)
    unit, scale = norm_parts(x[...].astype(F32))
    out[...] = resid_grad[...] + norm_back(grad, unit, scale, vecs[0:1])


def end_call(ga, gb, x, resid_grad, vecs):
    tok, dim = x.shape
    tile = min(128, tok)
    part = pl.BlockSpec((tile, dim), lambda i: (i, 0))
    return pl.pallas_call(
        end_kernel,
        grid=(tok // tile,),
        in_specs=[part, part, part, part, pl.BlockSpec(vecs.shape, lambda i: (0, 0))],
        out_specs=part,
        out_shape=jax.ShapeDtypeStruct((tok, dim), F32),
        compiler_params=params(40),
        cost_estimate=cost(20 * tok * dim, 14 * tok * dim),
        name="end",
    )(ga, gb, x, resid_grad, vecs)


def joined_out_kernel(ns, cols, info, *refs):
    parts, joined, outw = refs[:ns], refs[ns], refs[ns + 1]
    cw = parts[0].shape[1] - cols
    for rel in range(ns):
        joined[:, pl.ds(pl.multiple_of((info[0] ^ rel) * cols, cols), cols)] = parts[rel][:, :cols].astype(F32)
        outw[:, pl.ds(pl.multiple_of((info[0] ^ rel) * cw, cw), cw)] = parts[rel][:, cols:].astype(F32)


def joined_out(info, parts, cols):
    ns = len(parts)
    rows, wide = parts[0].shape
    shapes = [(rows, ns * cols), (rows, ns * (wide - cols))]
    return pl.pallas_call(
        functools.partial(joined_out_kernel, ns, cols),
        grid_spec=pltpu.PrefetchScalarGridSpec(
            num_scalar_prefetch=1,
            grid=(1,),
            in_specs=[once(part.shape) for part in parts],
            out_specs=[once(shape) for shape in shapes],
        ),
        out_shape=[jax.ShapeDtypeStruct(shape, F32) for shape in shapes],
        compiler_params=params(40),
        cost_estimate=cost(0, 6 * ns * rows * wide),
        name="joined_out",
    )(info, *parts)


def feed_out_kernel(ns, nb, rows, units, info, *refs):
    parts, expand, shrink = refs[:ns], refs[ns], refs[ns + 1]
    for rel in range(ns):
        seat = info[0] ^ rel
        shrink[pl.ds(pl.multiple_of(seat * units, units), units)] = parts[rel][rows:].astype(F32)
        for k in range(nb):
            col = pl.ds(pl.multiple_of((k * ns + seat) * units, units), units)
            expand[:, col] = parts[rel][:rows, k * units : (k + 1) * units].astype(F32)


def feed_out(info, parts, nb, rows):
    ns = len(parts)
    high, dim = parts[0].shape
    units = high - rows
    shapes = [(rows, ns * units * nb), (ns * units, dim)]
    return pl.pallas_call(
        functools.partial(feed_out_kernel, ns, nb, rows, units),
        grid_spec=pltpu.PrefetchScalarGridSpec(
            num_scalar_prefetch=1,
            grid=(1,),
            in_specs=[once(part.shape) for part in parts],
            out_specs=[once(shape) for shape in shapes],
        ),
        out_shape=[jax.ShapeDtypeStruct(shape, F32) for shape in shapes],
        compiler_params=params(40),
        cost_estimate=cost(0, 6 * ns * high * dim),
        name="feed_out",
    )(info, *parts)


def body(
    layer_input,
    lengths,
    first_gain,
    first_shift,
    joined_weight,
    joined_bias,
    output_weight,
    output_bias,
    second_gain,
    second_shift,
    expand_weight,
    expand_bias,
    shrink_weight,
    shrink_bias,
    out_grad,
):
    ns = lax.axis_size("seq")
    nb = lax.axis_size("batch")
    si = lax.axis_index("seq")
    bi = lax.axis_index("batch")
    tok = layer_input.shape[1]
    dim = layer_input.shape[2]
    heads = H // ns
    np = heads // 2
    cols = 3 * HD * heads
    cw = HD * heads
    rows = dim // nb
    ff = expand_weight.shape[1] // ns
    units = ff // nb
    x = layer_input[0]
    cot = out_grad[0]
    live = ns == 4 and nb == 8
    ring = Ring(nb, bi, live)
    info = jnp.concatenate([jnp.stack([si, lengths[0]]), ring.table()]).astype(jnp.int32)
    head_ids = si * heads + jnp.arange(heads, dtype=jnp.int32) + 1
    slopes = 2.0 ** (-8.0 * head_ids.astype(F32) / H)

    smalls = (first_gain, first_shift, joined_bias, output_bias, second_gain, second_shift, expand_bias, shrink_bias)
    smalls = jnp.concatenate([small.reshape(-1, rows) for small in smalls], 0)
    seat = si.reshape(1).astype(jnp.int32)
    one = first_pack(seat, joined_weight, output_weight, cols, cw)

    def step(held, t):
        if t < ring.half:
            held[t] = ring.back(held[t - 1])
        held[nb - t] = ring.ahead(held[(nb - t + 1) % nb])

    if live:
        x, one = tie(x, one)
        ones = {0: one}
        step(ones, 1)
        xs = gather_rel(x, "seq", ns)
        expand_weight, shrink_weight, _ = tie(expand_weight, shrink_weight, one)
        two = second_pack(seat, expand_weight, shrink_weight, nb, ns)
        smalls, _ = tie(smalls, one)
        smalls = smalls[None]
        for t in range(2, ring.half + 1):
            bit = bits_low_last(nb)[t - 2]
            smalls = jnp.concatenate([smalls, lax.ppermute(smalls, "batch", pairs(nb, bit))], 0)
            if t == 2:
                smalls, ones[1], ones[7], two, xs[1], cot = tie(smalls, ones[1], ones[7], two, xs[1], cot)
                cots = {0: cot, 1: lax.ppermute(cot, "seq", pairs(ns, 1))}
            elif t == 3:
                smalls, ones[2], ones[6], cots[1] = tie(smalls, ones[2], ones[6], cots[1])
            else:
                smalls, ones[3], ones[5], xs[2], two = tie(smalls, ones[3], ones[5], xs[2], two)
                twos = {0: two}
                step(twos, 1)
                cot, _ = tie(cot, two)
                cots[2] = lax.ppermute(cot, "seq", pairs(ns, 2))
            step(ones, t)
        smalls = jnp.take(smalls, place_table(bi, nb), axis=0)
        ones[4], twos[1], twos[7] = tie(ones[4], twos[1], twos[7])
        one_parts = [ones[slot][None] for slot in range(nb)]
    else:
        xs = gather_rel(x, "seq", ns)
        cots = gather_rel(cot, "seq", ns)
        smalls = gather_all(smalls, "batch", nb, bi)
        one_parts = [lax.all_gather(one, "batch")]

    vecs = smalls.astype(F32).transpose(1, 0, 2).reshape(12, dim)
    low = vecs[2:4].reshape(2, nb, rows).transpose(1, 0, 2).reshape(2 * dim)
    low = lax.dynamic_slice(low, (si * 2 * cw,), (2 * cw,)).reshape(heads, 2, HD)
    jbias = jnp.stack([low[:, 0], jnp.zeros_like(low[:, 0]), low[:, 1]], 1).reshape(1, cols)
    ebias = vecs[7:11].reshape(4, nb, rows).transpose(1, 0, 2).reshape(nb, ns, units)
    ebias = lax.dynamic_slice(ebias, (0, si, 0), (nb, 1, units)).reshape(1, ff)
    normed, joined, joined_full, outw_own = first_call(
        info, vecs, jbias, [xs[rel] for rel in range(ns)], one_parts, live
    )
    if live:
        step(twos, 2)
        joined, twos[2], twos[6], cots[2] = tie(joined, twos[2], twos[6], cots[2])
        step(twos, 3)
        cots[3] = lax.ppermute(cots[2], "seq", pairs(ns, 1))
    outw_all = gather_rel(outw_own, "seq", ns)
    mixed = []
    log_sums = []
    merged_parts = []

    def to_tokens(out):
        parts = []
        for rel in range(ns):
            block = lax.dynamic_slice(out, ((si ^ rel) * tok, 0), (tok, 2 * HD))
            parts.append(lax.ppermute(block, "seq", pairs(ns, rel)) if rel else block)
        return parts

    for pair in range(np):
        out, logs = attend(joined, info, slopes, pair)
        if live and pair == 0:
            out, joined, twos[3], twos[5], cots[3], outw_all[2], outw_all[1] = tie(
                out, joined, twos[3], twos[5], cots[3], outw_all[2], outw_all[1]
            )
            step(twos, 4)
            outw_all[3] = lax.ppermute(outw_all[2], "seq", pairs(ns, 1))
        mixed.append(out)
        log_sums.append(logs)
        merged_parts.append(to_tokens(out))
        if live and pair == 1:
            out, twos[4], outw_all[3], *merged_parts[0] = tie(out, twos[4], outw_all[3], *merged_parts[0])
            mixed[1] = out
            merged_parts[1] = to_tokens(out)
    merged_parts = [block for parts in merged_parts for block in parts]
    merged, resid, second, outw_full = middle_call(
        info, x, vecs, merged_parts, [outw_all[rel] for rel in range(ns)]
    )
    if live:
        two_parts = [twos[slot][None] for slot in range(nb)]
    else:
        expand_part = expand_weight.reshape(rows, nb, ns, units)
        expand_part = lax.dynamic_slice(expand_part, (0, 0, si, 0), (rows, nb, 1, units)).reshape(rows, ff)
        shrink_part = lax.dynamic_slice(shrink_weight, (si * units, 0), (units, dim))
        two_parts = [lax.all_gather(expand_part, "batch"), lax.all_gather(shrink_part, "batch")]
    out_parts = {}
    back_parts = {}
    activs = []
    pre_grads = []
    bias_sum = 0.0
    if live:
        seconds = {0: second, 2: lax.ppermute(second, "seq", pairs(ns, 2)), 1: lax.ppermute(second, "seq", pairs(ns, 1))}
    else:
        seconds = gather_rel(second, "seq", ns)
    for rel in range(0, ns, 2):
        activ, pre_grad, oa, ob, ba, bb, bgrad = feed_call(
            info, seconds[rel], seconds[rel + 1], cots[rel], cots[rel + 1], ebias, two_parts, rows, units, nb, live
        )
        if live and rel == 0:
            activ, ob, bb, seconds[2] = tie(activ, ob, bb, seconds[2])
            seconds[3] = lax.ppermute(seconds[2], "seq", pairs(ns, 1))
            seconds[2], seconds[3] = tie(seconds[2], seconds[3])
            near_back = lax.ppermute(bb, "seq", pairs(ns, 1))
            near_out = lax.ppermute(ob, "seq", pairs(ns, 1))
        activs.append(activ)
        pre_grads.append(pre_grad)
        bias_sum = bias_sum + bgrad
        out_parts.update({rel: oa, rel + 1: ob})
        back_parts.update({rel: ba, rel + 1: bb})
    if live:
        back_parts[3], near_back, near_out = tie(back_parts[3], near_back, near_out)
        back_a = add16(back_parts[0], near_back)
        out_a = add16(out_parts[0], near_out)
        far_back = lax.ppermute(back_parts[3], "seq", pairs(ns, 1))
        far_back, out_far = tie(far_back, out_parts[3])
        back_b = lax.ppermute(add16(back_parts[2], far_back), "seq", pairs(ns, 2))
        far_out = lax.ppermute(out_far, "seq", pairs(ns, 1))
    else:
        back_a, back_b = scatter_rel(back_parts, "seq", ns, last=False)
        out_a, out_b = scatter_rel(out_parts, "seq", ns, last=False)
    feed_stack = feed_grad_call(
        info,
        activs,
        [cots[rel] for rel in range(ns)],
        [seconds[rel] for rel in range(ns)],
        pre_grads,
        nb,
        live,
    )

    class Scatter:
        def __init__(self, parts):
            self.parts = [part[0] for part in parts]
            self.t = 0
            self.ahead = self.parts[ring.half]
            self.back = self.parts[ring.half + 1]

        def send(self):
            self.t += 1
            self.got_ahead = ring.ahead(self.ahead)
            self.got_back = ring.back(self.back) if self.t > 1 else None

        def take(self, *after):
            if after:
                self.got_ahead, *_ = tie(self.got_ahead, *after)
            if self.t == ring.half:
                total = self.parts[0].astype(F32) + self.got_ahead.astype(F32) + self.got_back.astype(F32)
                return total.astype(BF)
            self.ahead = add16(self.parts[ring.half - self.t], self.got_ahead)
            if self.t > 1:
                self.back = add16(self.parts[nb - ring.half + self.t], self.got_back)

    if live:
        feed_ring = Scatter(feed_stack)
        feed_ring.send()
        back_b, back_a, out_a, far_out, _ = tie(back_b, back_a, out_a, far_out, feed_stack[0])
        out_b = add16(out_parts[2], far_out)
    resid_grad, branch, *mixed_grads, turn_sums = turn_call(
        info, back_a, back_b, resid, cot, vecs, outw_full, ns, np
    )
    outw_stack = split_grad(info, merged, branch, ns)
    joined_grads = []
    sides = []

    def to_heads(pair):
        blocks = mixed_grads[pair * ns : (pair + 1) * ns]
        return [lax.ppermute(block, "seq", pairs(ns, rel)) if rel else block for rel, block in enumerate(blocks)]

    grads = to_heads(0)
    if live:
        feed_ring.take(*grads, *outw_stack)
        grads[0], *rest = tie(grads[0], feed_ring.ahead, *grads[1:], *outw_stack, *mixed_grads[ns:])
        feed_ring.ahead, grads[1:], outw_stack = rest[0], rest[1:ns], rest[ns : 2 * ns]
        mixed_grads[ns:] = rest[2 * ns :]
        feed_ring.send()
    for pair in range(np):
        if pair:
            grads = after
        out, side = attend_back(joined, grads, mixed[pair], log_sums[pair], info, slopes, pair)
        if pair + 1 < np:
            after = to_heads(pair + 1)
        if live and pair == 0:
            feed_ring.take(out, *after)
            after[0], feed_ring.ahead, feed_ring.back, out, *outw_stack = tie(
                after[0], feed_ring.ahead, feed_ring.back, out, *outw_stack
            )
            feed_ring.send()
        elif live:
            feed_ring.take(out)
        joined_grads.append(out)
        sides.append(side)
    outw_share = scatter_rel(dict(enumerate(outw_stack)), "seq", ns)
    if live:
        joined_grads[1], outw_share, feed_ring.ahead, feed_ring.back = tie(
            joined_grads[1], outw_share, feed_ring.ahead, feed_ring.back
        )
        feed_ring.send()
        out_b, _ = tie(out_b, outw_share)
        out_b = lax.ppermute(out_b, "seq", pairs(ns, 2))
    joined_stack = joined_grad_call(info, normed, joined_grads, outw_share, nb, live)
    if live:
        feed_share = feed_ring.take(joined_stack[0])
        feed_share, *joined_stack = tie(feed_share, *joined_stack)
        joined_ring = Scatter(joined_stack)
        joined_ring.send()
        joined_grads[0], _ = tie(joined_grads[0], joined_stack[0])
    *normed_parts, last_sums = last_call(info, joined_grads, normed, joined_full, ns)
    if live:
        joined_ring.take(last_sums, out_b)
        joined_ring.ahead, out_b, feed_share, sent, last_sums = tie(
            joined_ring.ahead, out_b, feed_share, normed_parts[2], last_sums
        )
        joined_ring.send()
        got = lax.ppermute(sent, "seq", pairs(ns, 1))
        feed_parts = {0: feed_share, 2: lax.ppermute(feed_share, "seq", pairs(ns, 2))}
        norm_a = add16(normed_parts[0], got[0])
        far = add16(normed_parts[1], got[1])
    else:
        norm_a, norm_b = scatter_rel(dict(enumerate(normed_parts)), "seq", ns, last=False)
    layer_output = (resid + out_a.astype(F32) + out_b.astype(F32) + vecs[11:12]).astype(BF)

    shift_one = last_sums[1:2]
    gain_one = (last_sums[0:1] - vecs[1:2] * shift_one) / vecs[0:1]
    side = jnp.concatenate(sides, 1).reshape(heads, 3, HD)
    side = jnp.stack([side[:, 0], side[:, 2]], 1).reshape(2 * cw)
    side = lax.dynamic_update_slice(jnp.zeros((2 * dim,), F32), side, (si * 2 * cw,))
    side = side.reshape(nb, 2, rows).transpose(1, 0, 2).reshape(2, dim)
    spread_bias = lax.dynamic_update_slice(
        jnp.zeros((nb, ns, units), F32), bias_sum.reshape(nb, 1, units), (0, si, 0)
    )
    spread_bias = spread_bias.reshape(nb, 4, rows).transpose(1, 0, 2).reshape(4, dim)
    shares = jnp.concatenate(
        [gain_one, shift_one, side, turn_sums[2:3], turn_sums[0:2], spread_bias, turn_sums[3:4]], 0
    )
    shares = shares.astype(BF).reshape(12, nb, rows).transpose(1, 0, 2)

    def ordered(block):
        parts = gather_rel(block, "seq", ns)
        return [parts[rel] for rel in range(ns)]

    if live:
        shares = jnp.take(shares, owner_table(bi, nb), axis=0)

        def fold(stack, bit):
            half = stack.shape[0] // 2
            return add16(stack[:half], lax.ppermute(stack[half:], "batch", pairs(nb, bit)))

        shares = fold(shares, 1)
        joined_ring.take(shares, far, feed_parts[2])
        joined_ring.ahead, joined_ring.back, shares, far, feed_parts[0], feed_parts[2] = tie(
            joined_ring.ahead, joined_ring.back, shares, far, feed_parts[0], feed_parts[2]
        )
        joined_ring.send()
        norm_b = lax.ppermute(far, "seq", pairs(ns, 2))
        feed_parts[1] = lax.ppermute(feed_parts[0], "seq", pairs(ns, 1))
        shares = fold(shares, 4)
        joined_ring.take(shares, feed_parts[1])
        joined_ring.ahead, joined_ring.back, shares, feed_parts[1], feed_parts[2] = tie(
            joined_ring.ahead, joined_ring.back, shares, feed_parts[1], feed_parts[2]
        )
        joined_ring.send()
        feed_parts[3] = lax.ppermute(feed_parts[2], "seq", pairs(ns, 1))
        shares = fold(shares, 2)[0]
        expand_grad, shrink_grad = feed_out(info, [feed_parts[rel] for rel in range(ns)], nb, rows)
        joined_share = joined_ring.take(norm_b, shares, expand_grad)
        joined_share, norm_b, shares = tie(joined_share, norm_b, shares)
        joined_parts = {0: joined_share, 2: lax.ppermute(joined_share, "seq", pairs(ns, 2))}
        joined_parts[1] = lax.ppermute(joined_share, "seq", pairs(ns, 1))
        shares = add16(shares, lax.ppermute(shares, "seq", pairs(ns, 1)))
        input_grad = end_call(norm_a, norm_b, x, resid_grad, vecs)
        joined_parts[2], joined_parts[1], shares, _ = tie(joined_parts[2], joined_parts[1], shares, input_grad)
        joined_parts[3] = lax.ppermute(joined_parts[2], "seq", pairs(ns, 1))
        shares = add16(shares, lax.ppermute(shares, "seq", pairs(ns, 2)))
        joined_parts = [joined_parts[rel] for rel in range(ns)]
    else:
        input_grad = end_call(norm_a, norm_b, x, resid_grad, vecs)
        shares = scatter_all(shares, "batch", nb, bi)
        for bit in bits_low_last(ns)[::-1]:
            shares = add16(shares, lax.ppermute(shares, "seq", pairs(ns, bit)))
        joined_share = lax.psum_scatter(joined_stack[0], "batch", scatter_dimension=0)
        expand_share = lax.psum_scatter(feed_stack[0], "batch", scatter_dimension=0)
        shrink_share = lax.psum_scatter(feed_stack[1], "batch", scatter_dimension=0)
        seats = jnp.arange(ns, dtype=jnp.int32) ^ si
        shrink_grad = jnp.take(jnp.stack(ordered(shrink_share)), seats, axis=0).astype(F32).reshape(ns * units, dim)
        expand_grad = jnp.take(jnp.stack(ordered(expand_share)), seats, axis=0).astype(F32)
        expand_grad = expand_grad.reshape(ns, rows, nb, units).transpose(1, 2, 0, 3).reshape(rows, ns * ff)
        joined_parts = ordered(joined_share)
    shares = shares.astype(F32)
    joined_wgrad, outw_grad = joined_out(info, joined_parts, cols)
    small = []
    at = 0
    for size in (1, 1, 2, 1, 1, 1, 4, 1):
        small.append(shares[at : at + size].reshape(size * rows))
        at += size
    return (
        layer_output[None],
        input_grad[None],
        small[0],
        small[1],
        joined_wgrad,
        small[2],
        outw_grad,
        small[3],
        small[4],
        small[5],
        expand_grad,
        small[6],
        shrink_grad,
        small[7],
    )


def solution(mesh):
    row = P("batch")
    mat = P("batch", None)
    act = P("batch", "seq", None)
    return jax.shard_map(
        body,
        mesh=mesh,
        in_specs=(act, row, row, row, mat, row, mat, row, row, row, mat, row, mat, row, act),
        out_specs=(act, act, row, row, mat, row, mat, row, row, row, mat, row, mat, row),
        check_vma=False,
    )
```

time: 543 us -> 404 us (0.74)
  waiting for transfers between devices: 194 us -> 104 us
  local copies, waits for them, and re-layouts: 79.7 us -> 37.2 us
  other arithmetic: 53 us -> 29.4 us
  Pallas kernels: 149 us -> 164 us
    ppermute x35 -> x69, waiting for transfers between devices: 167 us -> 91.3 us  [the longest x16 22.2 us: ahead(): return lax.ppermute(value, 'batch', self.forward)]
    concatenate x16 -> x6, other arithmetic: 22.1 us -> 0.14 us  [the longest x1 0.08 us: body(): jnp.concatenate([jnp.stack([si, lengths[0]]), ring.table()])]
    ppermute x24 -> x5, waiting for transfers between devices: 22.2 us -> 3.14 us  [gather_rel(): out[rel | bit] = lax.ppermute(out[rel], axis, pairs(size, bit))]
    ppermute x35 -> x69, starting transfers between devices: 40.3 us -> 56.7 us  [the longest x12 18.8 us: back(): return lax.ppermute(value, 'batch', self.backward)]
    squeeze x7 -> x0, local copies, waits for them, and re-layouts: 11.4 us -> none  [the longest x1 3.02 us: body(): normed_parts[rel]]
    pallas_call x12 -> x15, Pallas kernels: 112 us -> 122 us  [the longest x2 32.1 us: feed_call(): pl.pallas_call(functools.partial(feed_kernel, nt, nb, rows, units, live),...]
    reshape x8 -> x5, local copies, waits for them, and re-layouts: 10.9 us -> 2.37 us  [the longest x3 1.68 us: body(): small.append(shares[at:at + size].reshape(size * rows))]
    convert_element_type x21 -> x20, other arithmetic: 14.1 us -> 22.3 us  [add16(): return (left.astype(F32) + right.astype(F32)).astype(BF)]
  transfers between devices with their start and end apart: 71 -> 77, of which waited for: 21 -> 29; matrix products, arithmetic and copies ran while one was open for 20% -> 8% of each run, Pallas kernels for 27% -> 39%
where the time goes in v2:
time: 404 us; the launch traced here: 399 us
  Pallas kernels  164 us (41%)
  waiting for transfers between devices  104 us (26%)
  starting transfers between devices  61.4 us (15%)
  local copies, waits for them, and re-layouts  37.2 us (9%)
  other arithmetic  29.4 us (7%)
    pallas_call x2, Pallas kernels, attend_back(): pl.pallas_call(functools.partial(attend_back_kernel, count, min(512, coun...  39.3 us
    pallas_call x2, Pallas kernels, feed_call(): pl.pallas_call(functools.partial(feed_kernel, nt, nb, rows, units, live),...  32.1 us
    unnamed x152, local copies, waits for them, and re-layouts  27.6 us
    pallas_call x2, Pallas kernels, attend(): pl.pallas_call(functools.partial(attend_kernel, count, min(512, count), p...  22.4 us
    convert_element_type x20, other arithmetic, add16(): return (left.astype(F32) + right.astype(F32)).astype(BF)  22.3 us
    ppermute x16, waiting for transfers between devices, ahead(): return lax.ppermute(value, 'batch', self.forward)  22.2 us
    pallas_call x1, Pallas kernels, feed_grad_call(): pl.pallas_call(functools.partial(feed_grad_kernel, ns, nb, rows, units, s...  19 us
    ppermute x12, starting transfers between devices, back(): return lax.ppermute(value, 'batch', self.backward)  18.8 us
  transfers between devices with their start and end apart: 77, of which 29 were waited for; matrix products, arithmetic and copies ran while one was open for 8% of the time, Pallas kernels for 39%

profile of v2, /device:TPU:0, one launch (start us, length us, event | category | flops | bytes accessed | tf_op | source)
XLA Modules:
  0.0 398.7 jit_solution(939315056905680345)
XLA Ops:
  3.4 2.6 collective-permute-start.1
  6.2 2.2 concatenate.34
  8.4 1.9 collective-permute-start
  20.3 4.5 %collective-permute-done.4 = bf16[2,12,128]{2,1,0:T(8,128)(2,1)S(1)} collective-permute-done((bf16[2,12,128]{2,1,0:T(8,128)(2,1)S(1)}, bf16[2,12,128]{2,1,0:T(8,128)(2,1)S(1)}, u32[]{:S(2)}, u32[]{:S(2)}) %collective-permute-start.4) | collective-permute-done | bytes 6176 | tf_op jit(solution)/shard_map/ppermute | solution.py:950
  26.9 2.9 collective-permute-start.9
  29.8 2.0 collective-permute-start.8
  31.8 5.1 %collective-permute-done.8 = bf16[4,12,128]{2,1,0:T(8,128)(2,1)S(1)} collective-permute-done((bf16[4,12,128]{2,1,0:T(8,128)(2,1)S(1)}, bf16[4,12,128]{2,1,0:T(8,128)(2,1)S(1)}, u32[]{:S(2)}, u32[]{:S(2)}) %collective-permute-start.8) | collective-permute-done | bytes 12320 | tf_op jit(solution)/shard_map/ppermute | solution.py:950
  36.9 3.1 collective-permute-done.11.refs_2_
  47.2 14.2 %collective-permute-done.13 = bf16[128,1024]{1,0:T(8,128)(2,1)S(1)} collective-permute-done((bf16[128,1024]{1,0:T(8,128)(2,1)}, bf16[128,1024]{1,0:T(8,128)(2,1)S(1)}, u32[]{:S(2)}, u32[]{:S(2)}) %collective-permute-start.13) | collective-permute-done | bytes 262176 | tf_op jit(solution)/shard_map/ppermute | solution.py:148
  69.1 11.3 %first.1 = (bf16[2048,1024]{1,0:T(8,128)(2,1)}, bf16[2048,768]{1,0:T(8,128)(2,1)S(1)}, bf16[1024,768]{1,0:T(8,128)(2,1)S(1)}, bf16[1024,256]{1,0:T(8,128)(2,1)S(1)}) custom-call(s32[18]{0:T(128)S(1)} %pad_add_fusion.info, f32[12,1024]{1,0:T(8,128)S(1)} %bitcast.160, f32[1,768]{1,0:T(1,128)S(1)} %reshape.178.jbias, bf16[512,1024]{1,0:T(8,128)(2,1)S(1)} %bitcast.150, ...), custom_call_target="tpu_custom_call" | custom-call | flops 3221225 | bytes 11534 | tf_op jit(solution)/shard_map/first/pallas_call | solution.py:271
  88.5 11.2 %attend.2 = (bf16[2048,128]{1,0:T(8,128)(2,1)}, f32[2048,128]{1,0:T(8,128)}) custom-call(s32[18]{0:T(128)} %copy-done.39, f32[4]{0:T(128)} %multiply_power_fusion.slopes, bf16[2048,768]{1,0:T(8,128)(2,1)} %copy-done), custom_call_target="tpu_custom_call" | custom-call | flops 4294967 | bytes 2621 | tf_op jit(solution)/shard_map/attend/pallas_call | solution.py:359
  105.5 11.2 %attend.3 = (bf16[2048,128]{1,0:T(8,128)(2,1)}, f32[2048,128]{1,0:T(8,128)}) custom-call(s32[18]{0:T(128)} %copy-done.39, f32[4]{0:T(128)} %multiply_power_fusion.slopes, bf16[2048,768]{1,0:T(8,128)(2,1)} %copy-done), custom_call_target="tpu_custom_call" | custom-call | flops 4294967 | bytes 2621 | tf_op jit(solution)/shard_map/attend/pallas_call | solution.py:359
  120.4 4.9 %collective-permute-done.30.refs_6_ = bf16[512,128]{1,0:T(8,128)(2,1)S(1)} collective-permute-done((bf16[512,128]{1,0:T(8,128)(2,1)S(1)}, bf16[512,128]{1,0:T(8,128)(2,1)S(1)}, u32[]{:S(2)}, u32[]{:S(2)}) %collective-permute-start.30) | collective-permute-done | bytes 131104 | tf_op jit(solution)/shard_map/ppermute | solution.py:995
  129.5 4.3 %middle.1 = (bf16[512,1024]{1,0:T(8,128)(2,1)S(1)}, f32[512,1024]{1,0:T(8,128)S(1)}, bf16[512,1024]{1,0:T(8,128)(2,1)}, bf16[1024,1024]{1,0:T(8,128)(2,1)S(1)}) custom-call(s32[18]{0:T(128)S(1)} %copy-done.40, bf16[512,1024]{1,0:T(8,128)(2,1)S(1)} %bitcast.151, f32[12,1024]{1,0:T(8,128)S(1)} %bitcast.161, bf16[512,128]{1,0:T(8,128)(2,1)S(1)} %get-tuple-element.242.refs_0_, ...), custom_call_target="tpu_custom_call" | custom-call | flops 1073741 | bytes 10485 | tf_op jit(solution)/shard_map/middle/pallas_call | solution.py:475
  139.4 16.1 %feed.2 = (bf16[1024,1024]{1,0:T(8,128)(2,1)}, bf16[1024,1024]{1,0:T(8,128)(2,1)}, bf16[512,1024]{1,0:T(8,128)(2,1)}, bf16[512,1024]{1,0:T(8,128)(2,1)}, bf16[51...) custom-call(s32[18]{0:T(128)} %copy-done.39, bf16[512,1024]{1,0:T(8,128)(2,1)} %get-tuple-element.250.sa.refs_6_, ...), custom_call_target="tpu_custom_call" | custom-call | flops 8589934 | bytes 16777 | tf_op jit(solution)/shard_map/feed/pallas_call | solution.py:550
  155.5 6.7 %collective-permute-done.33.sa.refs_8_ = bf16[512,1024]{1,0:T(8,128)(2,1)} collective-permute-done((bf16[512,1024]{1,0:T(8,128)(2,1)}, bf16[512,1024]{1,0:T(8,128)(2,1)}, u32[]{:S(2)}, u32[]{:S(2)}) %collective-permute-start.33) | collective-permute-done | bytes 1048608 | tf_op jit(solution)/shard_map/ppermute | solution.py:1030
  162.7 2.4 collective-permute-done.34.sb.refs_9_
  166.1 16.1 %feed.3 = (bf16[1024,1024]{1,0:T(8,128)(2,1)}, bf16[1024,1024]{1,0:T(8,128)(2,1)}, bf16[512,1024]{1,0:T(8,128)(2,1)}, bf16[512,1024]{1,0:T(8,128)(2,1)}, bf16[51...) custom-call(s32[18]{0:T(128)} %copy-done.39, ...), custom_call_target="tpu_custom_call" | custom-call | flops 8589934 | bytes 16777 | tf_op jit(solution)/shard_map/feed/pallas_call | solution.py:550
  182.4 2.7 collective-permute-done.37
  185.1 2.6 add_convert_fusion.4
  188.2 19.0 %feed_grad.1 = (bf16[1,256,1024]{2,1,0:T(8,128)(2,1)}, bf16[1,256,1024]{2,1,0:T(8,128)(2,1)}, bf16[1,256,1024]{2,1,0:T(8,128)(2,1)}, bf16[1,256,1024]{2,1,0:T(8,...) custom-call(s32[18]{0:T(128)} %copy-done.39, ...), custom_call_target="tpu_custom_call" | custom-call | flops 8589934 | bytes 20971 | tf_op jit(solution)/shard_map/feed_grad/pallas_call | solution.py:619
  210.9 2.2 collective-permute-done.38.gb
  213.2 4.0 %turn.1 = (f32[512,1024]{1,0:T(8,128)S(1)}, bf16[512,1024]{1,0:T(8,128)(2,1)S(1)}, bf16[512,128]{1,0:T(8,128)(2,1)S(1)}, bf16[512,128]{1,0:T(8,128)(2,1)S(1)}, b...) custom-call(s32[18]{0:T(128)S(1)} %copy-done.41, ...), custom_call_target="tpu_custom_call" | custom-call | flops 1073741 | bytes 10485 | tf_op jit(solution)/shard_map/turn/pallas_call | solution.py:731
  221.9 2.9 split_grad.1
  224.9 1.9 collective-permute-done.43.refs_3_
  230.0 4.6 %collective-permute-done.48 = bf16[256,1024]{1,0:T(8,128)(2,1)S(1)} collective-permute-done((bf16[256,1024]{1,0:T(8,128)(2,1)S(1)}, bf16[256,1024]{1,0:T(8,128)(2,1)S(1)}, u32[]{:S(2)}, u32[]{:S(2)}) %collective-permute-start.48) | collective-permute-done | bytes 524320 | tf_op jit(solution)/shard_map/ppermute | solution.py:151
  234.9 19.7 %attend_back.2 = (bf16[2048,384]{1,0:T(8,128)(2,1)}, f32[1,384]{1,0:T(1,128)}) custom-call(s32[18]{0:T(128)} %copy-done.39, f32[4]{0:T(128)} %multiply_power_fusion.slopes, bf16[2048,768]{1,0:T(8,128)(2,1)} %copy-done, bf16[2048,128]{1,0:T(8,128)(2,1)} %get-tuple-element.241.mixed, f32[2048,128]{1,0:T(8,128)} %get-tuple-element.303.sums, ...), custom_call_target="tpu_custom_call" | custom-call | flops 10737418 | bytes 5242 | tf_op jit(solution)/shard_map/attend_back/pallas_call | solution.py:435
  254.7 2.0 fusion.6
  259.0 19.5 %attend_back.3 = (bf16[2048,384]{1,0:T(8,128)(2,1)}, f32[1,384]{1,0:T(1,128)}) custom-call(s32[18]{0:T(128)} %copy-done.39, f32[4]{0:T(128)} %multiply_power_fusion.slopes, bf16[2048,768]{1,0:T(8,128)(2,1)} %copy-done, bf16[2048,128]{1,0:T(8,128)(2,1)} %get-tuple-element.246.mixed, f32[2048,128]{1,0:T(8,128)} %get-tuple-element.279.sums, ...), custom_call_target="tpu_custom_call" | custom-call | flops 10737418 | bytes 5242 | tf_op jit(solution)/shard_map/attend_back/pallas_call | solution.py:435
  280.3 2.1 fusion.4
  283.7 9.9 %collective-permute-done.51 = bf16[1024,256]{1,0:T(8,128)(2,1)S(1)} collective-permute-done((bf16[1024,256]{1,0:T(8,128)(2,1)S(1)}, bf16[1024,256]{1,0:T(8,128)(2,1)S(1)}, u32[]{:S(2)}, u32[]{:S(2)}) %collective-permute-start.51) | collective-permute-done | bytes 524320 | tf_op jit(solution)/shard_map/ppermute | solution.py:83
  293.6 2.0 add_convert_fusion.5.other
  299.6 10.6 %joined_grad.1 = (bf16[1,128,1024]{2,1,0:T(8,128)(2,1)}, bf16[1,128,1024]{2,1,0:T(8,128)(2,1)}, bf16[1,128,1024]{2,1,0:T(8,128)(2,1)}, bf16[1,128,1024]{2,1,0:T(...) custom-call(s32[18]{0:T(128)} %copy-done.39, ...), custom_call_target="tpu_custom_call" | custom-call | flops 3221225 | bytes 11534 | tf_op jit(solution)/shard_map/joined_grad/pallas_call | solution.py:683
  310.2 2.5 fusion.9.refs_0_
  316.1 10.0 %last.1 = (bf16[512,1024]{1,0:T(8,128)(2,1)S(1)}, bf16[512,1024]{1,0:T(8,128)(2,1)S(1)}, bf16[2,512,1024]{2,1,0:T(8,128)(2,1)}, f32[8,1024]{1,0:T(8,128)S(1)}) custom-call(s32[18]{0:T(128)S(1)} %copy-done.42, bf16[2048,1024]{1,0:T(8,128)(2,1)S(1)} %copy-done.1, bf16[1024,768]{1,0:T(8,128)(2,1)S(1)} %copy-done.14, bf16[2048,384]{1,0:T(8,128)(2,1)S(1)} %copy-done.5, ...), custom_call_target="tpu_custom_call" | custom-call | flops 3221225 | bytes 11534 | tf_op jit(solution)/shard_map/last/pallas_call | solution.py:796
  333.5 4.9 %collective-permute-done.62 = bf16[128,1024]{1,0:T(8,128)(2,1)} collective-permute-done((bf16[128,1024]{1,0:T(8,128)(2,1)}, bf16[128,1024]{1,0:T(8,128)(2,1)}, u32[]{:S(2)}, u32[]{:S(2)}) %collective-permute-start.62) | collective-permute-done | bytes 262176 | tf_op jit(solution)/shard_map/ppermute | solution.py:151
  341.8 3.2 fusion
  345.0 2.7 collective-permute-done.59
  347.7 7.0 %collective-permute-done.61.refs_2_ = bf16[256,1024]{1,0:T(8,128)(2,1)S(1)} collective-permute-done((bf16[256,1024]{1,0:T(8,128)(2,1)}, bf16[256,1024]{1,0:T(8,128)(2,1)S(1)}, u32[]{:S(2)}, u32[]{:S(2)}) %collective-permute-start.61) | collective-permute-done | bytes 524320 | tf_op jit(solution)/shard_map/ppermute | solution.py:1153
  355.3 2.4 collective-permute-start.64
  360.0 4.5 %collective-permute-done.64 = bf16[2,12,128]{2,1,0:T(8,128)(2,1)S(1)} collective-permute-done((bf16[2,12,128]{2,1,0:T(8,128)(2,1)S(1)}, bf16[2,12,128]{2,1,0:T(8,128)(2,1)S(1)}, u32[]{:S(2)}, u32[]{:S(2)}) %collective-permute-start.64) | collective-permute-done | bytes 6176 | tf_op jit(solution)/shard_map/ppermute | solution.py:1184
  369.7 6.4 %collective-permute-done.69 = bf16[1,12,128]{2,1,0:T(8,128)(2,1)S(1)} collective-permute-done((bf16[1,12,128]{2,1,0:T(8,128)(2,1)S(1)}, bf16[1,12,128]{2,1,0:T(8,128)(2,1)S(1)}, u32[]{:S(2)}, u32[]{:S(2)}) %collective-permute-start.69) | collective-permute-done | bytes 3104 | tf_op jit(solution)/shard_map/ppermute | solution.py:1184
  376.2 3.0 feed_out.1
  379.1 4.9 %collective-permute-done.68.gb = bf16[512,1024]{1,0:T(8,128)(2,1)S(1)} collective-permute-done((bf16[512,1024]{1,0:T(8,128)(2,1)S(1)}, bf16[512,1024]{1,0:T(8,128)(2,1)S(1)}, u32[]{:S(2)}, u32[]{:S(2)}) %collective-permute-start.68) | collective-permute-done | bytes 1048608 | tf_op jit(solution)/shard_map/ppermute | solution.py:1192
  385.4 2.9 end.1
  388.3 2.9 collective-permute-done.72.refs_2_
  391.8 2.7 fusion.2
  396.5 2.0 joined_out.1
  (352 shorter events, 105.7 us)
Async XLA Ops:
  2.9 11.4 %collective-permute-start.3 = (bf16[512,1024]{1,0:T(8,128)(2,1)}, bf16[512,1024]{1,0:T(8,128)(2,1)}, u32[]{:S(2)}, u32[]{:S(2)}) collective-permute-start(bf16[512,1024]{1,0:T(8,128)(2,1)} %bitcast.148), channel_id=1, source_target_pairs={{0,8},{8,0},{16,24},{24,16},{1,9},{9,1},{17,25},{25,17},{2,10},{10... | collective-permute-start | bytes 3145736 | tf_op jit(solution)/shard_map/ppermute | solution.py:73
  14.4 11.6 %collective-permute-start.7 = (bf16[512,1024]{1,0:T(8,128)(2,1)S(1)}, bf16[512,1024]{1,0:T(8,128)(2,1)S(1)}, u32[]{:S(2)}, u32[]{:S(2)}) collective-permute-start(bf16[512,1024]{1,0:T(8,128)(2,1)S(1)} %bitcast.155), channel_id=1, source_target_pairs={{0,8},{8,0},{16,24},{24,16},{1,9},{9,1},{17,25},{25,17},{2,10},{10... | collective-permute-start | bytes 3145736 | tf_op jit(solution)/shard_map/ppermute | solution.py:953
  14.4 25.7 %collective-permute-start.11 = (bf16[512,1024]{1,0:T(8,128)(2,1)S(1)}, bf16[512,1024]{1,0:T(8,128)(2,1)}, u32[]{:S(2)}, u32[]{:S(2)}) collective-permute-start(bf16[512,1024]{1,0:T(8,128)(2,1)S(1)} %bitcast.149), channel_id=1, source_target_pairs={{0,16},{8,24},{16,0},{24,8},{1,17},{9,25},{17,1},{25,9},{2,18},{10... | collective-permute-start | bytes 3145736 | tf_op jit(solution)/shard_map/ppermute | solution.py:73
  26.9 13.1 %collective-permute-start.9 = (bf16[128,1024]{1,0:T(8,128)(2,1)}, bf16[128,1024]{1,0:T(8,128)(2,1)S(1)}, u32[]{:S(2)}, u32[]{:S(2)}) collective-permute-start(bf16[128,1024]{1,0:T(8,128)(2,1)} %collective-permute-done.5), channel_id=1, source_target_pairs={{2,0},{4,2},{6,4},{7,6},{5,7},{3,5},{1,3},{0,1},{10,8},{12,10},{14... | collective-permute-start | bytes 786440 | tf_op jit(solution)/shard_map/ppermute | solution.py:151
  29.8 11.0 %collective-permute-start.10 = (bf16[128,1024]{1,0:T(8,128)(2,1)}, bf16[128,1024]{1,0:T(8,128)(2,1)}, u32[]{:S(2)}, u32[]{:S(2)}) collective-permute-start(bf16[128,1024]{1,0:T(8,128)(2,1)} %collective-permute-done.6), channel_id=1, source_target_pairs={{0,2},{2,4},{4,6},{6,7},{7,5},{5,3},{3,1},{1,0},{8,10},{10,12},{12... | collective-permute-start | bytes 786440 | tf_op jit(solution)/shard_map/ppermute | solution.py:148
  40.8 21.3 %collective-permute-start.14 = (bf16[256,1024]{1,0:T(8,128)(2,1)S(1)}, bf16[256,1024]{1,0:T(8,128)(2,1)}, u32[]{:S(2)}, u32[]{:S(2)}) collective-permute-start(bf16[256,1024]{1,0:T(8,128)(2,1)S(1)} %second_pack.1), channel_id=1, source_target_pairs={{2,0},{4,2},{6,4},{7,6},{5,7},{3,5},{1,3},{0,1},{10,8},{12,10},{14... | collective-permute-start | bytes 1572872 | tf_op jit(solution)/shard_map/ppermute | solution.py:151
  42.6 19.5 %collective-permute-start.15 = (bf16[256,1024]{1,0:T(8,128)(2,1)S(1)}, bf16[256,1024]{1,0:T(8,128)(2,1)}, u32[]{:S(2)}, u32[]{:S(2)}) collective-permute-start(bf16[256,1024]{1,0:T(8,128)(2,1)S(1)} %second_pack.1), channel_id=1, source_target_pairs={{0,2},{2,4},{4,6},{6,7},{7,5},{5,3},{3,1},{1,0},{8,10},{10,12},{12... | collective-permute-start | bytes 1572872 | tf_op jit(solution)/shard_map/ppermute | solution.py:148
  42.8 22.4 %collective-permute-start.12 = (bf16[512,1024]{1,0:T(8,128)(2,1)}, bf16[512,1024]{1,0:T(8,128)(2,1)}, u32[]{:S(2)}, u32[]{:S(2)}) collective-permute-start(bf16[512,1024]{1,0:T(8,128)(2,1)} %collective-permute-done.11.refs_2_), channel_id=1, source_target_pairs={{0,8},{8,0},{16,24},{24,16},{1,9},{9,1},{17,25},{25,17},{2,10},{10... | collective-permute-start | bytes 3145736 | tf_op jit(solution)/shard_map/ppermute | solution.py:73
  42.9 40.8 %collective-permute-start.18 = (bf16[512,1024]{1,0:T(8,128)(2,1)S(1)}, bf16[512,1024]{1,0:T(8,128)(2,1)}, u32[]{:S(2)}, u32[]{:S(2)}) collective-permute-start(bf16[512,1024]{1,0:T(8,128)(2,1)S(1)} %bitcast.156), channel_id=1, source_target_pairs={{0,16},{8,24},{16,0},{24,8},{1,17},{9,25},{17,1},{25,9},{2,18},{10... | collective-permute-start | bytes 3145736 | tf_op jit(solution)/shard_map/ppermute | solution.py:961
  45.2 16.2 %collective-permute-start.13 = (bf16[128,1024]{1,0:T(8,128)(2,1)}, bf16[128,1024]{1,0:T(8,128)(2,1)S(1)}, u32[]{:S(2)}, u32[]{:S(2)}) collective-permute-start(bf16[128,1024]{1,0:T(8,128)(2,1)} %collective-permute-done.10), channel_id=1, source_target_pairs={{0,2},{2,4},{4,6},{6,7},{7,5},{5,3},{3,1},{1,0},{8,10},{10,12},{12... | collective-permute-start | bytes 786440 | tf_op jit(solution)/shard_map/ppermute | solution.py:148
  62.1 21.6 %collective-permute-start.16 = (bf16[256,1024]{1,0:T(8,128)(2,1)}, bf16[256,1024]{1,0:T(8,128)(2,1)}, u32[]{:S(2)}, u32[]{:S(2)}) collective-permute-start(bf16[256,1024]{1,0:T(8,128)(2,1)} %collective-permute-done.14), channel_id=1, source_target_pairs={{2,0},{4,2},{6,4},{7,6},{5,7},{3,5},{1,3},{0,1},{10,8},{12,10},{14... | collective-permute-start | bytes 1572872 | tf_op jit(solution)/shard_map/ppermute | solution.py:151
  63.5 20.2 %collective-permute-start.17 = (bf16[256,1024]{1,0:T(8,128)(2,1)}, bf16[256,1024]{1,0:T(8,128)(2,1)}, u32[]{:S(2)}, u32[]{:S(2)}) collective-permute-start(bf16[256,1024]{1,0:T(8,128)(2,1)} %collective-permute-done.15), channel_id=1, source_target_pairs={{0,2},{2,4},{4,6},{6,7},{7,5},{5,3},{3,1},{1,0},{8,10},{10,12},{12... | collective-permute-start | bytes 1572872 | tf_op jit(solution)/shard_map/ppermute | solution.py:148
  83.7 17.9 %collective-permute-start.21 = (bf16[512,1024]{1,0:T(8,128)(2,1)}, bf16[512,1024]{1,0:T(8,128)(2,1)}, u32[]{:S(2)}, u32[]{:S(2)}) collective-permute-start(bf16[512,1024]{1,0:T(8,128)(2,1)} %collective-permute-done.18.ca.refs_4_), channel_id=1, source_target_pairs={{0,8},{8,0},{16,24},{24,16},{1,9},{9,1},{17,25},{25,17},{2,10},{10... | collective-permute-start | bytes 3145736 | tf_op jit(solution)/shard_map/ppermute | solution.py:985
  83.8 15.9 %collective-permute-start.22 = (bf16[1024,256]{1,0:T(8,128)(2,1)S(1)}, bf16[1024,256]{1,0:T(8,128)(2,1)S(1)}, u32[]{:S(2)}, u32[]{:S(2)}) collective-permute-start(bf16[1024,256]{1,0:T(8,128)(2,1)S(1)} %get-tuple-element.236.refs_8_), channel_id=1, source_target_pairs={{0,16},{8,24},{16,0},{24,8},{1,17},{9,25},{17,1},{25,9},{2,18},{10... | collective-permute-start | bytes 1572872 | tf_op jit(solution)/shard_map/ppermute | solution.py:73
  85.4 14.4 %collective-permute-start.23 = (bf16[1024,256]{1,0:T(8,128)(2,1)S(1)}, bf16[1024,256]{1,0:T(8,128)(2,1)S(1)}, u32[]{:S(2)}, u32[]{:S(2)}) collective-permute-start(bf16[1024,256]{1,0:T(8,128)(2,1)S(1)} %get-tuple-element.236.refs_8_), channel_id=1, source_target_pairs={{0,8},{8,0},{16,24},{24,16},{1,9},{9,1},{17,25},{25,17},{2,10},{10... | collective-permute-start | bytes 1572872 | tf_op jit(solution)/shard_map/ppermute | solution.py:73
  85.5 14.4 %collective-permute-start.19 = (bf16[256,1024]{1,0:T(8,128)(2,1)}, bf16[256,1024]{1,0:T(8,128)(2,1)S(1)}, u32[]{:S(2)}, u32[]{:S(2)}) collective-permute-start(bf16[256,1024]{1,0:T(8,128)(2,1)} %collective-permute-done.16), channel_id=1, source_target_pairs={{2,0},{4,2},{6,4},{7,6},{5,7},{3,5},{1,3},{0,1},{10,8},{12,10},{14... | collective-permute-start | bytes 1572872 | tf_op jit(solution)/shard_map/ppermute | solution.py:151
  86.9 14.7 %collective-permute-start.20 = (bf16[256,1024]{1,0:T(8,128)(2,1)}, bf16[256,1024]{1,0:T(8,128)(2,1)}, u32[]{:S(2)}, u32[]{:S(2)}) collective-permute-start(bf16[256,1024]{1,0:T(8,128)(2,1)} %collective-permute-done.17), channel_id=1, source_target_pairs={{0,2},{2,4},{4,6},{6,7},{7,5},{5,3},{3,1},{1,0},{8,10},{10,12},{12... | collective-permute-start | bytes 1572872 | tf_op jit(solution)/shard_map/ppermute | solution.py:148
  101.6 15.2 %collective-permute-start.24 = (bf16[256,1024]{1,0:T(8,128)(2,1)}, bf16[256,1024]{1,0:T(8,128)(2,1)}, u32[]{:S(2)}, u32[]{:S(2)}) collective-permute-start(bf16[256,1024]{1,0:T(8,128)(2,1)} %collective-permute-done.20), channel_id=1, source_target_pairs={{0,2},{2,4},{4,6},{6,7},{7,5},{5,3},{3,1},{1,0},{8,10},{10,12},{12... | collective-permute-start | bytes 1572872 | tf_op jit(solution)/shard_map/ppermute | solution.py:148
  102.4 14.4 %collective-permute-start.25 = (bf16[1024,256]{1,0:T(8,128)(2,1)S(1)}, bf16[1024,256]{1,0:T(8,128)(2,1)S(1)}, u32[]{:S(2)}, u32[]{:S(2)}) collective-permute-start(bf16[1024,256]{1,0:T(8,128)(2,1)S(1)} %collective-permute-done.22.refs_10_), channel_id=1, source_target_pairs={{0,8},{8,0},{16,24},{24,16},{1,9},{9,1},{17,25},{25,17},{2,10},{10... | collective-permute-start | bytes 1572872 | tf_op jit(solution)/shard_map/ppermute | solution.py:1005
  103.5 13.2 %collective-permute-start.26 = (bf16[512,128]{1,0:T(8,128)(2,1)S(1)}, bf16[512,128]{1,0:T(8,128)(2,1)S(1)}, u32[]{:S(2)}, u32[]{:S(2)}) collective-permute-start(bf16[512,128]{1,0:T(8,128)(2,1)S(1)} %get-tuple-element.407), channel_id=1, source_target_pairs={{0,8},{8,0},{16,24},{24,16},{1,9},{9,1},{17,25},{25,17},{2,10},{10... | collective-permute-start | bytes 393224 | tf_op jit(solution)/shard_map/ppermute | solution.py:995
  104.1 12.7 %collective-permute-start.27 = (bf16[512,128]{1,0:T(8,128)(2,1)S(1)}, bf16[512,128]{1,0:T(8,128)(2,1)S(1)}, u32[]{:S(2)}, u32[]{:S(2)}) collective-permute-start(bf16[512,128]{1,0:T(8,128)(2,1)S(1)} %get-tuple-element.406), channel_id=1, source_target_pairs={{0,16},{8,24},{16,0},{24,8},{1,17},{9,25},{17,1},{25,9},{2,18},{10... | collective-permute-start | bytes 393224 | tf_op jit(solution)/shard_map/ppermute | solution.py:995
  104.6 12.2 %collective-permute-start.28 = (bf16[512,128]{1,0:T(8,128)(2,1)S(1)}, bf16[512,128]{1,0:T(8,128)(2,1)S(1)}, u32[]{:S(2)}, u32[]{:S(2)}) collective-permute-start(bf16[512,128]{1,0:T(8,128)(2,1)S(1)} %get-tuple-element.405), channel_id=1, source_target_pairs={{0,24},{8,16},{16,8},{24,0},{1,25},{9,17},{17,9},{25,1},{2,26},{10... | collective-permute-start | bytes 393224 | tf_op jit(solution)/shard_map/ppermute | solution.py:995
  136.8 25.4 %collective-permute-start.33 = (bf16[512,1024]{1,0:T(8,128)(2,1)}, bf16[512,1024]{1,0:T(8,128)(2,1)}, u32[]{:S(2)}, u32[]{:S(2)}) collective-permute-start(bf16[512,1024]{1,0:T(8,128)(2,1)} %get-tuple-element.250.sa.refs_6_), channel_id=1, source_target_pairs={{0,16},{8,24},{16,0},{24,8},{1,17},{9,25},{17,1},{25,9},{2,18},{10... | collective-permute-start | bytes 3145736 | tf_op jit(solution)/shard_map/ppermute | solution.py:1030
  162.2 19.9 %collective-permute-start.35 = (bf16[512,1024]{1,0:T(8,128)(2,1)}, bf16[512,1024]{1,0:T(8,128)(2,1)S(1)}, u32[]{:S(2)}, u32[]{:S(2)}) collective-permute-start(bf16[512,1024]{1,0:T(8,128)(2,1)} %get-tuple-element.263), channel_id=1, source_target_pairs={{0,8},{8,0},{16,24},{24,16},{1,9},{9,1},{17,25},{25,17},{2,10},{10... | collective-permute-start | bytes 3145736 | tf_op jit(solution)/shard_map/ppermute | solution.py:1041
  162.7 19.4 %collective-permute-start.36 = (bf16[512,1024]{1,0:T(8,128)(2,1)}, bf16[512,1024]{1,0:T(8,128)(2,1)S(1)}, u32[]{:S(2)}, u32[]{:S(2)}) collective-permute-start(bf16[512,1024]{1,0:T(8,128)(2,1)} %get-tuple-element.264), channel_id=1, source_target_pairs={{0,8},{8,0},{16,24},{24,16},{1,9},{9,1},{17,25},{25,17},{2,10},{10... | collective-permute-start | bytes 3145736 | tf_op jit(solution)/shard_map/ppermute | solution.py:1042
  187.7 25.4 %collective-permute-start.38 = (bf16[512,1024]{1,0:T(8,128)(2,1)}, bf16[512,1024]{1,0:T(8,128)(2,1)S(1)}, u32[]{:S(2)}, u32[]{:S(2)}) collective-permute-start(bf16[512,1024]{1,0:T(8,128)(2,1)} %add_convert_fusion.4), channel_id=1, source_target_pairs={{0,16},{8,24},{16,0},{24,8},{1,17},{9,25},{17,1},{25,9},{2,18},{10... | collective-permute-start | bytes 3145736 | tf_op jit(solution)/shard_map/ppermute | solution.py:1054
  188.2 24.9 %collective-permute-start.39 = (bf16[512,1024]{1,0:T(8,128)(2,1)}, bf16[512,1024]{1,0:T(8,128)(2,1)S(1)}, u32[]{:S(2)}, u32[]{:S(2)}) collective-permute-start(bf16[512,1024]{1,0:T(8,128)(2,1)} %get-tuple-element.272), channel_id=1, source_target_pairs={{0,8},{8,0},{16,24},{24,16},{1,9},{9,1},{17,25},{25,17},{2,10},{10... | collective-permute-start | bytes 3145736 | tf_op jit(solution)/shard_map/ppermute | solution.py:1055
  207.3 17.5 %collective-permute-start.40 = (bf16[256,1024]{1,0:T(8,128)(2,1)}, bf16[256,1024]{1,0:T(8,128)(2,1)S(1)}, u32[]{:S(2)}, u32[]{:S(2)}) collective-permute-start(bf16[256,1024]{1,0:T(8,128)(2,1)} %bitcast.189), channel_id=1, source_target_pairs={{0,2},{2,4},{4,6},{6,7},{7,5},{5,3},{3,1},{1,0},{8,10},{10,12},{12... | collective-permute-start | bytes 1572872 | tf_op jit(solution)/shard_map/ppermute | solution.py:148
  220.4 14.2 %collective-permute-start.48 = (bf16[256,1024]{1,0:T(8,128)(2,1)S(1)}, bf16[256,1024]{1,0:T(8,128)(2,1)S(1)}, u32[]{:S(2)}, u32[]{:S(2)}) collective-permute-start(bf16[256,1024]{1,0:T(8,128)(2,1)S(1)} %bitcast.188), channel_id=1, source_target_pairs={{2,0},{4,2},{6,4},{7,6},{5,7},{3,5},{1,3},{0,1},{10,8},{12,10},{14... | collective-permute-start | bytes 1572872 | tf_op jit(solution)/shard_map/ppermute | solution.py:151
  227.8 26.8 %collective-permute-start.44 = (bf16[256,1024]{1,0:T(8,128)(2,1)}, bf16[256,1024]{1,0:T(8,128)(2,1)}, u32[]{:S(2)}, u32[]{:S(2)}) collective-permute-start(bf16[256,1024]{1,0:T(8,128)(2,1)} %fusion.7), channel_id=1, source_target_pairs={{0,2},{2,4},{4,6},{6,7},{7,5},{5,3},{3,1},{1,0},{8,10},{10,12},{12... | collective-permute-start | bytes 1572872 | tf_op jit(solution)/shard_map/ppermute | solution.py:148
  228.1 26.5 %collective-permute-start.45 = (bf16[512,128]{1,0:T(8,128)(2,1)S(1)}, bf16[512,128]{1,0:T(8,128)(2,1)S(1)}, u32[]{:S(2)}, u32[]{:S(2)}) collective-permute-start(bf16[512,128]{1,0:T(8,128)(2,1)S(1)} %get-tuple-element.309), channel_id=1, source_target_pairs={{0,8},{8,0},{16,24},{24,16},{1,9},{9,1},{17,25},{25,17},{2,10},{10... | collective-permute-start | bytes 393224 | tf_op jit(solution)/shard_map/ppermute | solution.py:1105
  228.4 26.2 %collective-permute-start.46 = (bf16[512,128]{1,0:T(8,128)(2,1)S(1)}, bf16[512,128]{1,0:T(8,128)(2,1)}, u32[]{:S(2)}, u32[]{:S(2)}) collective-permute-start(bf16[512,128]{1,0:T(8,128)(2,1)S(1)} %get-tuple-element.310), channel_id=1, source_target_pairs={{0,16},{8,24},{16,0},{24,8},{1,17},{9,25},{17,1},{25,9},{2,18},{10... | collective-permute-start | bytes 393224 | tf_op jit(solution)/shard_map/ppermute | solution.py:1105
  228.9 25.7 %collective-permute-start.47 = (bf16[512,128]{1,0:T(8,128)(2,1)S(1)}, bf16[512,128]{1,0:T(8,128)(2,1)}, u32[]{:S(2)}, u32[]{:S(2)}) collective-permute-start(bf16[512,128]{1,0:T(8,128)(2,1)S(1)} %get-tuple-element.311), channel_id=1, source_target_pairs={{0,24},{8,16},{16,8},{24,0},{1,25},{9,17},{17,9},{25,1},{2,26},{10... | collective-permute-start | bytes 393224 | tf_op jit(solution)/shard_map/ppermute | solution.py:1105
  256.7 21.8 %collective-permute-start.50 = (bf16[1024,256]{1,0:T(8,128)(2,1)S(1)}, bf16[1024,256]{1,0:T(8,128)(2,1)}, u32[]{:S(2)}, u32[]{:S(2)}) collective-permute-start(bf16[1024,256]{1,0:T(8,128)(2,1)S(1)} %get-tuple-element.324), channel_id=1, source_target_pairs={{0,8},{8,0},{16,24},{24,16},{1,9},{9,1},{17,25},{25,17},{2,10},{10... | collective-permute-start | bytes 1572872 | tf_op jit(solution)/shard_map/ppermute | solution.py:83
  256.7 23.6 %collective-permute-start.52 = (bf16[256,1024]{1,0:T(8,128)(2,1)}, bf16[256,1024]{1,0:T(8,128)(2,1)}, u32[]{:S(2)}, u32[]{:S(2)}) collective-permute-start(bf16[256,1024]{1,0:T(8,128)(2,1)} %fusion.6), channel_id=1, source_target_pairs={{0,2},{2,4},{4,6},{6,7},{7,5},{5,3},{3,1},{1,0},{8,10},{10,12},{12... | collective-permute-start | bytes 1572872 | tf_op jit(solution)/shard_map/ppermute | solution.py:148
  257.0 26.7 %collective-permute-start.49 = (bf16[1024,256]{1,0:T(8,128)(2,1)S(1)}, bf16[1024,256]{1,0:T(8,128)(2,1)}, u32[]{:S(2)}, u32[]{:S(2)}) collective-permute-start(bf16[1024,256]{1,0:T(8,128)(2,1)S(1)} %get-tuple-element.322), channel_id=1, source_target_pairs={{0,8},{8,0},{16,24},{24,16},{1,9},{9,1},{17,25},{25,17},{2,10},{10... | collective-permute-start | bytes 1572872 | tf_op jit(solution)/shard_map/ppermute | solution.py:83
  257.2 25.1 %collective-permute-start.53 = (bf16[256,1024]{1,0:T(8,128)(2,1)S(1)}, bf16[256,1024]{1,0:T(8,128)(2,1)}, u32[]{:S(2)}, u32[]{:S(2)}) collective-permute-start(bf16[256,1024]{1,0:T(8,128)(2,1)S(1)} %fusion.5), channel_id=1, source_target_pairs={{2,0},{4,2},{6,4},{7,6},{5,7},{3,5},{1,3},{0,1},{10,8},{12,10},{14... | collective-permute-start | bytes 1572872 | tf_op jit(solution)/shard_map/ppermute | solution.py:151
  279.7 13.9 %collective-permute-start.51 = (bf16[1024,256]{1,0:T(8,128)(2,1)S(1)}, bf16[1024,256]{1,0:T(8,128)(2,1)S(1)}, u32[]{:S(2)}, u32[]{:S(2)}) collective-permute-start(bf16[1024,256]{1,0:T(8,128)(2,1)S(1)} %add_convert_fusion.6), channel_id=1, source_target_pairs={{0,16},{8,24},{16,0},{24,8},{1,17},{9,25},{17,1},{25,9},{2,18},{10... | collective-permute-start | bytes 1572872 | tf_op jit(solution)/shard_map/ppermute | solution.py:83
  295.7 14.6 %collective-permute-start.55 = (bf16[256,1024]{1,0:T(8,128)(2,1)S(1)}, bf16[256,1024]{1,0:T(8,128)(2,1)}, u32[]{:S(2)}, u32[]{:S(2)}) collective-permute-start(bf16[256,1024]{1,0:T(8,128)(2,1)S(1)} %fusion.3), channel_id=1, source_target_pairs={{2,0},{4,2},{6,4},{7,6},{5,7},{3,5},{1,3},{0,1},{10,8},{12,10},{14... | collective-permute-start | bytes 1572872 | tf_op jit(solution)/shard_map/ppermute | solution.py:151
  297.1 13.1 %collective-permute-start.54 = (bf16[256,1024]{1,0:T(8,128)(2,1)}, bf16[256,1024]{1,0:T(8,128)(2,1)}, u32[]{:S(2)}, u32[]{:S(2)}) collective-permute-start(bf16[256,1024]{1,0:T(8,128)(2,1)} %fusion.4), channel_id=1, source_target_pairs={{0,2},{2,4},{4,6},{6,7},{7,5},{5,3},{3,1},{1,0},{8,10},{10,12},{12... | collective-permute-start | bytes 1572872 | tf_op jit(solution)/shard_map/ppermute | solution.py:148
  299.1 29.0 %collective-permute-start.57 = (bf16[512,1024]{1,0:T(8,128)(2,1)}, bf16[512,1024]{1,0:T(8,128)(2,1)}, u32[]{:S(2)}, u32[]{:S(2)}) collective-permute-start(bf16[512,1024]{1,0:T(8,128)(2,1)} %add_convert_fusion.1), channel_id=1, source_target_pairs={{0,16},{8,24},{16,0},{24,8},{1,17},{9,25},{17,1},{25,9},{2,18},{10... | collective-permute-start | bytes 3145736 | tf_op jit(solution)/shard_map/ppermute | solution.py:1137
  312.8 15.3 %collective-permute-start.56 = (bf16[128,1024]{1,0:T(8,128)(2,1)S(1)}, bf16[128,1024]{1,0:T(8,128)(2,1)S(1)}, u32[]{:S(2)}, u32[]{:S(2)}) collective-permute-start(bf16[128,1024]{1,0:T(8,128)(2,1)S(1)} %bitcast.191), channel_id=1, source_target_pairs={{0,2},{2,4},{4,6},{6,7},{7,5},{5,3},{3,1},{1,0},{8,10},{10,12},{12... | collective-permute-start | bytes 786440 | tf_op jit(solution)/shard_map/ppermute | solution.py:148
  328.8 12.9 %collective-permute-start.58 = (bf16[2,512,1024]{2,1,0:T(8,128)(2,1)}, bf16[2,512,1024]{2,1,0:T(8,128)(2,1)}, u32[]{:S(2)}, u32[]{:S(2)}) collective-permute-start(bf16[2,512,1024]{2,1,0:T(8,128)(2,1)} %get-tuple-element.359), channel_id=1, source_target_pairs={{0,8},{8,0},{16,24},{24,16},{1,9},{9,1},{17,25},{25,17},{2,10},{10... | collective-permute-start | bytes 6291464 | tf_op jit(solution)/shard_map/ppermute | solution.py:1152
  341.2 13.5 %collective-permute-start.61 = (bf16[256,1024]{1,0:T(8,128)(2,1)}, bf16[256,1024]{1,0:T(8,128)(2,1)S(1)}, u32[]{:S(2)}, u32[]{:S(2)}) collective-permute-start(bf16[256,1024]{1,0:T(8,128)(2,1)} %fusion.9.refs_0_), channel_id=1, source_target_pairs={{0,16},{8,24},{16,0},{24,8},{1,17},{9,25},{17,1},{25,9},{2,18},{10... | collective-permute-start | bytes 1572872 | tf_op jit(solution)/shard_map/ppermute | solution.py:1153
  354.8 11.1 %collective-permute-start.65 = (bf16[256,1024]{1,0:T(8,128)(2,1)S(1)}, bf16[256,1024]{1,0:T(8,128)(2,1)S(1)}, u32[]{:S(2)}, u32[]{:S(2)}) collective-permute-start(bf16[256,1024]{1,0:T(8,128)(2,1)S(1)} %copy-done.10), channel_id=1, source_target_pairs={{0,8},{8,0},{16,24},{24,16},{1,9},{9,1},{17,25},{25,17},{2,10},{10... | collective-permute-start | bytes 1572872 | tf_op jit(solution)/shard_map/ppermute | solution.py:1193
  359.4 24.7 %collective-permute-start.68 = (bf16[512,1024]{1,0:T(8,128)(2,1)S(1)}, bf16[512,1024]{1,0:T(8,128)(2,1)S(1)}, u32[]{:S(2)}, u32[]{:S(2)}) collective-permute-start(bf16[512,1024]{1,0:T(8,128)(2,1)S(1)} %get-tuple-element.382), channel_id=1, source_target_pairs={{0,16},{8,24},{16,0},{24,8},{1,17},{9,25},{17,1},{25,9},{2,18},{10... | collective-permute-start | bytes 3145736 | tf_op jit(solution)/shard_map/ppermute | solution.py:1192
  366.0 13.1 %collective-permute-start.67 = (bf16[128,1024]{1,0:T(8,128)(2,1)S(1)}, bf16[128,1024]{1,0:T(8,128)(2,1)S(1)}, u32[]{:S(2)}, u32[]{:S(2)}) collective-permute-start(bf16[128,1024]{1,0:T(8,128)(2,1)S(1)} %fusion.13), channel_id=1, source_target_pairs={{0,2},{2,4},{4,6},{6,7},{7,5},{5,3},{3,1},{1,0},{8,10},{10,12},{12... | collective-permute-start | bytes 786440 | tf_op jit(solution)/shard_map/ppermute | solution.py:148
  367.7 16.4 %collective-permute-start.71 = (bf16[128,1024]{1,0:T(8,128)(2,1)S(1)}, bf16[128,1024]{1,0:T(8,128)(2,1)S(1)}, u32[]{:S(2)}, u32[]{:S(2)}) collective-permute-start(bf16[128,1024]{1,0:T(8,128)(2,1)S(1)} %fusion.10), channel_id=1, source_target_pairs={{2,0},{4,2},{6,4},{7,6},{5,7},{3,5},{1,3},{0,1},{10,8},{12,10},{14... | collective-permute-start | bytes 786440 | tf_op jit(solution)/shard_map/ppermute | solution.py:151
  (104 other events, 892.4 us)

commit v3 on v2

--- a/solution.py
+++ b/solution.py
@@ -89,38 +89,6 @@
 
 def tie(*values):
     return lax.optimization_barrier(values)
-
-
-def place_table(me, size):
-    index = jnp.arange(size, dtype=jnp.int32) ^ me
-    place = jnp.zeros_like(index)
-    for at, bit in enumerate(bits_low_last(size)):
-        place = place | jnp.where(index & bit, 1 << at, 0)
-    return place
-
-
-def owner_table(me, size):
-    place = jnp.arange(size, dtype=jnp.int32)
-    rel = jnp.zeros_like(place)
-    for at, bit in enumerate(bits_low_last(size)):
-        rel = rel | jnp.where(place & (1 << at), bit, 0)
-    return rel ^ me
-
-
-def gather_all(block, axis, size, me):
-    order = bits_low_last(size)
-    out = block[None]
-    for bit in order:
-        out = jnp.concatenate([out, lax.ppermute(out, axis, pairs(size, bit))], 0)
-    return jnp.take(out, place_table(me, size), axis=0)
-
-
-def scatter_all(blocks, axis, size, me):
-    stack = jnp.take(blocks, owner_table(me, size), axis=0)
-    for bit in bits_low_last(size)[::-1]:
-        half = stack.shape[0] // 2
-        stack = add16(stack[:half], lax.ppermute(stack[half:], axis, pairs(size, bit)))
-    return stack[0]
 
 
 class Ring:
@@ -155,15 +123,15 @@
     return info[2 + nb + slot] if live else slot
 
 
-def put(outs, slot, value):
+def put(outs, slot, value, rows, cols):
     if len(outs) == 1:
-        outs[0][slot] = value
+        outs[0][slot, rows, cols] = value
         return
     for at, out in enumerate(outs):
 
         @pl.when(slot == at)
         def _():
-            out[0] = value
+            out[0, rows, cols] = value
 
 
 def blocks_of(refs):
@@ -177,14 +145,21 @@
     return pl.BlockSpec(shape, lambda i, *_: (0,) * len(shape), pipeline_mode=pl.Buffered(1))
 
 
-def first_pack_kernel(info, joined, outw, out):
-    cols = joined.shape[1]
-    out[:, :cols] = joined[...]
-    out[:, cols:] = outw[...]
-
-
-def first_pack(info, joined, outw, cols, cw):
+def first_pack_kernel(info, joined, outw, *refs):
+    smalls, out = refs[:-1], refs[-1]
+    rows, cols = joined.shape
+    out[:rows, :cols] = joined[...]
+    out[:rows, cols:] = outw[...]
+    pieces = [small[...].astype(F32) for small in smalls]
+    count = sum(piece.shape[0] for piece in pieces)
+    pieces.append(jnp.zeros((16 - count, rows), F32))
+    out[rows:, :rows] = jnp.concatenate(pieces, 0).astype(BF)
+    out[rows:, rows:] = jnp.zeros((16, out.shape[1] - rows), BF)
+
+
+def first_pack(info, joined, outw, smalls, cols, cw):
     rows = joined.shape[0]
+    shape = (rows + 16, cols + cw)
     return pl.pallas_call(
         first_pack_kernel,
         grid_spec=pltpu.PrefetchScalarGridSpec(
@@ -193,13 +168,14 @@
             in_specs=[
                 pl.BlockSpec((rows, cols), lambda i, info: (0, info[0])),
                 pl.BlockSpec((rows, cw), lambda i, info: (0, info[0])),
-            ],
-            out_specs=pl.BlockSpec((rows, cols + cw), lambda i, info: (0, 0)),
+            ]
+            + [once(small.shape) for small in smalls],
+            out_specs=pl.BlockSpec(shape, lambda i, info: (0, 0)),
         ),
-        out_shape=jax.ShapeDtypeStruct((rows, cols + cw), BF),
-        compiler_params=params(40),
+        out_shape=jax.ShapeDtypeStruct(shape, BF),
+        compiler_params=params(60),
         name="first_pack",
-    )(info, joined, outw)
+    )(info, joined, outw, *smalls)
 
 
 def second_pack_kernel(nb, ns, units, info, expand, shrink, out):
@@ -226,14 +202,15 @@
             out_specs=pl.BlockSpec((rows + units, dim), lambda i, info: (0, 0)),
         ),
         out_shape=jax.ShapeDtypeStruct((rows + units, dim), BF),
-        compiler_params=params(40),
+        compiler_params=params(60),
         name="second_pack",
     )(info, expand, shrink)
 
 
-def first_kernel(ns, nt, nb, rows, cols, live, info, vecs, jbias, *refs):
-    xs, weights = refs[:ns], refs[ns:-4]
-    normed, joined, full, outw = refs[-4:]
+def first_kernel(ns, nt, nb, rows, cols, live, info, *refs):
+    jbias_in, refs = (None, refs) if live else (refs[0], refs[1:])
+    xs, weights = refs[:ns], refs[ns:-6]
+    normed, joined, full, outw, vecs, jbias = refs[-6:]
     step = pl.program_id(0)
 
     @pl.when(step == 0)
@@ -241,8 +218,19 @@
         for slot, (ref, at) in enumerate(blocks_of(weights)):
             high = owner_at(info, live, nb, slot) * rows
             high = pl.multiple_of(high, rows) if live else high
-            full[pl.ds(high, rows)] = ref[at, :, :cols]
-            outw[pl.ds(high, rows)] = ref[at, :, cols:]
+            full[pl.ds(high, rows)] = ref[at, :rows, :cols]
+            outw[pl.ds(high, rows)] = ref[at, :rows, cols:]
+            vecs[:, pl.ds(high, rows)] = ref[at, rows:, :rows].astype(F32)
+        if live:
+            heads = cols // (3 * HD)
+            for head in range(heads):
+                at = info[0] * heads + head
+                col = pl.ds(pl.multiple_of(lax.div(at, 2) * rows, rows), rows)
+                row = vecs[0:8, col][2 + head % 2 : 3 + head % 2]
+                pieces = [row[:, :HD], jnp.zeros((1, HD), F32), row[:, HD:]]
+                jbias[:, head * 3 * HD : (head + 1) * 3 * HD] = jnp.concatenate(pieces, 1)
+        else:
+            jbias[...] = jbias_in[...]
 
     for rel in range(ns):
 
@@ -254,15 +242,15 @@
             joined[...] = (dg(value, full[...], NN) + jbias[...]).astype(BF)
 
 
-def first_call(info, vecs, jbias, xs, weights, live):
+def first_call(info, jbias, xs, weights, cols, live):
     ns = len(xs)
     tok, dim = xs[0].shape
     nb = sum(weight.shape[0] for weight in weights)
     rows = dim // nb
-    cols = jbias.shape[1]
     cw = weights[0].shape[2] - cols
     tile = min(256, tok)
     nt = tok // tile
+    extra = [] if live else [jbias]
     place = lambda i, info: ((info[0] ^ lax.div(i, nt)) * nt + lax.rem(i, nt), 0)
 
     def source(rel):
@@ -273,7 +261,7 @@
         grid_spec=pltpu.PrefetchScalarGridSpec(
             num_scalar_prefetch=1,
             grid=(ns * nt,),
-            in_specs=[once(vecs.shape), once(jbias.shape)]
+            in_specs=[once(value.shape) for value in extra]
             + [source(rel) for rel in range(ns)]
             + [once(weight.shape) for weight in weights],
             out_specs=[
@@ -281,18 +269,21 @@
                 pl.BlockSpec((tile, cols), place),
                 once((dim, cols)),
                 once((dim, cw)),
+                once((16, dim)),
             ],
+            scratch_shapes=[pltpu.VMEM((1, cols), F32)],
         ),
         out_shape=[
             jax.ShapeDtypeStruct((ns * tok, dim), BF),
             jax.ShapeDtypeStruct((ns * tok, cols), BF),
             jax.ShapeDtypeStruct((dim, cols), BF),
             jax.ShapeDtypeStruct((dim, cw), BF),
+            jax.ShapeDtypeStruct((16, dim), F32),
         ],
-        compiler_params=params(40),
+        compiler_params=params(60),
         cost_estimate=cost(2 * ns * tok * dim * cols, 2 * ns * tok * (2 * dim + cols)),
         name="first",
-    )(info, vecs, jbias, *xs, *weights)
+    )(info, *extra, *xs, *weights)
 
 
 def three(value):
@@ -366,7 +357,7 @@
             jax.ShapeDtypeStruct((count, 2 * HD), F32),
         ],
         scratch_shapes=[pltpu.VMEM((2, count, 2 * HD), BF)],
-        compiler_params=params(),
+        compiler_params=params(60),
         cost_estimate=cost(area * 1024, 20 * count * HD, area),
         name="attend",
     )(info, slopes, joined)
@@ -430,7 +421,7 @@
     smem = pl.BlockSpec(memory_space=pltpu.SMEM)
     wide = pl.BlockSpec((count, 6 * HD), lambda i: (0, pair))
     narrow = pl.BlockSpec((count, 2 * HD), lambda i: (0, 0))
-    piece = pl.BlockSpec((count // ns, 2 * HD), lambda i: (0, 0))
+    piece = pl.BlockSpec((count // ns, 2 * HD), lambda i: (0, pair))
     area = count * count
     return pl.pallas_call(
         functools.partial(attend_back_kernel, count, min(512, count), ns, pair),
@@ -439,7 +430,7 @@
         out_specs=[pl.BlockSpec((count, 6 * HD), lambda i: (0, 0)), pl.BlockSpec((1, 6 * HD), lambda i: (0, 0))],
         out_shape=[jax.ShapeDtypeStruct((count, 6 * HD), BF), jax.ShapeDtypeStruct((1, 6 * HD), F32)],
         scratch_shapes=[pltpu.VMEM((2, count, 2 * HD), BF)] * 4 + [pltpu.VMEM((2, 2 * HD, count), F32)],
-        compiler_params=params(),
+        compiler_params=params(60),
         cost_estimate=cost(area * 2560, 40 * count * HD, area),
         name="attend_back",
     )(info, slopes, joined, mixed, sums, *grads)
@@ -488,7 +479,7 @@
             jax.ShapeDtypeStruct((tok, dim), BF),
             jax.ShapeDtypeStruct((dim, dim), BF),
         ],
-        compiler_params=params(40),
+        compiler_params=params(60),
         cost_estimate=cost(2 * tok * dim * dim, 12 * tok * dim + 4 * dim * dim),
         name="middle",
     )(info, x, vecs, *mixed, *weights)
@@ -559,7 +550,7 @@
         out_shape=[jax.ShapeDtypeStruct((2 * tok, ff), BF)] * 2
         + [shape] * 4
         + [jax.ShapeDtypeStruct((1, ff), F32)],
-        compiler_params=params(),
+        compiler_params=params(60),
         cost_estimate=cost(16 * tok * dim * ff, 16 * tok * dim + 8 * dim * ff, 2 * tok * ff),
         name="feed",
     )(info, sa, sb, ca, cb, ebias, *weights)
@@ -628,85 +619,130 @@
             out_specs=[once(shape) for shape in shapes],
         ),
         out_shape=[jax.ShapeDtypeStruct(shape, BF) for shape in shapes],
-        compiler_params=params(),
+        compiler_params=params(60),
         cost_estimate=cost(4 * tok * dim * ff, 4 * tok * (dim + ff) + 4 * dim * ff),
         name="feed_grad",
     )(info, *activs, *cots, *seconds, *grads)
 
 
+def pair_shapes(shape, ns):
+    return [shape, shape, (2, *shape)] if ns == 4 else [shape] * ns
+
+
+def pair_put(outs, ns, rel, rows, value):
+    if ns == 4 and rel % 2:
+        outs[2][rel // 2, rows] = value
+    elif ns == 4:
+        outs[rel // 2][rows] = value
+    else:
+        outs[rel][rows] = value
+
+
 def split_grad_kernel(ns, info, left, right, *refs):
-    outs, held = refs[:ns], refs[ns]
+    outs, held = refs[:-1], refs[-1]
     held[...] = dg(left[...], right[...], TN)
+    tile = held.shape[0]
     cw = held.shape[1] // ns
+    rows = pl.ds(pl.multiple_of(pl.program_id(0) * tile, tile), tile)
     for rel in range(ns):
         col = pl.ds(pl.multiple_of((info[0] ^ rel) * cw, cw), cw)
-        outs[rel][...] = held[:, col].astype(BF)
+        pair_put(outs, ns, rel, rows, held[:, col].astype(BF))
 
 
 def split_grad(info, left, right, ns):
     tok, dim = left.shape
     tile = 256
-    cw = dim // ns
+    shapes = pair_shapes((dim, dim // ns), ns)
     return pl.pallas_call(
         functools.partial(split_grad_kernel, ns),
         grid_spec=pltpu.PrefetchScalarGridSpec(
             num_scalar_prefetch=1,
             grid=(dim // tile,),
             in_specs=[pl.BlockSpec((tok, tile), lambda i, info: (0, i)), once((tok, dim))],
-            out_specs=[pl.BlockSpec((tile, cw), lambda i, info: (i, 0))] * ns,
+            out_specs=[once(shape) for shape in shapes],
             scratch_shapes=[pltpu.VMEM((tile, dim), F32)],
         ),
-        out_shape=[jax.ShapeDtypeStruct((dim, cw), BF)] * ns,
-        compiler_params=params(40),
+        out_shape=[jax.ShapeDtypeStruct(shape, BF) for shape in shapes],
+        compiler_params=params(60),
         cost_estimate=cost(2 * tok * dim * dim, 6 * dim * dim),
         name="split_grad",
     )(info, left, right)
 
 
-def joined_grad_kernel(nb, rows, np, info, left, other, *refs):
-    rights, outs = refs[:np], refs[np:]
-    totals = [dg(left[...], right[...], TN).astype(BF) for right in rights]
-    value = jnp.concatenate(totals + [other[...]], 1)
-    tile = value.shape[0]
+def joined_grad_kernel(nb, rows, np, live, info, left, other, weight, vecs, *refs):
+    smalls, refs = (refs[:3], refs[3:]) if live else (refs[:1], refs[1:])
+    rights, sides, outs = refs[:np], refs[np : 2 * np], refs[2 * np :]
+    totals = [dg(left[...], right[...], TN) for right in rights]
+    tile, cw = other.shape
+    cols = weight.shape[1]
     first = pl.program_id(0) * (tile // rows)
+    low = jnp.concatenate(totals, 1).astype(BF)
+    weights = weight[...].astype(F32)
+    moment = jnp.sum(jnp.concatenate(totals, 1) * weights, axis=1, keepdims=True)
+    shift = jnp.sum(jnp.concatenate([side[...] for side in sides], 1) * weights, axis=1, keepdims=True)
+    moment = jnp.broadcast_to(moment, (tile, 128)).T[:1]
+    shift = jnp.broadcast_to(shift, (tile, 128)).T[:1]
+    gain = (moment - vecs[1:2] * shift) / vecs[0:1]
+    row = lax.broadcasted_iota(jnp.int32, (16, tile), 0)
+    held = jnp.zeros((16, tile), F32) if live else smalls[0][...]
+    held = jnp.where(row == 0, gain, jnp.where(row == 1, shift, held))
+    if live:
+        turned = smalls[0][...]
+        for at, source in ((4, 2), (5, 0), (6, 1), (11, 3)):
+            held = jnp.where(row == at, turned[source : source + 1], held)
+        held = jnp.where(row == 7 + info[0], smalls[1][...] + smalls[2][...], held)
+        for part in range(2):
+            pieces = []
+            for side in sides:
+                base = part * 3 * HD
+                pieces += [side[:, base : base + HD], side[:, base + 2 * HD : base + 3 * HD]]
+            bias = jnp.where(pl.program_id(0) == info[0], jnp.concatenate(pieces, 1), 0.0)
+            held = jnp.where(row == 2 + part, bias, held)
+    held = held.astype(BF)
     for k in range(tile // rows):
-        put(outs, info[2 + first + k], value[k * rows : (k + 1) * rows])
-
-
-def joined_grad_call(info, left, rights, other, nb, live):
+        slot = info[2 + first + k]
+        high = slice(k * rows, (k + 1) * rows)
+        put(outs, slot, low[high], slice(0, rows), slice(0, cols))
+        put(outs, slot, other[high], slice(0, rows), slice(cols, cols + cw))
+        put(outs, slot, held[:, high], slice(rows, rows + 16), slice(0, rows))
+
+
+def joined_grad_call(info, left, rights, sides, other, weight, vecs, shares, turned, biases, nb, live):
     count, dim = left.shape
-    cols = sum(right.shape[1] for right in rights)
+    cols = weight.shape[1]
     cw = other.shape[1]
     rows = dim // nb
     tile = 256
-    shapes = [(1, rows, cols + cw)] * nb if live else [(nb, rows, cols + cw)]
-    return pl.pallas_call(
-        functools.partial(joined_grad_kernel, nb, rows, len(rights)),
+    wide = (rows + 16, cols + cw)
+    shapes = [(1, *wide)] * nb if live else [(nb, *wide)]
+    flat = lambda width: pl.BlockSpec((tile, width), lambda i, info: (i, 0))
+    tall = lambda value: pl.BlockSpec((value.shape[0], tile), lambda i, info: (0, i))
+    smalls = (turned, *biases) if live else (shares,)
+    return pl.pallas_call(
+        functools.partial(joined_grad_kernel, nb, rows, len(rights), live),
         grid_spec=pltpu.PrefetchScalarGridSpec(
             num_scalar_prefetch=1,
             grid=(dim // tile,),
-            in_specs=[
-                pl.BlockSpec((count, tile), lambda i, info: (0, i)),
-                pl.BlockSpec((tile, cw), lambda i, info: (i, 0)),
-            ]
-            + [once(right.shape) for right in rights],
+            in_specs=[pl.BlockSpec((count, tile), lambda i, info: (0, i)), flat(cw), flat(cols), tall(vecs)]
+            + [tall(value) for value in smalls]
+            + [once(value.shape) for value in (*rights, *sides)],
             out_specs=[once(shape) for shape in shapes],
         ),
         out_shape=[jax.ShapeDtypeStruct(shape, BF) for shape in shapes],
-        compiler_params=params(),
+        compiler_params=params(60),
         cost_estimate=cost(2 * count * dim * cols, 2 * count * (dim + cols) + 4 * dim * dim),
         name="joined_grad",
-    )(info, left, other, *rights)
-
-
-def turn_kernel(ns, np, cw, info, ga, gb, resid, cot, vecs, full, resid_grad, branch, *refs):
+    )(info, left, other, weight, vecs, *smalls, *rights, *sides)
+
+
+def turn_kernel(ns, np, cw, info, ga, gb, gc, resid, cot, vecs, full, resid_grad, branch, *refs):
     mixed_grads, sums, held = refs[: ns * np], refs[ns * np], refs[ns * np + 1]
 
     @pl.when(pl.program_id(0) == 0)
     def _():
         sums[...] = jnp.zeros_like(sums)
 
-    grad = ga[...].astype(F32) + gb[...].astype(F32)
+    grad = ga[...].astype(F32) + gb[...].astype(F32) + gc[...].astype(F32)
     unit, scale = norm_parts(resid[...])
     outer = cot[...].astype(F32)
     value = outer + norm_back(grad, unit, scale, vecs[5:6])
@@ -723,7 +759,7 @@
         sums[at : at + 1] += jnp.sum(term, axis=0, keepdims=True)
 
 
-def turn_call(info, ga, gb, resid, cot, vecs, full, ns, np):
+def turn_call(info, terms, resid, cot, vecs, full, ns, np):
     tok, dim = resid.shape
     cw = dim // ns
     tile = min(256, tok)
@@ -733,7 +769,7 @@
         grid_spec=pltpu.PrefetchScalarGridSpec(
             num_scalar_prefetch=1,
             grid=(tok // tile,),
-            in_specs=[part, part, part, part, once(vecs.shape), once(full.shape)],
+            in_specs=[part, part, part, part, part, once(vecs.shape), once(full.shape)],
             out_specs=[part, part]
             + [pl.BlockSpec((tile, cw // np), lambda i, info: (i, 0))] * (ns * np)
             + [pl.BlockSpec((8, dim), lambda i, info: (0, 0))],
@@ -745,20 +781,15 @@
         ]
         + [jax.ShapeDtypeStruct((tok, cw // np), BF)] * (ns * np)
         + [jax.ShapeDtypeStruct((8, dim), F32)],
-        compiler_params=params(40),
+        compiler_params=params(60),
         cost_estimate=cost(2 * tok * dim * dim, 16 * tok * dim + 2 * dim * dim),
         name="turn",
-    )(info, ga, gb, resid, cot, vecs, full)
-
-
-def last_kernel(ns, nt, np, info, normed, weight, *refs):
-    rights, outs, sums = refs[:np], refs[np:-1], refs[-1]
+    )(info, *terms, resid, cot, vecs, full)
+
+
+def last_kernel(ns, nt, np, info, weight, *refs):
+    rights, outs = refs[:np], refs[np:]
     step = pl.program_id(0)
-
-    @pl.when(step == 0)
-    def _():
-        sums[...] = jnp.zeros_like(sums)
-
     grad = None
     at = 0
     for right in rights:
@@ -767,82 +798,105 @@
         grad = term if grad is None else grad + term
         at += width
     low = grad.astype(BF)
-    rel = ns - 1 - lax.div(step, nt)
     tile = low.shape[0]
-    row = pl.multiple_of(lax.rem(step, nt) * tile, tile)
-    for mine in range(ns):
-
-        @pl.when(rel == mine)
+    rows = pl.ds(pl.multiple_of(lax.rem(step, nt) * tile, tile), tile)
+    for rel in range(ns):
+
+        @pl.when(ns - 1 - lax.div(step, nt) == rel)
         def _():
-            if ns == 4 and mine % 2:
-                outs[2][mine // 2, pl.ds(row, tile)] = low
-            elif ns == 4:
-                outs[mine // 2][pl.ds(row, tile)] = low
-            else:
-                outs[mine][pl.ds(row, tile)] = low
-
-    sums[0:1] += jnp.sum(grad * normed[...].astype(F32), axis=0, keepdims=True)
-    sums[1:2] += jnp.sum(grad, axis=0, keepdims=True)
-
-
-def last_call(info, rights, normed, weight, ns):
-    count, dim = normed.shape
-    cols = weight.shape[1]
+            pair_put(outs, ns, rel, rows, low)
+
+
+def last_call(info, rights, weight, ns):
+    count = rights[0].shape[0]
+    dim, cols = weight.shape
     tok = count // ns
     tile = min(256, tok)
     nt = tok // tile
     source = lambda i, info: ((info[0] ^ (ns - 1 - lax.div(i, nt))) * nt + lax.rem(i, nt), 0)
-    shapes = [(tok, dim)] * 2 + [(2, tok, dim)] if ns == 4 else [(tok, dim)] * ns
+    shapes = pair_shapes((tok, dim), ns)
     return pl.pallas_call(
         functools.partial(last_kernel, ns, nt, len(rights)),
         grid_spec=pltpu.PrefetchScalarGridSpec(
             num_scalar_prefetch=1,
             grid=(ns * nt,),
-            in_specs=[pl.BlockSpec((tile, dim), source), once(weight.shape)]
-            + [pl.BlockSpec((tile, right.shape[1]), source) for right in rights],
-            out_specs=[once(shape) for shape in shapes] + [pl.BlockSpec((8, dim), lambda i, info: (0, 0))],
+            in_specs=[once(weight.shape)] + [pl.BlockSpec((tile, right.shape[1]), source) for right in rights],
+            out_specs=[once(shape) for shape in shapes],
         ),
-        out_shape=[jax.ShapeDtypeStruct(shape, BF) for shape in shapes] + [jax.ShapeDtypeStruct((8, dim), F32)],
-        compiler_params=params(40),
+        out_shape=[jax.ShapeDtypeStruct(shape, BF) for shape in shapes],
+        compiler_params=params(60),
         cost_estimate=cost(2 * count * dim * cols, 2 * count * (2 * dim + cols)),
         name="last",
-    )(info, normed, weight, *rights)
-
-
-def end_kernel(ga, gb, x, resid_grad, vecs, out):
-    grad = ga[...].astype(F32) + gb[...].astype(F32)
+    )(info, weight, *rights)
+
+
+def end_kernel(ga, gb, gc, x, resid_grad, vecs, out):
+    grad = ga[...].astype(F32) + gb[...].astype(F32) + gc[...].astype(F32)
     unit, scale = norm_parts(x[...].astype(F32))
     out[...] = resid_grad[...] + norm_back(grad, unit, scale, vecs[0:1])
 
 
-def end_call(ga, gb, x, resid_grad, vecs):
+def end_call(terms, x, resid_grad, vecs):
     tok, dim = x.shape
     tile = min(128, tok)
     part = pl.BlockSpec((tile, dim), lambda i: (i, 0))
+    head = pl.BlockSpec((None, tile, dim), lambda i: (0, i, 0))
     return pl.pallas_call(
         end_kernel,
         grid=(tok // tile,),
-        in_specs=[part, part, part, part, pl.BlockSpec(vecs.shape, lambda i: (0, 0))],
+        in_specs=[head if term.ndim == 3 else part for term in terms]
+        + [part, part, pl.BlockSpec(vecs.shape, lambda i: (0, 0))],
         out_specs=part,
         out_shape=jax.ShapeDtypeStruct((tok, dim), F32),
         compiler_params=params(40),
         cost_estimate=cost(20 * tok * dim, 14 * tok * dim),
         name="end",
-    )(ga, gb, x, resid_grad, vecs)
+    )(*terms, x, resid_grad, vecs)
+
+
+def add_pairs_kernel(count, *refs):
+    for at in range(count):
+        left, right, out = refs[at], refs[count + at], refs[2 * count + at]
+        out[...] = (left[...].astype(F32) + right[...].astype(F32)).astype(BF)
+
+
+def add_pairs(lefts, rights):
+    count = len(lefts)
+    return pl.pallas_call(
+        functools.partial(add_pairs_kernel, count),
+        in_specs=[pl.BlockSpec(memory_space=pltpu.VMEM)] * (2 * count),
+        out_specs=[pl.BlockSpec(memory_space=pltpu.VMEM)] * count,
+        out_shape=[jax.ShapeDtypeStruct(left.shape, BF) for left in lefts],
+        compiler_params=params(20),
+        cost_estimate=cost(1, 1),
+        name="add_pairs",
+    )(*lefts, *rights)
 
 
 def joined_out_kernel(ns, cols, info, *refs):
-    parts, joined, outw = refs[:ns], refs[ns], refs[ns + 1]
+    parts, joined, outw, smalls = refs[:ns], refs[ns], refs[ns + 1], refs[ns + 2 :]
+    rows = joined.shape[0]
     cw = parts[0].shape[1] - cols
+    total = None
     for rel in range(ns):
-        joined[:, pl.ds(pl.multiple_of((info[0] ^ rel) * cols, cols), cols)] = parts[rel][:, :cols].astype(F32)
-        outw[:, pl.ds(pl.multiple_of((info[0] ^ rel) * cw, cw), cw)] = parts[rel][:, cols:].astype(F32)
+        part = parts[rel]
+        joined[:, pl.ds(pl.multiple_of((info[0] ^ rel) * cols, cols), cols)] = part[:rows, :cols].astype(F32)
+        outw[:, pl.ds(pl.multiple_of((info[0] ^ rel) * cw, cw), cw)] = part[:rows, cols:].astype(F32)
+        term = part[rows:, :rows].astype(F32)
+        total = term if total is None else total + term
+    at = 0
+    for small in smalls:
+        for row in range(small.shape[0]):
+            small[row : row + 1] = total[at + row : at + row + 1]
+        at += small.shape[0]
 
 
 def joined_out(info, parts, cols):
     ns = len(parts)
-    rows, wide = parts[0].shape
+    high, wide = parts[0].shape
+    rows = high - 16
     shapes = [(rows, ns * cols), (rows, ns * (wide - cols))]
+    shapes += [(count, rows) for count in (1, 1, 2, 1, 1, 1, 4, 1)]
     return pl.pallas_call(
         functools.partial(joined_out_kernel, ns, cols),
         grid_spec=pltpu.PrefetchScalarGridSpec(
@@ -852,7 +906,7 @@
             out_specs=[once(shape) for shape in shapes],
         ),
         out_shape=[jax.ShapeDtypeStruct(shape, F32) for shape in shapes],
-        compiler_params=params(40),
+        compiler_params=params(60),
         cost_estimate=cost(0, 6 * ns * rows * wide),
         name="joined_out",
     )(info, *parts)
@@ -882,7 +936,7 @@
             out_specs=[once(shape) for shape in shapes],
         ),
         out_shape=[jax.ShapeDtypeStruct(shape, F32) for shape in shapes],
-        compiler_params=params(40),
+        compiler_params=params(60),
         cost_estimate=cost(0, 6 * ns * high * dim),
         name="feed_out",
     )(info, *parts)
@@ -927,9 +981,10 @@
     slopes = 2.0 ** (-8.0 * head_ids.astype(F32) / H)
 
     smalls = (first_gain, first_shift, joined_bias, output_bias, second_gain, second_shift, expand_bias, shrink_bias)
-    smalls = jnp.concatenate([small.reshape(-1, rows) for small in smalls], 0)
+    smalls = [small.reshape(-1, rows) for small in smalls]
     seat = si.reshape(1).astype(jnp.int32)
-    one = first_pack(seat, joined_weight, output_weight, cols, cw)
+    one = first_pack(seat, joined_weight, output_weight, smalls, cols, cw)
+    jbias = None
 
     def step(held, t):
         if t < ring.half:
@@ -937,52 +992,45 @@
         held[nb - t] = ring.ahead(held[(nb - t + 1) % nb])
 
     if live:
-        x, one = tie(x, one)
+        x, cot, one = tie(x, cot, one)
         ones = {0: one}
         step(ones, 1)
-        xs = gather_rel(x, "seq", ns)
+        xs = {0: x, 1: lax.ppermute(x, "seq", pairs(ns, 1)), 2: lax.ppermute(x, "seq", pairs(ns, 2))}
         expand_weight, shrink_weight, _ = tie(expand_weight, shrink_weight, one)
         two = second_pack(seat, expand_weight, shrink_weight, nb, ns)
-        smalls, _ = tie(smalls, one)
-        smalls = smalls[None]
-        for t in range(2, ring.half + 1):
-            bit = bits_low_last(nb)[t - 2]
-            smalls = jnp.concatenate([smalls, lax.ppermute(smalls, "batch", pairs(nb, bit))], 0)
-            if t == 2:
-                smalls, ones[1], ones[7], two, xs[1], cot = tie(smalls, ones[1], ones[7], two, xs[1], cot)
-                cots = {0: cot, 1: lax.ppermute(cot, "seq", pairs(ns, 1))}
-            elif t == 3:
-                smalls, ones[2], ones[6], cots[1] = tie(smalls, ones[2], ones[6], cots[1])
-            else:
-                smalls, ones[3], ones[5], xs[2], two = tie(smalls, ones[3], ones[5], xs[2], two)
-                twos = {0: two}
-                step(twos, 1)
-                cot, _ = tie(cot, two)
-                cots[2] = lax.ppermute(cot, "seq", pairs(ns, 2))
-            step(ones, t)
-        smalls = jnp.take(smalls, place_table(bi, nb), axis=0)
-        ones[4], twos[1], twos[7] = tie(ones[4], twos[1], twos[7])
+        ones[1], ones[7], two, xs[1], cot = tie(ones[1], ones[7], two, xs[1], cot)
+        step(ones, 2)
+        cots = {0: cot, 1: lax.ppermute(cot, "seq", pairs(ns, 1))}
+        ones[2], ones[6], cots[1], xs[2], cot = tie(ones[2], ones[6], cots[1], xs[2], cot)
+        step(ones, 3)
+        xs[3] = lax.ppermute(xs[2], "seq", pairs(ns, 1))
+        cots[2] = lax.ppermute(cot, "seq", pairs(ns, 2))
+        ones[3], ones[5], xs[3] = tie(ones[3], ones[5], xs[3])
+        step(ones, 4)
+        ones[4], two = tie(ones[4], two)
+        twos = {0: two}
+        step(twos, 1)
         one_parts = [ones[slot][None] for slot in range(nb)]
     else:
         xs = gather_rel(x, "seq", ns)
         cots = gather_rel(cot, "seq", ns)
-        smalls = gather_all(smalls, "batch", nb, bi)
         one_parts = [lax.all_gather(one, "batch")]
-
-    vecs = smalls.astype(F32).transpose(1, 0, 2).reshape(12, dim)
-    low = vecs[2:4].reshape(2, nb, rows).transpose(1, 0, 2).reshape(2 * dim)
-    low = lax.dynamic_slice(low, (si * 2 * cw,), (2 * cw,)).reshape(heads, 2, HD)
-    jbias = jnp.stack([low[:, 0], jnp.zeros_like(low[:, 0]), low[:, 1]], 1).reshape(1, cols)
-    ebias = vecs[7:11].reshape(4, nb, rows).transpose(1, 0, 2).reshape(nb, ns, units)
-    ebias = lax.dynamic_slice(ebias, (0, si, 0), (nb, 1, units)).reshape(1, ff)
-    normed, joined, joined_full, outw_own = first_call(
-        info, vecs, jbias, [xs[rel] for rel in range(ns)], one_parts, live
+        low = one_parts[0][:, rows + 2 : rows + 4, :rows].astype(F32).reshape(2 * dim)
+        low = lax.dynamic_slice(low, (si * 2 * cw,), (2 * cw,)).reshape(heads, 2, HD)
+        jbias = jnp.stack([low[:, 0], jnp.zeros_like(low[:, 0]), low[:, 1]], 1).reshape(1, cols)
+
+    normed, joined, joined_full, outw_own, vecs = first_call(
+        info, jbias, [xs[rel] for rel in range(ns)], one_parts, cols, live
     )
     if live:
+        joined, twos[1], twos[7], cots[2] = tie(joined, twos[1], twos[7], cots[2])
         step(twos, 2)
-        joined, twos[2], twos[6], cots[2] = tie(joined, twos[2], twos[6], cots[2])
-        step(twos, 3)
         cots[3] = lax.ppermute(cots[2], "seq", pairs(ns, 1))
+    if units == rows:
+        ebias = lax.dynamic_slice(vecs, (7 + si, 0), (1, dim))
+    else:
+        ebias = vecs[7:11].reshape(4, nb, rows).transpose(1, 0, 2).reshape(nb, ns, units)
+        ebias = lax.dynamic_slice(ebias, (0, si, 0), (nb, 1, units)).reshape(1, ff)
     outw_all = gather_rel(outw_own, "seq", ns)
     mixed = []
     log_sums = []
@@ -998,25 +1046,26 @@
     for pair in range(np):
         out, logs = attend(joined, info, slopes, pair)
         if live and pair == 0:
-            out, joined, twos[3], twos[5], cots[3], outw_all[2], outw_all[1] = tie(
-                out, joined, twos[3], twos[5], cots[3], outw_all[2], outw_all[1]
+            out, joined, twos[2], twos[6], cots[3], outw_all[2], outw_all[1] = tie(
+                out, joined, twos[2], twos[6], cots[3], outw_all[2], outw_all[1]
             )
-            step(twos, 4)
+            step(twos, 3)
             outw_all[3] = lax.ppermute(outw_all[2], "seq", pairs(ns, 1))
         mixed.append(out)
         log_sums.append(logs)
         merged_parts.append(to_tokens(out))
         if live and pair == 1:
-            out, twos[4], outw_all[3], *merged_parts[0] = tie(out, twos[4], outw_all[3], *merged_parts[0])
+            out, twos[3], twos[5], outw_all[3], *merged_parts[0] = tie(
+                out, twos[3], twos[5], outw_all[3], *merged_parts[0]
+            )
+            step(twos, 4)
             mixed[1] = out
             merged_parts[1] = to_tokens(out)
     merged_parts = [block for parts in merged_parts for block in parts]
     merged, resid, second, outw_full = middle_call(
         info, x, vecs, merged_parts, [outw_all[rel] for rel in range(ns)]
     )
-    if live:
-        two_parts = [twos[slot][None] for slot in range(nb)]
-    else:
+    if not live:
         expand_part = expand_weight.reshape(rows, nb, ns, units)
         expand_part = lax.dynamic_slice(expand_part, (0, 0, si, 0), (rows, nb, 1, units)).reshape(rows, ff)
         shrink_part = lax.dynamic_slice(shrink_weight, (si * units, 0), (units, dim))
@@ -1025,8 +1074,10 @@
     back_parts = {}
     activs = []
     pre_grads = []
-    bias_sum = 0.0
+    bias_sums = []
     if live:
+        second, twos[4] = tie(second, twos[4])
+        two_parts = [twos[slot][None] for slot in range(nb)]
         seconds = {0: second, 2: lax.ppermute(second, "seq", pairs(ns, 2)), 1: lax.ppermute(second, "seq", pairs(ns, 1))}
     else:
         seconds = gather_rel(second, "seq", ns)
@@ -1042,19 +1093,17 @@
             near_out = lax.ppermute(ob, "seq", pairs(ns, 1))
         activs.append(activ)
         pre_grads.append(pre_grad)
-        bias_sum = bias_sum + bgrad
+        bias_sums.append(bgrad)
         out_parts.update({rel: oa, rel + 1: ob})
         back_parts.update({rel: ba, rel + 1: bb})
     if live:
         back_parts[3], near_back, near_out = tie(back_parts[3], near_back, near_out)
-        back_a = add16(back_parts[0], near_back)
-        out_a = add16(out_parts[0], near_out)
         far_back = lax.ppermute(back_parts[3], "seq", pairs(ns, 1))
         far_back, out_far = tie(far_back, out_parts[3])
         back_b = lax.ppermute(add16(back_parts[2], far_back), "seq", pairs(ns, 2))
         far_out = lax.ppermute(out_far, "seq", pairs(ns, 1))
     else:
-        back_a, back_b = scatter_rel(back_parts, "seq", ns, last=False)
+        back_terms = (*scatter_rel(back_parts, "seq", ns, last=False), jnp.zeros((tok, dim), BF))
         out_a, out_b = scatter_rel(out_parts, "seq", ns, last=False)
     feed_stack = feed_grad_call(
         info,
@@ -1078,143 +1127,131 @@
             self.got_ahead = ring.ahead(self.ahead)
             self.got_back = ring.back(self.back) if self.t > 1 else None
 
-        def take(self, *after):
-            if after:
-                self.got_ahead, *_ = tie(self.got_ahead, *after)
+        def take(self, *others):
+            both = self.t > 1
+            got = (self.got_ahead, self.got_back) if both else (self.got_ahead,)
+            tied = tie(*got, *others)
+            got, others = tied[: len(got)], tied[len(got) :]
             if self.t == ring.half:
-                total = self.parts[0].astype(F32) + self.got_ahead.astype(F32) + self.got_back.astype(F32)
-                return total.astype(BF)
-            self.ahead = add16(self.parts[ring.half - self.t], self.got_ahead)
-            if self.t > 1:
-                self.back = add16(self.parts[nb - ring.half + self.t], self.got_back)
+                total = self.parts[0].astype(F32) + got[0].astype(F32) + got[1].astype(F32)
+                return (total.astype(BF), *others)
+            mine = self.parts[ring.half - self.t]
+            if both:
+                self.ahead, self.back = add_pairs((mine, self.parts[nb - ring.half + self.t]), got)
+            else:
+                self.ahead = add16(mine, got[0])
+            return others
 
     if live:
         feed_ring = Scatter(feed_stack)
         feed_ring.send()
-        back_b, back_a, out_a, far_out, _ = tie(back_b, back_a, out_a, far_out, feed_stack[0])
+        back_b, far_out, _ = tie(back_b, far_out, feed_stack[0])
+        back_terms = (back_parts[0], near_back, back_b)
         out_b = add16(out_parts[2], far_out)
     resid_grad, branch, *mixed_grads, turn_sums = turn_call(
-        info, back_a, back_b, resid, cot, vecs, outw_full, ns, np
+        info, back_terms, resid, cot, vecs, outw_full, ns, 1
     )
-    outw_stack = split_grad(info, merged, branch, ns)
+    outw_parts = split_grad(info, merged, branch, ns)
     joined_grads = []
     sides = []
 
-    def to_heads(pair):
-        blocks = mixed_grads[pair * ns : (pair + 1) * ns]
-        return [lax.ppermute(block, "seq", pairs(ns, rel)) if rel else block for rel, block in enumerate(blocks)]
-
-    grads = to_heads(0)
+    grads = [
+        lax.ppermute(block, "seq", pairs(ns, rel)) if rel else block for rel, block in enumerate(mixed_grads)
+    ]
     if live:
-        feed_ring.take(*grads, *outw_stack)
-        grads[0], *rest = tie(grads[0], feed_ring.ahead, *grads[1:], *outw_stack, *mixed_grads[ns:])
-        feed_ring.ahead, grads[1:], outw_stack = rest[0], rest[1:ns], rest[ns : 2 * ns]
-        mixed_grads[ns:] = rest[2 * ns :]
+        grads[0], *outw_parts = tie(grads[0], *outw_parts)
+        grads = feed_ring.take(*grads)
+        *grads, feed_ring.ahead, outw_near = tie(*grads, feed_ring.ahead, outw_parts[2])
         feed_ring.send()
+        outw_near = lax.ppermute(outw_near, "seq", pairs(ns, 1))
     for pair in range(np):
-        if pair:
-            grads = after
         out, side = attend_back(joined, grads, mixed[pair], log_sums[pair], info, slopes, pair)
-        if pair + 1 < np:
-            after = to_heads(pair + 1)
-        if live and pair == 0:
-            feed_ring.take(out, *after)
-            after[0], feed_ring.ahead, feed_ring.back, out, *outw_stack = tie(
-                after[0], feed_ring.ahead, feed_ring.back, out, *outw_stack
-            )
-            feed_ring.send()
-        elif live:
-            feed_ring.take(out)
         joined_grads.append(out)
         sides.append(side)
-    outw_share = scatter_rel(dict(enumerate(outw_stack)), "seq", ns)
+        if live and pair == 0:
+            out, outw_near = feed_ring.take(out, outw_near)
+            outw_far = add16(outw_parts[1], outw_near[1])
+            out, joined, feed_ring.ahead, feed_ring.back, outw_far = tie(
+                out, joined, feed_ring.ahead, feed_ring.back, outw_far
+            )
+            joined_grads[0] = out
+            feed_ring.send()
+            outw_far = lax.ppermute(outw_far, "seq", pairs(ns, 2))
+        elif live:
+            joined_grads[1], outw_far = feed_ring.take(out, outw_far)
+
     if live:
-        joined_grads[1], outw_share, feed_ring.ahead, feed_ring.back = tie(
-            joined_grads[1], outw_share, feed_ring.ahead, feed_ring.back
+        shares = None
+        outw_share = outw_parts[0].astype(F32) + outw_near[0].astype(F32) + outw_far.astype(F32)
+        outw_share = outw_share.astype(BF)
+        joined_grads[1], outw_share, feed_ring.ahead, feed_ring.back, out_b = tie(
+            joined_grads[1], outw_share, feed_ring.ahead, feed_ring.back, out_b
         )
         feed_ring.send()
-        out_b, _ = tie(out_b, outw_share)
         out_b = lax.ppermute(out_b, "seq", pairs(ns, 2))
-    joined_stack = joined_grad_call(info, normed, joined_grads, outw_share, nb, live)
+    else:
+        spread_bias = lax.dynamic_update_slice(
+            jnp.zeros((nb, ns, units), F32), sum(bias_sums).reshape(nb, 1, units), (0, si, 0)
+        )
+        spread_bias = spread_bias.reshape(nb, 4, rows).transpose(1, 0, 2).reshape(4, dim)
+        side = jnp.concatenate(sides, 1).reshape(heads, 3, HD)
+        side = jnp.stack([side[:, 0], side[:, 2]], 1).reshape(2 * cw)
+        side = lax.dynamic_update_slice(jnp.zeros((2 * dim,), F32), side, (si * 2 * cw,))
+        side = side.reshape(nb, 2, rows).transpose(1, 0, 2).reshape(2, dim)
+        none = jnp.zeros((2, dim), F32)
+        shares = [none, side, turn_sums[2:3], turn_sums[0:2], spread_bias, turn_sums[3:4], none, none]
+        shares = jnp.concatenate(shares, 0)
+        outw_share = scatter_rel(dict(enumerate(outw_parts)), "seq", ns)
+    joined_stack = joined_grad_call(
+        info, normed, joined_grads, sides, outw_share, joined_full, vecs, shares, turn_sums, bias_sums, nb, live
+    )
     if live:
-        feed_share = feed_ring.take(joined_stack[0])
+        feed_share, *joined_stack = feed_ring.take(*joined_stack)
         feed_share, *joined_stack = tie(feed_share, *joined_stack)
         joined_ring = Scatter(joined_stack)
         joined_ring.send()
         joined_grads[0], _ = tie(joined_grads[0], joined_stack[0])
-    *normed_parts, last_sums = last_call(info, joined_grads, normed, joined_full, ns)
+    normed_parts = last_call(info, joined_grads, joined_full, ns)
+
+    def ordered(block):
+        parts = gather_rel(block, "seq", ns)
+        return [parts[rel] for rel in range(ns)]
+
     if live:
-        joined_ring.take(last_sums, out_b)
-        joined_ring.ahead, out_b, feed_share, sent, last_sums = tie(
-            joined_ring.ahead, out_b, feed_share, normed_parts[2], last_sums
-        )
+        sent, out_b = joined_ring.take(normed_parts[2], out_b)
+        joined_ring.ahead, out_b, feed_share, sent = tie(joined_ring.ahead, out_b, feed_share, sent)
         joined_ring.send()
         got = lax.ppermute(sent, "seq", pairs(ns, 1))
         feed_parts = {0: feed_share, 2: lax.ppermute(feed_share, "seq", pairs(ns, 2))}
-        norm_a = add16(normed_parts[0], got[0])
+        out_terms = out_parts[0].astype(F32) + near_out.astype(F32) + out_b.astype(F32)
+        layer_output = (resid + out_terms + vecs[11:12]).astype(BF)
+        got, feed_parts[2] = joined_ring.take(got, feed_parts[2])
         far = add16(normed_parts[1], got[1])
-    else:
-        norm_a, norm_b = scatter_rel(dict(enumerate(normed_parts)), "seq", ns, last=False)
-    layer_output = (resid + out_a.astype(F32) + out_b.astype(F32) + vecs[11:12]).astype(BF)
-
-    shift_one = last_sums[1:2]
-    gain_one = (last_sums[0:1] - vecs[1:2] * shift_one) / vecs[0:1]
-    side = jnp.concatenate(sides, 1).reshape(heads, 3, HD)
-    side = jnp.stack([side[:, 0], side[:, 2]], 1).reshape(2 * cw)
-    side = lax.dynamic_update_slice(jnp.zeros((2 * dim,), F32), side, (si * 2 * cw,))
-    side = side.reshape(nb, 2, rows).transpose(1, 0, 2).reshape(2, dim)
-    spread_bias = lax.dynamic_update_slice(
-        jnp.zeros((nb, ns, units), F32), bias_sum.reshape(nb, 1, units), (0, si, 0)
-    )
-    spread_bias = spread_bias.reshape(nb, 4, rows).transpose(1, 0, 2).reshape(4, dim)
-    shares = jnp.concatenate(
-        [gain_one, shift_one, side, turn_sums[2:3], turn_sums[0:2], spread_bias, turn_sums[3:4]], 0
-    )
-    shares = shares.astype(BF).reshape(12, nb, rows).transpose(1, 0, 2)
-
-    def ordered(block):
-        parts = gather_rel(block, "seq", ns)
-        return [parts[rel] for rel in range(ns)]
-
-    if live:
-        shares = jnp.take(shares, owner_table(bi, nb), axis=0)
-
-        def fold(stack, bit):
-            half = stack.shape[0] // 2
-            return add16(stack[:half], lax.ppermute(stack[half:], "batch", pairs(nb, bit)))
-
-        shares = fold(shares, 1)
-        joined_ring.take(shares, far, feed_parts[2])
-        joined_ring.ahead, joined_ring.back, shares, far, feed_parts[0], feed_parts[2] = tie(
-            joined_ring.ahead, joined_ring.back, shares, far, feed_parts[0], feed_parts[2]
+        joined_ring.ahead, joined_ring.back, far, feed_parts[0], feed_parts[2] = tie(
+            joined_ring.ahead, joined_ring.back, far, feed_parts[0], feed_parts[2]
         )
         joined_ring.send()
         norm_b = lax.ppermute(far, "seq", pairs(ns, 2))
         feed_parts[1] = lax.ppermute(feed_parts[0], "seq", pairs(ns, 1))
-        shares = fold(shares, 4)
-        joined_ring.take(shares, feed_parts[1])
-        joined_ring.ahead, joined_ring.back, shares, feed_parts[1], feed_parts[2] = tie(
-            joined_ring.ahead, joined_ring.back, shares, feed_parts[1], feed_parts[2]
+        feed_parts[1], feed_parts[2], layer_output = joined_ring.take(feed_parts[1], feed_parts[2], layer_output)
+        joined_ring.ahead, joined_ring.back, feed_parts[1], feed_parts[2] = tie(
+            joined_ring.ahead, joined_ring.back, feed_parts[1], feed_parts[2]
         )
         joined_ring.send()
         feed_parts[3] = lax.ppermute(feed_parts[2], "seq", pairs(ns, 1))
-        shares = fold(shares, 2)[0]
         expand_grad, shrink_grad = feed_out(info, [feed_parts[rel] for rel in range(ns)], nb, rows)
-        joined_share = joined_ring.take(norm_b, shares, expand_grad)
-        joined_share, norm_b, shares = tie(joined_share, norm_b, shares)
+        joined_share, norm_b, expand_grad, shrink_grad = joined_ring.take(norm_b, expand_grad, shrink_grad)
+        joined_share, norm_b = tie(joined_share, norm_b)
         joined_parts = {0: joined_share, 2: lax.ppermute(joined_share, "seq", pairs(ns, 2))}
         joined_parts[1] = lax.ppermute(joined_share, "seq", pairs(ns, 1))
-        shares = add16(shares, lax.ppermute(shares, "seq", pairs(ns, 1)))
-        input_grad = end_call(norm_a, norm_b, x, resid_grad, vecs)
-        joined_parts[2], joined_parts[1], shares, _ = tie(joined_parts[2], joined_parts[1], shares, input_grad)
+        input_grad = end_call((normed_parts[0], got, norm_b), x, resid_grad, vecs)
+        joined_parts[2], joined_parts[1], input_grad = tie(joined_parts[2], joined_parts[1], input_grad)
         joined_parts[3] = lax.ppermute(joined_parts[2], "seq", pairs(ns, 1))
-        shares = add16(shares, lax.ppermute(shares, "seq", pairs(ns, 2)))
         joined_parts = [joined_parts[rel] for rel in range(ns)]
     else:
-        input_grad = end_call(norm_a, norm_b, x, resid_grad, vecs)
-        shares = scatter_all(shares, "batch", nb, bi)
-        for bit in bits_low_last(ns)[::-1]:
-            shares = add16(shares, lax.ppermute(shares, "seq", pairs(ns, bit)))
+        layer_output = (resid + out_a.astype(F32) + out_b.astype(F32) + vecs[11:12]).astype(BF)
+        norm_terms = scatter_rel(dict(enumerate(normed_parts)), "seq", ns, last=False)
+        input_grad = end_call((*norm_terms, jnp.zeros((tok, dim), BF)), x, resid_grad, vecs)
         joined_share = lax.psum_scatter(joined_stack[0], "batch", scatter_dimension=0)
         expand_share = lax.psum_scatter(feed_stack[0], "batch", scatter_dimension=0)
         shrink_share = lax.psum_scatter(feed_stack[1], "batch", scatter_dimension=0)
@@ -1223,13 +1260,8 @@
         expand_grad = jnp.take(jnp.stack(ordered(expand_share)), seats, axis=0).astype(F32)
         expand_grad = expand_grad.reshape(ns, rows, nb, units).transpose(1, 2, 0, 3).reshape(rows, ns * ff)
         joined_parts = ordered(joined_share)
-    shares = shares.astype(F32)
-    joined_wgrad, outw_grad = joined_out(info, joined_parts, cols)
-    small = []
-    at = 0
-    for size in (1, 1, 2, 1, 1, 1, 4, 1):
-        small.append(shares[at : at + size].reshape(size * rows))
-        at += size
+    joined_wgrad, outw_grad, *small = joined_out(info, joined_parts, cols)
+    small = [value.reshape(-1) for value in small]
     return (
         layer_output[None],
         input_grad[None],

time: 404 us -> 376 us (0.931)
  Pallas kernels: 164 us -> 187 us
  local copies, waits for them, and re-layouts: 37.2 us -> 14.8 us
  starting transfers between devices: 61.4 us -> 51.1 us
  other arithmetic: 29.4 us -> 19.4 us
  waiting for transfers between devices: 104 us -> 96.2 us
    unnamed x152 -> x126, local copies, waits for them, and re-layouts: 27.6 us -> 9.91 us
    ppermute x17 -> x8, waiting for transfers between devices: 33 us -> 20.5 us  [the longest x1 14.1 us: body(): lax.ppermute(x, 'seq', pairs(ns, 2))]
    convert_element_type x20 -> x6, other arithmetic: 22.3 us -> 10.3 us  [add16(): return (left.astype(F32) + right.astype(F32)).astype(BF)]
    ppermute x17 -> x8, starting transfers between devices: 16.9 us -> 5.33 us  [the longest x1 1.97 us: body(): lax.ppermute(x, 'seq', pairs(ns, 2))]
    ppermute x16, starting transfers between devices: 11 us -> 20.2 us  [ahead(): return lax.ppermute(value, 'batch', self.forward)]
    ppermute x12, starting transfers between devices: 18.8 us -> 10.3 us  [back(): return lax.ppermute(value, 'batch', self.backward)]
    ppermute x12, waiting for transfers between devices: 9.73 us -> 16.8 us  [back(): return lax.ppermute(value, 'batch', self.backward)]
    convert_element_type x3 -> x4, other arithmetic: 2.68 us -> 7.89 us  [the longest x1 3.07 us: body(): layer_output = (resid + out_terms + vecs[11:12]).astype(BF)]
  transfers between devices with their start and end apart: 77 -> 65, of which waited for: 29 -> 27; matrix products, arithmetic and copies ran while one was open for 8% -> 3% of each run, Pallas kernels for 39% -> 49%
where the time goes in v3:
time: 376 us; the launch traced here: 371 us
  Pallas kernels  187 us (50%)
  waiting for transfers between devices  96.2 us (26%)
  starting transfers between devices  51.1 us (14%)
  other arithmetic  19.4 us (5%)
  local copies, waits for them, and re-layouts  14.8 us (4%)
    pallas_call x2, Pallas kernels, attend_back(): pl.pallas_call(functools.partial(attend_back_kernel, count, min(512, coun...  39.3 us
    pallas_call x2, Pallas kernels, feed_call(): pl.pallas_call(functools.partial(feed_kernel, nt, nb, rows, units, live),...  32.3 us
    pallas_call x2, Pallas kernels, attend(): pl.pallas_call(functools.partial(attend_kernel, count, min(512, count), p...  22.4 us
    ppermute x16, waiting for transfers between devices, ahead(): return lax.ppermute(value, 'batch', self.forward)  20.7 us
    ppermute x16, starting transfers between devices, ahead(): return lax.ppermute(value, 'batch', self.forward)  20.2 us
    pallas_call x1, Pallas kernels, feed_grad_call(): pl.pallas_call(functools.partial(feed_grad_kernel, ns, nb, rows, units, s...  18.8 us
    ppermute x12, waiting for transfers between devices, back(): return lax.ppermute(value, 'batch', self.backward)  16.8 us
    ppermute x1, waiting for transfers between devices, body(): lax.ppermute(x, 'seq', pairs(ns, 2))  14.1 us
  transfers between devices with their start and end apart: 65, of which 27 were waited for; matrix products, arithmetic and copies ran while one was open for 3% of the time, Pallas kernels for 49%

profile of v3, /device:TPU:0, one launch (start us, length us, event | category | flops | bytes accessed | tf_op | source)
XLA Modules:
  0.0 370.7 jit_solution(9344150371050424028)
XLA Ops:
  0.7 1.8 first_pack.1
  3.0 2.6 collective-permute-start.1
  5.5 2.0 collective-permute-start.6
  7.5 2.2 second_pack.1
  9.7 3.7 collective-permute-done.1
  15.4 1.7 collective-permute-start.4
  17.1 14.1 %collective-permute-done.6.refs_2_ = bf16[512,1024]{1,0:T(8,128)(2,1)} collective-permute-done((bf16[512,1024]{1,0:T(8,128)(2,1)}, bf16[512,1024]{1,0:T(8,128)(2,1)}, u32[]{:S(2)}, u32[]{:S(2)}) %collective-permute-start.6) | collective-permute-done | bytes 1048608 | tf_op jit(solution)/shard_map/ppermute | solution.py:998
  31.3 1.7 collective-permute-start.7
  33.4 1.7 collective-permute-start.13
  35.0 5.6 %collective-permute-done.7 = bf16[144,1024]{1,0:T(8,128)(2,1)S(1)} collective-permute-done((bf16[144,1024]{1,0:T(8,128)(2,1)S(1)}, bf16[144,1024]{1,0:T(8,128)(2,1)S(1)}, u32[]{:S(2)}, u32[]{:S(2)}) %collective-permute-start.7) | collective-permute-done | bytes 294944 | tf_op jit(solution)/shard_map/ppermute | solution.py:119
  43.9 7.2 %collective-permute-done.10 = bf16[144,1024]{1,0:T(8,128)(2,1)S(1)} collective-permute-done((bf16[144,1024]{1,0:T(8,128)(2,1)S(1)}, bf16[144,1024]{1,0:T(8,128)(2,1)S(1)}, u32[]{:S(2)}, u32[]{:S(2)}) %collective-permute-start.10) | collective-permute-done | bytes 294944 | tf_op jit(solution)/shard_map/ppermute | solution.py:116
  55.2 13.4 %first.1 = (bf16[2048,1024]{1,0:T(8,128)(2,1)}, bf16[2048,768]{1,0:T(8,128)(2,1)}, bf16[1024,768]{1,0:T(8,128)(2,1)}, bf16[1024,256]{1,0:T(8,128)(2,1)}, f32[16,1024]{1,0:T(8,128)}) custom-call(s32[18]{0:T(128)} %pad_add_fusion.info, bf16[512,1024]{1,0:T(8,128)(2,1)} %bitcast.73, bf16[512,1024]{1,0:T(8,128)(2,1)} %copy-done.36, ...), custom_call_target="tpu_custom_call" | custom-call | flops 3221225 | bytes 11534 | tf_op jit(solution)/shard_map/first/pallas_call | solution.py:259
  73.5 11.2 %attend.2 = (bf16[2048,128]{1,0:T(8,128)(2,1)}, f32[2048,128]{1,0:T(8,128)}) custom-call(s32[18]{0:T(128)} %pad_add_fusion.info, f32[4]{0:T(128)} %multiply_power_fusion.slopes, bf16[2048,768]{1,0:T(8,128)(2,1)} %get-tuple-element.345.joined), custom_call_target="tpu_custom_call" | custom-call | flops 4294967 | bytes 2621 | tf_op jit(solution)/shard_map/attend/pallas_call | solution.py:350
  88.3 1.8 constant_dynamic-slice_fusion.5
  92.2 3.0 collective-permute-done.24.refs_3_
  96.8 11.2 %attend.3 = (bf16[2048,128]{1,0:T(8,128)(2,1)}, f32[2048,128]{1,0:T(8,128)}) custom-call(s32[18]{0:T(128)} %pad_add_fusion.info, f32[4]{0:T(128)} %multiply_power_fusion.slopes, bf16[2048,768]{1,0:T(8,128)(2,1)} %get-tuple-element.345.joined), custom_call_target="tpu_custom_call" | custom-call | flops 4294967 | bytes 2621 | tf_op jit(solution)/shard_map/attend/pallas_call | solution.py:350
  109.0 1.8 constant_dynamic-slice_fusion.1
  112.7 3.9 %collective-permute-done.27.refs_7_ = bf16[512,128]{1,0:T(8,128)(2,1)S(1)} collective-permute-done((bf16[512,128]{1,0:T(8,128)(2,1)S(1)}, bf16[512,128]{1,0:T(8,128)(2,1)S(1)}, u32[]{:S(2)}, u32[]{:S(2)}) %collective-permute-start.27) | collective-permute-done | bytes 131104 | tf_op jit(solution)/shard_map/ppermute | solution.py:1043
  116.6 2.7 collective-permute-done.26.refs_6_
  120.0 6.6 %middle.1 = (bf16[512,1024]{1,0:T(8,128)(2,1)}, f32[512,1024]{1,0:T(8,128)}, bf16[512,1024]{1,0:T(8,128)(2,1)}, bf16[1024,1024]{1,0:T(8,128)(2,1)}) custom-call(s32[18]{0:T(128)} %pad_add_fusion.info, bf16[512,1024]{1,0:T(8,128)(2,1)} %bitcast.74, f32[16,1024]{1,0:T(8,128)} %get-tuple-element.253.vecs, bf16[512,128]{1,0:T(8,128)(2,1)} %get-tuple-element.269.refs_0_, ...), custom_call_target="tpu_custom_call" | custom-call | flops 1073741 | bytes 10485 | tf_op jit(solution)/shard_map/middle/pallas_call | solution.py:466
  130.6 16.1 %feed.2 = (bf16[1024,1024]{1,0:T(8,128)(2,1)}, bf16[1024,1024]{1,0:T(8,128)(2,1)}, bf16[512,1024]{1,0:T(8,128)(2,1)}, bf16[512,1024]{1,0:T(8,128)(2,1)}, bf16[51...) custom-call(s32[18]{0:T(128)} %pad_add_fusion.info, ...), custom_call_target="tpu_custom_call" | custom-call | flops 8589934 | bytes 16777 | tf_op jit(solution)/shard_map/feed/pallas_call | solution.py:541
  146.7 5.8 %collective-permute-done.30.sa.refs_8_ = bf16[512,1024]{1,0:T(8,128)(2,1)S(1)} collective-permute-done((bf16[512,1024]{1,0:T(8,128)(2,1)}, bf16[512,1024]{1,0:T(8,128)(2,1)S(1)}, u32[]{:S(2)}, u32[]{:S(2)}) %collective-permute-start.30) | collective-permute-done | bytes 1048608 | tf_op jit(solution)/shard_map/ppermute | solution.py:1081
  153.0 3.6 collective-permute-done.31.sb.refs_9_
  157.6 16.2 %feed.3 = (bf16[1024,1024]{1,0:T(8,128)(2,1)}, bf16[1024,1024]{1,0:T(8,128)(2,1)}, bf16[512,1024]{1,0:T(8,128)(2,1)}, bf16[512,1024]{1,0:T(8,128)(2,1)}, bf16[51...) custom-call(s32[18]{0:T(128)} %pad_add_fusion.info, bf16[512,1024]{1,0:T(8,128)(2,1)} %copy-done.18, ...), custom_call_target="tpu_custom_call" | custom-call | flops 8589934 | bytes 16777 | tf_op jit(solution)/shard_map/feed/pallas_call | solution.py:541
  174.1 2.7 collective-permute-done.35
  176.8 2.6 add_convert_fusion.2
  180.1 18.8 %feed_grad.1 = (bf16[1,256,1024]{2,1,0:T(8,128)(2,1)}, bf16[1,256,1024]{2,1,0:T(8,128)(2,1)}, bf16[1,256,1024]{2,1,0:T(8,128)(2,1)}, bf16[1,256,1024]{2,1,0:T(8,...) custom-call(s32[18]{0:T(128)} %pad_add_fusion.info, ...), custom_call_target="tpu_custom_call" | custom-call | flops 8589934 | bytes 20971 | tf_op jit(solution)/shard_map/feed_grad/pallas_call | solution.py:610
  200.3 4.6 %collective-permute-done.36.gc = bf16[512,1024]{1,0:T(8,128)(2,1)S(1)} collective-permute-done((bf16[512,1024]{1,0:T(8,128)(2,1)}, bf16[512,1024]{1,0:T(8,128)(2,1)S(1)}, u32[]{:S(2)}, u32[]{:S(2)}) %collective-permute-start.36) | collective-permute-done | bytes 1048608 | tf_op jit(solution)/shard_map/ppermute | solution.py:1103
  205.9 7.9 %turn.1 = (f32[512,1024]{1,0:T(8,128)}, bf16[512,1024]{1,0:T(8,128)(2,1)}, bf16[512,256]{1,0:T(8,128)(2,1)}, bf16[512,256]{1,0:T(8,128)(2,1)}, bf16[512,256]{1,0...) custom-call(s32[18]{0:T(128)} %pad_add_fusion.info, bf16[512,1024]{1,0:T(8,128)(2,1)} %get-tuple-element.295.ga, ...), custom_call_target="tpu_custom_call" | custom-call | flops 1073741 | bytes 10485 | tf_op jit(solution)/shard_map/turn/pallas_call | solution.py:767
  215.8 5.9 %split_grad.1 = (bf16[1024,256]{1,0:T(8,128)(2,1)}, bf16[1024,256]{1,0:T(8,128)(2,1)}, bf16[2,1024,256]{2,1,0:T(8,128)(2,1)}) custom-call(s32[18]{0:T(128)} %pad_add_fusion.info, bf16[512,1024]{1,0:T(8,128)(2,1)} %get-tuple-element.309.left, bf16[512,1024]{1,0:T(8,128)(2,1)} %get-tuple-element.310.right), custom_call_target="tpu_custom_call" | custom-call | flops 1073741 | bytes 6291 | tf_op jit(solution)/shard_map/split_grad/pallas_call | solution.py:656
  221.7 1.6 collective-permute-done.39.refs_2_
  223.3 4.7 %collective-permute-done.40.refs_3_ = bf16[512,256]{1,0:T(8,128)(2,1)S(1)} collective-permute-done((bf16[512,256]{1,0:T(8,128)(2,1)}, bf16[512,256]{1,0:T(8,128)(2,1)S(1)}, u32[]{:S(2)}, u32[]{:S(2)}) %collective-permute-start.40) | collective-permute-done | bytes 262176 | tf_op jit(solution)/shard_map/ppermute | solution.py:1159
  231.4 19.8 %attend_back.2 = (bf16[2048,384]{1,0:T(8,128)(2,1)}, f32[1,384]{1,0:T(1,128)}) custom-call(s32[18]{0:T(128)} %pad_add_fusion.info, f32[4]{0:T(128)} %multiply_power_fusion.slopes, bf16[2048,768]{1,0:T(8,128)(2,1)} %get-tuple-element.345.joined, bf16[2048,128]{1,0:T(8,128)(2,1)} %get-tuple-element.268.mixed, f32[2048,128]{1,0:T(8,128)} %get-tuple-element.327.sums, ...), custom_call_target="tpu_custom_call" | custom-call | flops 10737418 | bytes 5242 | tf_op jit(solution)/shard_map/attend_back/pallas_call | solution.py:426
  251.2 2.4 fusion.3
  258.0 19.6 %attend_back.3 = (bf16[2048,384]{1,0:T(8,128)(2,1)}, f32[1,384]{1,0:T(1,128)}) custom-call(s32[18]{0:T(128)} %pad_add_fusion.info, f32[4]{0:T(128)} %multiply_power_fusion.slopes, bf16[2048,768]{1,0:T(8,128)(2,1)} %get-tuple-element.345.joined, bf16[2048,128]{1,0:T(8,128)(2,1)} %get-tuple-element.273.mixed, f32[2048,128]{1,0:T(8,128)} %get-tuple-element.346.sums, ...), custom_call_target="tpu_custom_call" | custom-call | flops 10737418 | bytes 5242 | tf_op jit(solution)/shard_map/attend_back/pallas_call | solution.py:426
  277.6 2.2 fusion.2.other
  283.5 11.6 %joined_grad.1 = (bf16[1,144,1024]{2,1,0:T(8,128)(2,1)}, bf16[1,144,1024]{2,1,0:T(8,128)(2,1)}, bf16[1,144,1024]{2,1,0:T(8,128)(2,1)}, bf16[1,144,1024]{2,1,0:T(...) custom-call(s32[18]{0:T(128)} %pad_add_fusion.info, ...), custom_call_target="tpu_custom_call" | custom-call | flops 3221225 | bytes 11534 | tf_op jit(solution)/shard_map/joined_grad/pallas_call | solution.py:721
  298.1 11.6 %last.1 = (bf16[512,1024]{1,0:T(8,128)(2,1)}, bf16[512,1024]{1,0:T(8,128)(2,1)}, bf16[2,512,1024]{2,1,0:T(8,128)(2,1)}) custom-call(s32[18]{0:T(128)} %pad_add_fusion.info, bf16[1024,768]{1,0:T(8,128)(2,1)} %get-tuple-element.364.weight, bf16[2048,384]{1,0:T(8,128)(2,1)} %get-tuple-element.395.refs_3_.refs_0_, ...), custom_call_target="tpu_custom_call" | custom-call | flops 3221225 | bytes 11534 | tf_op jit(solution)/shard_map/last/pallas_call | solution.py:818
  313.6 7.1 %collective-permute-done.52.refs_3_ = bf16[144,1024]{1,0:T(8,128)(2,1)S(1)} collective-permute-done((bf16[144,1024]{1,0:T(8,128)(2,1)S(1)}, bf16[144,1024]{1,0:T(8,128)(2,1)S(1)}, u32[]{:S(2)}, u32[]{:S(2)}) %collective-permute-start.52) | collective-permute-done | bytes 294944 | tf_op jit(solution)/shard_map/ppermute | solution.py:119
  321.0 4.2 %collective-permute-done.54.refs_2_ = bf16[256,1024]{1,0:T(8,128)(2,1)S(1)} collective-permute-done((bf16[256,1024]{1,0:T(8,128)(2,1)S(1)}, bf16[256,1024]{1,0:T(8,128)(2,1)S(1)}, u32[]{:S(2)}, u32[]{:S(2)}) %collective-permute-start.54) | collective-permute-done | bytes 524320 | tf_op jit(solution)/shard_map/ppermute | solution.py:1225
  325.2 2.8 fusion
  331.0 3.1 add_convert_fusion
  334.1 4.0 %collective-permute-done.55.refs_2_ = bf16[144,1024]{1,0:T(8,128)(2,1)S(1)} collective-permute-done((bf16[144,1024]{1,0:T(8,128)(2,1)S(1)}, bf16[144,1024]{1,0:T(8,128)(2,1)S(1)}, u32[]{:S(2)}, u32[]{:S(2)}) %collective-permute-start.55) | collective-permute-done | bytes 294944 | tf_op jit(solution)/shard_map/ppermute | solution.py:116
  341.7 4.6 %feed_out.1 = (f32[128,4096]{1,0:T(8,128)}, f32[512,1024]{1,0:T(8,128)}) custom-call(s32[18]{0:T(128)} %pad_add_fusion.info, bf16[256,1024]{1,0:T(8,128)(2,1)} %copy-done.20, bf16[256,1024]{1,0:T(8,128)(2,1)} %copy-done.41, bf16[256,1024]{1,0:T(8,128)(2,1)} %copy-done.39, bf16[256,1024]{1,0:T(8,128)(2,1)} %collective-permute-done.61.refs_3_), custom_call_target="tpu_custom_call" | custom-call | bytes 6291 | tf_op jit(solution)/shard_map/feed_out/pallas_call | solution.py:930
  346.3 2.8 collective-permute-done.58
  350.4 3.8 %collective-permute-done.60.gc = bf16[512,1024]{1,0:T(8,128)(2,1)} collective-permute-done((bf16[512,1024]{1,0:T(8,128)(2,1)}, bf16[512,1024]{1,0:T(8,128)(2,1)}, u32[]{:S(2)}, u32[]{:S(2)}) %collective-permute-start.60) | collective-permute-done | bytes 1048608 | tf_op jit(solution)/shard_map/ppermute | solution.py:1234
  359.0 4.4 %end.1 = f32[512,1024]{1,0:T(8,128)} custom-call(bf16[512,1024]{1,0:T(8,128)(2,1)S(1)} %copy-done.3, bf16[2,512,1024]{2,1,0:T(8,128)(2,1)S(1)} %collective-permute-done.53.gb, bf16[512,1024]{1,0:T(8,128)(2,1)} %collective-permute-done.60.gc, bf16[512,1024]{1,0:T(8,128)(2,1)S(1)} %bitcast.75, f32[512,1024]{1,0:T(8,128)S(1)} %copy-done.1, f32[16,1024]{1,0:T(8,128)S(1)} %copy-done.2), custom_call_target="tpu_custom_call" | custom-call | flops 10485 | bytes 7340 | tf_op jit(solution)/shard_map/end/pallas_call | solution.py:844
  367.2 3.4 joined_out.1
  (246 shorter events, 70.9 us)
Async XLA Ops:
  2.5 12.4 %collective-permute-start.2 = (bf16[512,1024]{1,0:T(8,128)(2,1)}, bf16[512,1024]{1,0:T(8,128)(2,1)S(1)}, u32[]{:S(2)}, u32[]{:S(2)}) collective-permute-start(bf16[512,1024]{1,0:T(8,128)(2,1)} %bitcast.71), channel_id=1, source_target_pairs={{0,8},{8,0},{16,24},{24,16},{1,9},{9,1},{17,25},{25,17},{2,10},{10... | collective-permute-start | bytes 3145736 | tf_op jit(solution)/shard_map/ppermute | solution.py:998
  3.0 10.4 %collective-permute-start.1 = (bf16[144,1024]{1,0:T(8,128)(2,1)}, bf16[144,1024]{1,0:T(8,128)(2,1)S(1)}, u32[]{:S(2)}, u32[]{:S(2)}) collective-permute-start(bf16[144,1024]{1,0:T(8,128)(2,1)} %first_pack.1), channel_id=1, source_target_pairs={{0,2},{2,4},{4,6},{6,7},{7,5},{5,3},{3,1},{1,0},{8,10},{10,12},{12... | collective-permute-start | bytes 884744 | tf_op jit(solution)/shard_map/ppermute | solution.py:116
  5.5 9.4 %collective-permute-start = (bf16[144,1024]{1,0:T(8,128)(2,1)}, bf16[144,1024]{1,0:T(8,128)(2,1)S(1)}, u32[]{:S(2)}, u32[]{:S(2)}) collective-permute-start(bf16[144,1024]{1,0:T(8,128)(2,1)} %first_pack.1), channel_id=1, source_target_pairs={{2,0},{4,2},{6,4},{7,6},{5,7},{3,5},{1,3},{0,1},{10,8},{12,10},{14... | collective-permute-start | bytes 884744 | tf_op jit(solution)/shard_map/ppermute | solution.py:119
  5.5 25.6 %collective-permute-start.6 = (bf16[512,1024]{1,0:T(8,128)(2,1)}, bf16[512,1024]{1,0:T(8,128)(2,1)}, u32[]{:S(2)}, u32[]{:S(2)}) collective-permute-start(bf16[512,1024]{1,0:T(8,128)(2,1)} %bitcast.72), channel_id=1, source_target_pairs={{0,16},{8,24},{16,0},{24,8},{1,17},{9,25},{17,1},{25,9},{2,18},{10... | collective-permute-start | bytes 3145736 | tf_op jit(solution)/shard_map/ppermute | solution.py:998
  14.9 16.3 %collective-permute-start.5 = (bf16[512,1024]{1,0:T(8,128)(2,1)S(1)}, bf16[512,1024]{1,0:T(8,128)(2,1)S(1)}, u32[]{:S(2)}, u32[]{:S(2)}) collective-permute-start(bf16[512,1024]{1,0:T(8,128)(2,1)S(1)} %bitcast.87), channel_id=1, source_target_pairs={{0,8},{8,0},{16,24},{24,16},{1,9},{9,1},{17,25},{25,17},{2,10},{10... | collective-permute-start | bytes 3145736 | tf_op jit(solution)/shard_map/ppermute | solution.py:1003
  15.0 16.2 %collective-permute-start.3 = (bf16[144,1024]{1,0:T(8,128)(2,1)S(1)}, bf16[144,1024]{1,0:T(8,128)(2,1)S(1)}, u32[]{:S(2)}, u32[]{:S(2)}) collective-permute-start(bf16[144,1024]{1,0:T(8,128)(2,1)S(1)} %collective-permute-done), channel_id=1, source_target_pairs={{2,0},{4,2},{6,4},{7,6},{5,7},{3,5},{1,3},{0,1},{10,8},{12,10},{14... | collective-permute-start | bytes 884744 | tf_op jit(solution)/shard_map/ppermute | solution.py:119
  15.4 15.8 %collective-permute-start.4 = (bf16[144,1024]{1,0:T(8,128)(2,1)S(1)}, bf16[144,1024]{1,0:T(8,128)(2,1)S(1)}, u32[]{:S(2)}, u32[]{:S(2)}) collective-permute-start(bf16[144,1024]{1,0:T(8,128)(2,1)S(1)} %collective-permute-done.1), channel_id=1, source_target_pairs={{0,2},{2,4},{4,6},{6,7},{7,5},{5,3},{3,1},{1,0},{8,10},{10,12},{12... | collective-permute-start | bytes 884744 | tf_op jit(solution)/shard_map/ppermute | solution.py:116
  31.2 10.9 %collective-permute-start.9 = (bf16[512,1024]{1,0:T(8,128)(2,1)}, bf16[512,1024]{1,0:T(8,128)(2,1)}, u32[]{:S(2)}, u32[]{:S(2)}) collective-permute-start(bf16[512,1024]{1,0:T(8,128)(2,1)} %collective-permute-done.6.refs_2_), channel_id=1, source_target_pairs={{0,8},{8,0},{16,24},{24,16},{1,9},{9,1},{17,25},{25,17},{2,10},{10... | collective-permute-start | bytes 3145736 | tf_op jit(solution)/shard_map/ppermute | solution.py:1006
  31.3 9.4 %collective-permute-start.7 = (bf16[144,1024]{1,0:T(8,128)(2,1)S(1)}, bf16[144,1024]{1,0:T(8,128)(2,1)S(1)}, u32[]{:S(2)}, u32[]{:S(2)}) collective-permute-start(bf16[144,1024]{1,0:T(8,128)(2,1)S(1)} %collective-permute-done.3), channel_id=1, source_target_pairs={{2,0},{4,2},{6,4},{7,6},{5,7},{3,5},{1,3},{0,1},{10,8},{12,10},{14... | collective-permute-start | bytes 884744 | tf_op jit(solution)/shard_map/ppermute | solution.py:119
  33.4 35.3 %collective-permute-start.13 = (bf16[512,1024]{1,0:T(8,128)(2,1)S(1)}, bf16[512,1024]{1,0:T(8,128)(2,1)S(1)}, u32[]{:S(2)}, u32[]{:S(2)}) collective-permute-start(bf16[512,1024]{1,0:T(8,128)(2,1)S(1)} %bitcast.88), channel_id=1, source_target_pairs={{0,16},{8,24},{16,0},{24,8},{1,17},{9,25},{17,1},{25,9},{2,18},{10... | collective-permute-start | bytes 3145736 | tf_op jit(solution)/shard_map/ppermute | solution.py:1007
  51.8 16.8 %collective-permute-start.12 = (bf16[256,1024]{1,0:T(8,128)(2,1)}, bf16[256,1024]{1,0:T(8,128)(2,1)}, u32[]{:S(2)}, u32[]{:S(2)}) collective-permute-start(bf16[256,1024]{1,0:T(8,128)(2,1)} %second_pack.1), channel_id=1, source_target_pairs={{0,2},{2,4},{4,6},{6,7},{7,5},{5,3},{3,1},{1,0},{8,10},{10,12},{12... | collective-permute-start | bytes 1572872 | tf_op jit(solution)/shard_map/ppermute | solution.py:116
  53.2 15.4 %collective-permute-start.11 = (bf16[256,1024]{1,0:T(8,128)(2,1)}, bf16[256,1024]{1,0:T(8,128)(2,1)}, u32[]{:S(2)}, u32[]{:S(2)}) collective-permute-start(bf16[256,1024]{1,0:T(8,128)(2,1)} %second_pack.1), channel_id=1, source_target_pairs={{2,0},{4,2},{6,4},{7,6},{5,7},{3,5},{1,3},{0,1},{10,8},{12,10},{14... | collective-permute-start | bytes 1572872 | tf_op jit(solution)/shard_map/ppermute | solution.py:119
  68.7 17.4 %collective-permute-start.16 = (bf16[512,1024]{1,0:T(8,128)(2,1)S(1)}, bf16[512,1024]{1,0:T(8,128)(2,1)S(1)}, u32[]{:S(2)}, u32[]{:S(2)}) collective-permute-start(bf16[512,1024]{1,0:T(8,128)(2,1)S(1)} %collective-permute-done.13.ca.refs_4_), channel_id=1, source_target_pairs={{0,8},{8,0},{16,24},{24,16},{1,9},{9,1},{17,25},{25,17},{2,10},{10... | collective-permute-start | bytes 3145736 | tf_op jit(solution)/shard_map/ppermute | solution.py:1028
  68.7 15.9 %collective-permute-start.18 = (bf16[1024,256]{1,0:T(8,128)(2,1)}, bf16[1024,256]{1,0:T(8,128)(2,1)}, u32[]{:S(2)}, u32[]{:S(2)}) collective-permute-start(bf16[1024,256]{1,0:T(8,128)(2,1)} %get-tuple-element.262.refs_8_), channel_id=1, source_target_pairs={{0,8},{8,0},{16,24},{24,16},{1,9},{9,1},{17,25},{25,17},{2,10},{10... | collective-permute-start | bytes 1572872 | tf_op jit(solution)/shard_map/ppermute | solution.py:73
  69.2 15.4 %collective-permute-start.17 = (bf16[1024,256]{1,0:T(8,128)(2,1)}, bf16[1024,256]{1,0:T(8,128)(2,1)}, u32[]{:S(2)}, u32[]{:S(2)}) collective-permute-start(bf16[1024,256]{1,0:T(8,128)(2,1)} %get-tuple-element.262.refs_8_), channel_id=1, source_target_pairs={{0,16},{8,24},{16,0},{24,8},{1,17},{9,25},{17,1},{25,9},{2,18},{10... | collective-permute-start | bytes 1572872 | tf_op jit(solution)/shard_map/ppermute | solution.py:73
  70.8 13.9 %collective-permute-start.14 = (bf16[256,1024]{1,0:T(8,128)(2,1)}, bf16[256,1024]{1,0:T(8,128)(2,1)S(1)}, u32[]{:S(2)}, u32[]{:S(2)}) collective-permute-start(bf16[256,1024]{1,0:T(8,128)(2,1)} %collective-permute-done.11), channel_id=1, source_target_pairs={{2,0},{4,2},{6,4},{7,6},{5,7},{3,5},{1,3},{0,1},{10,8},{12,10},{14... | collective-permute-start | bytes 1572872 | tf_op jit(solution)/shard_map/ppermute | solution.py:119
  72.3 13.7 %collective-permute-start.15 = (bf16[256,1024]{1,0:T(8,128)(2,1)}, bf16[256,1024]{1,0:T(8,128)(2,1)S(1)}, u32[]{:S(2)}, u32[]{:S(2)}) collective-permute-start(bf16[256,1024]{1,0:T(8,128)(2,1)} %collective-permute-done.12), channel_id=1, source_target_pairs={{0,2},{2,4},{4,6},{6,7},{7,5},{5,3},{3,1},{1,0},{8,10},{10,12},{12... | collective-permute-start | bytes 1572872 | tf_op jit(solution)/shard_map/ppermute | solution.py:116
  86.0 22.0 %collective-permute-start.19 = (bf16[256,1024]{1,0:T(8,128)(2,1)S(1)}, bf16[256,1024]{1,0:T(8,128)(2,1)}, u32[]{:S(2)}, u32[]{:S(2)}) collective-permute-start(bf16[256,1024]{1,0:T(8,128)(2,1)S(1)} %collective-permute-done.14), channel_id=1, source_target_pairs={{2,0},{4,2},{6,4},{7,6},{5,7},{3,5},{1,3},{0,1},{10,8},{12,10},{14... | collective-permute-start | bytes 1572872 | tf_op jit(solution)/shard_map/ppermute | solution.py:119
  87.7 20.4 %collective-permute-start.20 = (bf16[256,1024]{1,0:T(8,128)(2,1)S(1)}, bf16[256,1024]{1,0:T(8,128)(2,1)}, u32[]{:S(2)}, u32[]{:S(2)}) collective-permute-start(bf16[256,1024]{1,0:T(8,128)(2,1)S(1)} %collective-permute-done.15), channel_id=1, source_target_pairs={{0,2},{2,4},{4,6},{6,7},{7,5},{5,3},{3,1},{1,0},{8,10},{10,12},{12... | collective-permute-start | bytes 1572872 | tf_op jit(solution)/shard_map/ppermute | solution.py:116
  88.3 19.7 %collective-permute-start.21 = (bf16[1024,256]{1,0:T(8,128)(2,1)}, bf16[1024,256]{1,0:T(8,128)(2,1)}, u32[]{:S(2)}, u32[]{:S(2)}) collective-permute-start(bf16[1024,256]{1,0:T(8,128)(2,1)} %collective-permute-done.17.refs_10_), channel_id=1, source_target_pairs={{0,8},{8,0},{16,24},{24,16},{1,9},{9,1},{17,25},{25,17},{2,10},{10... | collective-permute-start | bytes 1572872 | tf_op jit(solution)/shard_map/ppermute | solution.py:1053
  90.7 17.3 %collective-permute-start.23 = (bf16[512,128]{1,0:T(8,128)(2,1)S(1)}, bf16[512,128]{1,0:T(8,128)(2,1)S(1)}, u32[]{:S(2)}, u32[]{:S(2)}) collective-permute-start(bf16[512,128]{1,0:T(8,128)(2,1)S(1)} %get-tuple-element.463), channel_id=1, source_target_pairs={{0,16},{8,24},{16,0},{24,8},{1,17},{9,25},{17,1},{25,9},{2,18},{10... | collective-permute-start | bytes 393224 | tf_op jit(solution)/shard_map/ppermute | solution.py:1043
  95.3 12.8 %collective-permute-start.22 = (bf16[512,128]{1,0:T(8,128)(2,1)S(1)}, bf16[512,128]{1,0:T(8,128)(2,1)S(1)}, u32[]{:S(2)}, u32[]{:S(2)}) collective-permute-start(bf16[512,128]{1,0:T(8,128)(2,1)S(1)} %get-tuple-element.464), channel_id=1, source_target_pairs={{0,8},{8,0},{16,24},{24,16},{1,9},{9,1},{17,25},{25,17},{2,10},{10... | collective-permute-start | bytes 393224 | tf_op jit(solution)/shard_map/ppermute | solution.py:1043
  108.1 18.6 %collective-permute-start.28 = (bf16[256,1024]{1,0:T(8,128)(2,1)}, bf16[256,1024]{1,0:T(8,128)(2,1)S(1)}, u32[]{:S(2)}, u32[]{:S(2)}) collective-permute-start(bf16[256,1024]{1,0:T(8,128)(2,1)} %collective-permute-done.20), channel_id=1, source_target_pairs={{0,2},{2,4},{4,6},{6,7},{7,5},{5,3},{3,1},{1,0},{8,10},{10,12},{12... | collective-permute-start | bytes 1572872 | tf_op jit(solution)/shard_map/ppermute | solution.py:116
  126.9 25.6 %collective-permute-start.30 = (bf16[512,1024]{1,0:T(8,128)(2,1)}, bf16[512,1024]{1,0:T(8,128)(2,1)S(1)}, u32[]{:S(2)}, u32[]{:S(2)}) collective-permute-start(bf16[512,1024]{1,0:T(8,128)(2,1)} %get-tuple-element.278.sa.refs_6_), channel_id=1, source_target_pairs={{0,16},{8,24},{16,0},{24,8},{1,17},{9,25},{17,1},{25,9},{2,18},{10... | collective-permute-start | bytes 3145736 | tf_op jit(solution)/shard_map/ppermute | solution.py:1081
  152.5 21.3 %collective-permute-start.33 = (bf16[512,1024]{1,0:T(8,128)(2,1)}, bf16[512,1024]{1,0:T(8,128)(2,1)S(1)}, u32[]{:S(2)}, u32[]{:S(2)}) collective-permute-start(bf16[512,1024]{1,0:T(8,128)(2,1)} %get-tuple-element.297), channel_id=1, source_target_pairs={{0,8},{8,0},{16,24},{24,16},{1,9},{9,1},{17,25},{25,17},{2,10},{10... | collective-permute-start | bytes 3145736 | tf_op jit(solution)/shard_map/ppermute | solution.py:1092
  153.0 20.9 %collective-permute-start.34 = (bf16[512,1024]{1,0:T(8,128)(2,1)}, bf16[512,1024]{1,0:T(8,128)(2,1)}, u32[]{:S(2)}, u32[]{:S(2)}) collective-permute-start(bf16[512,1024]{1,0:T(8,128)(2,1)} %get-tuple-element.298), channel_id=1, source_target_pairs={{0,8},{8,0},{16,24},{24,16},{1,9},{9,1},{17,25},{25,17},{2,10},{10... | collective-permute-start | bytes 3145736 | tf_op jit(solution)/shard_map/ppermute | solution.py:1093
  179.4 25.4 %collective-permute-start.36 = (bf16[512,1024]{1,0:T(8,128)(2,1)}, bf16[512,1024]{1,0:T(8,128)(2,1)S(1)}, u32[]{:S(2)}, u32[]{:S(2)}) collective-permute-start(bf16[512,1024]{1,0:T(8,128)(2,1)} %add_convert_fusion.2), channel_id=1, source_target_pairs={{0,16},{8,24},{16,0},{24,8},{1,17},{9,25},{17,1},{25,9},{2,18},{10... | collective-permute-start | bytes 3145736 | tf_op jit(solution)/shard_map/ppermute | solution.py:1103
  180.1 24.8 %collective-permute-start.37 = (bf16[512,1024]{1,0:T(8,128)(2,1)}, bf16[512,1024]{1,0:T(8,128)(2,1)S(1)}, u32[]{:S(2)}, u32[]{:S(2)}) collective-permute-start(bf16[512,1024]{1,0:T(8,128)(2,1)} %get-tuple-element.304), channel_id=1, source_target_pairs={{0,8},{8,0},{16,24},{24,16},{1,9},{9,1},{17,25},{25,17},{2,10},{10... | collective-permute-start | bytes 3145736 | tf_op jit(solution)/shard_map/ppermute | solution.py:1104
  198.9 22.8 %collective-permute-start.32 = (bf16[256,1024]{1,0:T(8,128)(2,1)}, bf16[256,1024]{1,0:T(8,128)(2,1)S(1)}, u32[]{:S(2)}, u32[]{:S(2)}) collective-permute-start(bf16[256,1024]{1,0:T(8,128)(2,1)} %bitcast.116), channel_id=1, source_target_pairs={{0,2},{2,4},{4,6},{6,7},{7,5},{5,3},{3,1},{1,0},{8,10},{10,12},{12... | collective-permute-start | bytes 1572872 | tf_op jit(solution)/shard_map/ppermute | solution.py:116
  213.9 9.4 %collective-permute-start.39 = (bf16[512,256]{1,0:T(8,128)(2,1)}, bf16[512,256]{1,0:T(8,128)(2,1)S(1)}, u32[]{:S(2)}, u32[]{:S(2)}) collective-permute-start(bf16[512,256]{1,0:T(8,128)(2,1)} %get-tuple-element.316), channel_id=1, source_target_pairs={{0,16},{8,24},{16,0},{24,8},{1,17},{9,25},{17,1},{25,9},{2,18},{10... | collective-permute-start | bytes 786440 | tf_op jit(solution)/shard_map/ppermute | solution.py:1159
  214.6 13.4 %collective-permute-start.40 = (bf16[512,256]{1,0:T(8,128)(2,1)}, bf16[512,256]{1,0:T(8,128)(2,1)S(1)}, u32[]{:S(2)}, u32[]{:S(2)}) collective-permute-start(bf16[512,256]{1,0:T(8,128)(2,1)} %get-tuple-element.317), channel_id=1, source_target_pairs={{0,24},{8,16},{16,8},{24,0},{1,25},{9,17},{17,9},{25,1},{2,26},{10... | collective-permute-start | bytes 786440 | tf_op jit(solution)/shard_map/ppermute | solution.py:1159
  229.1 22.1 %collective-permute-start.43 = (bf16[2,1024,256]{2,1,0:T(8,128)(2,1)}, bf16[2,1024,256]{2,1,0:T(8,128)(2,1)S(1)}, u32[]{:S(2)}, u32[]{:S(2)}) collective-permute-start(bf16[2,1024,256]{2,1,0:T(8,128)(2,1)} %get-tuple-element.333), channel_id=1, source_target_pairs={{0,8},{8,0},{16,24},{24,16},{1,9},{9,1},{17,25},{25,17},{2,10},{10... | collective-permute-start | bytes 3145736 | tf_op jit(solution)/shard_map/ppermute | solution.py:1166
  229.3 21.8 %collective-permute-start.42 = (bf16[256,1024]{1,0:T(8,128)(2,1)}, bf16[256,1024]{1,0:T(8,128)(2,1)S(1)}, u32[]{:S(2)}, u32[]{:S(2)}) collective-permute-start(bf16[256,1024]{1,0:T(8,128)(2,1)} %bitcast.30), channel_id=1, source_target_pairs={{2,0},{4,2},{6,4},{7,6},{5,7},{3,5},{1,3},{0,1},{10,8},{12,10},{14... | collective-permute-start | bytes 1572872 | tf_op jit(solution)/shard_map/ppermute | solution.py:119
  230.9 20.3 %collective-permute-start.41 = (bf16[256,1024]{1,0:T(8,128)(2,1)}, bf16[256,1024]{1,0:T(8,128)(2,1)S(1)}, u32[]{:S(2)}, u32[]{:S(2)}) collective-permute-start(bf16[256,1024]{1,0:T(8,128)(2,1)} %fusion.4), channel_id=1, source_target_pairs={{0,2},{2,4},{4,6},{6,7},{7,5},{5,3},{3,1},{1,0},{8,10},{10,12},{12... | collective-permute-start | bytes 1572872 | tf_op jit(solution)/shard_map/ppermute | solution.py:116
  253.9 23.7 %collective-permute-start.44 = (bf16[256,1024]{1,0:T(8,128)(2,1)S(1)}, bf16[256,1024]{1,0:T(8,128)(2,1)S(1)}, u32[]{:S(2)}, u32[]{:S(2)}) collective-permute-start(bf16[256,1024]{1,0:T(8,128)(2,1)S(1)} %get-tuple-element.343), channel_id=1, source_target_pairs={{0,2},{2,4},{4,6},{6,7},{7,5},{5,3},{3,1},{1,0},{8,10},{10,12},{12... | collective-permute-start | bytes 1572872 | tf_op jit(solution)/shard_map/ppermute | solution.py:116
  255.3 22.2 %collective-permute-start.45 = (bf16[256,1024]{1,0:T(8,128)(2,1)S(1)}, bf16[256,1024]{1,0:T(8,128)(2,1)S(1)}, u32[]{:S(2)}, u32[]{:S(2)}) collective-permute-start(bf16[256,1024]{1,0:T(8,128)(2,1)S(1)} %get-tuple-element.344), channel_id=1, source_target_pairs={{2,0},{4,2},{6,4},{7,6},{5,7},{3,5},{1,3},{0,1},{10,8},{12,10},{14... | collective-permute-start | bytes 1572872 | tf_op jit(solution)/shard_map/ppermute | solution.py:119
  256.0 21.6 %collective-permute-start.46 = (bf16[1024,256]{1,0:T(8,128)(2,1)}, bf16[1024,256]{1,0:T(8,128)(2,1)S(1)}, u32[]{:S(2)}, u32[]{:S(2)}) collective-permute-start(bf16[1024,256]{1,0:T(8,128)(2,1)} %fusion.3), channel_id=1, source_target_pairs={{0,16},{8,24},{16,0},{24,8},{1,17},{9,25},{17,1},{25,9},{2,18},{10... | collective-permute-start | bytes 1572872 | tf_op jit(solution)/shard_map/ppermute | solution.py:1179
  280.0 15.1 %collective-permute-start.47 = (bf16[256,1024]{1,0:T(8,128)(2,1)S(1)}, bf16[256,1024]{1,0:T(8,128)(2,1)}, u32[]{:S(2)}, u32[]{:S(2)}) collective-permute-start(bf16[256,1024]{1,0:T(8,128)(2,1)S(1)} %get-tuple-element.360), channel_id=1, source_target_pairs={{0,2},{2,4},{4,6},{6,7},{7,5},{5,3},{3,1},{1,0},{8,10},{10,12},{12... | collective-permute-start | bytes 1572872 | tf_op jit(solution)/shard_map/ppermute | solution.py:116
  281.5 13.6 %collective-permute-start.48 = (bf16[256,1024]{1,0:T(8,128)(2,1)S(1)}, bf16[256,1024]{1,0:T(8,128)(2,1)}, u32[]{:S(2)}, u32[]{:S(2)}) collective-permute-start(bf16[256,1024]{1,0:T(8,128)(2,1)S(1)} %get-tuple-element.361), channel_id=1, source_target_pairs={{2,0},{4,2},{6,4},{7,6},{5,7},{3,5},{1,3},{0,1},{10,8},{12,10},{14... | collective-permute-start | bytes 1572872 | tf_op jit(solution)/shard_map/ppermute | solution.py:119
  282.1 27.6 %collective-permute-start.50 = (bf16[512,1024]{1,0:T(8,128)(2,1)S(1)}, bf16[512,1024]{1,0:T(8,128)(2,1)S(1)}, u32[]{:S(2)}, u32[]{:S(2)}) collective-permute-start(bf16[512,1024]{1,0:T(8,128)(2,1)S(1)} %copy-done.28), channel_id=1, source_target_pairs={{0,16},{8,24},{16,0},{24,8},{1,17},{9,25},{17,1},{25,9},{2,18},{10... | collective-permute-start | bytes 3145736 | tf_op jit(solution)/shard_map/ppermute | solution.py:1191
  296.7 13.0 %collective-permute-start.49 = (bf16[144,1024]{1,0:T(8,128)(2,1)}, bf16[144,1024]{1,0:T(8,128)(2,1)S(1)}, u32[]{:S(2)}, u32[]{:S(2)}) collective-permute-start(bf16[144,1024]{1,0:T(8,128)(2,1)} %bitcast.40), channel_id=1, source_target_pairs={{0,2},{2,4},{4,6},{6,7},{7,5},{5,3},{3,1},{1,0},{8,10},{10,12},{12... | collective-permute-start | bytes 884744 | tf_op jit(solution)/shard_map/ppermute | solution.py:116
  310.8 14.4 %collective-permute-start.53 = (bf16[2,512,1024]{2,1,0:T(8,128)(2,1)}, bf16[2,512,1024]{2,1,0:T(8,128)(2,1)S(1)}, u32[]{:S(2)}, u32[]{:S(2)}) collective-permute-start(bf16[2,512,1024]{2,1,0:T(8,128)(2,1)} %get-tuple-element.404), channel_id=1, source_target_pairs={{0,8},{8,0},{16,24},{24,16},{1,9},{9,1},{17,25},{25,17},{2,10},{10... | collective-permute-start | bytes 6291464 | tf_op jit(solution)/shard_map/ppermute | solution.py:1224
  310.8 14.3 %collective-permute-start.54 = (bf16[256,1024]{1,0:T(8,128)(2,1)S(1)}, bf16[256,1024]{1,0:T(8,128)(2,1)S(1)}, u32[]{:S(2)}, u32[]{:S(2)}) collective-permute-start(bf16[256,1024]{1,0:T(8,128)(2,1)S(1)} %fusion.6.refs_0_), channel_id=1, source_target_pairs={{0,16},{8,24},{16,0},{24,8},{1,17},{9,25},{17,1},{25,9},{2,18},{10... | collective-permute-start | bytes 1572872 | tf_op jit(solution)/shard_map/ppermute | solution.py:1225
  328.2 11.1 %collective-permute-start.57 = (bf16[256,1024]{1,0:T(8,128)(2,1)S(1)}, bf16[256,1024]{1,0:T(8,128)(2,1)S(1)}, u32[]{:S(2)}, u32[]{:S(2)}) collective-permute-start(bf16[256,1024]{1,0:T(8,128)(2,1)S(1)} %fusion.6.refs_0_), channel_id=1, source_target_pairs={{0,8},{8,0},{16,24},{24,16},{1,9},{9,1},{17,25},{25,17},{2,10},{10... | collective-permute-start | bytes 1572872 | tf_op jit(solution)/shard_map/ppermute | solution.py:1235
  328.3 25.9 %collective-permute-start.60 = (bf16[512,1024]{1,0:T(8,128)(2,1)}, bf16[512,1024]{1,0:T(8,128)(2,1)}, u32[]{:S(2)}, u32[]{:S(2)}) collective-permute-start(bf16[512,1024]{1,0:T(8,128)(2,1)} %fusion), channel_id=1, source_target_pairs={{0,16},{8,24},{16,0},{24,8},{1,17},{9,25},{17,1},{25,9},{2,18},{10... | collective-permute-start | bytes 3145736 | tf_op jit(solution)/shard_map/ppermute | solution.py:1234
  339.6 9.5 %collective-permute-start.58 = (bf16[144,1024]{1,0:T(8,128)(2,1)S(1)}, bf16[144,1024]{1,0:T(8,128)(2,1)}, u32[]{:S(2)}, u32[]{:S(2)}) collective-permute-start(bf16[144,1024]{1,0:T(8,128)(2,1)S(1)} %get-tuple-element.429), channel_id=1, source_target_pairs={{0,2},{2,4},{4,6},{6,7},{7,5},{5,3},{3,1},{1,0},{8,10},{10,12},{12... | collective-permute-start | bytes 884744 | tf_op jit(solution)/shard_map/ppermute | solution.py:116
  341.2 9.2 %collective-permute-start.59 = (bf16[144,1024]{1,0:T(8,128)(2,1)S(1)}, bf16[144,1024]{1,0:T(8,128)(2,1)}, u32[]{:S(2)}, u32[]{:S(2)}) collective-permute-start(bf16[144,1024]{1,0:T(8,128)(2,1)S(1)} %get-tuple-element.430), channel_id=1, source_target_pairs={{2,0},{4,2},{6,4},{7,6},{5,7},{3,5},{1,3},{0,1},{10,8},{12,10},{14... | collective-permute-start | bytes 884744 | tf_op jit(solution)/shard_map/ppermute | solution.py:119
  355.5 9.4 %collective-permute-start.62 = (bf16[144,1024]{1,0:T(8,128)(2,1)S(1)}, bf16[144,1024]{1,0:T(8,128)(2,1)S(1)}, u32[]{:S(2)}, u32[]{:S(2)}) collective-permute-start(bf16[144,1024]{1,0:T(8,128)(2,1)S(1)} %fusion.8.refs_0_), channel_id=1, source_target_pairs={{0,16},{8,24},{16,0},{24,8},{1,17},{9,25},{17,1},{25,9},{2,18},{10... | collective-permute-start | bytes 884744 | tf_op jit(solution)/shard_map/ppermute | solution.py:1245
  (80 other events, 782.3 us)

commit v4 on v3

--- a/solution.py
+++ b/solution.py
@@ -207,9 +207,10 @@
     )(info, expand, shrink)
 
 
-def first_kernel(ns, nt, nb, rows, cols, live, info, *refs):
+def first_kernel(starts, nb, rows, cols, live, info, *refs):
     jbias_in, refs = (None, refs) if live else (refs[0], refs[1:])
-    xs, weights = refs[:ns], refs[ns:-6]
+    count = len(starts) - 1
+    xs, weights = refs[:count], refs[count:-6]
     normed, joined, full, outw, vecs, jbias = refs[-6:]
     step = pl.program_id(0)
 
@@ -232,37 +233,41 @@
         else:
             jbias[...] = jbias_in[...]
 
-    for rel in range(ns):
-
-        @pl.when(lax.div(step, nt) == rel)
+    for at in range(count):
+
+        @pl.when((step >= starts[at]) & (step < starts[at + 1]))
         def _():
-            unit, _ = norm_parts(xs[rel][...].astype(F32))
+            unit, _ = norm_parts(xs[at][...].astype(F32))
             value = (unit * vecs[0:1] + vecs[1:2]).astype(BF)
             normed[...] = value
             joined[...] = (dg(value, full[...], NN) + jbias[...]).astype(BF)
 
 
-def first_call(info, jbias, xs, weights, cols, live):
-    ns = len(xs)
-    tok, dim = xs[0].shape
+def first_call(info, jbias, xs, weights, cols, live, ns):
+    dim = xs[0].shape[1]
+    tok = sum(piece.shape[0] for piece in xs) // ns
     nb = sum(weight.shape[0] for weight in weights)
     rows = dim // nb
     cw = weights[0].shape[2] - cols
     tile = min(256, tok)
     nt = tok // tile
+    starts = [0]
+    for piece in xs:
+        starts.append(starts[-1] + piece.shape[0] // tile)
     extra = [] if live else [jbias]
     place = lambda i, info: ((info[0] ^ lax.div(i, nt)) * nt + lax.rem(i, nt), 0)
 
-    def source(rel):
-        return pl.BlockSpec((tile, dim), lambda i, info: (jnp.clip(i - rel * nt, 0, nt - 1), 0))
-
-    return pl.pallas_call(
-        functools.partial(first_kernel, ns, nt, nb, rows, cols, live),
+    def source(at):
+        last = starts[at + 1] - starts[at] - 1
+        return pl.BlockSpec((tile, dim), lambda i, info: (jnp.clip(i - starts[at], 0, last), 0))
+
+    return pl.pallas_call(
+        functools.partial(first_kernel, starts, nb, rows, cols, live),
         grid_spec=pltpu.PrefetchScalarGridSpec(
             num_scalar_prefetch=1,
             grid=(ns * nt,),
             in_specs=[once(value.shape) for value in extra]
-            + [source(rel) for rel in range(ns)]
+            + [source(at) for at in range(len(xs))]
             + [once(weight.shape) for weight in weights],
             out_specs=[
                 pl.BlockSpec((tile, dim), place),
@@ -343,24 +348,33 @@
         sums[low:high] = jnp.concatenate(logs, 1)
 
 
-def attend(joined, info, slopes, pair):
-    count = joined.shape[0]
+def attend(joined, info, slopes, pair, held):
+    count, width = joined.shape
+    groups = width // (6 * HD)
     smem = pl.BlockSpec(memory_space=pltpu.SMEM)
+    narrow = pl.BlockSpec((count, 2 * HD), lambda i: (0, pair))
     area = count * count
-    return pl.pallas_call(
-        functools.partial(attend_kernel, count, min(512, count), pair),
+    extra = [] if held is None else list(held)
+
+    def kernel(*refs):
+        attend_kernel(count, min(512, count), pair, *refs[:3], *refs[3 + len(extra) :])
+
+    return pl.pallas_call(
+        kernel,
         grid=(1,),
-        in_specs=[smem, smem, pl.BlockSpec((count, 6 * HD), lambda i: (0, pair))],
-        out_specs=[pl.BlockSpec((count, 2 * HD), lambda i: (0, 0))] * 2,
+        in_specs=[smem, smem, pl.BlockSpec((count, 6 * HD), lambda i: (0, pair))]
+        + [pl.BlockSpec(memory_space=pl.ANY)] * len(extra),
+        out_specs=[narrow, narrow],
         out_shape=[
-            jax.ShapeDtypeStruct((count, 2 * HD), BF),
-            jax.ShapeDtypeStruct((count, 2 * HD), F32),
+            jax.ShapeDtypeStruct((count, groups * 2 * HD), BF),
+            jax.ShapeDtypeStruct((count, groups * 2 * HD), F32),
         ],
+        input_output_aliases={3: 0, 4: 1} if extra else {},
         scratch_shapes=[pltpu.VMEM((2, count, 2 * HD), BF)],
         compiler_params=params(60),
         cost_estimate=cost(area * 1024, 20 * count * HD, area),
         name="attend",
-    )(info, slopes, joined)
+    )(info, slopes, joined, *extra)
 
 
 def attend_back_kernel(count, size, ns, pair, info, slopes, joined, mixed, sums, *refs):
@@ -415,25 +429,34 @@
     sides[...] = jnp.sum(out[...].astype(F32), axis=0, keepdims=True)
 
 
-def attend_back(joined, grads, mixed, sums, info, slopes, pair):
-    count = joined.shape[0]
+def attend_back(joined, grads, mixed, sums, info, slopes, pair, held):
+    count, width = joined.shape
     ns = len(grads)
     smem = pl.BlockSpec(memory_space=pltpu.SMEM)
     wide = pl.BlockSpec((count, 6 * HD), lambda i: (0, pair))
-    narrow = pl.BlockSpec((count, 2 * HD), lambda i: (0, 0))
+    narrow = pl.BlockSpec((count, 2 * HD), lambda i: (0, pair))
     piece = pl.BlockSpec((count // ns, 2 * HD), lambda i: (0, pair))
     area = count * count
-    return pl.pallas_call(
-        functools.partial(attend_back_kernel, count, min(512, count), ns, pair),
+    extra = [] if held is None else [held]
+
+    def kernel(*refs):
+        inputs, rest = refs[: 5 + ns], refs[5 + ns + len(extra) :]
+        attend_back_kernel(count, min(512, count), ns, pair, *inputs, *rest)
+
+    return pl.pallas_call(
+        kernel,
         grid=(1,),
-        in_specs=[smem, smem, wide, narrow, narrow] + [piece] * ns,
-        out_specs=[pl.BlockSpec((count, 6 * HD), lambda i: (0, 0)), pl.BlockSpec((1, 6 * HD), lambda i: (0, 0))],
-        out_shape=[jax.ShapeDtypeStruct((count, 6 * HD), BF), jax.ShapeDtypeStruct((1, 6 * HD), F32)],
+        in_specs=[smem, smem, wide, narrow, narrow]
+        + [piece] * ns
+        + [pl.BlockSpec(memory_space=pl.ANY)] * len(extra),
+        out_specs=[wide, pl.BlockSpec((1, 6 * HD), lambda i: (0, 0))],
+        out_shape=[jax.ShapeDtypeStruct((count, width), BF), jax.ShapeDtypeStruct((1, 6 * HD), F32)],
+        input_output_aliases={5 + ns: 0} if extra else {},
         scratch_shapes=[pltpu.VMEM((2, count, 2 * HD), BF)] * 4 + [pltpu.VMEM((2, 2 * HD, count), F32)],
         compiler_params=params(60),
         cost_estimate=cost(area * 2560, 40 * count * HD, area),
         name="attend_back",
-    )(info, slopes, joined, mixed, sums, *grads)
+    )(info, slopes, joined, mixed, sums, *grads, *extra)
 
 
 def middle_kernel(ns, np, info, x, vecs, *refs):
@@ -489,6 +512,10 @@
     weights = refs[:-9]
     activ, pre_grad, oa, ob, ba, bb, bgrad, wide, tall = refs[-9:]
     step = pl.program_id(0)
+    bias = ebias[...]
+    if live:
+        row = lax.broadcasted_iota(jnp.int32, bias.shape, 0)
+        bias = jnp.sum(jnp.where(row == 7 + info[0], bias, 0.0), axis=0, keepdims=True)
 
     @pl.when(step == 0)
     def _():
@@ -507,7 +534,7 @@
         bgrad[...] = jnp.zeros_like(bgrad)
 
     def work(second, cot, out, back):
-        pre = dg(second[...], wide[...], NN) + ebias[...]
+        pre = dg(second[...], wide[...], NN) + bias
         square = pre * pre
         bend = jnp.tanh(0.7978845608028654 * pre * (1.0 + 0.044715 * square))
         half = 0.5 + 0.5 * bend
@@ -671,14 +698,14 @@
 
 def joined_grad_kernel(nb, rows, np, live, info, left, other, weight, vecs, *refs):
     smalls, refs = (refs[:3], refs[3:]) if live else (refs[:1], refs[1:])
-    rights, sides, outs = refs[:np], refs[np : 2 * np], refs[2 * np :]
-    totals = [dg(left[...], right[...], TN) for right in rights]
+    right, sides, outs = refs[0], refs[1 : 1 + np], refs[1 + np :]
+    total = dg(left[...], right[...], TN)
     tile, cw = other.shape
     cols = weight.shape[1]
     first = pl.program_id(0) * (tile // rows)
-    low = jnp.concatenate(totals, 1).astype(BF)
+    low = total.astype(BF)
     weights = weight[...].astype(F32)
-    moment = jnp.sum(jnp.concatenate(totals, 1) * weights, axis=1, keepdims=True)
+    moment = jnp.sum(total * weights, axis=1, keepdims=True)
     shift = jnp.sum(jnp.concatenate([side[...] for side in sides], 1) * weights, axis=1, keepdims=True)
     moment = jnp.broadcast_to(moment, (tile, 128)).T[:1]
     shift = jnp.broadcast_to(shift, (tile, 128)).T[:1]
@@ -707,7 +734,7 @@
         put(outs, slot, held[:, high], slice(rows, rows + 16), slice(0, rows))
 
 
-def joined_grad_call(info, left, rights, sides, other, weight, vecs, shares, turned, biases, nb, live):
+def joined_grad_call(info, left, right, sides, other, weight, vecs, shares, turned, biases, nb, live):
     count, dim = left.shape
     cols = weight.shape[1]
     cw = other.shape[1]
@@ -719,20 +746,20 @@
     tall = lambda value: pl.BlockSpec((value.shape[0], tile), lambda i, info: (0, i))
     smalls = (turned, *biases) if live else (shares,)
     return pl.pallas_call(
-        functools.partial(joined_grad_kernel, nb, rows, len(rights), live),
+        functools.partial(joined_grad_kernel, nb, rows, len(sides), live),
         grid_spec=pltpu.PrefetchScalarGridSpec(
             num_scalar_prefetch=1,
             grid=(dim // tile,),
             in_specs=[pl.BlockSpec((count, tile), lambda i, info: (0, i)), flat(cw), flat(cols), tall(vecs)]
             + [tall(value) for value in smalls]
-            + [once(value.shape) for value in (*rights, *sides)],
+            + [once(value.shape) for value in (right, *sides)],
             out_specs=[once(shape) for shape in shapes],
         ),
         out_shape=[jax.ShapeDtypeStruct(shape, BF) for shape in shapes],
         compiler_params=params(60),
         cost_estimate=cost(2 * count * dim * cols, 2 * count * (dim + cols) + 4 * dim * dim),
         name="joined_grad",
-    )(info, left, other, weight, vecs, *smalls, *rights, *sides)
+    )(info, left, other, weight, vecs, *smalls, right, *sides)
 
 
 def turn_kernel(ns, np, cw, info, ga, gb, gc, resid, cot, vecs, full, resid_grad, branch, *refs):
@@ -787,47 +814,43 @@
     )(info, *terms, resid, cot, vecs, full)
 
 
-def last_kernel(ns, nt, np, info, weight, *refs):
-    rights, outs = refs[:np], refs[np:]
+def last_kernel(ns, info, weight, right, *outs):
     step = pl.program_id(0)
-    grad = None
-    at = 0
-    for right in rights:
-        width = right.shape[1]
-        term = dg(right[...], weight[:, at : at + width], NT)
-        grad = term if grad is None else grad + term
-        at += width
-    low = grad.astype(BF)
-    tile = low.shape[0]
-    rows = pl.ds(pl.multiple_of(lax.rem(step, nt) * tile, tile), tile)
+    low = dg(right[...], weight[...], NT).astype(BF)
     for rel in range(ns):
 
-        @pl.when(ns - 1 - lax.div(step, nt) == rel)
+        @pl.when(ns - 1 - step == rel)
         def _():
-            pair_put(outs, ns, rel, rows, low)
-
-
-def last_call(info, rights, weight, ns):
-    count = rights[0].shape[0]
+            if ns == 4 and rel % 2:
+                outs[2][0] = low
+            else:
+                outs[rel // 2 if ns == 4 else rel][...] = low
+
+
+def last_call(info, right, weight, ns):
+    count = right.shape[0]
     dim, cols = weight.shape
     tok = count // ns
-    tile = min(256, tok)
-    nt = tok // tile
-    source = lambda i, info: ((info[0] ^ (ns - 1 - lax.div(i, nt))) * nt + lax.rem(i, nt), 0)
     shapes = pair_shapes((tok, dim), ns)
-    return pl.pallas_call(
-        functools.partial(last_kernel, ns, nt, len(rights)),
+    specs = [pl.BlockSpec((tok, dim), lambda i, info: (0, 0))] * ns
+    if ns == 4:
+        specs[2:] = [pl.BlockSpec((1, tok, dim), lambda i, info: (jnp.where(i < 2, 1, 0), 0, 0))]
+    return pl.pallas_call(
+        functools.partial(last_kernel, ns),
         grid_spec=pltpu.PrefetchScalarGridSpec(
             num_scalar_prefetch=1,
-            grid=(ns * nt,),
-            in_specs=[once(weight.shape)] + [pl.BlockSpec((tile, right.shape[1]), source) for right in rights],
-            out_specs=[once(shape) for shape in shapes],
+            grid=(ns,),
+            in_specs=[
+                once(weight.shape),
+                pl.BlockSpec((tok, cols), lambda i, info: (info[0] ^ (ns - 1 - i), 0)),
+            ],
+            out_specs=specs,
         ),
         out_shape=[jax.ShapeDtypeStruct(shape, BF) for shape in shapes],
         compiler_params=params(60),
         cost_estimate=cost(2 * count * dim * cols, 2 * count * (2 * dim + cols)),
         name="last",
-    )(info, weight, *rights)
+    )(info, weight, right)
 
 
 def end_kernel(ga, gb, gc, x, resid_grad, vecs, out):
@@ -992,27 +1015,33 @@
         held[nb - t] = ring.ahead(held[(nb - t + 1) % nb])
 
     if live:
-        x, cot, one = tie(x, cot, one)
+        cot, one = tie(cot, one)
         ones = {0: one}
         step(ones, 1)
-        xs = {0: x, 1: lax.ppermute(x, "seq", pairs(ns, 1)), 2: lax.ppermute(x, "seq", pairs(ns, 2))}
+        half = tok // 2
+        near = lax.ppermute(x, "seq", pairs(ns, 1))
+        far_a = lax.ppermute(x[:half], "seq", pairs(ns, 2))
         expand_weight, shrink_weight, _ = tie(expand_weight, shrink_weight, one)
         two = second_pack(seat, expand_weight, shrink_weight, nb, ns)
-        ones[1], ones[7], two, xs[1], cot = tie(ones[1], ones[7], two, xs[1], cot)
+        ones[1], ones[7], two, near, cot, x = tie(ones[1], ones[7], two, near, cot, x)
         step(ones, 2)
+        far_b = lax.ppermute(x[half:], "seq", pairs(ns, 2))
         cots = {0: cot, 1: lax.ppermute(cot, "seq", pairs(ns, 1))}
-        ones[2], ones[6], cots[1], xs[2], cot = tie(ones[2], ones[6], cots[1], xs[2], cot)
+        ones[2], ones[6], cots[1], far_a, cot = tie(ones[2], ones[6], cots[1], far_a, cot)
         step(ones, 3)
-        xs[3] = lax.ppermute(xs[2], "seq", pairs(ns, 1))
+        far_c = lax.ppermute(far_a, "seq", pairs(ns, 1))
+        ones[3], ones[5], far_b, far_c, cot = tie(ones[3], ones[5], far_b, far_c, cot)
+        step(ones, 4)
+        far_d = lax.ppermute(far_b, "seq", pairs(ns, 1))
         cots[2] = lax.ppermute(cot, "seq", pairs(ns, 2))
-        ones[3], ones[5], xs[3] = tie(ones[3], ones[5], xs[3])
-        step(ones, 4)
+        xs = [x, near, far_a, far_b, far_c, far_d]
         ones[4], two = tie(ones[4], two)
         twos = {0: two}
         step(twos, 1)
         one_parts = [ones[slot][None] for slot in range(nb)]
     else:
         xs = gather_rel(x, "seq", ns)
+        xs = [xs[rel] for rel in range(ns)]
         cots = gather_rel(cot, "seq", ns)
         one_parts = [lax.all_gather(one, "batch")]
         low = one_parts[0][:, rows + 2 : rows + 4, :rows].astype(F32).reshape(2 * dim)
@@ -1020,67 +1049,55 @@
         jbias = jnp.stack([low[:, 0], jnp.zeros_like(low[:, 0]), low[:, 1]], 1).reshape(1, cols)
 
     normed, joined, joined_full, outw_own, vecs = first_call(
-        info, jbias, [xs[rel] for rel in range(ns)], one_parts, cols, live
+        info, jbias, xs, one_parts, cols, live, ns
     )
     if live:
-        joined, twos[1], twos[7], cots[2] = tie(joined, twos[1], twos[7], cots[2])
+        joined, twos[1], twos[7] = tie(joined, twos[1], twos[7])
         step(twos, 2)
-        cots[3] = lax.ppermute(cots[2], "seq", pairs(ns, 1))
-    if units == rows:
-        ebias = lax.dynamic_slice(vecs, (7 + si, 0), (1, dim))
+    if live:
+        ebias = vecs
     else:
         ebias = vecs[7:11].reshape(4, nb, rows).transpose(1, 0, 2).reshape(nb, ns, units)
         ebias = lax.dynamic_slice(ebias, (0, si, 0), (nb, 1, units)).reshape(1, ff)
     outw_all = gather_rel(outw_own, "seq", ns)
-    mixed = []
-    log_sums = []
-    merged_parts = []
-
-    def to_tokens(out):
-        parts = []
-        for rel in range(ns):
-            block = lax.dynamic_slice(out, ((si ^ rel) * tok, 0), (tok, 2 * HD))
-            parts.append(lax.ppermute(block, "seq", pairs(ns, rel)) if rel else block)
-        return parts
-
+    attended = None
     for pair in range(np):
-        out, logs = attend(joined, info, slopes, pair)
+        attended = attend(joined, info, slopes, pair, attended)
         if live and pair == 0:
-            out, joined, twos[2], twos[6], cots[3], outw_all[2], outw_all[1] = tie(
-                out, joined, twos[2], twos[6], cots[3], outw_all[2], outw_all[1]
+            out, joined, twos[2], twos[6], outw_all[1], outw_all[2], cots[2] = tie(
+                attended[0], joined, twos[2], twos[6], outw_all[1], outw_all[2], cots[2]
             )
+            attended = (out, attended[1])
             step(twos, 3)
             outw_all[3] = lax.ppermute(outw_all[2], "seq", pairs(ns, 1))
-        mixed.append(out)
-        log_sums.append(logs)
-        merged_parts.append(to_tokens(out))
-        if live and pair == 1:
-            out, twos[3], twos[5], outw_all[3], *merged_parts[0] = tie(
-                out, twos[3], twos[5], outw_all[3], *merged_parts[0]
-            )
-            step(twos, 4)
-            mixed[1] = out
-            merged_parts[1] = to_tokens(out)
-    merged_parts = [block for parts in merged_parts for block in parts]
+    mixed, log_sums = attended
+    if live:
+        mixed, twos[3], twos[5], outw_all[3], cots[2] = tie(mixed, twos[3], twos[5], outw_all[3], cots[2])
+        step(twos, 4)
+        cots[3] = lax.ppermute(cots[2], "seq", pairs(ns, 1))
+    merged_parts = []
+    for rel in range(ns):
+        block = lax.dynamic_slice(mixed, ((si ^ rel) * tok, 0), (tok, cw))
+        merged_parts.append(lax.ppermute(block, "seq", pairs(ns, rel)) if rel else block)
+    if live:
+        cots[3], twos[4], *merged_parts = tie(cots[3], twos[4], *merged_parts)
     merged, resid, second, outw_full = middle_call(
         info, x, vecs, merged_parts, [outw_all[rel] for rel in range(ns)]
     )
-    if not live:
-        expand_part = expand_weight.reshape(rows, nb, ns, units)
-        expand_part = lax.dynamic_slice(expand_part, (0, 0, si, 0), (rows, nb, 1, units)).reshape(rows, ff)
-        shrink_part = lax.dynamic_slice(shrink_weight, (si * units, 0), (units, dim))
-        two_parts = [lax.all_gather(expand_part, "batch"), lax.all_gather(shrink_part, "batch")]
     out_parts = {}
     back_parts = {}
     activs = []
     pre_grads = []
     bias_sums = []
     if live:
-        second, twos[4] = tie(second, twos[4])
+        seconds = {0: second, 2: lax.ppermute(second, "seq", pairs(ns, 2)), 1: lax.ppermute(second, "seq", pairs(ns, 1))}
         two_parts = [twos[slot][None] for slot in range(nb)]
-        seconds = {0: second, 2: lax.ppermute(second, "seq", pairs(ns, 2)), 1: lax.ppermute(second, "seq", pairs(ns, 1))}
     else:
         seconds = gather_rel(second, "seq", ns)
+        expand_part = expand_weight.reshape(rows, nb, ns, units)
+        expand_part = lax.dynamic_slice(expand_part, (0, 0, si, 0), (rows, nb, 1, units)).reshape(rows, ff)
+        shrink_part = lax.dynamic_slice(shrink_weight, (si * units, 0), (units, dim))
+        two_parts = [lax.all_gather(expand_part, "batch"), lax.all_gather(shrink_part, "batch")]
     for rel in range(0, ns, 2):
         activ, pre_grad, oa, ob, ba, bb, bgrad = feed_call(
             info, seconds[rel], seconds[rel + 1], cots[rel], cots[rel + 1], ebias, two_parts, rows, units, nb, live
@@ -1146,13 +1163,13 @@
         feed_ring = Scatter(feed_stack)
         feed_ring.send()
         back_b, far_out, _ = tie(back_b, far_out, feed_stack[0])
+        out_b = add16(out_parts[2], far_out)
+        back_b, out_b = tie(back_b, out_b)
         back_terms = (back_parts[0], near_back, back_b)
-        out_b = add16(out_parts[2], far_out)
     resid_grad, branch, *mixed_grads, turn_sums = turn_call(
         info, back_terms, resid, cot, vecs, outw_full, ns, 1
     )
     outw_parts = split_grad(info, merged, branch, ns)
-    joined_grads = []
     sides = []
 
     grads = [
@@ -1161,34 +1178,33 @@
     if live:
         grads[0], *outw_parts = tie(grads[0], *outw_parts)
         grads = feed_ring.take(*grads)
-        *grads, feed_ring.ahead, outw_near = tie(*grads, feed_ring.ahead, outw_parts[2])
+        *grads, feed_ring.ahead, outw_near, out_b = tie(*grads, feed_ring.ahead, outw_parts[2], out_b)
+        out_b = lax.ppermute(out_b, "seq", pairs(ns, 2))
         feed_ring.send()
         outw_near = lax.ppermute(outw_near, "seq", pairs(ns, 1))
+    joined_grad = None
     for pair in range(np):
-        out, side = attend_back(joined, grads, mixed[pair], log_sums[pair], info, slopes, pair)
-        joined_grads.append(out)
+        joined_grad, side = attend_back(joined, grads, mixed, log_sums, info, slopes, pair, joined_grad)
         sides.append(side)
         if live and pair == 0:
-            out, outw_near = feed_ring.take(out, outw_near)
+            joined_grad, outw_near = feed_ring.take(joined_grad, outw_near)
             outw_far = add16(outw_parts[1], outw_near[1])
-            out, joined, feed_ring.ahead, feed_ring.back, outw_far = tie(
-                out, joined, feed_ring.ahead, feed_ring.back, outw_far
+            joined_grad, joined, feed_ring.ahead, feed_ring.back, outw_far = tie(
+                joined_grad, joined, feed_ring.ahead, feed_ring.back, outw_far
             )
-            joined_grads[0] = out
             feed_ring.send()
             outw_far = lax.ppermute(outw_far, "seq", pairs(ns, 2))
         elif live:
-            joined_grads[1], outw_far = feed_ring.take(out, outw_far)
+            joined_grad, outw_far, out_b = feed_ring.take(joined_grad, outw_far, out_b)
 
     if live:
         shares = None
         outw_share = outw_parts[0].astype(F32) + outw_near[0].astype(F32) + outw_far.astype(F32)
         outw_share = outw_share.astype(BF)
-        joined_grads[1], outw_share, feed_ring.ahead, feed_ring.back, out_b = tie(
-            joined_grads[1], outw_share, feed_ring.ahead, feed_ring.back, out_b
+        joined_grad, outw_share, feed_ring.ahead, feed_ring.back = tie(
+            joined_grad, outw_share, feed_ring.ahead, feed_ring.back
         )
         feed_ring.send()
-        out_b = lax.ppermute(out_b, "seq", pairs(ns, 2))
     else:
         spread_bias = lax.dynamic_update_slice(
             jnp.zeros((nb, ns, units), F32), sum(bias_sums).reshape(nb, 1, units), (0, si, 0)
@@ -1203,49 +1219,50 @@
         shares = jnp.concatenate(shares, 0)
         outw_share = scatter_rel(dict(enumerate(outw_parts)), "seq", ns)
     joined_stack = joined_grad_call(
-        info, normed, joined_grads, sides, outw_share, joined_full, vecs, shares, turn_sums, bias_sums, nb, live
+        info, normed, joined_grad, sides, outw_share, joined_full, vecs, shares, turn_sums, bias_sums, nb, live
     )
     if live:
         feed_share, *joined_stack = feed_ring.take(*joined_stack)
         feed_share, *joined_stack = tie(feed_share, *joined_stack)
+        feed_parts = {0: feed_share, 2: lax.ppermute(feed_share, "seq", pairs(ns, 2))}
         joined_ring = Scatter(joined_stack)
         joined_ring.send()
-        joined_grads[0], _ = tie(joined_grads[0], joined_stack[0])
-    normed_parts = last_call(info, joined_grads, joined_full, ns)
+        joined_grad, _ = tie(joined_grad, joined_stack[0])
+    normed_parts = last_call(info, joined_grad, joined_full, ns)
 
     def ordered(block):
         parts = gather_rel(block, "seq", ns)
         return [parts[rel] for rel in range(ns)]
 
     if live:
-        sent, out_b = joined_ring.take(normed_parts[2], out_b)
-        joined_ring.ahead, out_b, feed_share, sent = tie(joined_ring.ahead, out_b, feed_share, sent)
+        sent, feed_parts[2] = joined_ring.take(normed_parts[2], feed_parts[2])
+        joined_ring.ahead, sent = tie(joined_ring.ahead, sent)
         joined_ring.send()
         got = lax.ppermute(sent, "seq", pairs(ns, 1))
-        feed_parts = {0: feed_share, 2: lax.ppermute(feed_share, "seq", pairs(ns, 2))}
+        far = add16(normed_parts[1], got[1])
+        (far,) = joined_ring.take(far)
+        joined_ring.ahead, joined_ring.back, far = tie(joined_ring.ahead, joined_ring.back, far)
+        joined_ring.send()
+        norm_b = lax.ppermute(far, "seq", pairs(ns, 2))
+        out_b, out_parts[0], _ = tie(out_b, out_parts[0], far)
         out_terms = out_parts[0].astype(F32) + near_out.astype(F32) + out_b.astype(F32)
         layer_output = (resid + out_terms + vecs[11:12]).astype(BF)
-        got, feed_parts[2] = joined_ring.take(got, feed_parts[2])
-        far = add16(normed_parts[1], got[1])
-        joined_ring.ahead, joined_ring.back, far, feed_parts[0], feed_parts[2] = tie(
-            joined_ring.ahead, joined_ring.back, far, feed_parts[0], feed_parts[2]
+        layer_output, feed_parts[0], feed_parts[2] = joined_ring.take(layer_output, feed_parts[0], feed_parts[2])
+        joined_ring.ahead, joined_ring.back, feed_parts[0], feed_parts[2] = tie(
+            joined_ring.ahead, joined_ring.back, feed_parts[0], feed_parts[2]
         )
         joined_ring.send()
-        norm_b = lax.ppermute(far, "seq", pairs(ns, 2))
         feed_parts[1] = lax.ppermute(feed_parts[0], "seq", pairs(ns, 1))
-        feed_parts[1], feed_parts[2], layer_output = joined_ring.take(feed_parts[1], feed_parts[2], layer_output)
-        joined_ring.ahead, joined_ring.back, feed_parts[1], feed_parts[2] = tie(
-            joined_ring.ahead, joined_ring.back, feed_parts[1], feed_parts[2]
-        )
-        joined_ring.send()
         feed_parts[3] = lax.ppermute(feed_parts[2], "seq", pairs(ns, 1))
-        expand_grad, shrink_grad = feed_out(info, [feed_parts[rel] for rel in range(ns)], nb, rows)
-        joined_share, norm_b, expand_grad, shrink_grad = joined_ring.take(norm_b, expand_grad, shrink_grad)
-        joined_share, norm_b = tie(joined_share, norm_b)
+        joined_share, norm_b, feed_parts[1], feed_parts[3] = joined_ring.take(norm_b, feed_parts[1], feed_parts[3])
+        joined_share, norm_b, feed_parts[1] = tie(joined_share, norm_b, feed_parts[1])
         joined_parts = {0: joined_share, 2: lax.ppermute(joined_share, "seq", pairs(ns, 2))}
         joined_parts[1] = lax.ppermute(joined_share, "seq", pairs(ns, 1))
+        expand_grad, shrink_grad = feed_out(info, [feed_parts[rel] for rel in range(ns)], nb, rows)
         input_grad = end_call((normed_parts[0], got, norm_b), x, resid_grad, vecs)
-        joined_parts[2], joined_parts[1], input_grad = tie(joined_parts[2], joined_parts[1], input_grad)
+        joined_parts[2], joined_parts[1], input_grad, expand_grad, shrink_grad = tie(
+            joined_parts[2], joined_parts[1], input_grad, expand_grad, shrink_grad
+        )
         joined_parts[3] = lax.ppermute(joined_parts[2], "seq", pairs(ns, 1))
         joined_parts = [joined_parts[rel] for rel in range(ns)]
     else:

time: 376 us -> 362 us (0.963)
  local copies, waits for them, and re-layouts: 14.8 us -> 8.02 us
  Pallas kernels: 187 us -> 183 us
    ppermute x3 -> x6, waiting for transfers between devices: 6.36 us -> 18.4 us  [body(): lax.ppermute(block, 'seq', pairs(ns, rel))]
    ppermute x9 -> x5, starting transfers between devices: 8 us -> 2.75 us  [the longest x1 1.58 us: body(): far_a = lax.ppermute(x[:half], 'seq', pairs(ns, 2))]
    ppermute x9 -> x5, waiting for transfers between devices: 23.7 us -> 19.3 us  [the longest x1 10.6 us: body(): far_a = lax.ppermute(x[:half], 'seq', pairs(ns, 2))]
    ppermute x12, waiting for transfers between devices: 16.8 us -> 12.5 us  [back(): return lax.ppermute(value, 'batch', self.backward)]
    ppermute x1, waiting for transfers between devices: 4.21 us -> 0.01 us  [body(): lax.ppermute(feed_share, 'seq', pairs(ns, 2))]
    unnamed x126, local copies, waits for them, and re-layouts: 9.91 us -> 5.99 us
    ppermute x12, starting transfers between devices: 10.3 us -> 14.1 us  [back(): return lax.ppermute(value, 'batch', self.backward)]
    pallas_call x7, Pallas kernels: 98.4 us -> 94.6 us  [the longest x2 39.5 us: attend_back(): pl.pallas_call(kernel, grid=(1,), in_specs=[smem, smem, wide, narrow, nar...]
  transfers between devices with their start and end apart: 65 -> 64, of which waited for: 27 -> 25; matrix products, arithmetic and copies ran while one was open for 3% -> 4% of each run, Pallas kernels for 49% -> 48%
where the time goes in v4:
time: 362 us; the launch traced here: 356 us
  Pallas kernels  183 us (51%)
  waiting for transfers between devices  96.5 us (27%)
  starting transfers between devices  50.6 us (14%)
  other arithmetic  16 us (4%)
  local copies, waits for them, and re-layouts  8.02 us (2%)
    pallas_call x2, Pallas kernels, attend_back(): pl.pallas_call(kernel, grid=(1,), in_specs=[smem, smem, wide, narrow, nar...  39.5 us
    pallas_call x2, Pallas kernels, feed_call(): pl.pallas_call(functools.partial(feed_kernel, nt, nb, rows, units, live),...  32.4 us
    pallas_call x2, Pallas kernels, attend(): pl.pallas_call(kernel, grid=(1,), in_specs=[smem, smem, pl.BlockSpec((cou...  22.4 us
    ppermute x16, waiting for transfers between devices, ahead(): return lax.ppermute(value, 'batch', self.forward)  19.2 us
    pallas_call x1, Pallas kernels, feed_grad_call(): pl.pallas_call(functools.partial(feed_grad_kernel, ns, nb, rows, units, s...  19.1 us
    ppermute x6, waiting for transfers between devices, body(): lax.ppermute(block, 'seq', pairs(ns, rel))  18.4 us
    ppermute x16, starting transfers between devices, ahead(): return lax.ppermute(value, 'batch', self.forward)  16.5 us
    ppermute x12, starting transfers between devices, back(): return lax.ppermute(value, 'batch', self.backward)  14.1 us
  transfers between devices with their start and end apart: 64, of which 25 were waited for; matrix products, arithmetic and copies ran while one was open for 4% of the time, Pallas kernels for 48%

profile of v4, /device:TPU:0, one launch (start us, length us, event | category | flops | bytes accessed | tf_op | source)
XLA Modules:
  0.0 356.3 jit_solution(552373339751357040)
XLA Ops:
  1.2 1.8 first_pack.1
  3.0 2.6 collective-permute-start
  5.7 2.2 second_pack.1
  7.9 5.6 %collective-permute-done = bf16[144,1024]{1,0:T(8,128)(2,1)S(1)} collective-permute-done((bf16[144,1024]{1,0:T(8,128)(2,1)}, bf16[144,1024]{1,0:T(8,128)(2,1)S(1)}, u32[]{:S(2)}, u32[]{:S(2)}) %collective-permute-start) | collective-permute-done | bytes 294944 | tf_op jit(solution)/shard_map/ppermute | solution.py:119
  19.2 10.6 %collective-permute-done.6.refs_2_ = bf16[256,1024]{1,0:T(8,128)(2,1)S(1)} collective-permute-done((bf16[256,1024]{1,0:T(8,128)(2,1)S(1)}, bf16[256,1024]{1,0:T(8,128)(2,1)S(1)}, u32[]{:S(2)}, u32[]{:S(2)}) %collective-permute-start.6) | collective-permute-done | bytes 524320 | tf_op jit(solution)/shard_map/ppermute | solution.py:1023
  29.8 1.6 collective-permute-start.7
  31.9 8.7 %collective-permute-done.9.refs_3_ = bf16[256,1024]{1,0:T(8,128)(2,1)} collective-permute-done((bf16[256,1024]{1,0:T(8,128)(2,1)S(1)}, bf16[256,1024]{1,0:T(8,128)(2,1)}, u32[]{:S(2)}, u32[]{:S(2)}) %collective-permute-start.9) | collective-permute-done | bytes 524320 | tf_op jit(solution)/shard_map/ppermute | solution.py:1028
  41.1 8.2 %collective-permute-done.12 = bf16[144,1024]{1,0:T(8,128)(2,1)S(1)} collective-permute-done((bf16[144,1024]{1,0:T(8,128)(2,1)S(1)}, bf16[144,1024]{1,0:T(8,128)(2,1)S(1)}, u32[]{:S(2)}, u32[]{:S(2)}) %collective-permute-start.12) | collective-permute-done | bytes 294944 | tf_op jit(solution)/shard_map/ppermute | solution.py:116
  54.4 13.3 %first.1 = (bf16[2048,1024]{1,0:T(8,128)(2,1)}, bf16[2048,768]{1,0:T(8,128)(2,1)}, bf16[1024,768]{1,0:T(8,128)(2,1)}, bf16[1024,256]{1,0:T(8,128)(2,1)}, f32[16,1024]{1,0:T(8,128)}) custom-call(s32[18]{0:T(128)} %pad_add_fusion.info.refs_0_, bf16[512,1024]{1,0:T(8,128)(2,1)} %bitcast.76, bf16[512,1024]{1,0:T(8,128)(2,1)} %collective-permute-done.2.refs_1_, ...), custom_call_target="tpu_custom_call" | custom-call | flops 3221225 | bytes 11534 | tf_op jit(solution)/shard_map/first/pallas_call | solution.py:264
  71.4 11.2 %attend.2 = (bf16[2048,256]{1,0:T(8,128)(2,1)}, f32[2048,256]{1,0:T(8,128)}) custom-call(s32[18]{0:T(128)} %pad_add_fusion.info.refs_0_, f32[4]{0:T(128)} %multiply_power_fusion.refs_1_, bf16[2048,768]{1,0:T(8,128)(2,1)} %get-tuple-element.357.refs_2_), custom_call_target="tpu_custom_call" | custom-call | flops 4294967 | bytes 2621 | tf_op jit(solution)/shard_map/attend/pallas_call | solution.py:362
  82.6 3.6 %collective-permute-done.18.refs_6_ = bf16[1024,256]{1,0:T(8,128)(2,1)} collective-permute-done((bf16[1024,256]{1,0:T(8,128)(2,1)}, bf16[1024,256]{1,0:T(8,128)(2,1)}, u32[]{:S(2)}, u32[]{:S(2)}) %collective-permute-start.18) | collective-permute-done | bytes 524320 | tf_op jit(solution)/shard_map/ppermute | solution.py:73
  86.2 1.6 collective-permute-start.20
  88.5 11.2 %attend.3 = (bf16[2048,256]{1,0:T(8,128)(2,1)}, f32[2048,256]{1,0:T(8,128)}) custom-call(s32[18]{0:T(128)} %pad_add_fusion.info.refs_0_, f32[4]{0:T(128)} %multiply_power_fusion.refs_1_, bf16[2048,768]{1,0:T(8,128)(2,1)} %get-tuple-element.357.refs_2_, bf16[2048,256]{1,0:T(8,128)(2,1)} %get-tuple-element.270.refs_3_, ...), custom_call_target="tpu_custom_call", output_to_operand_aliasing={{0}: (3, {}), {1}: (4, {})} | custom-call | flops 4294967 | bytes 2621 | tf_op jit(solution)/shard_map/attend/pallas_call | solution.py:362
  102.9 2.0 constant_dynamic-slice_fusion
  106.7 7.2 %collective-permute-done.26.refs_2_ = bf16[512,256]{1,0:T(8,128)(2,1)S(1)} collective-permute-done((bf16[512,256]{1,0:T(8,128)(2,1)S(1)}, bf16[512,256]{1,0:T(8,128)(2,1)S(1)}, u32[]{:S(2)}, u32[]{:S(2)}) %collective-permute-start.26) | collective-permute-done | bytes 262176 | tf_op jit(solution)/shard_map/ppermute | solution.py:1081
  114.0 4.8 %collective-permute-done.27.refs_3_ = bf16[512,256]{1,0:T(8,128)(2,1)S(1)} collective-permute-done((bf16[512,256]{1,0:T(8,128)(2,1)S(1)}, bf16[512,256]{1,0:T(8,128)(2,1)S(1)}, u32[]{:S(2)}, u32[]{:S(2)}) %collective-permute-start.27) | collective-permute-done | bytes 262176 | tf_op jit(solution)/shard_map/ppermute | solution.py:1081
  119.5 7.3 %middle.1 = (bf16[512,1024]{1,0:T(8,128)(2,1)}, f32[512,1024]{1,0:T(8,128)}, bf16[512,1024]{1,0:T(8,128)(2,1)}, bf16[1024,1024]{1,0:T(8,128)(2,1)}) custom-call(s32[18]{0:T(128)} %pad_add_fusion.info.refs_0_, bf16[512,1024]{1,0:T(8,128)(2,1)} %bitcast.77, f32[16,1024]{1,0:T(8,128)} %get-tuple-element.260.vecs.ebias, ...), custom_call_target="tpu_custom_call" | custom-call | flops 1073741 | bytes 10485 | tf_op jit(solution)/shard_map/middle/pallas_call | solution.py:489
  130.8 16.2 %feed.2 = (bf16[1024,1024]{1,0:T(8,128)(2,1)}, bf16[1024,1024]{1,0:T(8,128)(2,1)}, bf16[512,1024]{1,0:T(8,128)(2,1)}, bf16[512,1024]{1,0:T(8,128)(2,1)}, bf16[51...) custom-call(s32[18]{0:T(128)} %pad_add_fusion.info.refs_0_, ...), custom_call_target="tpu_custom_call" | custom-call | flops 8589934 | bytes 16777 | tf_op jit(solution)/shard_map/feed/pallas_call | solution.py:568
  146.9 5.8 %collective-permute-done.29.sa.refs_8_ = bf16[512,1024]{1,0:T(8,128)(2,1)S(1)} collective-permute-done((bf16[512,1024]{1,0:T(8,128)(2,1)}, bf16[512,1024]{1,0:T(8,128)(2,1)S(1)}, u32[]{:S(2)}, u32[]{:S(2)}) %collective-permute-start.29) | collective-permute-done | bytes 1048608 | tf_op jit(solution)/shard_map/ppermute | solution.py:1093
  153.2 3.6 %collective-permute-done.30.sb.refs_9_ = bf16[512,1024]{1,0:T(8,128)(2,1)S(1)} collective-permute-done((bf16[512,1024]{1,0:T(8,128)(2,1)S(1)}, bf16[512,1024]{1,0:T(8,128)(2,1)S(1)}, u32[]{:S(2)}, u32[]{:S(2)}) %collective-permute-start.30) | collective-permute-done | bytes 1048608 | tf_op jit(solution)/shard_map/ppermute | solution.py:1107
  157.8 16.3 %feed.3 = (bf16[1024,1024]{1,0:T(8,128)(2,1)}, bf16[1024,1024]{1,0:T(8,128)(2,1)}, bf16[512,1024]{1,0:T(8,128)(2,1)}, bf16[512,1024]{1,0:T(8,128)(2,1)}, bf16[51...) custom-call(s32[18]{0:T(128)} %pad_add_fusion.info.refs_0_, bf16[512,1024]{1,0:T(8,128)(2,1)} %copy-done.19, ...), custom_call_target="tpu_custom_call" | custom-call | flops 8589934 | bytes 16777 | tf_op jit(solution)/shard_map/feed/pallas_call | solution.py:568
  174.3 2.7 collective-permute-done.34
  177.1 2.6 add_convert_fusion.2
  181.2 19.1 %feed_grad.1 = (bf16[1,256,1024]{2,1,0:T(8,128)(2,1)}, bf16[1,256,1024]{2,1,0:T(8,128)(2,1)}, bf16[1,256,1024]{2,1,0:T(8,128)(2,1)}, bf16[1,256,1024]{2,1,0:T(8,...) custom-call(s32[18]{0:T(128)} %pad_add_fusion.info.refs_0_, ...), custom_call_target="tpu_custom_call" | custom-call | flops 8589934 | bytes 20971 | tf_op jit(solution)/shard_map/feed_grad/pallas_call | solution.py:637
  200.3 1.6 collective-permute-start.31
  201.9 3.2 collective-permute-done.35.gc
  205.1 3.0 add_convert_fusion.1
  208.1 8.0 %turn.1 = (f32[512,1024]{1,0:T(8,128)}, bf16[512,1024]{1,0:T(8,128)(2,1)}, bf16[512,256]{1,0:T(8,128)(2,1)}, bf16[512,256]{1,0:T(8,128)(2,1)}, bf16[512,256]{1,0...) custom-call(s32[18]{0:T(128)} %pad_add_fusion.info.refs_0_, bf16[512,1024]{1,0:T(8,128)(2,1)} %get-tuple-element.303.ga, ...), custom_call_target="tpu_custom_call" | custom-call | flops 1073741 | bytes 10485 | tf_op jit(solution)/shard_map/turn/pallas_call | solution.py:794
  218.0 5.9 %split_grad.1 = (bf16[1024,256]{1,0:T(8,128)(2,1)}, bf16[1024,256]{1,0:T(8,128)(2,1)}, bf16[2,1024,256]{2,1,0:T(8,128)(2,1)}) custom-call(s32[18]{0:T(128)} %pad_add_fusion.info.refs_0_, bf16[512,1024]{1,0:T(8,128)(2,1)} %get-tuple-element.320.left, bf16[512,1024]{1,0:T(8,128)(2,1)} %get-tuple-element.321.right), custom_call_target="tpu_custom_call" | custom-call | flops 1073741 | bytes 6291 | tf_op jit(solution)/shard_map/split_grad/pallas_call | solution.py:683
  223.9 1.6 collective-permute-done.38.refs_7_
  225.6 4.7 %collective-permute-done.39.refs_8_ = bf16[512,256]{1,0:T(8,128)(2,1)S(1)} collective-permute-done((bf16[512,256]{1,0:T(8,128)(2,1)}, bf16[512,256]{1,0:T(8,128)(2,1)S(1)}, u32[]{:S(2)}, u32[]{:S(2)}) %collective-permute-start.39) | collective-permute-done | bytes 262176 | tf_op jit(solution)/shard_map/ppermute | solution.py:1176
  234.4 20.0 %attend_back.2 = (bf16[2048,768]{1,0:T(8,128)(2,1)}, f32[1,384]{1,0:T(1,128)}) custom-call(s32[18]{0:T(128)} %pad_add_fusion.info.refs_0_, f32[4]{0:T(128)} %multiply_power_fusion.refs_1_, bf16[2048,768]{1,0:T(8,128)(2,1)} %get-tuple-element.357.refs_2_, bf16[2048,256]{1,0:T(8,128)(2,1)} %get-tuple-element.279.refs_3_, ...), custom_call_target="tpu_custom_call" | custom-call | flops 10737418 | bytes 5242 | tf_op jit(solution)/shard_map/attend_back/pallas_call | solution.py:446
  256.6 1.6 collective-permute-start.43
  259.2 19.5 %attend_back.3 = (bf16[2048,768]{1,0:T(8,128)(2,1)}, f32[1,384]{1,0:T(1,128)}) custom-call(s32[18]{0:T(128)} %pad_add_fusion.info.refs_0_, f32[4]{0:T(128)} %multiply_power_fusion.refs_1_, bf16[2048,768]{1,0:T(8,128)(2,1)} %get-tuple-element.357.refs_2_, bf16[2048,256]{1,0:T(8,128)(2,1)} %get-tuple-element.279.refs_3_, ...), custom_call_target="tpu_custom_call", output_to_operand_aliasing={{0}: (9, {})} | custom-call | flops 10737418 | bytes 5242 | tf_op jit(solution)/shard_map/attend_back/pallas_call | solution.py:446
  278.7 2.1 fusion.2.other
  281.1 1.6 collective-permute-start.47
  283.2 10.5 %joined_grad.1 = (bf16[1,144,1024]{2,1,0:T(8,128)(2,1)}, bf16[1,144,1024]{2,1,0:T(8,128)(2,1)}, bf16[1,144,1024]{2,1,0:T(8,128)(2,1)}, bf16[1,144,1024]{2,1,0:T(...) custom-call(s32[18]{0:T(128)} %pad_add_fusion.info.refs_0_, ...), custom_call_target="tpu_custom_call" | custom-call | flops 3221225 | bytes 11534 | tf_op jit(solution)/shard_map/joined_grad/pallas_call | solution.py:748
  298.3 8.9 %last.1 = (bf16[512,1024]{1,0:T(8,128)(2,1)}, bf16[512,1024]{1,0:T(8,128)(2,1)}, bf16[2,512,1024]{2,1,0:T(8,128)(2,1)}) custom-call(s32[18]{0:T(128)} %pad_add_fusion.info.refs_0_, bf16[1024,768]{1,0:T(8,128)(2,1)} %get-tuple-element.375.weight, bf16[2048,768]{1,0:T(8,128)(2,1)} %get-tuple-element.405.refs_3_.right), custom_call_target="tpu_custom_call" | custom-call | flops 3221225 | bytes 11534 | tf_op jit(solution)/shard_map/last/pallas_call | solution.py:838
  309.5 2.3 collective-permute-done.53.gb
  311.8 1.8 fusion
  313.5 3.3 collective-permute-done.52.refs_3_
  320.0 3.5 add_convert_fusion
  323.5 2.5 collective-permute-done.54.refs_2_
  330.1 7.0 %collective-permute-done.56 = bf16[144,1024]{1,0:T(8,128)(2,1)S(1)} collective-permute-done((bf16[144,1024]{1,0:T(8,128)(2,1)S(1)}, bf16[144,1024]{1,0:T(8,128)(2,1)S(1)}, u32[]{:S(2)}, u32[]{:S(2)}) %collective-permute-start.56) | collective-permute-done | bytes 294944 | tf_op jit(solution)/shard_map/ppermute | solution.py:116
  338.3 3.5 collective-permute-done.58.gc
  342.6 3.0 end.1
  345.6 4.6 %feed_out.1 = (f32[128,4096]{1,0:T(8,128)}, f32[512,1024]{1,0:T(8,128)}) custom-call(s32[18]{0:T(128)} %pad_add_fusion.info.refs_0_, bf16[256,1024]{1,0:T(8,128)(2,1)} %copy-done.26, bf16[256,1024]{1,0:T(8,128)(2,1)} %copy-done.39, bf16[256,1024]{1,0:T(8,128)(2,1)} %copy-done.35, bf16[256,1024]{1,0:T(8,128)(2,1)} %copy-done.40), custom_call_target="tpu_custom_call" | custom-call | bytes 6291 | tf_op jit(solution)/shard_map/feed_out/pallas_call | solution.py:953
  352.7 3.4 joined_out.1
  (245 shorter events, 57.3 us)
Async XLA Ops:
  0.7 14.1 %collective-permute-start.2 = (bf16[512,1024]{1,0:T(8,128)(2,1)}, bf16[512,1024]{1,0:T(8,128)(2,1)}, u32[]{:S(2)}, u32[]{:S(2)}) collective-permute-start(bf16[512,1024]{1,0:T(8,128)(2,1)} %bitcast.75), channel_id=1, source_target_pairs={{0,8},{8,0},{16,24},{24,16},{1,9},{9,1},{17,25},{25,17},{2,10},{10... | collective-permute-start | bytes 3145736 | tf_op jit(solution)/shard_map/ppermute | solution.py:1022
  3.0 10.5 %collective-permute-start = (bf16[144,1024]{1,0:T(8,128)(2,1)}, bf16[144,1024]{1,0:T(8,128)(2,1)S(1)}, u32[]{:S(2)}, u32[]{:S(2)}) collective-permute-start(bf16[144,1024]{1,0:T(8,128)(2,1)} %first_pack.1), channel_id=1, source_target_pairs={{2,0},{4,2},{6,4},{7,6},{5,7},{3,5},{1,3},{0,1},{10,8},{12,10},{14... | collective-permute-start | bytes 884744 | tf_op jit(solution)/shard_map/ppermute | solution.py:119
  5.6 9.2 %collective-permute-start.1 = (bf16[144,1024]{1,0:T(8,128)(2,1)}, bf16[144,1024]{1,0:T(8,128)(2,1)S(1)}, u32[]{:S(2)}, u32[]{:S(2)}) collective-permute-start(bf16[144,1024]{1,0:T(8,128)(2,1)} %first_pack.1), channel_id=1, source_target_pairs={{0,2},{2,4},{4,6},{6,7},{7,5},{5,3},{3,1},{1,0},{8,10},{10,12},{12... | collective-permute-start | bytes 884744 | tf_op jit(solution)/shard_map/ppermute | solution.py:116
  14.8 14.9 %collective-permute-start.5 = (bf16[512,1024]{1,0:T(8,128)(2,1)S(1)}, bf16[512,1024]{1,0:T(8,128)(2,1)S(1)}, u32[]{:S(2)}, u32[]{:S(2)}) collective-permute-start(bf16[512,1024]{1,0:T(8,128)(2,1)S(1)} %bitcast.91), channel_id=1, source_target_pairs={{0,8},{8,0},{16,24},{24,16},{1,9},{9,1},{17,25},{25,17},{2,10},{10... | collective-permute-start | bytes 3145736 | tf_op jit(solution)/shard_map/ppermute | solution.py:1029
  14.9 14.8 %collective-permute-start.6 = (bf16[256,1024]{1,0:T(8,128)(2,1)S(1)}, bf16[256,1024]{1,0:T(8,128)(2,1)S(1)}, u32[]{:S(2)}, u32[]{:S(2)}) collective-permute-start(bf16[256,1024]{1,0:T(8,128)(2,1)S(1)} %slice_bitcast_fusion.1), channel_id=1, source_target_pairs={{0,16},{8,24},{16,0},{24,8},{1,17},{9,25},{17,1},{25,9},{2,18},{10... | collective-permute-start | bytes 1572872 | tf_op jit(solution)/shard_map/ppermute | solution.py:1023
  16.5 13.2 %collective-permute-start.3 = (bf16[144,1024]{1,0:T(8,128)(2,1)S(1)}, bf16[144,1024]{1,0:T(8,128)(2,1)S(1)}, u32[]{:S(2)}, u32[]{:S(2)}) collective-permute-start(bf16[144,1024]{1,0:T(8,128)(2,1)S(1)} %collective-permute-done), channel_id=1, source_target_pairs={{2,0},{4,2},{6,4},{7,6},{5,7},{3,5},{1,3},{0,1},{10,8},{12,10},{14... | collective-permute-start | bytes 884744 | tf_op jit(solution)/shard_map/ppermute | solution.py:119
  18.1 11.6 %collective-permute-start.4 = (bf16[144,1024]{1,0:T(8,128)(2,1)S(1)}, bf16[144,1024]{1,0:T(8,128)(2,1)S(1)}, u32[]{:S(2)}, u32[]{:S(2)}) collective-permute-start(bf16[144,1024]{1,0:T(8,128)(2,1)S(1)} %collective-permute-done.1), channel_id=1, source_target_pairs={{0,2},{2,4},{4,6},{6,7},{7,5},{5,3},{3,1},{1,0},{8,10},{10,12},{12... | collective-permute-start | bytes 884744 | tf_op jit(solution)/shard_map/ppermute | solution.py:116
  18.6 22.1 %collective-permute-start.9 = (bf16[256,1024]{1,0:T(8,128)(2,1)S(1)}, bf16[256,1024]{1,0:T(8,128)(2,1)}, u32[]{:S(2)}, u32[]{:S(2)}) collective-permute-start(bf16[256,1024]{1,0:T(8,128)(2,1)S(1)} %slice.23), channel_id=1, source_target_pairs={{0,16},{8,24},{16,0},{24,8},{1,17},{9,25},{17,1},{25,9},{2,18},{10... | collective-permute-start | bytes 1572872 | tf_op jit(solution)/shard_map/ppermute | solution.py:1028
  29.8 10.9 %collective-permute-start.10 = (bf16[256,1024]{1,0:T(8,128)(2,1)S(1)}, bf16[256,1024]{1,0:T(8,128)(2,1)S(1)}, u32[]{:S(2)}, u32[]{:S(2)}) collective-permute-start(bf16[256,1024]{1,0:T(8,128)(2,1)S(1)} %collective-permute-done.6.refs_2_), channel_id=1, source_target_pairs={{0,8},{8,0},{16,24},{24,16},{1,9},{9,1},{17,25},{25,17},{2,10},{10... | collective-permute-start | bytes 1572872 | tf_op jit(solution)/shard_map/ppermute | solution.py:1032
  29.8 10.8 %collective-permute-start.7 = (bf16[144,1024]{1,0:T(8,128)(2,1)S(1)}, bf16[144,1024]{1,0:T(8,128)(2,1)S(1)}, u32[]{:S(2)}, u32[]{:S(2)}) collective-permute-start(bf16[144,1024]{1,0:T(8,128)(2,1)S(1)} %collective-permute-done.3), channel_id=1, source_target_pairs={{2,0},{4,2},{6,4},{7,6},{5,7},{3,5},{1,3},{0,1},{10,8},{12,10},{14... | collective-permute-start | bytes 884744 | tf_op jit(solution)/shard_map/ppermute | solution.py:119
  31.5 9.2 %collective-permute-start.8 = (bf16[144,1024]{1,0:T(8,128)(2,1)S(1)}, bf16[144,1024]{1,0:T(8,128)(2,1)S(1)}, u32[]{:S(2)}, u32[]{:S(2)}) collective-permute-start(bf16[144,1024]{1,0:T(8,128)(2,1)S(1)} %collective-permute-done.4), channel_id=1, source_target_pairs={{0,2},{2,4},{4,6},{6,7},{7,5},{5,3},{3,1},{1,0},{8,10},{10,12},{12... | collective-permute-start | bytes 884744 | tf_op jit(solution)/shard_map/ppermute | solution.py:116
  41.1 13.3 %collective-permute-start.11 = (bf16[256,1024]{1,0:T(8,128)(2,1)}, bf16[256,1024]{1,0:T(8,128)(2,1)}, u32[]{:S(2)}, u32[]{:S(2)}) collective-permute-start(bf16[256,1024]{1,0:T(8,128)(2,1)} %collective-permute-done.9.refs_3_), channel_id=1, source_target_pairs={{0,8},{8,0},{16,24},{24,16},{1,9},{9,1},{17,25},{25,17},{2,10},{10... | collective-permute-start | bytes 1572872 | tf_op jit(solution)/shard_map/ppermute | solution.py:1035
  49.4 19.0 %collective-permute-start.13 = (bf16[256,1024]{1,0:T(8,128)(2,1)}, bf16[256,1024]{1,0:T(8,128)(2,1)}, u32[]{:S(2)}, u32[]{:S(2)}) collective-permute-start(bf16[256,1024]{1,0:T(8,128)(2,1)} %second_pack.1), channel_id=1, source_target_pairs={{2,0},{4,2},{6,4},{7,6},{5,7},{3,5},{1,3},{0,1},{10,8},{12,10},{14... | collective-permute-start | bytes 1572872 | tf_op jit(solution)/shard_map/ppermute | solution.py:119
  51.0 17.4 %collective-permute-start.14 = (bf16[256,1024]{1,0:T(8,128)(2,1)}, bf16[256,1024]{1,0:T(8,128)(2,1)}, u32[]{:S(2)}, u32[]{:S(2)}) collective-permute-start(bf16[256,1024]{1,0:T(8,128)(2,1)} %second_pack.1), channel_id=1, source_target_pairs={{0,2},{2,4},{4,6},{6,7},{7,5},{5,3},{3,1},{1,0},{8,10},{10,12},{12... | collective-permute-start | bytes 1572872 | tf_op jit(solution)/shard_map/ppermute | solution.py:116
  51.5 34.7 %collective-permute-start.19 = (bf16[512,1024]{1,0:T(8,128)(2,1)S(1)}, bf16[512,1024]{1,0:T(8,128)(2,1)S(1)}, u32[]{:S(2)}, u32[]{:S(2)}) collective-permute-start(bf16[512,1024]{1,0:T(8,128)(2,1)S(1)} %bitcast.92), channel_id=1, source_target_pairs={{0,16},{8,24},{16,0},{24,8},{1,17},{9,25},{17,1},{25,9},{2,18},{10... | collective-permute-start | bytes 3145736 | tf_op jit(solution)/shard_map/ppermute | solution.py:1036
  67.7 14.8 %collective-permute-start.17 = (bf16[1024,256]{1,0:T(8,128)(2,1)}, bf16[1024,256]{1,0:T(8,128)(2,1)}, u32[]{:S(2)}, u32[]{:S(2)}) collective-permute-start(bf16[1024,256]{1,0:T(8,128)(2,1)} %get-tuple-element.267.refs_4_), channel_id=1, source_target_pairs={{0,8},{8,0},{16,24},{24,16},{1,9},{9,1},{17,25},{25,17},{2,10},{10... | collective-permute-start | bytes 1572872 | tf_op jit(solution)/shard_map/ppermute | solution.py:73
  67.8 18.4 %collective-permute-start.18 = (bf16[1024,256]{1,0:T(8,128)(2,1)}, bf16[1024,256]{1,0:T(8,128)(2,1)}, u32[]{:S(2)}, u32[]{:S(2)}) collective-permute-start(bf16[1024,256]{1,0:T(8,128)(2,1)} %get-tuple-element.267.refs_4_), channel_id=1, source_target_pairs={{0,16},{8,24},{16,0},{24,8},{1,17},{9,25},{17,1},{25,9},{2,18},{10... | collective-permute-start | bytes 1572872 | tf_op jit(solution)/shard_map/ppermute | solution.py:73
  68.4 17.9 %collective-permute-start.15 = (bf16[256,1024]{1,0:T(8,128)(2,1)}, bf16[256,1024]{1,0:T(8,128)(2,1)S(1)}, u32[]{:S(2)}, u32[]{:S(2)}) collective-permute-start(bf16[256,1024]{1,0:T(8,128)(2,1)} %collective-permute-done.13), channel_id=1, source_target_pairs={{2,0},{4,2},{6,4},{7,6},{5,7},{3,5},{1,3},{0,1},{10,8},{12,10},{14... | collective-permute-start | bytes 1572872 | tf_op jit(solution)/shard_map/ppermute | solution.py:119
  69.9 16.3 %collective-permute-start.16 = (bf16[256,1024]{1,0:T(8,128)(2,1)}, bf16[256,1024]{1,0:T(8,128)(2,1)S(1)}, u32[]{:S(2)}, u32[]{:S(2)}) collective-permute-start(bf16[256,1024]{1,0:T(8,128)(2,1)} %collective-permute-done.14), channel_id=1, source_target_pairs={{0,2},{2,4},{4,6},{6,7},{7,5},{5,3},{3,1},{1,0},{8,10},{10,12},{12... | collective-permute-start | bytes 1572872 | tf_op jit(solution)/shard_map/ppermute | solution.py:116
  86.2 13.4 %collective-permute-start.20 = (bf16[256,1024]{1,0:T(8,128)(2,1)S(1)}, bf16[256,1024]{1,0:T(8,128)(2,1)S(1)}, u32[]{:S(2)}, u32[]{:S(2)}) collective-permute-start(bf16[256,1024]{1,0:T(8,128)(2,1)S(1)} %collective-permute-done.15), channel_id=1, source_target_pairs={{2,0},{4,2},{6,4},{7,6},{5,7},{3,5},{1,3},{0,1},{10,8},{12,10},{14... | collective-permute-start | bytes 1572872 | tf_op jit(solution)/shard_map/ppermute | solution.py:119
  87.9 11.8 %collective-permute-start.21 = (bf16[256,1024]{1,0:T(8,128)(2,1)S(1)}, bf16[256,1024]{1,0:T(8,128)(2,1)S(1)}, u32[]{:S(2)}, u32[]{:S(2)}) collective-permute-start(bf16[256,1024]{1,0:T(8,128)(2,1)S(1)} %collective-permute-done.16), channel_id=1, source_target_pairs={{0,2},{2,4},{4,6},{6,7},{7,5},{5,3},{3,1},{1,0},{8,10},{10,12},{12... | collective-permute-start | bytes 1572872 | tf_op jit(solution)/shard_map/ppermute | solution.py:116
  88.5 11.3 %collective-permute-start.22 = (bf16[1024,256]{1,0:T(8,128)(2,1)}, bf16[1024,256]{1,0:T(8,128)(2,1)S(1)}, u32[]{:S(2)}, u32[]{:S(2)}) collective-permute-start(bf16[1024,256]{1,0:T(8,128)(2,1)} %collective-permute-done.18.refs_6_), channel_id=1, source_target_pairs={{0,8},{8,0},{16,24},{24,16},{1,9},{9,1},{17,25},{25,17},{2,10},{10... | collective-permute-start | bytes 1572872 | tf_op jit(solution)/shard_map/ppermute | solution.py:1072
  101.4 17.5 %collective-permute-start.23 = (bf16[512,1024]{1,0:T(8,128)(2,1)S(1)}, bf16[512,1024]{1,0:T(8,128)(2,1)S(1)}, u32[]{:S(2)}, u32[]{:S(2)}) collective-permute-start(bf16[512,1024]{1,0:T(8,128)(2,1)S(1)} %collective-permute-done.19.ca.refs_4_), channel_id=1, source_target_pairs={{0,8},{8,0},{16,24},{24,16},{1,9},{9,1},{17,25},{25,17},{2,10},{10... | collective-permute-start | bytes 3145736 | tf_op jit(solution)/shard_map/ppermute | solution.py:1077
  101.9 16.9 %collective-permute-start.24 = (bf16[256,1024]{1,0:T(8,128)(2,1)}, bf16[256,1024]{1,0:T(8,128)(2,1)S(1)}, u32[]{:S(2)}, u32[]{:S(2)}) collective-permute-start(bf16[256,1024]{1,0:T(8,128)(2,1)} %copy-done.24), channel_id=1, source_target_pairs={{0,2},{2,4},{4,6},{6,7},{7,5},{5,3},{3,1},{1,0},{8,10},{10,12},{12... | collective-permute-start | bytes 1572872 | tf_op jit(solution)/shard_map/ppermute | solution.py:116
  106.4 12.4 %collective-permute-start.27 = (bf16[512,256]{1,0:T(8,128)(2,1)S(1)}, bf16[512,256]{1,0:T(8,128)(2,1)S(1)}, u32[]{:S(2)}, u32[]{:S(2)}) collective-permute-start(bf16[512,256]{1,0:T(8,128)(2,1)S(1)} %get-tuple-element.468), channel_id=1, source_target_pairs={{0,24},{8,16},{16,8},{24,0},{1,25},{9,17},{17,9},{25,1},{2,26},{10... | collective-permute-start | bytes 786440 | tf_op jit(solution)/shard_map/ppermute | solution.py:1081
  127.1 25.6 %collective-permute-start.29 = (bf16[512,1024]{1,0:T(8,128)(2,1)}, bf16[512,1024]{1,0:T(8,128)(2,1)S(1)}, u32[]{:S(2)}, u32[]{:S(2)}) collective-permute-start(bf16[512,1024]{1,0:T(8,128)(2,1)} %get-tuple-element.286.sa.refs_6_), channel_id=1, source_target_pairs={{0,16},{8,24},{16,0},{24,8},{1,17},{9,25},{17,1},{25,9},{2,18},{10... | collective-permute-start | bytes 3145736 | tf_op jit(solution)/shard_map/ppermute | solution.py:1093
  152.7 21.4 %collective-permute-start.32 = (bf16[512,1024]{1,0:T(8,128)(2,1)}, bf16[512,1024]{1,0:T(8,128)(2,1)S(1)}, u32[]{:S(2)}, u32[]{:S(2)}) collective-permute-start(bf16[512,1024]{1,0:T(8,128)(2,1)} %get-tuple-element.305), channel_id=1, source_target_pairs={{0,8},{8,0},{16,24},{24,16},{1,9},{9,1},{17,25},{25,17},{2,10},{10... | collective-permute-start | bytes 3145736 | tf_op jit(solution)/shard_map/ppermute | solution.py:1109
  153.2 20.9 %collective-permute-start.33 = (bf16[512,1024]{1,0:T(8,128)(2,1)}, bf16[512,1024]{1,0:T(8,128)(2,1)}, u32[]{:S(2)}, u32[]{:S(2)}) collective-permute-start(bf16[512,1024]{1,0:T(8,128)(2,1)} %get-tuple-element.306), channel_id=1, source_target_pairs={{0,8},{8,0},{16,24},{24,16},{1,9},{9,1},{17,25},{25,17},{2,10},{10... | collective-permute-start | bytes 3145736 | tf_op jit(solution)/shard_map/ppermute | solution.py:1110
  179.7 25.4 %collective-permute-start.35 = (bf16[512,1024]{1,0:T(8,128)(2,1)}, bf16[512,1024]{1,0:T(8,128)(2,1)S(1)}, u32[]{:S(2)}, u32[]{:S(2)}) collective-permute-start(bf16[512,1024]{1,0:T(8,128)(2,1)} %add_convert_fusion.2), channel_id=1, source_target_pairs={{0,16},{8,24},{16,0},{24,8},{1,17},{9,25},{17,1},{25,9},{2,18},{10... | collective-permute-start | bytes 3145736 | tf_op jit(solution)/shard_map/ppermute | solution.py:1120
  181.2 23.9 %collective-permute-start.36 = (bf16[512,1024]{1,0:T(8,128)(2,1)}, bf16[512,1024]{1,0:T(8,128)(2,1)}, u32[]{:S(2)}, u32[]{:S(2)}) collective-permute-start(bf16[512,1024]{1,0:T(8,128)(2,1)} %get-tuple-element.312), channel_id=1, source_target_pairs={{0,8},{8,0},{16,24},{24,16},{1,9},{9,1},{17,25},{25,17},{2,10},{10... | collective-permute-start | bytes 3145736 | tf_op jit(solution)/shard_map/ppermute | solution.py:1121
  200.3 23.6 %collective-permute-start.31 = (bf16[256,1024]{1,0:T(8,128)(2,1)}, bf16[256,1024]{1,0:T(8,128)(2,1)S(1)}, u32[]{:S(2)}, u32[]{:S(2)}) collective-permute-start(bf16[256,1024]{1,0:T(8,128)(2,1)} %bitcast.125), channel_id=1, source_target_pairs={{0,2},{2,4},{4,6},{6,7},{7,5},{5,3},{3,1},{1,0},{8,10},{10,12},{12... | collective-permute-start | bytes 1572872 | tf_op jit(solution)/shard_map/ppermute | solution.py:116
  216.2 9.4 %collective-permute-start.38 = (bf16[512,256]{1,0:T(8,128)(2,1)}, bf16[512,256]{1,0:T(8,128)(2,1)S(1)}, u32[]{:S(2)}, u32[]{:S(2)}) collective-permute-start(bf16[512,256]{1,0:T(8,128)(2,1)} %get-tuple-element.327), channel_id=1, source_target_pairs={{0,16},{8,24},{16,0},{24,8},{1,17},{9,25},{17,1},{25,9},{2,18},{10... | collective-permute-start | bytes 786440 | tf_op jit(solution)/shard_map/ppermute | solution.py:1176
  217.8 12.5 %collective-permute-start.39 = (bf16[512,256]{1,0:T(8,128)(2,1)}, bf16[512,256]{1,0:T(8,128)(2,1)S(1)}, u32[]{:S(2)}, u32[]{:S(2)}) collective-permute-start(bf16[512,256]{1,0:T(8,128)(2,1)} %get-tuple-element.328), channel_id=1, source_target_pairs={{0,24},{8,16},{16,8},{24,0},{1,25},{9,17},{17,9},{25,1},{2,26},{10... | collective-permute-start | bytes 786440 | tf_op jit(solution)/shard_map/ppermute | solution.py:1176
  230.5 23.9 %collective-permute-start.42 = (bf16[2,1024,256]{2,1,0:T(8,128)(2,1)}, bf16[2,1024,256]{2,1,0:T(8,128)(2,1)}, u32[]{:S(2)}, u32[]{:S(2)}) collective-permute-start(bf16[2,1024,256]{2,1,0:T(8,128)(2,1)} %get-tuple-element.345), channel_id=1, source_target_pairs={{0,8},{8,0},{16,24},{24,16},{1,9},{9,1},{17,25},{25,17},{2,10},{10... | collective-permute-start | bytes 3145736 | tf_op jit(solution)/shard_map/ppermute | solution.py:1184
  230.8 23.5 %collective-permute-start.41 = (bf16[256,1024]{1,0:T(8,128)(2,1)S(1)}, bf16[256,1024]{1,0:T(8,128)(2,1)S(1)}, u32[]{:S(2)}, u32[]{:S(2)}) collective-permute-start(bf16[256,1024]{1,0:T(8,128)(2,1)S(1)} %bitcast.124), channel_id=1, source_target_pairs={{2,0},{4,2},{6,4},{7,6},{5,7},{3,5},{1,3},{0,1},{10,8},{12,10},{14... | collective-permute-start | bytes 1572872 | tf_op jit(solution)/shard_map/ppermute | solution.py:119
  231.8 22.6 %collective-permute-start.40 = (bf16[256,1024]{1,0:T(8,128)(2,1)S(1)}, bf16[256,1024]{1,0:T(8,128)(2,1)S(1)}, u32[]{:S(2)}, u32[]{:S(2)}) collective-permute-start(bf16[256,1024]{1,0:T(8,128)(2,1)S(1)} %fusion.4), channel_id=1, source_target_pairs={{0,2},{2,4},{4,6},{6,7},{7,5},{5,3},{3,1},{1,0},{8,10},{10,12},{12... | collective-permute-start | bytes 1572872 | tf_op jit(solution)/shard_map/ppermute | solution.py:116
  232.8 45.8 %collective-permute-start.46 = (bf16[512,1024]{1,0:T(8,128)(2,1)}, bf16[512,1024]{1,0:T(8,128)(2,1)}, u32[]{:S(2)}, u32[]{:S(2)}) collective-permute-start(bf16[512,1024]{1,0:T(8,128)(2,1)} %add_convert_fusion.1), channel_id=1, source_target_pairs={{0,16},{8,24},{16,0},{24,8},{1,17},{9,25},{17,1},{25,9},{2,18},{10... | collective-permute-start | bytes 3145736 | tf_op jit(solution)/shard_map/ppermute | solution.py:1182
  256.6 22.1 %collective-permute-start.43 = (bf16[256,1024]{1,0:T(8,128)(2,1)S(1)}, bf16[256,1024]{1,0:T(8,128)(2,1)S(1)}, u32[]{:S(2)}, u32[]{:S(2)}) collective-permute-start(bf16[256,1024]{1,0:T(8,128)(2,1)S(1)} %get-tuple-element.355), channel_id=1, source_target_pairs={{0,2},{2,4},{4,6},{6,7},{7,5},{5,3},{3,1},{1,0},{8,10},{10,12},{12... | collective-permute-start | bytes 1572872 | tf_op jit(solution)/shard_map/ppermute | solution.py:116
  258.2 20.5 %collective-permute-start.44 = (bf16[256,1024]{1,0:T(8,128)(2,1)S(1)}, bf16[256,1024]{1,0:T(8,128)(2,1)S(1)}, u32[]{:S(2)}, u32[]{:S(2)}) collective-permute-start(bf16[256,1024]{1,0:T(8,128)(2,1)S(1)} %get-tuple-element.356), channel_id=1, source_target_pairs={{2,0},{4,2},{6,4},{7,6},{5,7},{3,5},{1,3},{0,1},{10,8},{12,10},{14... | collective-permute-start | bytes 1572872 | tf_op jit(solution)/shard_map/ppermute | solution.py:119
  258.7 20.1 %collective-permute-start.45 = (bf16[1024,256]{1,0:T(8,128)(2,1)S(1)}, bf16[1024,256]{1,0:T(8,128)(2,1)S(1)}, u32[]{:S(2)}, u32[]{:S(2)}) collective-permute-start(bf16[1024,256]{1,0:T(8,128)(2,1)S(1)} %fusion.3), channel_id=1, source_target_pairs={{0,16},{8,24},{16,0},{24,8},{1,17},{9,25},{17,1},{25,9},{2,18},{10... | collective-permute-start | bytes 1572872 | tf_op jit(solution)/shard_map/ppermute | solution.py:1196
  281.1 12.6 %collective-permute-start.47 = (bf16[256,1024]{1,0:T(8,128)(2,1)S(1)}, bf16[256,1024]{1,0:T(8,128)(2,1)S(1)}, u32[]{:S(2)}, u32[]{:S(2)}) collective-permute-start(bf16[256,1024]{1,0:T(8,128)(2,1)S(1)} %get-tuple-element.371), channel_id=1, source_target_pairs={{0,2},{2,4},{4,6},{6,7},{7,5},{5,3},{3,1},{1,0},{8,10},{10,12},{12... | collective-permute-start | bytes 1572872 | tf_op jit(solution)/shard_map/ppermute | solution.py:116
  282.7 12.1 %collective-permute-start.48 = (bf16[256,1024]{1,0:T(8,128)(2,1)S(1)}, bf16[256,1024]{1,0:T(8,128)(2,1)S(1)}, u32[]{:S(2)}, u32[]{:S(2)}) collective-permute-start(bf16[256,1024]{1,0:T(8,128)(2,1)S(1)} %get-tuple-element.372), channel_id=1, source_target_pairs={{2,0},{4,2},{6,4},{7,6},{5,7},{3,5},{1,3},{0,1},{10,8},{12,10},{14... | collective-permute-start | bytes 1572872 | tf_op jit(solution)/shard_map/ppermute | solution.py:119
  295.1 12.1 %collective-permute-start.50 = (bf16[256,1024]{1,0:T(8,128)(2,1)S(1)}, bf16[256,1024]{1,0:T(8,128)(2,1)S(1)}, u32[]{:S(2)}, u32[]{:S(2)}) collective-permute-start(bf16[256,1024]{1,0:T(8,128)(2,1)S(1)} %fusion.6.refs_0_), channel_id=1, source_target_pairs={{0,16},{8,24},{16,0},{24,8},{1,17},{9,25},{17,1},{25,9},{2,18},{10... | collective-permute-start | bytes 1572872 | tf_op jit(solution)/shard_map/ppermute | solution.py:1227
  296.7 10.5 %collective-permute-start.49 = (bf16[144,1024]{1,0:T(8,128)(2,1)S(1)}, bf16[144,1024]{1,0:T(8,128)(2,1)S(1)}, u32[]{:S(2)}, u32[]{:S(2)}) collective-permute-start(bf16[144,1024]{1,0:T(8,128)(2,1)S(1)} %bitcast.127), channel_id=1, source_target_pairs={{0,2},{2,4},{4,6},{6,7},{7,5},{5,3},{3,1},{1,0},{8,10},{10,12},{12... | collective-permute-start | bytes 884744 | tf_op jit(solution)/shard_map/ppermute | solution.py:116
  307.4 9.4 %collective-permute-start.52 = (bf16[144,1024]{1,0:T(8,128)(2,1)S(1)}, bf16[144,1024]{1,0:T(8,128)(2,1)S(1)}, u32[]{:S(2)}, u32[]{:S(2)}) collective-permute-start(bf16[144,1024]{1,0:T(8,128)(2,1)S(1)} %bitcast.126), channel_id=1, source_target_pairs={{2,0},{4,2},{6,4},{7,6},{5,7},{3,5},{1,3},{0,1},{10,8},{12,10},{14... | collective-permute-start | bytes 884744 | tf_op jit(solution)/shard_map/ppermute | solution.py:119
  317.1 24.6 %collective-permute-start.58 = (bf16[512,1024]{1,0:T(8,128)(2,1)S(1)}, bf16[512,1024]{1,0:T(8,128)(2,1)S(1)}, u32[]{:S(2)}, u32[]{:S(2)}) collective-permute-start(bf16[512,1024]{1,0:T(8,128)(2,1)S(1)} %fusion), channel_id=1, source_target_pairs={{0,16},{8,24},{16,0},{24,8},{1,17},{9,25},{17,1},{25,9},{2,18},{10... | collective-permute-start | bytes 3145736 | tf_op jit(solution)/shard_map/ppermute | solution.py:1246
  327.5 10.8 %collective-permute-start.59 = (bf16[256,1024]{1,0:T(8,128)(2,1)S(1)}, bf16[256,1024]{1,0:T(8,128)(2,1)S(1)}, u32[]{:S(2)}, u32[]{:S(2)}) collective-permute-start(bf16[256,1024]{1,0:T(8,128)(2,1)S(1)} %fusion.6.refs_0_), channel_id=1, source_target_pairs={{0,8},{8,0},{16,24},{24,16},{1,9},{9,1},{17,25},{25,17},{2,10},{10... | collective-permute-start | bytes 1572872 | tf_op jit(solution)/shard_map/ppermute | solution.py:1255
  327.6 10.7 %collective-permute-start.60 = (bf16[256,1024]{1,0:T(8,128)(2,1)S(1)}, bf16[256,1024]{1,0:T(8,128)(2,1)S(1)}, u32[]{:S(2)}, u32[]{:S(2)}) collective-permute-start(bf16[256,1024]{1,0:T(8,128)(2,1)S(1)} %collective-permute-done.50.refs_2_), channel_id=1, source_target_pairs={{0,8},{8,0},{16,24},{24,16},{1,9},{9,1},{17,25},{25,17},{2,10},{10... | collective-permute-start | bytes 1572872 | tf_op jit(solution)/shard_map/ppermute | solution.py:1256
  (79 other events, 853.3 us)

commit v5 on v4

--- a/solution.py
+++ b/solution.py
@@ -627,7 +627,7 @@
     dim = cots[0].shape[1]
     ff = activs[0].shape[1]
     rows, units = dim // nb, ff // nb
-    tile = 256
+    tile = 512
     steps = ff // tile
     tok = ns * cots[0].shape[0]
     left = lambda a: pl.BlockSpec((a.shape[0], tile), lambda i, info: (0, jnp.minimum(i, steps - 1)))
@@ -696,7 +696,12 @@
     )(info, left, right)
 
 
-def joined_grad_kernel(nb, rows, np, live, info, left, other, weight, vecs, *refs):
+def joined_grad_kernel(nb, rows, np, terms, live, info, left, weight, vecs, *refs):
+    others, refs = refs[:terms], refs[terms:]
+    other = others[0][...].astype(F32)
+    for term in others[1:]:
+        other += term[...].astype(F32)
+    other = other.astype(BF)
     smalls, refs = (refs[:3], refs[3:]) if live else (refs[:1], refs[1:])
     right, sides, outs = refs[0], refs[1 : 1 + np], refs[1 + np :]
     total = dg(left[...], right[...], TN)
@@ -734,23 +739,25 @@
         put(outs, slot, held[:, high], slice(rows, rows + 16), slice(0, rows))
 
 
-def joined_grad_call(info, left, right, sides, other, weight, vecs, shares, turned, biases, nb, live):
+def joined_grad_call(info, left, right, sides, others, weight, vecs, shares, turned, biases, nb, live):
     count, dim = left.shape
     cols = weight.shape[1]
-    cw = other.shape[1]
+    cw = others[0].shape[1]
     rows = dim // nb
     tile = 256
     wide = (rows + 16, cols + cw)
     shapes = [(1, *wide)] * nb if live else [(nb, *wide)]
     flat = lambda width: pl.BlockSpec((tile, width), lambda i, info: (i, 0))
+    first = lambda width: pl.BlockSpec((None, tile, width), lambda i, info: (0, i, 0))
     tall = lambda value: pl.BlockSpec((value.shape[0], tile), lambda i, info: (0, i))
     smalls = (turned, *biases) if live else (shares,)
     return pl.pallas_call(
-        functools.partial(joined_grad_kernel, nb, rows, len(sides), live),
+        functools.partial(joined_grad_kernel, nb, rows, len(sides), len(others), live),
         grid_spec=pltpu.PrefetchScalarGridSpec(
             num_scalar_prefetch=1,
             grid=(dim // tile,),
-            in_specs=[pl.BlockSpec((count, tile), lambda i, info: (0, i)), flat(cw), flat(cols), tall(vecs)]
+            in_specs=[pl.BlockSpec((count, tile), lambda i, info: (0, i)), flat(cols), tall(vecs)]
+            + [first(cw) if term.ndim == 3 else flat(cw) for term in others]
             + [tall(value) for value in smalls]
             + [once(value.shape) for value in (right, *sides)],
             out_specs=[once(shape) for shape in shapes],
@@ -759,7 +766,7 @@
         compiler_params=params(60),
         cost_estimate=cost(2 * count * dim * cols, 2 * count * (dim + cols) + 4 * dim * dim),
         name="joined_grad",
-    )(info, left, other, weight, vecs, *smalls, right, *sides)
+    )(info, left, weight, vecs, *others, *smalls, right, *sides)
 
 
 def turn_kernel(ns, np, cw, info, ga, gb, gc, resid, cot, vecs, full, resid_grad, branch, *refs):
@@ -1117,7 +1124,8 @@
         back_parts[3], near_back, near_out = tie(back_parts[3], near_back, near_out)
         far_back = lax.ppermute(back_parts[3], "seq", pairs(ns, 1))
         far_back, out_far = tie(far_back, out_parts[3])
-        back_b = lax.ppermute(add16(back_parts[2], far_back), "seq", pairs(ns, 2))
+        (back_b,) = add_pairs((back_parts[2],), (far_back,))
+        back_b = lax.ppermute(back_b, "seq", pairs(ns, 2))
         far_out = lax.ppermute(out_far, "seq", pairs(ns, 1))
     else:
         back_terms = (*scatter_rel(back_parts, "seq", ns, last=False), jnp.zeros((tok, dim), BF))
@@ -1156,15 +1164,14 @@
             if both:
                 self.ahead, self.back = add_pairs((mine, self.parts[nb - ring.half + self.t]), got)
             else:
-                self.ahead = add16(mine, got[0])
+                (self.ahead,) = add_pairs((mine,), got)
             return others
 
     if live:
         feed_ring = Scatter(feed_stack)
         feed_ring.send()
-        back_b, far_out, _ = tie(back_b, far_out, feed_stack[0])
-        out_b = add16(out_parts[2], far_out)
-        back_b, out_b = tie(back_b, out_b)
+        (out_b,) = add_pairs((out_parts[2],), (far_out,))
+        back_b, out_b, _ = tie(back_b, out_b, feed_stack[0])
         back_terms = (back_parts[0], near_back, back_b)
     resid_grad, branch, *mixed_grads, turn_sums = turn_call(
         info, back_terms, resid, cot, vecs, outw_full, ns, 1
@@ -1199,11 +1206,8 @@
 
     if live:
         shares = None
-        outw_share = outw_parts[0].astype(F32) + outw_near[0].astype(F32) + outw_far.astype(F32)
-        outw_share = outw_share.astype(BF)
-        joined_grad, outw_share, feed_ring.ahead, feed_ring.back = tie(
-            joined_grad, outw_share, feed_ring.ahead, feed_ring.back
-        )
+        outw_share = (outw_parts[0], outw_near, outw_far)
+        joined_grad, feed_ring.ahead, feed_ring.back = tie(joined_grad, feed_ring.ahead, feed_ring.back)
         feed_ring.send()
     else:
         spread_bias = lax.dynamic_update_slice(
@@ -1217,7 +1221,7 @@
         none = jnp.zeros((2, dim), F32)
         shares = [none, side, turn_sums[2:3], turn_sums[0:2], spread_bias, turn_sums[3:4], none, none]
         shares = jnp.concatenate(shares, 0)
-        outw_share = scatter_rel(dict(enumerate(outw_parts)), "seq", ns)
+        outw_share = (scatter_rel(dict(enumerate(outw_parts)), "seq", ns),)
     joined_stack = joined_grad_call(
         info, normed, joined_grad, sides, outw_share, joined_full, vecs, shares, turn_sums, bias_sums, nb, live
     )

time: 362 us -> 359 us (level)
  other arithmetic: 16 us -> 8.77 us
    convert_element_type x6 -> x2, other arithmetic: 8.83 us -> 3.74 us  [add16(): return (left.astype(F32) + right.astype(F32)).astype(BF)]
  transfers between devices with their start and end apart: 64 -> 64, of which waited for: 25 -> 25; matrix products, arithmetic and copies ran while one was open for 4% -> 3% of each run, Pallas kernels for 48% -> 49%
where the time goes in v5:
time: 359 us; the launch traced here: 353 us
  Pallas kernels  186 us (52%)
  waiting for transfers between devices  95.9 us (27%)
  starting transfers between devices  51.6 us (14%)
  local copies, waits for them, and re-layouts  9.21 us (3%)
  other arithmetic  8.77 us (2%)
    pallas_call x2, Pallas kernels, attend_back(): pl.pallas_call(kernel, grid=(1,), in_specs=[smem, smem, wide, narrow, nar...  39.5 us
    pallas_call x2, Pallas kernels, feed_call(): pl.pallas_call(functools.partial(feed_kernel, nt, nb, rows, units, live),...  32.5 us
    pallas_call x2, Pallas kernels, attend(): pl.pallas_call(kernel, grid=(1,), in_specs=[smem, smem, pl.BlockSpec((cou...  22.4 us
    ppermute x16, waiting for transfers between devices, ahead(): return lax.ppermute(value, 'batch', self.forward)  19.2 us
    pallas_call x1, Pallas kernels, feed_grad_call(): pl.pallas_call(functools.partial(feed_grad_kernel, ns, nb, rows, units, s...  19 us
    ppermute x6, waiting for transfers between devices, body(): lax.ppermute(block, 'seq', pairs(ns, rel))  18.4 us
    ppermute x16, starting transfers between devices, ahead(): return lax.ppermute(value, 'batch', self.forward)  16.2 us
    ppermute x12, starting transfers between devices, back(): return lax.ppermute(value, 'batch', self.backward)  14.5 us
  transfers between devices with their start and end apart: 64, of which 25 were waited for; matrix products, arithmetic and copies ran while one was open for 3% of the time, Pallas kernels for 49%

profile of v5, /device:TPU:0, one launch (start us, length us, event | category | flops | bytes accessed | tf_op | source)
XLA Modules:
  0.0 353.4 jit_solution(10183630068132150449)
XLA Ops:
  1.2 1.8 first_pack.1
  3.0 2.6 collective-permute-start
  5.7 2.2 second_pack.1
  7.8 5.6 %collective-permute-done = bf16[144,1024]{1,0:T(8,128)(2,1)S(1)} collective-permute-done((bf16[144,1024]{1,0:T(8,128)(2,1)}, bf16[144,1024]{1,0:T(8,128)(2,1)S(1)}, u32[]{:S(2)}, u32[]{:S(2)}) %collective-permute-start) | collective-permute-done | bytes 294944 | tf_op jit(solution)/shard_map/ppermute | solution.py:119
  14.9 1.6 collective-permute-start.6
  19.2 10.6 %collective-permute-done.6.refs_2_ = bf16[256,1024]{1,0:T(8,128)(2,1)S(1)} collective-permute-done((bf16[256,1024]{1,0:T(8,128)(2,1)S(1)}, bf16[256,1024]{1,0:T(8,128)(2,1)S(1)}, u32[]{:S(2)}, u32[]{:S(2)}) %collective-permute-start.6) | collective-permute-done | bytes 524320 | tf_op jit(solution)/shard_map/ppermute | solution.py:1030
  29.8 1.6 collective-permute-start.7
  31.9 8.7 %collective-permute-done.9.refs_3_ = bf16[256,1024]{1,0:T(8,128)(2,1)} collective-permute-done((bf16[256,1024]{1,0:T(8,128)(2,1)S(1)}, bf16[256,1024]{1,0:T(8,128)(2,1)}, u32[]{:S(2)}, u32[]{:S(2)}) %collective-permute-start.9) | collective-permute-done | bytes 524320 | tf_op jit(solution)/shard_map/ppermute | solution.py:1035
  41.1 8.2 %collective-permute-done.12 = bf16[144,1024]{1,0:T(8,128)(2,1)S(1)} collective-permute-done((bf16[144,1024]{1,0:T(8,128)(2,1)S(1)}, bf16[144,1024]{1,0:T(8,128)(2,1)S(1)}, u32[]{:S(2)}, u32[]{:S(2)}) %collective-permute-start.12) | collective-permute-done | bytes 294944 | tf_op jit(solution)/shard_map/ppermute | solution.py:116
  51.5 1.6 collective-permute-start.19
  54.4 13.3 %first.1 = (bf16[2048,1024]{1,0:T(8,128)(2,1)}, bf16[2048,768]{1,0:T(8,128)(2,1)}, bf16[1024,768]{1,0:T(8,128)(2,1)}, bf16[1024,256]{1,0:T(8,128)(2,1)}, f32[16,1024]{1,0:T(8,128)}) custom-call(s32[18]{0:T(128)} %pad_add_fusion.info.refs_0_, bf16[512,1024]{1,0:T(8,128)(2,1)} %bitcast.69, bf16[512,1024]{1,0:T(8,128)(2,1)} %collective-permute-done.2.refs_1_, ...), custom_call_target="tpu_custom_call" | custom-call | flops 3221225 | bytes 11534 | tf_op jit(solution)/shard_map/first/pallas_call | solution.py:264
  71.3 11.2 %attend.2 = (bf16[2048,256]{1,0:T(8,128)(2,1)}, f32[2048,256]{1,0:T(8,128)}) custom-call(s32[18]{0:T(128)} %pad_add_fusion.info.refs_0_, f32[4]{0:T(128)} %multiply_power_fusion.refs_1_, bf16[2048,768]{1,0:T(8,128)(2,1)} %get-tuple-element.352.refs_2_), custom_call_target="tpu_custom_call" | custom-call | flops 4294967 | bytes 2621 | tf_op jit(solution)/shard_map/attend/pallas_call | solution.py:362
  82.5 3.7 %collective-permute-done.18.refs_6_ = bf16[1024,256]{1,0:T(8,128)(2,1)} collective-permute-done((bf16[1024,256]{1,0:T(8,128)(2,1)}, bf16[1024,256]{1,0:T(8,128)(2,1)}, u32[]{:S(2)}, u32[]{:S(2)}) %collective-permute-start.18) | collective-permute-done | bytes 524320 | tf_op jit(solution)/shard_map/ppermute | solution.py:73
  86.2 1.6 collective-permute-start.20
  88.5 11.2 %attend.3 = (bf16[2048,256]{1,0:T(8,128)(2,1)}, f32[2048,256]{1,0:T(8,128)}) custom-call(s32[18]{0:T(128)} %pad_add_fusion.info.refs_0_, f32[4]{0:T(128)} %multiply_power_fusion.refs_1_, bf16[2048,768]{1,0:T(8,128)(2,1)} %get-tuple-element.352.refs_2_, bf16[2048,256]{1,0:T(8,128)(2,1)} %get-tuple-element.267.refs_3_, ...), custom_call_target="tpu_custom_call", output_to_operand_aliasing={{0}: (3, {}), {1}: (4, {})} | custom-call | flops 4294967 | bytes 2621 | tf_op jit(solution)/shard_map/attend/pallas_call | solution.py:362
  102.9 1.9 constant_dynamic-slice_fusion
  106.7 7.2 %collective-permute-done.26.refs_2_ = bf16[512,256]{1,0:T(8,128)(2,1)S(1)} collective-permute-done((bf16[512,256]{1,0:T(8,128)(2,1)S(1)}, bf16[512,256]{1,0:T(8,128)(2,1)S(1)}, u32[]{:S(2)}, u32[]{:S(2)}) %collective-permute-start.26) | collective-permute-done | bytes 262176 | tf_op jit(solution)/shard_map/ppermute | solution.py:1088
  114.0 4.8 %collective-permute-done.27.refs_3_ = bf16[512,256]{1,0:T(8,128)(2,1)S(1)} collective-permute-done((bf16[512,256]{1,0:T(8,128)(2,1)S(1)}, bf16[512,256]{1,0:T(8,128)(2,1)S(1)}, u32[]{:S(2)}, u32[]{:S(2)}) %collective-permute-start.27) | collective-permute-done | bytes 262176 | tf_op jit(solution)/shard_map/ppermute | solution.py:1088
  119.5 7.1 %middle.1 = (bf16[512,1024]{1,0:T(8,128)(2,1)}, f32[512,1024]{1,0:T(8,128)}, bf16[512,1024]{1,0:T(8,128)(2,1)}, bf16[1024,1024]{1,0:T(8,128)(2,1)}) custom-call(s32[18]{0:T(128)} %pad_add_fusion.info.refs_0_, bf16[512,1024]{1,0:T(8,128)(2,1)} %bitcast.70, f32[16,1024]{1,0:T(8,128)} %get-tuple-element.257.vecs.ebias, ...), custom_call_target="tpu_custom_call" | custom-call | flops 1073741 | bytes 10485 | tf_op jit(solution)/shard_map/middle/pallas_call | solution.py:489
  130.6 16.2 %feed.2 = (bf16[1024,1024]{1,0:T(8,128)(2,1)}, bf16[1024,1024]{1,0:T(8,128)(2,1)}, bf16[512,1024]{1,0:T(8,128)(2,1)}, bf16[512,1024]{1,0:T(8,128)(2,1)}, bf16[51...) custom-call(s32[18]{0:T(128)} %pad_add_fusion.info.refs_0_, ...), custom_call_target="tpu_custom_call" | custom-call | flops 8589934 | bytes 16777 | tf_op jit(solution)/shard_map/feed/pallas_call | solution.py:568
  146.8 5.7 %collective-permute-done.29.sa.refs_8_ = bf16[512,1024]{1,0:T(8,128)(2,1)S(1)} collective-permute-done((bf16[512,1024]{1,0:T(8,128)(2,1)}, bf16[512,1024]{1,0:T(8,128)(2,1)S(1)}, u32[]{:S(2)}, u32[]{:S(2)}) %collective-permute-start.29) | collective-permute-done | bytes 1048608 | tf_op jit(solution)/shard_map/ppermute | solution.py:1100
  153.0 3.6 %collective-permute-done.30.sb.refs_9_ = bf16[512,1024]{1,0:T(8,128)(2,1)S(1)} collective-permute-done((bf16[512,1024]{1,0:T(8,128)(2,1)S(1)}, bf16[512,1024]{1,0:T(8,128)(2,1)S(1)}, u32[]{:S(2)}, u32[]{:S(2)}) %collective-permute-start.30) | collective-permute-done | bytes 1048608 | tf_op jit(solution)/shard_map/ppermute | solution.py:1114
  157.6 16.3 %feed.3 = (bf16[1024,1024]{1,0:T(8,128)(2,1)}, bf16[1024,1024]{1,0:T(8,128)(2,1)}, bf16[512,1024]{1,0:T(8,128)(2,1)}, bf16[512,1024]{1,0:T(8,128)(2,1)}, bf16[51...) custom-call(s32[18]{0:T(128)} %pad_add_fusion.info.refs_0_, bf16[512,1024]{1,0:T(8,128)(2,1)} %copy-done.23, ...), custom_call_target="tpu_custom_call" | custom-call | flops 8589934 | bytes 16777 | tf_op jit(solution)/shard_map/feed/pallas_call | solution.py:568
  174.2 2.7 collective-permute-done.34.refs_1_
  181.1 19.0 %feed_grad.1 = (bf16[1,256,1024]{2,1,0:T(8,128)(2,1)}, bf16[1,256,1024]{2,1,0:T(8,128)(2,1)}, bf16[1,256,1024]{2,1,0:T(8,128)(2,1)}, bf16[1,256,1024]{2,1,0:T(8,...) custom-call(s32[18]{0:T(128)} %pad_add_fusion.info.refs_0_, ...), custom_call_target="tpu_custom_call" | custom-call | flops 8589934 | bytes 20971 | tf_op jit(solution)/shard_map/feed_grad/pallas_call | solution.py:637
  200.1 1.6 collective-permute-start.31
  202.0 3.3 collective-permute-done.35.gc
  205.3 8.0 %turn.1 = (f32[512,1024]{1,0:T(8,128)}, bf16[512,1024]{1,0:T(8,128)(2,1)}, bf16[512,256]{1,0:T(8,128)(2,1)}, bf16[512,256]{1,0:T(8,128)(2,1)}, bf16[512,256]{1,0...) custom-call(s32[18]{0:T(128)} %pad_add_fusion.info.refs_0_, bf16[512,1024]{1,0:T(8,128)(2,1)} %get-tuple-element.300.ga, ...), custom_call_target="tpu_custom_call" | custom-call | flops 1073741 | bytes 10485 | tf_op jit(solution)/shard_map/turn/pallas_call | solution.py:801
  215.2 5.9 %split_grad.1 = (bf16[1024,256]{1,0:T(8,128)(2,1)}, bf16[1024,256]{1,0:T(8,128)(2,1)}, bf16[2,1024,256]{2,1,0:T(8,128)(2,1)}) custom-call(s32[18]{0:T(128)} %pad_add_fusion.info.refs_0_, bf16[512,1024]{1,0:T(8,128)(2,1)} %get-tuple-element.315.left, bf16[512,1024]{1,0:T(8,128)(2,1)} %get-tuple-element.316.right), custom_call_target="tpu_custom_call" | custom-call | flops 1073741 | bytes 6291 | tf_op jit(solution)/shard_map/split_grad/pallas_call | solution.py:683
  221.1 1.6 collective-permute-done.38.refs_7_
  222.7 4.7 %collective-permute-done.39.refs_8_ = bf16[512,256]{1,0:T(8,128)(2,1)S(1)} collective-permute-done((bf16[512,256]{1,0:T(8,128)(2,1)}, bf16[512,256]{1,0:T(8,128)(2,1)S(1)}, u32[]{:S(2)}, u32[]{:S(2)}) %collective-permute-start.39) | collective-permute-done | bytes 262176 | tf_op jit(solution)/shard_map/ppermute | solution.py:1183
  232.3 19.8 %attend_back.2 = (bf16[2048,768]{1,0:T(8,128)(2,1)}, f32[1,384]{1,0:T(1,128)}) custom-call(s32[18]{0:T(128)} %pad_add_fusion.info.refs_0_, f32[4]{0:T(128)} %multiply_power_fusion.refs_1_, bf16[2048,768]{1,0:T(8,128)(2,1)} %get-tuple-element.352.refs_2_, bf16[2048,256]{1,0:T(8,128)(2,1)} %get-tuple-element.276.refs_3_, ...), custom_call_target="tpu_custom_call" | custom-call | flops 10737418 | bytes 5242 | tf_op jit(solution)/shard_map/attend_back/pallas_call | solution.py:446
  253.4 2.0 fusion.1
  257.9 19.7 %attend_back.3 = (bf16[2048,768]{1,0:T(8,128)(2,1)}, f32[1,384]{1,0:T(1,128)}) custom-call(s32[18]{0:T(128)} %pad_add_fusion.info.refs_0_, f32[4]{0:T(128)} %multiply_power_fusion.refs_1_, bf16[2048,768]{1,0:T(8,128)(2,1)} %get-tuple-element.352.refs_2_, bf16[2048,256]{1,0:T(8,128)(2,1)} %get-tuple-element.276.refs_3_, ...), custom_call_target="tpu_custom_call", output_to_operand_aliasing={{0}: (9, {})} | custom-call | flops 10737418 | bytes 5242 | tf_op jit(solution)/shard_map/attend_back/pallas_call | solution.py:446
  277.9 1.6 collective-permute-start.47
  279.9 10.9 %joined_grad.1 = (bf16[1,144,1024]{2,1,0:T(8,128)(2,1)}, bf16[1,144,1024]{2,1,0:T(8,128)(2,1)}, bf16[1,144,1024]{2,1,0:T(8,128)(2,1)}, bf16[1,144,1024]{2,1,0:T(...) custom-call(s32[18]{0:T(128)} %pad_add_fusion.info.refs_0_, ...), custom_call_target="tpu_custom_call" | custom-call | flops 3221225 | bytes 11534 | tf_op jit(solution)/shard_map/joined_grad/pallas_call | solution.py:754
  291.9 1.6 collective-permute-start.50
  295.0 8.9 %last.1 = (bf16[512,1024]{1,0:T(8,128)(2,1)}, bf16[512,1024]{1,0:T(8,128)(2,1)}, bf16[2,512,1024]{2,1,0:T(8,128)(2,1)}) custom-call(s32[18]{0:T(128)} %pad_add_fusion.info.refs_0_, bf16[1024,768]{1,0:T(8,128)(2,1)} %get-tuple-element.367.weight, bf16[2048,768]{1,0:T(8,128)(2,1)} %get-tuple-element.399.refs_6_.right), custom_call_target="tpu_custom_call" | custom-call | flops 3221225 | bytes 11534 | tf_op jit(solution)/shard_map/last/pallas_call | solution.py:845
  306.2 2.3 collective-permute-done.53.gb
  308.5 1.8 fusion
  310.3 3.3 collective-permute-done.52.refs_3_
  317.2 3.5 add_convert_fusion
  320.7 2.4 collective-permute-done.54.refs_2_
  326.8 7.0 %collective-permute-done.56 = bf16[144,1024]{1,0:T(8,128)(2,1)S(1)} collective-permute-done((bf16[144,1024]{1,0:T(8,128)(2,1)S(1)}, bf16[144,1024]{1,0:T(8,128)(2,1)S(1)}, u32[]{:S(2)}, u32[]{:S(2)}) %collective-permute-start.56) | collective-permute-done | bytes 294944 | tf_op jit(solution)/shard_map/ppermute | solution.py:116
  335.0 3.5 collective-permute-done.58.gc
  339.7 3.0 end.1
  342.7 4.6 %feed_out.1 = (f32[128,4096]{1,0:T(8,128)}, f32[512,1024]{1,0:T(8,128)}) custom-call(s32[18]{0:T(128)} %pad_add_fusion.info.refs_0_, bf16[256,1024]{1,0:T(8,128)(2,1)} %copy-done.30, bf16[256,1024]{1,0:T(8,128)(2,1)} %copy-done.41, bf16[256,1024]{1,0:T(8,128)(2,1)} %copy-done.37, bf16[256,1024]{1,0:T(8,128)(2,1)} %copy-done.42), custom_call_target="tpu_custom_call" | custom-call | bytes 6291 | tf_op jit(solution)/shard_map/feed_out/pallas_call | solution.py:960
  349.8 3.4 joined_out.1
  (242 shorter events, 56.8 us)
Async XLA Ops:
  0.7 14.1 %collective-permute-start.2 = (bf16[512,1024]{1,0:T(8,128)(2,1)}, bf16[512,1024]{1,0:T(8,128)(2,1)}, u32[]{:S(2)}, u32[]{:S(2)}) collective-permute-start(bf16[512,1024]{1,0:T(8,128)(2,1)} %bitcast.68), channel_id=1, source_target_pairs={{0,8},{8,0},{16,24},{24,16},{1,9},{9,1},{17,25},{25,17},{2,10},{10... | collective-permute-start | bytes 3145736 | tf_op jit(solution)/shard_map/ppermute | solution.py:1029
  3.0 10.5 %collective-permute-start = (bf16[144,1024]{1,0:T(8,128)(2,1)}, bf16[144,1024]{1,0:T(8,128)(2,1)S(1)}, u32[]{:S(2)}, u32[]{:S(2)}) collective-permute-start(bf16[144,1024]{1,0:T(8,128)(2,1)} %first_pack.1), channel_id=1, source_target_pairs={{2,0},{4,2},{6,4},{7,6},{5,7},{3,5},{1,3},{0,1},{10,8},{12,10},{14... | collective-permute-start | bytes 884744 | tf_op jit(solution)/shard_map/ppermute | solution.py:119
  5.6 9.2 %collective-permute-start.1 = (bf16[144,1024]{1,0:T(8,128)(2,1)}, bf16[144,1024]{1,0:T(8,128)(2,1)S(1)}, u32[]{:S(2)}, u32[]{:S(2)}) collective-permute-start(bf16[144,1024]{1,0:T(8,128)(2,1)} %first_pack.1), channel_id=1, source_target_pairs={{0,2},{2,4},{4,6},{6,7},{7,5},{5,3},{3,1},{1,0},{8,10},{10,12},{12... | collective-permute-start | bytes 884744 | tf_op jit(solution)/shard_map/ppermute | solution.py:116
  14.8 14.9 %collective-permute-start.5 = (bf16[512,1024]{1,0:T(8,128)(2,1)S(1)}, bf16[512,1024]{1,0:T(8,128)(2,1)S(1)}, u32[]{:S(2)}, u32[]{:S(2)}) collective-permute-start(bf16[512,1024]{1,0:T(8,128)(2,1)S(1)} %bitcast.86), channel_id=1, source_target_pairs={{0,8},{8,0},{16,24},{24,16},{1,9},{9,1},{17,25},{25,17},{2,10},{10... | collective-permute-start | bytes 3145736 | tf_op jit(solution)/shard_map/ppermute | solution.py:1036
  14.9 14.8 %collective-permute-start.6 = (bf16[256,1024]{1,0:T(8,128)(2,1)S(1)}, bf16[256,1024]{1,0:T(8,128)(2,1)S(1)}, u32[]{:S(2)}, u32[]{:S(2)}) collective-permute-start(bf16[256,1024]{1,0:T(8,128)(2,1)S(1)} %slice_bitcast_fusion.1), channel_id=1, source_target_pairs={{0,16},{8,24},{16,0},{24,8},{1,17},{9,25},{17,1},{25,9},{2,18},{10... | collective-permute-start | bytes 1572872 | tf_op jit(solution)/shard_map/ppermute | solution.py:1030
  16.5 13.2 %collective-permute-start.3 = (bf16[144,1024]{1,0:T(8,128)(2,1)S(1)}, bf16[144,1024]{1,0:T(8,128)(2,1)S(1)}, u32[]{:S(2)}, u32[]{:S(2)}) collective-permute-start(bf16[144,1024]{1,0:T(8,128)(2,1)S(1)} %collective-permute-done), channel_id=1, source_target_pairs={{2,0},{4,2},{6,4},{7,6},{5,7},{3,5},{1,3},{0,1},{10,8},{12,10},{14... | collective-permute-start | bytes 884744 | tf_op jit(solution)/shard_map/ppermute | solution.py:119
  18.1 11.6 %collective-permute-start.4 = (bf16[144,1024]{1,0:T(8,128)(2,1)S(1)}, bf16[144,1024]{1,0:T(8,128)(2,1)S(1)}, u32[]{:S(2)}, u32[]{:S(2)}) collective-permute-start(bf16[144,1024]{1,0:T(8,128)(2,1)S(1)} %collective-permute-done.1), channel_id=1, source_target_pairs={{0,2},{2,4},{4,6},{6,7},{7,5},{5,3},{3,1},{1,0},{8,10},{10,12},{12... | collective-permute-start | bytes 884744 | tf_op jit(solution)/shard_map/ppermute | solution.py:116
  18.6 22.1 %collective-permute-start.9 = (bf16[256,1024]{1,0:T(8,128)(2,1)S(1)}, bf16[256,1024]{1,0:T(8,128)(2,1)}, u32[]{:S(2)}, u32[]{:S(2)}) collective-permute-start(bf16[256,1024]{1,0:T(8,128)(2,1)S(1)} %slice.20), channel_id=1, source_target_pairs={{0,16},{8,24},{16,0},{24,8},{1,17},{9,25},{17,1},{25,9},{2,18},{10... | collective-permute-start | bytes 1572872 | tf_op jit(solution)/shard_map/ppermute | solution.py:1035
  29.8 10.9 %collective-permute-start.10 = (bf16[256,1024]{1,0:T(8,128)(2,1)S(1)}, bf16[256,1024]{1,0:T(8,128)(2,1)S(1)}, u32[]{:S(2)}, u32[]{:S(2)}) collective-permute-start(bf16[256,1024]{1,0:T(8,128)(2,1)S(1)} %collective-permute-done.6.refs_2_), channel_id=1, source_target_pairs={{0,8},{8,0},{16,24},{24,16},{1,9},{9,1},{17,25},{25,17},{2,10},{10... | collective-permute-start | bytes 1572872 | tf_op jit(solution)/shard_map/ppermute | solution.py:1039
  29.8 10.8 %collective-permute-start.7 = (bf16[144,1024]{1,0:T(8,128)(2,1)S(1)}, bf16[144,1024]{1,0:T(8,128)(2,1)S(1)}, u32[]{:S(2)}, u32[]{:S(2)}) collective-permute-start(bf16[144,1024]{1,0:T(8,128)(2,1)S(1)} %collective-permute-done.3), channel_id=1, source_target_pairs={{2,0},{4,2},{6,4},{7,6},{5,7},{3,5},{1,3},{0,1},{10,8},{12,10},{14... | collective-permute-start | bytes 884744 | tf_op jit(solution)/shard_map/ppermute | solution.py:119
  31.5 9.2 %collective-permute-start.8 = (bf16[144,1024]{1,0:T(8,128)(2,1)S(1)}, bf16[144,1024]{1,0:T(8,128)(2,1)S(1)}, u32[]{:S(2)}, u32[]{:S(2)}) collective-permute-start(bf16[144,1024]{1,0:T(8,128)(2,1)S(1)} %collective-permute-done.4), channel_id=1, source_target_pairs={{0,2},{2,4},{4,6},{6,7},{7,5},{5,3},{3,1},{1,0},{8,10},{10,12},{12... | collective-permute-start | bytes 884744 | tf_op jit(solution)/shard_map/ppermute | solution.py:116
  41.1 13.2 %collective-permute-start.11 = (bf16[256,1024]{1,0:T(8,128)(2,1)}, bf16[256,1024]{1,0:T(8,128)(2,1)}, u32[]{:S(2)}, u32[]{:S(2)}) collective-permute-start(bf16[256,1024]{1,0:T(8,128)(2,1)} %collective-permute-done.9.refs_3_), channel_id=1, source_target_pairs={{0,8},{8,0},{16,24},{24,16},{1,9},{9,1},{17,25},{25,17},{2,10},{10... | collective-permute-start | bytes 1572872 | tf_op jit(solution)/shard_map/ppermute | solution.py:1042
  49.4 19.0 %collective-permute-start.13 = (bf16[256,1024]{1,0:T(8,128)(2,1)}, bf16[256,1024]{1,0:T(8,128)(2,1)}, u32[]{:S(2)}, u32[]{:S(2)}) collective-permute-start(bf16[256,1024]{1,0:T(8,128)(2,1)} %second_pack.1), channel_id=1, source_target_pairs={{2,0},{4,2},{6,4},{7,6},{5,7},{3,5},{1,3},{0,1},{10,8},{12,10},{14... | collective-permute-start | bytes 1572872 | tf_op jit(solution)/shard_map/ppermute | solution.py:119
  51.0 17.4 %collective-permute-start.14 = (bf16[256,1024]{1,0:T(8,128)(2,1)}, bf16[256,1024]{1,0:T(8,128)(2,1)}, u32[]{:S(2)}, u32[]{:S(2)}) collective-permute-start(bf16[256,1024]{1,0:T(8,128)(2,1)} %second_pack.1), channel_id=1, source_target_pairs={{0,2},{2,4},{4,6},{6,7},{7,5},{5,3},{3,1},{1,0},{8,10},{10,12},{12... | collective-permute-start | bytes 1572872 | tf_op jit(solution)/shard_map/ppermute | solution.py:116
  51.5 34.7 %collective-permute-start.19 = (bf16[512,1024]{1,0:T(8,128)(2,1)S(1)}, bf16[512,1024]{1,0:T(8,128)(2,1)S(1)}, u32[]{:S(2)}, u32[]{:S(2)}) collective-permute-start(bf16[512,1024]{1,0:T(8,128)(2,1)S(1)} %bitcast.87), channel_id=1, source_target_pairs={{0,16},{8,24},{16,0},{24,8},{1,17},{9,25},{17,1},{25,9},{2,18},{10... | collective-permute-start | bytes 3145736 | tf_op jit(solution)/shard_map/ppermute | solution.py:1043
  67.7 14.9 %collective-permute-start.17 = (bf16[1024,256]{1,0:T(8,128)(2,1)}, bf16[1024,256]{1,0:T(8,128)(2,1)}, u32[]{:S(2)}, u32[]{:S(2)}) collective-permute-start(bf16[1024,256]{1,0:T(8,128)(2,1)} %get-tuple-element.264.refs_4_), channel_id=1, source_target_pairs={{0,8},{8,0},{16,24},{24,16},{1,9},{9,1},{17,25},{25,17},{2,10},{10... | collective-permute-start | bytes 1572872 | tf_op jit(solution)/shard_map/ppermute | solution.py:73
  67.8 18.5 %collective-permute-start.18 = (bf16[1024,256]{1,0:T(8,128)(2,1)}, bf16[1024,256]{1,0:T(8,128)(2,1)}, u32[]{:S(2)}, u32[]{:S(2)}) collective-permute-start(bf16[1024,256]{1,0:T(8,128)(2,1)} %get-tuple-element.264.refs_4_), channel_id=1, source_target_pairs={{0,16},{8,24},{16,0},{24,8},{1,17},{9,25},{17,1},{25,9},{2,18},{10... | collective-permute-start | bytes 1572872 | tf_op jit(solution)/shard_map/ppermute | solution.py:73
  68.3 17.9 %collective-permute-start.15 = (bf16[256,1024]{1,0:T(8,128)(2,1)}, bf16[256,1024]{1,0:T(8,128)(2,1)S(1)}, u32[]{:S(2)}, u32[]{:S(2)}) collective-permute-start(bf16[256,1024]{1,0:T(8,128)(2,1)} %collective-permute-done.13), channel_id=1, source_target_pairs={{2,0},{4,2},{6,4},{7,6},{5,7},{3,5},{1,3},{0,1},{10,8},{12,10},{14... | collective-permute-start | bytes 1572872 | tf_op jit(solution)/shard_map/ppermute | solution.py:119
  69.9 16.3 %collective-permute-start.16 = (bf16[256,1024]{1,0:T(8,128)(2,1)}, bf16[256,1024]{1,0:T(8,128)(2,1)S(1)}, u32[]{:S(2)}, u32[]{:S(2)}) collective-permute-start(bf16[256,1024]{1,0:T(8,128)(2,1)} %collective-permute-done.14), channel_id=1, source_target_pairs={{0,2},{2,4},{4,6},{6,7},{7,5},{5,3},{3,1},{1,0},{8,10},{10,12},{12... | collective-permute-start | bytes 1572872 | tf_op jit(solution)/shard_map/ppermute | solution.py:116
  86.2 13.4 %collective-permute-start.20 = (bf16[256,1024]{1,0:T(8,128)(2,1)S(1)}, bf16[256,1024]{1,0:T(8,128)(2,1)S(1)}, u32[]{:S(2)}, u32[]{:S(2)}) collective-permute-start(bf16[256,1024]{1,0:T(8,128)(2,1)S(1)} %collective-permute-done.15), channel_id=1, source_target_pairs={{2,0},{4,2},{6,4},{7,6},{5,7},{3,5},{1,3},{0,1},{10,8},{12,10},{14... | collective-permute-start | bytes 1572872 | tf_op jit(solution)/shard_map/ppermute | solution.py:119
  87.9 11.8 %collective-permute-start.21 = (bf16[256,1024]{1,0:T(8,128)(2,1)S(1)}, bf16[256,1024]{1,0:T(8,128)(2,1)S(1)}, u32[]{:S(2)}, u32[]{:S(2)}) collective-permute-start(bf16[256,1024]{1,0:T(8,128)(2,1)S(1)} %collective-permute-done.16), channel_id=1, source_target_pairs={{0,2},{2,4},{4,6},{6,7},{7,5},{5,3},{3,1},{1,0},{8,10},{10,12},{12... | collective-permute-start | bytes 1572872 | tf_op jit(solution)/shard_map/ppermute | solution.py:116
  88.5 11.3 %collective-permute-start.22 = (bf16[1024,256]{1,0:T(8,128)(2,1)}, bf16[1024,256]{1,0:T(8,128)(2,1)S(1)}, u32[]{:S(2)}, u32[]{:S(2)}) collective-permute-start(bf16[1024,256]{1,0:T(8,128)(2,1)} %collective-permute-done.18.refs_6_), channel_id=1, source_target_pairs={{0,8},{8,0},{16,24},{24,16},{1,9},{9,1},{17,25},{25,17},{2,10},{10... | collective-permute-start | bytes 1572872 | tf_op jit(solution)/shard_map/ppermute | solution.py:1079
  101.4 17.4 %collective-permute-start.23 = (bf16[512,1024]{1,0:T(8,128)(2,1)S(1)}, bf16[512,1024]{1,0:T(8,128)(2,1)S(1)}, u32[]{:S(2)}, u32[]{:S(2)}) collective-permute-start(bf16[512,1024]{1,0:T(8,128)(2,1)S(1)} %collective-permute-done.19.ca.refs_4_), channel_id=1, source_target_pairs={{0,8},{8,0},{16,24},{24,16},{1,9},{9,1},{17,25},{25,17},{2,10},{10... | collective-permute-start | bytes 3145736 | tf_op jit(solution)/shard_map/ppermute | solution.py:1084
  101.9 16.9 %collective-permute-start.24 = (bf16[256,1024]{1,0:T(8,128)(2,1)}, bf16[256,1024]{1,0:T(8,128)(2,1)S(1)}, u32[]{:S(2)}, u32[]{:S(2)}) collective-permute-start(bf16[256,1024]{1,0:T(8,128)(2,1)} %copy-done.28), channel_id=1, source_target_pairs={{0,2},{2,4},{4,6},{6,7},{7,5},{5,3},{3,1},{1,0},{8,10},{10,12},{12... | collective-permute-start | bytes 1572872 | tf_op jit(solution)/shard_map/ppermute | solution.py:116
  106.4 12.4 %collective-permute-start.27 = (bf16[512,256]{1,0:T(8,128)(2,1)S(1)}, bf16[512,256]{1,0:T(8,128)(2,1)S(1)}, u32[]{:S(2)}, u32[]{:S(2)}) collective-permute-start(bf16[512,256]{1,0:T(8,128)(2,1)S(1)} %get-tuple-element.462), channel_id=1, source_target_pairs={{0,24},{8,16},{16,8},{24,0},{1,25},{9,17},{17,9},{25,1},{2,26},{10... | collective-permute-start | bytes 786440 | tf_op jit(solution)/shard_map/ppermute | solution.py:1088
  126.9 25.6 %collective-permute-start.29 = (bf16[512,1024]{1,0:T(8,128)(2,1)}, bf16[512,1024]{1,0:T(8,128)(2,1)S(1)}, u32[]{:S(2)}, u32[]{:S(2)}) collective-permute-start(bf16[512,1024]{1,0:T(8,128)(2,1)} %get-tuple-element.283.sa.refs_6_), channel_id=1, source_target_pairs={{0,16},{8,24},{16,0},{24,8},{1,17},{9,25},{17,1},{25,9},{2,18},{10... | collective-permute-start | bytes 3145736 | tf_op jit(solution)/shard_map/ppermute | solution.py:1100
  152.5 21.4 %collective-permute-start.32 = (bf16[512,1024]{1,0:T(8,128)(2,1)}, bf16[512,1024]{1,0:T(8,128)(2,1)S(1)}, u32[]{:S(2)}, u32[]{:S(2)}) collective-permute-start(bf16[512,1024]{1,0:T(8,128)(2,1)} %get-tuple-element.302), channel_id=1, source_target_pairs={{0,8},{8,0},{16,24},{24,16},{1,9},{9,1},{17,25},{25,17},{2,10},{10... | collective-permute-start | bytes 3145736 | tf_op jit(solution)/shard_map/ppermute | solution.py:1116
  153.0 21.0 %collective-permute-start.33 = (bf16[512,1024]{1,0:T(8,128)(2,1)}, bf16[512,1024]{1,0:T(8,128)(2,1)}, u32[]{:S(2)}, u32[]{:S(2)}) collective-permute-start(bf16[512,1024]{1,0:T(8,128)(2,1)} %get-tuple-element.303), channel_id=1, source_target_pairs={{0,8},{8,0},{16,24},{24,16},{1,9},{9,1},{17,25},{25,17},{2,10},{10... | collective-permute-start | bytes 3145736 | tf_op jit(solution)/shard_map/ppermute | solution.py:1117
  176.9 24.8 %collective-permute-start.36 = (bf16[512,1024]{1,0:T(8,128)(2,1)}, bf16[512,1024]{1,0:T(8,128)(2,1)S(1)}, u32[]{:S(2)}, u32[]{:S(2)}) collective-permute-start(bf16[512,1024]{1,0:T(8,128)(2,1)} %get-tuple-element.310), channel_id=1, source_target_pairs={{0,8},{8,0},{16,24},{24,16},{1,9},{9,1},{17,25},{25,17},{2,10},{10... | collective-permute-start | bytes 3145736 | tf_op jit(solution)/shard_map/ppermute | solution.py:1129
  179.5 25.7 %collective-permute-start.35 = (bf16[512,1024]{1,0:T(8,128)(2,1)}, bf16[512,1024]{1,0:T(8,128)(2,1)}, u32[]{:S(2)}, u32[]{:S(2)}) collective-permute-start(bf16[512,1024]{1,0:T(8,128)(2,1)} %add_pairs.8), channel_id=1, source_target_pairs={{0,16},{8,24},{16,0},{24,8},{1,17},{9,25},{17,1},{25,9},{2,18},{10... | collective-permute-start | bytes 3145736 | tf_op jit(solution)/shard_map/ppermute | solution.py:1128
  200.1 21.0 %collective-permute-start.31 = (bf16[256,1024]{1,0:T(8,128)(2,1)}, bf16[256,1024]{1,0:T(8,128)(2,1)S(1)}, u32[]{:S(2)}, u32[]{:S(2)}) collective-permute-start(bf16[256,1024]{1,0:T(8,128)(2,1)} %bitcast.119), channel_id=1, source_target_pairs={{0,2},{2,4},{4,6},{6,7},{7,5},{5,3},{3,1},{1,0},{8,10},{10,12},{12... | collective-permute-start | bytes 1572872 | tf_op jit(solution)/shard_map/ppermute | solution.py:116
  213.4 9.4 %collective-permute-start.38 = (bf16[512,256]{1,0:T(8,128)(2,1)}, bf16[512,256]{1,0:T(8,128)(2,1)S(1)}, u32[]{:S(2)}, u32[]{:S(2)}) collective-permute-start(bf16[512,256]{1,0:T(8,128)(2,1)} %get-tuple-element.322), channel_id=1, source_target_pairs={{0,16},{8,24},{16,0},{24,8},{1,17},{9,25},{17,1},{25,9},{2,18},{10... | collective-permute-start | bytes 786440 | tf_op jit(solution)/shard_map/ppermute | solution.py:1183
  214.9 12.5 %collective-permute-start.39 = (bf16[512,256]{1,0:T(8,128)(2,1)}, bf16[512,256]{1,0:T(8,128)(2,1)S(1)}, u32[]{:S(2)}, u32[]{:S(2)}) collective-permute-start(bf16[512,256]{1,0:T(8,128)(2,1)} %get-tuple-element.323), channel_id=1, source_target_pairs={{0,24},{8,16},{16,8},{24,0},{1,25},{9,17},{17,9},{25,1},{2,26},{10... | collective-permute-start | bytes 786440 | tf_op jit(solution)/shard_map/ppermute | solution.py:1183
  228.3 23.9 %collective-permute-start.42 = (bf16[2,1024,256]{2,1,0:T(8,128)(2,1)}, bf16[2,1024,256]{2,1,0:T(8,128)(2,1)}, u32[]{:S(2)}, u32[]{:S(2)}) collective-permute-start(bf16[2,1024,256]{2,1,0:T(8,128)(2,1)} %get-tuple-element.340), channel_id=1, source_target_pairs={{0,8},{8,0},{16,24},{24,16},{1,9},{9,1},{17,25},{25,17},{2,10},{10... | collective-permute-start | bytes 3145736 | tf_op jit(solution)/shard_map/ppermute | solution.py:1191
  228.6 23.5 %collective-permute-start.41 = (bf16[256,1024]{1,0:T(8,128)(2,1)}, bf16[256,1024]{1,0:T(8,128)(2,1)S(1)}, u32[]{:S(2)}, u32[]{:S(2)}) collective-permute-start(bf16[256,1024]{1,0:T(8,128)(2,1)} %bitcast.31), channel_id=1, source_target_pairs={{2,0},{4,2},{6,4},{7,6},{5,7},{3,5},{1,3},{0,1},{10,8},{12,10},{14... | collective-permute-start | bytes 1572872 | tf_op jit(solution)/shard_map/ppermute | solution.py:119
  229.6 22.5 %collective-permute-start.40 = (bf16[256,1024]{1,0:T(8,128)(2,1)S(1)}, bf16[256,1024]{1,0:T(8,128)(2,1)S(1)}, u32[]{:S(2)}, u32[]{:S(2)}) collective-permute-start(bf16[256,1024]{1,0:T(8,128)(2,1)S(1)} %add_pairs.10), channel_id=1, source_target_pairs={{0,2},{2,4},{4,6},{6,7},{7,5},{5,3},{3,1},{1,0},{8,10},{10,12},{12... | collective-permute-start | bytes 1572872 | tf_op jit(solution)/shard_map/ppermute | solution.py:116
  230.8 46.7 %collective-permute-start.46 = (bf16[512,1024]{1,0:T(8,128)(2,1)S(1)}, bf16[512,1024]{1,0:T(8,128)(2,1)}, u32[]{:S(2)}, u32[]{:S(2)}) collective-permute-start(bf16[512,1024]{1,0:T(8,128)(2,1)S(1)} %add_pairs.9), channel_id=1, source_target_pairs={{0,16},{8,24},{16,0},{24,8},{1,17},{9,25},{17,1},{25,9},{2,18},{10... | collective-permute-start | bytes 3145736 | tf_op jit(solution)/shard_map/ppermute | solution.py:1189
  255.3 22.2 %collective-permute-start.43 = (bf16[256,1024]{1,0:T(8,128)(2,1)}, bf16[256,1024]{1,0:T(8,128)(2,1)S(1)}, u32[]{:S(2)}, u32[]{:S(2)}) collective-permute-start(bf16[256,1024]{1,0:T(8,128)(2,1)} %get-tuple-element.350), channel_id=1, source_target_pairs={{0,2},{2,4},{4,6},{6,7},{7,5},{5,3},{3,1},{1,0},{8,10},{10,12},{12... | collective-permute-start | bytes 1572872 | tf_op jit(solution)/shard_map/ppermute | solution.py:116
  256.9 20.6 %collective-permute-start.44 = (bf16[256,1024]{1,0:T(8,128)(2,1)}, bf16[256,1024]{1,0:T(8,128)(2,1)S(1)}, u32[]{:S(2)}, u32[]{:S(2)}) collective-permute-start(bf16[256,1024]{1,0:T(8,128)(2,1)} %get-tuple-element.351), channel_id=1, source_target_pairs={{2,0},{4,2},{6,4},{7,6},{5,7},{3,5},{1,3},{0,1},{10,8},{12,10},{14... | collective-permute-start | bytes 1572872 | tf_op jit(solution)/shard_map/ppermute | solution.py:119
  257.4 20.2 %collective-permute-start.45 = (bf16[1024,256]{1,0:T(8,128)(2,1)}, bf16[1024,256]{1,0:T(8,128)(2,1)S(1)}, u32[]{:S(2)}, u32[]{:S(2)}) collective-permute-start(bf16[1024,256]{1,0:T(8,128)(2,1)} %fusion.1), channel_id=1, source_target_pairs={{0,16},{8,24},{16,0},{24,8},{1,17},{9,25},{17,1},{25,9},{2,18},{10... | collective-permute-start | bytes 1572872 | tf_op jit(solution)/shard_map/ppermute | solution.py:1203
  277.9 13.0 %collective-permute-start.47 = (bf16[256,1024]{1,0:T(8,128)(2,1)S(1)}, bf16[256,1024]{1,0:T(8,128)(2,1)S(1)}, u32[]{:S(2)}, u32[]{:S(2)}) collective-permute-start(bf16[256,1024]{1,0:T(8,128)(2,1)S(1)} %get-tuple-element.364), channel_id=1, source_target_pairs={{0,2},{2,4},{4,6},{6,7},{7,5},{5,3},{3,1},{1,0},{8,10},{10,12},{12... | collective-permute-start | bytes 1572872 | tf_op jit(solution)/shard_map/ppermute | solution.py:116
  279.5 12.1 %collective-permute-start.48 = (bf16[256,1024]{1,0:T(8,128)(2,1)S(1)}, bf16[256,1024]{1,0:T(8,128)(2,1)S(1)}, u32[]{:S(2)}, u32[]{:S(2)}) collective-permute-start(bf16[256,1024]{1,0:T(8,128)(2,1)S(1)} %get-tuple-element.365), channel_id=1, source_target_pairs={{2,0},{4,2},{6,4},{7,6},{5,7},{3,5},{1,3},{0,1},{10,8},{12,10},{14... | collective-permute-start | bytes 1572872 | tf_op jit(solution)/shard_map/ppermute | solution.py:119
  291.9 12.1 %collective-permute-start.50 = (bf16[256,1024]{1,0:T(8,128)(2,1)S(1)}, bf16[256,1024]{1,0:T(8,128)(2,1)S(1)}, u32[]{:S(2)}, u32[]{:S(2)}) collective-permute-start(bf16[256,1024]{1,0:T(8,128)(2,1)S(1)} %fusion.3.refs_0_), channel_id=1, source_target_pairs={{0,16},{8,24},{16,0},{24,8},{1,17},{9,25},{17,1},{25,9},{2,18},{10... | collective-permute-start | bytes 1572872 | tf_op jit(solution)/shard_map/ppermute | solution.py:1231
  293.5 10.5 %collective-permute-start.49 = (bf16[144,1024]{1,0:T(8,128)(2,1)S(1)}, bf16[144,1024]{1,0:T(8,128)(2,1)S(1)}, u32[]{:S(2)}, u32[]{:S(2)}) collective-permute-start(bf16[144,1024]{1,0:T(8,128)(2,1)S(1)} %bitcast.121), channel_id=1, source_target_pairs={{0,2},{2,4},{4,6},{6,7},{7,5},{5,3},{3,1},{1,0},{8,10},{10,12},{12... | collective-permute-start | bytes 884744 | tf_op jit(solution)/shard_map/ppermute | solution.py:116
  304.2 9.4 %collective-permute-start.52 = (bf16[144,1024]{1,0:T(8,128)(2,1)S(1)}, bf16[144,1024]{1,0:T(8,128)(2,1)S(1)}, u32[]{:S(2)}, u32[]{:S(2)}) collective-permute-start(bf16[144,1024]{1,0:T(8,128)(2,1)S(1)} %bitcast.120), channel_id=1, source_target_pairs={{2,0},{4,2},{6,4},{7,6},{5,7},{3,5},{1,3},{0,1},{10,8},{12,10},{14... | collective-permute-start | bytes 884744 | tf_op jit(solution)/shard_map/ppermute | solution.py:119
  313.9 24.6 %collective-permute-start.58 = (bf16[512,1024]{1,0:T(8,128)(2,1)S(1)}, bf16[512,1024]{1,0:T(8,128)(2,1)S(1)}, u32[]{:S(2)}, u32[]{:S(2)}) collective-permute-start(bf16[512,1024]{1,0:T(8,128)(2,1)S(1)} %fusion), channel_id=1, source_target_pairs={{0,16},{8,24},{16,0},{24,8},{1,17},{9,25},{17,1},{25,9},{2,18},{10... | collective-permute-start | bytes 3145736 | tf_op jit(solution)/shard_map/ppermute | solution.py:1250
  324.2 10.8 %collective-permute-start.59 = (bf16[256,1024]{1,0:T(8,128)(2,1)S(1)}, bf16[256,1024]{1,0:T(8,128)(2,1)S(1)}, u32[]{:S(2)}, u32[]{:S(2)}) collective-permute-start(bf16[256,1024]{1,0:T(8,128)(2,1)S(1)} %fusion.3.refs_0_), channel_id=1, source_target_pairs={{0,8},{8,0},{16,24},{24,16},{1,9},{9,1},{17,25},{25,17},{2,10},{10... | collective-permute-start | bytes 1572872 | tf_op jit(solution)/shard_map/ppermute | solution.py:1259
  324.3 10.7 %collective-permute-start.60 = (bf16[256,1024]{1,0:T(8,128)(2,1)S(1)}, bf16[256,1024]{1,0:T(8,128)(2,1)S(1)}, u32[]{:S(2)}, u32[]{:S(2)}) collective-permute-start(bf16[256,1024]{1,0:T(8,128)(2,1)S(1)} %collective-permute-done.50.refs_2_), channel_id=1, source_target_pairs={{0,8},{8,0},{16,24},{24,16},{1,9},{9,1},{17,25},{25,17},{2,10},{10... | collective-permute-start | bytes 1572872 | tf_op jit(solution)/shard_map/ppermute | solution.py:1260
  (78 other events, 824.7 us)

commit v6 on v5

--- a/solution.py
+++ b/solution.py
@@ -1244,10 +1244,10 @@
         joined_ring.send()
         got = lax.ppermute(sent, "seq", pairs(ns, 1))
         far = add16(normed_parts[1], got[1])
+        norm_b = lax.ppermute(far, "seq", pairs(ns, 2))
         (far,) = joined_ring.take(far)
         joined_ring.ahead, joined_ring.back, far = tie(joined_ring.ahead, joined_ring.back, far)
         joined_ring.send()
-        norm_b = lax.ppermute(far, "seq", pairs(ns, 2))
         out_b, out_parts[0], _ = tie(out_b, out_parts[0], far)
         out_terms = out_parts[0].astype(F32) + near_out.astype(F32) + out_b.astype(F32)
         layer_output = (resid + out_terms + vecs[11:12]).astype(BF)

time: 359 us -> 356 us (level)
  transfers between devices with their start and end apart: 64 -> 64, of which waited for: 25 -> 25; matrix products, arithmetic and copies ran while one was open for 3% -> 3% of each run, Pallas kernels for 49% -> 50%
where the time goes in v6:
time: 356 us; the launch traced here: 350 us
  Pallas kernels  186 us (52%)
  waiting for transfers between devices  93.5 us (26%)
  starting transfers between devices  50.8 us (14%)
  local copies, waits for them, and re-layouts  9.21 us (3%)
  other arithmetic  8.77 us (2%)
    pallas_call x2, Pallas kernels, attend_back(): pl.pallas_call(kernel, grid=(1,), in_specs=[smem, smem, wide, narrow, nar...  39.5 us
    pallas_call x2, Pallas kernels, feed_call(): pl.pallas_call(functools.partial(feed_kernel, nt, nb, rows, units, live),...  32.5 us
    pallas_call x2, Pallas kernels, attend(): pl.pallas_call(kernel, grid=(1,), in_specs=[smem, smem, pl.BlockSpec((cou...  22.4 us
    ppermute x16, waiting for transfers between devices, ahead(): return lax.ppermute(value, 'batch', self.forward)  19.6 us
    pallas_call x1, Pallas kernels, feed_grad_call(): pl.pallas_call(functools.partial(feed_grad_kernel, ns, nb, rows, units, s...  19 us
    ppermute x6, waiting for transfers between devices, body(): lax.ppermute(block, 'seq', pairs(ns, rel))  18.4 us
    ppermute x16, starting transfers between devices, ahead(): return lax.ppermute(value, 'batch', self.forward)  16.6 us
    ppermute x12, starting transfers between devices, back(): return lax.ppermute(value, 'batch', self.backward)  14.1 us
  transfers between devices with their start and end apart: 64, of which 25 were waited for; matrix products, arithmetic and copies ran while one was open for 3% of the time, Pallas kernels for 50%

profile of v6, /device:TPU:0, one launch (start us, length us, event | category | flops | bytes accessed | tf_op | source)
XLA Modules:
  0.0 350.1 jit_solution(4001760587262434552)
XLA Ops:
  1.2 1.8 first_pack.1
  3.0 2.6 collective-permute-start
  5.7 2.2 second_pack.1
  7.8 5.6 %collective-permute-done = bf16[144,1024]{1,0:T(8,128)(2,1)S(1)} collective-permute-done((bf16[144,1024]{1,0:T(8,128)(2,1)}, bf16[144,1024]{1,0:T(8,128)(2,1)S(1)}, u32[]{:S(2)}, u32[]{:S(2)}) %collective-permute-start) | collective-permute-done | bytes 294944 | tf_op jit(solution)/shard_map/ppermute | solution.py:119
  14.9 1.6 collective-permute-start.6
  19.2 10.6 %collective-permute-done.6.refs_2_ = bf16[256,1024]{1,0:T(8,128)(2,1)S(1)} collective-permute-done((bf16[256,1024]{1,0:T(8,128)(2,1)S(1)}, bf16[256,1024]{1,0:T(8,128)(2,1)S(1)}, u32[]{:S(2)}, u32[]{:S(2)}) %collective-permute-start.6) | collective-permute-done | bytes 524320 | tf_op jit(solution)/shard_map/ppermute | solution.py:1030
  29.8 1.6 collective-permute-start.7
  31.9 8.7 %collective-permute-done.9.refs_3_ = bf16[256,1024]{1,0:T(8,128)(2,1)} collective-permute-done((bf16[256,1024]{1,0:T(8,128)(2,1)S(1)}, bf16[256,1024]{1,0:T(8,128)(2,1)}, u32[]{:S(2)}, u32[]{:S(2)}) %collective-permute-start.9) | collective-permute-done | bytes 524320 | tf_op jit(solution)/shard_map/ppermute | solution.py:1035
  41.1 8.2 %collective-permute-done.12 = bf16[144,1024]{1,0:T(8,128)(2,1)S(1)} collective-permute-done((bf16[144,1024]{1,0:T(8,128)(2,1)S(1)}, bf16[144,1024]{1,0:T(8,128)(2,1)S(1)}, u32[]{:S(2)}, u32[]{:S(2)}) %collective-permute-start.12) | collective-permute-done | bytes 294944 | tf_op jit(solution)/shard_map/ppermute | solution.py:116
  51.5 1.6 collective-permute-start.19
  54.4 13.3 %first.1 = (bf16[2048,1024]{1,0:T(8,128)(2,1)}, bf16[2048,768]{1,0:T(8,128)(2,1)}, bf16[1024,768]{1,0:T(8,128)(2,1)}, bf16[1024,256]{1,0:T(8,128)(2,1)}, f32[16,1024]{1,0:T(8,128)}) custom-call(s32[18]{0:T(128)} %pad_add_fusion.info.refs_0_, bf16[512,1024]{1,0:T(8,128)(2,1)} %bitcast.69, bf16[512,1024]{1,0:T(8,128)(2,1)} %collective-permute-done.2.refs_1_, ...), custom_call_target="tpu_custom_call" | custom-call | flops 3221225 | bytes 11534 | tf_op jit(solution)/shard_map/first/pallas_call | solution.py:264
  71.3 11.2 %attend.2 = (bf16[2048,256]{1,0:T(8,128)(2,1)}, f32[2048,256]{1,0:T(8,128)}) custom-call(s32[18]{0:T(128)} %pad_add_fusion.info.refs_0_, f32[4]{0:T(128)} %multiply_power_fusion.refs_1_, bf16[2048,768]{1,0:T(8,128)(2,1)} %get-tuple-element.348.refs_2_), custom_call_target="tpu_custom_call" | custom-call | flops 4294967 | bytes 2621 | tf_op jit(solution)/shard_map/attend/pallas_call | solution.py:362
  82.5 3.7 %collective-permute-done.18.refs_6_ = bf16[1024,256]{1,0:T(8,128)(2,1)} collective-permute-done((bf16[1024,256]{1,0:T(8,128)(2,1)}, bf16[1024,256]{1,0:T(8,128)(2,1)}, u32[]{:S(2)}, u32[]{:S(2)}) %collective-permute-start.18) | collective-permute-done | bytes 524320 | tf_op jit(solution)/shard_map/ppermute | solution.py:73
  86.2 1.6 collective-permute-start.20
  88.5 11.2 %attend.3 = (bf16[2048,256]{1,0:T(8,128)(2,1)}, f32[2048,256]{1,0:T(8,128)}) custom-call(s32[18]{0:T(128)} %pad_add_fusion.info.refs_0_, f32[4]{0:T(128)} %multiply_power_fusion.refs_1_, bf16[2048,768]{1,0:T(8,128)(2,1)} %get-tuple-element.348.refs_2_, bf16[2048,256]{1,0:T(8,128)(2,1)} %get-tuple-element.263.refs_3_, ...), custom_call_target="tpu_custom_call", output_to_operand_aliasing={{0}: (3, {}), {1}: (4, {})} | custom-call | flops 4294967 | bytes 2621 | tf_op jit(solution)/shard_map/attend/pallas_call | solution.py:362
  102.9 1.9 constant_dynamic-slice_fusion
  106.7 7.2 %collective-permute-done.26.refs_2_ = bf16[512,256]{1,0:T(8,128)(2,1)S(1)} collective-permute-done((bf16[512,256]{1,0:T(8,128)(2,1)S(1)}, bf16[512,256]{1,0:T(8,128)(2,1)S(1)}, u32[]{:S(2)}, u32[]{:S(2)}) %collective-permute-start.26) | collective-permute-done | bytes 262176 | tf_op jit(solution)/shard_map/ppermute | solution.py:1088
  114.0 4.8 %collective-permute-done.27.refs_3_ = bf16[512,256]{1,0:T(8,128)(2,1)S(1)} collective-permute-done((bf16[512,256]{1,0:T(8,128)(2,1)S(1)}, bf16[512,256]{1,0:T(8,128)(2,1)S(1)}, u32[]{:S(2)}, u32[]{:S(2)}) %collective-permute-start.27) | collective-permute-done | bytes 262176 | tf_op jit(solution)/shard_map/ppermute | solution.py:1088
  119.5 7.1 %middle.1 = (bf16[512,1024]{1,0:T(8,128)(2,1)}, f32[512,1024]{1,0:T(8,128)}, bf16[512,1024]{1,0:T(8,128)(2,1)}, bf16[1024,1024]{1,0:T(8,128)(2,1)}) custom-call(s32[18]{0:T(128)} %pad_add_fusion.info.refs_0_, bf16[512,1024]{1,0:T(8,128)(2,1)} %bitcast.70, f32[16,1024]{1,0:T(8,128)} %get-tuple-element.253.vecs.ebias, ...), custom_call_target="tpu_custom_call" | custom-call | flops 1073741 | bytes 10485 | tf_op jit(solution)/shard_map/middle/pallas_call | solution.py:489
  130.6 16.2 %feed.2 = (bf16[1024,1024]{1,0:T(8,128)(2,1)}, bf16[1024,1024]{1,0:T(8,128)(2,1)}, bf16[512,1024]{1,0:T(8,128)(2,1)}, bf16[512,1024]{1,0:T(8,128)(2,1)}, bf16[51...) custom-call(s32[18]{0:T(128)} %pad_add_fusion.info.refs_0_, ...), custom_call_target="tpu_custom_call" | custom-call | flops 8589934 | bytes 16777 | tf_op jit(solution)/shard_map/feed/pallas_call | solution.py:568
  146.8 5.7 %collective-permute-done.29.sa.refs_8_ = bf16[512,1024]{1,0:T(8,128)(2,1)S(1)} collective-permute-done((bf16[512,1024]{1,0:T(8,128)(2,1)}, bf16[512,1024]{1,0:T(8,128)(2,1)S(1)}, u32[]{:S(2)}, u32[]{:S(2)}) %collective-permute-start.29) | collective-permute-done | bytes 1048608 | tf_op jit(solution)/shard_map/ppermute | solution.py:1100
  153.0 3.6 %collective-permute-done.30.sb.refs_9_ = bf16[512,1024]{1,0:T(8,128)(2,1)S(1)} collective-permute-done((bf16[512,1024]{1,0:T(8,128)(2,1)S(1)}, bf16[512,1024]{1,0:T(8,128)(2,1)S(1)}, u32[]{:S(2)}, u32[]{:S(2)}) %collective-permute-start.30) | collective-permute-done | bytes 1048608 | tf_op jit(solution)/shard_map/ppermute | solution.py:1114
  157.6 16.3 %feed.3 = (bf16[1024,1024]{1,0:T(8,128)(2,1)}, bf16[1024,1024]{1,0:T(8,128)(2,1)}, bf16[512,1024]{1,0:T(8,128)(2,1)}, bf16[512,1024]{1,0:T(8,128)(2,1)}, bf16[51...) custom-call(s32[18]{0:T(128)} %pad_add_fusion.info.refs_0_, bf16[512,1024]{1,0:T(8,128)(2,1)} %copy-done.23, ...), custom_call_target="tpu_custom_call" | custom-call | flops 8589934 | bytes 16777 | tf_op jit(solution)/shard_map/feed/pallas_call | solution.py:568
  174.2 2.7 collective-permute-done.34.refs_1_
  181.1 19.0 %feed_grad.1 = (bf16[1,256,1024]{2,1,0:T(8,128)(2,1)}, bf16[1,256,1024]{2,1,0:T(8,128)(2,1)}, bf16[1,256,1024]{2,1,0:T(8,128)(2,1)}, bf16[1,256,1024]{2,1,0:T(8,...) custom-call(s32[18]{0:T(128)} %pad_add_fusion.info.refs_0_, ...), custom_call_target="tpu_custom_call" | custom-call | flops 8589934 | bytes 20971 | tf_op jit(solution)/shard_map/feed_grad/pallas_call | solution.py:637
  200.1 1.6 collective-permute-start.31
  202.0 3.3 collective-permute-done.35.gc
  205.3 8.0 %turn.1 = (f32[512,1024]{1,0:T(8,128)}, bf16[512,1024]{1,0:T(8,128)(2,1)}, bf16[512,256]{1,0:T(8,128)(2,1)}, bf16[512,256]{1,0:T(8,128)(2,1)}, bf16[512,256]{1,0...) custom-call(s32[18]{0:T(128)} %pad_add_fusion.info.refs_0_, bf16[512,1024]{1,0:T(8,128)(2,1)} %get-tuple-element.296.ga, ...), custom_call_target="tpu_custom_call" | custom-call | flops 1073741 | bytes 10485 | tf_op jit(solution)/shard_map/turn/pallas_call | solution.py:801
  215.2 5.9 %split_grad.1 = (bf16[1024,256]{1,0:T(8,128)(2,1)}, bf16[1024,256]{1,0:T(8,128)(2,1)}, bf16[2,1024,256]{2,1,0:T(8,128)(2,1)}) custom-call(s32[18]{0:T(128)} %pad_add_fusion.info.refs_0_, bf16[512,1024]{1,0:T(8,128)(2,1)} %get-tuple-element.311.left, bf16[512,1024]{1,0:T(8,128)(2,1)} %get-tuple-element.312.right), custom_call_target="tpu_custom_call" | custom-call | flops 1073741 | bytes 6291 | tf_op jit(solution)/shard_map/split_grad/pallas_call | solution.py:683
  221.1 1.6 collective-permute-done.38.refs_7_
  222.7 4.7 %collective-permute-done.39.refs_8_ = bf16[512,256]{1,0:T(8,128)(2,1)S(1)} collective-permute-done((bf16[512,256]{1,0:T(8,128)(2,1)}, bf16[512,256]{1,0:T(8,128)(2,1)S(1)}, u32[]{:S(2)}, u32[]{:S(2)}) %collective-permute-start.39) | collective-permute-done | bytes 262176 | tf_op jit(solution)/shard_map/ppermute | solution.py:1183
  232.3 19.8 %attend_back.2 = (bf16[2048,768]{1,0:T(8,128)(2,1)}, f32[1,384]{1,0:T(1,128)}) custom-call(s32[18]{0:T(128)} %pad_add_fusion.info.refs_0_, f32[4]{0:T(128)} %multiply_power_fusion.refs_1_, bf16[2048,768]{1,0:T(8,128)(2,1)} %get-tuple-element.348.refs_2_, bf16[2048,256]{1,0:T(8,128)(2,1)} %get-tuple-element.272.refs_3_, ...), custom_call_target="tpu_custom_call" | custom-call | flops 10737418 | bytes 5242 | tf_op jit(solution)/shard_map/attend_back/pallas_call | solution.py:446
  253.4 2.0 fusion.1
  257.9 19.7 %attend_back.3 = (bf16[2048,768]{1,0:T(8,128)(2,1)}, f32[1,384]{1,0:T(1,128)}) custom-call(s32[18]{0:T(128)} %pad_add_fusion.info.refs_0_, f32[4]{0:T(128)} %multiply_power_fusion.refs_1_, bf16[2048,768]{1,0:T(8,128)(2,1)} %get-tuple-element.348.refs_2_, bf16[2048,256]{1,0:T(8,128)(2,1)} %get-tuple-element.272.refs_3_, ...), custom_call_target="tpu_custom_call", output_to_operand_aliasing={{0}: (9, {})} | custom-call | flops 10737418 | bytes 5242 | tf_op jit(solution)/shard_map/attend_back/pallas_call | solution.py:446
  277.9 1.6 collective-permute-start.47
  279.9 10.9 %joined_grad.1 = (bf16[1,144,1024]{2,1,0:T(8,128)(2,1)}, bf16[1,144,1024]{2,1,0:T(8,128)(2,1)}, bf16[1,144,1024]{2,1,0:T(8,128)(2,1)}, bf16[1,144,1024]{2,1,0:T(...) custom-call(s32[18]{0:T(128)} %pad_add_fusion.info.refs_0_, ...), custom_call_target="tpu_custom_call" | custom-call | flops 3221225 | bytes 11534 | tf_op jit(solution)/shard_map/joined_grad/pallas_call | solution.py:754
  291.9 1.6 collective-permute-start.50
  295.0 8.9 %last.1 = (bf16[512,1024]{1,0:T(8,128)(2,1)}, bf16[512,1024]{1,0:T(8,128)(2,1)}, bf16[2,512,1024]{2,1,0:T(8,128)(2,1)}) custom-call(s32[18]{0:T(128)} %pad_add_fusion.info.refs_0_, bf16[1024,768]{1,0:T(8,128)(2,1)} %get-tuple-element.363.weight, bf16[2048,768]{1,0:T(8,128)(2,1)} %get-tuple-element.395.refs_6_.right), custom_call_target="tpu_custom_call" | custom-call | flops 3221225 | bytes 11534 | tf_op jit(solution)/shard_map/last/pallas_call | solution.py:845
  306.3 2.3 collective-permute-done.53.gb
  308.5 1.8 fusion
  311.0 2.6 collective-permute-done.52.refs_3_
  313.9 1.6 collective-permute-start.54
  316.0 3.5 add_convert_fusion
  319.5 2.9 collective-permute-done.54.refs_2_
  326.3 7.0 %collective-permute-done.56 = bf16[144,1024]{1,0:T(8,128)(2,1)S(1)} collective-permute-done((bf16[144,1024]{1,0:T(8,128)(2,1)S(1)}, bf16[144,1024]{1,0:T(8,128)(2,1)S(1)}, u32[]{:S(2)}, u32[]{:S(2)}) %collective-permute-start.56) | collective-permute-done | bytes 294944 | tf_op jit(solution)/shard_map/ppermute | solution.py:116
  336.4 3.0 end.1
  339.4 4.6 %feed_out.1 = (f32[128,4096]{1,0:T(8,128)}, f32[512,1024]{1,0:T(8,128)}) custom-call(s32[18]{0:T(128)} %pad_add_fusion.info.refs_0_, bf16[256,1024]{1,0:T(8,128)(2,1)} %copy-done.30, bf16[256,1024]{1,0:T(8,128)(2,1)} %copy-done.41, bf16[256,1024]{1,0:T(8,128)(2,1)} %copy-done.37, bf16[256,1024]{1,0:T(8,128)(2,1)} %copy-done.42), custom_call_target="tpu_custom_call" | custom-call | bytes 6291 | tf_op jit(solution)/shard_map/feed_out/pallas_call | solution.py:960
  346.6 3.4 joined_out.1
  (242 shorter events, 55.6 us)
Async XLA Ops:
  0.7 14.1 %collective-permute-start.2 = (bf16[512,1024]{1,0:T(8,128)(2,1)}, bf16[512,1024]{1,0:T(8,128)(2,1)}, u32[]{:S(2)}, u32[]{:S(2)}) collective-permute-start(bf16[512,1024]{1,0:T(8,128)(2,1)} %bitcast.68), channel_id=1, source_target_pairs={{0,8},{8,0},{16,24},{24,16},{1,9},{9,1},{17,25},{25,17},{2,10},{10... | collective-permute-start | bytes 3145736 | tf_op jit(solution)/shard_map/ppermute | solution.py:1029
  3.0 10.5 %collective-permute-start = (bf16[144,1024]{1,0:T(8,128)(2,1)}, bf16[144,1024]{1,0:T(8,128)(2,1)S(1)}, u32[]{:S(2)}, u32[]{:S(2)}) collective-permute-start(bf16[144,1024]{1,0:T(8,128)(2,1)} %first_pack.1), channel_id=1, source_target_pairs={{2,0},{4,2},{6,4},{7,6},{5,7},{3,5},{1,3},{0,1},{10,8},{12,10},{14... | collective-permute-start | bytes 884744 | tf_op jit(solution)/shard_map/ppermute | solution.py:119
  5.6 9.2 %collective-permute-start.1 = (bf16[144,1024]{1,0:T(8,128)(2,1)}, bf16[144,1024]{1,0:T(8,128)(2,1)S(1)}, u32[]{:S(2)}, u32[]{:S(2)}) collective-permute-start(bf16[144,1024]{1,0:T(8,128)(2,1)} %first_pack.1), channel_id=1, source_target_pairs={{0,2},{2,4},{4,6},{6,7},{7,5},{5,3},{3,1},{1,0},{8,10},{10,12},{12... | collective-permute-start | bytes 884744 | tf_op jit(solution)/shard_map/ppermute | solution.py:116
  14.8 14.9 %collective-permute-start.5 = (bf16[512,1024]{1,0:T(8,128)(2,1)S(1)}, bf16[512,1024]{1,0:T(8,128)(2,1)S(1)}, u32[]{:S(2)}, u32[]{:S(2)}) collective-permute-start(bf16[512,1024]{1,0:T(8,128)(2,1)S(1)} %bitcast.86), channel_id=1, source_target_pairs={{0,8},{8,0},{16,24},{24,16},{1,9},{9,1},{17,25},{25,17},{2,10},{10... | collective-permute-start | bytes 3145736 | tf_op jit(solution)/shard_map/ppermute | solution.py:1036
  14.9 14.8 %collective-permute-start.6 = (bf16[256,1024]{1,0:T(8,128)(2,1)S(1)}, bf16[256,1024]{1,0:T(8,128)(2,1)S(1)}, u32[]{:S(2)}, u32[]{:S(2)}) collective-permute-start(bf16[256,1024]{1,0:T(8,128)(2,1)S(1)} %slice_bitcast_fusion.1), channel_id=1, source_target_pairs={{0,16},{8,24},{16,0},{24,8},{1,17},{9,25},{17,1},{25,9},{2,18},{10... | collective-permute-start | bytes 1572872 | tf_op jit(solution)/shard_map/ppermute | solution.py:1030
  16.5 13.2 %collective-permute-start.3 = (bf16[144,1024]{1,0:T(8,128)(2,1)S(1)}, bf16[144,1024]{1,0:T(8,128)(2,1)S(1)}, u32[]{:S(2)}, u32[]{:S(2)}) collective-permute-start(bf16[144,1024]{1,0:T(8,128)(2,1)S(1)} %collective-permute-done), channel_id=1, source_target_pairs={{2,0},{4,2},{6,4},{7,6},{5,7},{3,5},{1,3},{0,1},{10,8},{12,10},{14... | collective-permute-start | bytes 884744 | tf_op jit(solution)/shard_map/ppermute | solution.py:119
  18.1 11.6 %collective-permute-start.4 = (bf16[144,1024]{1,0:T(8,128)(2,1)S(1)}, bf16[144,1024]{1,0:T(8,128)(2,1)S(1)}, u32[]{:S(2)}, u32[]{:S(2)}) collective-permute-start(bf16[144,1024]{1,0:T(8,128)(2,1)S(1)} %collective-permute-done.1), channel_id=1, source_target_pairs={{0,2},{2,4},{4,6},{6,7},{7,5},{5,3},{3,1},{1,0},{8,10},{10,12},{12... | collective-permute-start | bytes 884744 | tf_op jit(solution)/shard_map/ppermute | solution.py:116
  18.6 22.1 %collective-permute-start.9 = (bf16[256,1024]{1,0:T(8,128)(2,1)S(1)}, bf16[256,1024]{1,0:T(8,128)(2,1)}, u32[]{:S(2)}, u32[]{:S(2)}) collective-permute-start(bf16[256,1024]{1,0:T(8,128)(2,1)S(1)} %slice.20), channel_id=1, source_target_pairs={{0,16},{8,24},{16,0},{24,8},{1,17},{9,25},{17,1},{25,9},{2,18},{10... | collective-permute-start | bytes 1572872 | tf_op jit(solution)/shard_map/ppermute | solution.py:1035
  29.8 10.9 %collective-permute-start.10 = (bf16[256,1024]{1,0:T(8,128)(2,1)S(1)}, bf16[256,1024]{1,0:T(8,128)(2,1)S(1)}, u32[]{:S(2)}, u32[]{:S(2)}) collective-permute-start(bf16[256,1024]{1,0:T(8,128)(2,1)S(1)} %collective-permute-done.6.refs_2_), channel_id=1, source_target_pairs={{0,8},{8,0},{16,24},{24,16},{1,9},{9,1},{17,25},{25,17},{2,10},{10... | collective-permute-start | bytes 1572872 | tf_op jit(solution)/shard_map/ppermute | solution.py:1039
  29.8 10.8 %collective-permute-start.7 = (bf16[144,1024]{1,0:T(8,128)(2,1)S(1)}, bf16[144,1024]{1,0:T(8,128)(2,1)S(1)}, u32[]{:S(2)}, u32[]{:S(2)}) collective-permute-start(bf16[144,1024]{1,0:T(8,128)(2,1)S(1)} %collective-permute-done.3), channel_id=1, source_target_pairs={{2,0},{4,2},{6,4},{7,6},{5,7},{3,5},{1,3},{0,1},{10,8},{12,10},{14... | collective-permute-start | bytes 884744 | tf_op jit(solution)/shard_map/ppermute | solution.py:119
  31.5 9.2 %collective-permute-start.8 = (bf16[144,1024]{1,0:T(8,128)(2,1)S(1)}, bf16[144,1024]{1,0:T(8,128)(2,1)S(1)}, u32[]{:S(2)}, u32[]{:S(2)}) collective-permute-start(bf16[144,1024]{1,0:T(8,128)(2,1)S(1)} %collective-permute-done.4), channel_id=1, source_target_pairs={{0,2},{2,4},{4,6},{6,7},{7,5},{5,3},{3,1},{1,0},{8,10},{10,12},{12... | collective-permute-start | bytes 884744 | tf_op jit(solution)/shard_map/ppermute | solution.py:116
  41.1 13.2 %collective-permute-start.11 = (bf16[256,1024]{1,0:T(8,128)(2,1)}, bf16[256,1024]{1,0:T(8,128)(2,1)}, u32[]{:S(2)}, u32[]{:S(2)}) collective-permute-start(bf16[256,1024]{1,0:T(8,128)(2,1)} %collective-permute-done.9.refs_3_), channel_id=1, source_target_pairs={{0,8},{8,0},{16,24},{24,16},{1,9},{9,1},{17,25},{25,17},{2,10},{10... | collective-permute-start | bytes 1572872 | tf_op jit(solution)/shard_map/ppermute | solution.py:1042
  49.4 19.0 %collective-permute-start.13 = (bf16[256,1024]{1,0:T(8,128)(2,1)}, bf16[256,1024]{1,0:T(8,128)(2,1)}, u32[]{:S(2)}, u32[]{:S(2)}) collective-permute-start(bf16[256,1024]{1,0:T(8,128)(2,1)} %second_pack.1), channel_id=1, source_target_pairs={{2,0},{4,2},{6,4},{7,6},{5,7},{3,5},{1,3},{0,1},{10,8},{12,10},{14... | collective-permute-start | bytes 1572872 | tf_op jit(solution)/shard_map/ppermute | solution.py:119
  51.0 17.4 %collective-permute-start.14 = (bf16[256,1024]{1,0:T(8,128)(2,1)}, bf16[256,1024]{1,0:T(8,128)(2,1)}, u32[]{:S(2)}, u32[]{:S(2)}) collective-permute-start(bf16[256,1024]{1,0:T(8,128)(2,1)} %second_pack.1), channel_id=1, source_target_pairs={{0,2},{2,4},{4,6},{6,7},{7,5},{5,3},{3,1},{1,0},{8,10},{10,12},{12... | collective-permute-start | bytes 1572872 | tf_op jit(solution)/shard_map/ppermute | solution.py:116
  51.5 34.7 %collective-permute-start.19 = (bf16[512,1024]{1,0:T(8,128)(2,1)S(1)}, bf16[512,1024]{1,0:T(8,128)(2,1)S(1)}, u32[]{:S(2)}, u32[]{:S(2)}) collective-permute-start(bf16[512,1024]{1,0:T(8,128)(2,1)S(1)} %bitcast.87), channel_id=1, source_target_pairs={{0,16},{8,24},{16,0},{24,8},{1,17},{9,25},{17,1},{25,9},{2,18},{10... | collective-permute-start | bytes 3145736 | tf_op jit(solution)/shard_map/ppermute | solution.py:1043
  67.7 14.9 %collective-permute-start.17 = (bf16[1024,256]{1,0:T(8,128)(2,1)}, bf16[1024,256]{1,0:T(8,128)(2,1)}, u32[]{:S(2)}, u32[]{:S(2)}) collective-permute-start(bf16[1024,256]{1,0:T(8,128)(2,1)} %get-tuple-element.260.refs_4_), channel_id=1, source_target_pairs={{0,8},{8,0},{16,24},{24,16},{1,9},{9,1},{17,25},{25,17},{2,10},{10... | collective-permute-start | bytes 1572872 | tf_op jit(solution)/shard_map/ppermute | solution.py:73
  67.8 18.5 %collective-permute-start.18 = (bf16[1024,256]{1,0:T(8,128)(2,1)}, bf16[1024,256]{1,0:T(8,128)(2,1)}, u32[]{:S(2)}, u32[]{:S(2)}) collective-permute-start(bf16[1024,256]{1,0:T(8,128)(2,1)} %get-tuple-element.260.refs_4_), channel_id=1, source_target_pairs={{0,16},{8,24},{16,0},{24,8},{1,17},{9,25},{17,1},{25,9},{2,18},{10... | collective-permute-start | bytes 1572872 | tf_op jit(solution)/shard_map/ppermute | solution.py:73
  68.3 17.9 %collective-permute-start.15 = (bf16[256,1024]{1,0:T(8,128)(2,1)}, bf16[256,1024]{1,0:T(8,128)(2,1)S(1)}, u32[]{:S(2)}, u32[]{:S(2)}) collective-permute-start(bf16[256,1024]{1,0:T(8,128)(2,1)} %collective-permute-done.13), channel_id=1, source_target_pairs={{2,0},{4,2},{6,4},{7,6},{5,7},{3,5},{1,3},{0,1},{10,8},{12,10},{14... | collective-permute-start | bytes 1572872 | tf_op jit(solution)/shard_map/ppermute | solution.py:119
  69.9 16.3 %collective-permute-start.16 = (bf16[256,1024]{1,0:T(8,128)(2,1)}, bf16[256,1024]{1,0:T(8,128)(2,1)S(1)}, u32[]{:S(2)}, u32[]{:S(2)}) collective-permute-start(bf16[256,1024]{1,0:T(8,128)(2,1)} %collective-permute-done.14), channel_id=1, source_target_pairs={{0,2},{2,4},{4,6},{6,7},{7,5},{5,3},{3,1},{1,0},{8,10},{10,12},{12... | collective-permute-start | bytes 1572872 | tf_op jit(solution)/shard_map/ppermute | solution.py:116
  86.2 13.4 %collective-permute-start.20 = (bf16[256,1024]{1,0:T(8,128)(2,1)S(1)}, bf16[256,1024]{1,0:T(8,128)(2,1)S(1)}, u32[]{:S(2)}, u32[]{:S(2)}) collective-permute-start(bf16[256,1024]{1,0:T(8,128)(2,1)S(1)} %collective-permute-done.15), channel_id=1, source_target_pairs={{2,0},{4,2},{6,4},{7,6},{5,7},{3,5},{1,3},{0,1},{10,8},{12,10},{14... | collective-permute-start | bytes 1572872 | tf_op jit(solution)/shard_map/ppermute | solution.py:119
  87.9 11.8 %collective-permute-start.21 = (bf16[256,1024]{1,0:T(8,128)(2,1)S(1)}, bf16[256,1024]{1,0:T(8,128)(2,1)S(1)}, u32[]{:S(2)}, u32[]{:S(2)}) collective-permute-start(bf16[256,1024]{1,0:T(8,128)(2,1)S(1)} %collective-permute-done.16), channel_id=1, source_target_pairs={{0,2},{2,4},{4,6},{6,7},{7,5},{5,3},{3,1},{1,0},{8,10},{10,12},{12... | collective-permute-start | bytes 1572872 | tf_op jit(solution)/shard_map/ppermute | solution.py:116
  88.5 11.3 %collective-permute-start.22 = (bf16[1024,256]{1,0:T(8,128)(2,1)}, bf16[1024,256]{1,0:T(8,128)(2,1)S(1)}, u32[]{:S(2)}, u32[]{:S(2)}) collective-permute-start(bf16[1024,256]{1,0:T(8,128)(2,1)} %collective-permute-done.18.refs_6_), channel_id=1, source_target_pairs={{0,8},{8,0},{16,24},{24,16},{1,9},{9,1},{17,25},{25,17},{2,10},{10... | collective-permute-start | bytes 1572872 | tf_op jit(solution)/shard_map/ppermute | solution.py:1079
  101.4 17.4 %collective-permute-start.23 = (bf16[512,1024]{1,0:T(8,128)(2,1)S(1)}, bf16[512,1024]{1,0:T(8,128)(2,1)S(1)}, u32[]{:S(2)}, u32[]{:S(2)}) collective-permute-start(bf16[512,1024]{1,0:T(8,128)(2,1)S(1)} %collective-permute-done.19.ca.refs_4_), channel_id=1, source_target_pairs={{0,8},{8,0},{16,24},{24,16},{1,9},{9,1},{17,25},{25,17},{2,10},{10... | collective-permute-start | bytes 3145736 | tf_op jit(solution)/shard_map/ppermute | solution.py:1084
  101.9 16.9 %collective-permute-start.24 = (bf16[256,1024]{1,0:T(8,128)(2,1)}, bf16[256,1024]{1,0:T(8,128)(2,1)S(1)}, u32[]{:S(2)}, u32[]{:S(2)}) collective-permute-start(bf16[256,1024]{1,0:T(8,128)(2,1)} %copy-done.28), channel_id=1, source_target_pairs={{0,2},{2,4},{4,6},{6,7},{7,5},{5,3},{3,1},{1,0},{8,10},{10,12},{12... | collective-permute-start | bytes 1572872 | tf_op jit(solution)/shard_map/ppermute | solution.py:116
  106.4 12.4 %collective-permute-start.27 = (bf16[512,256]{1,0:T(8,128)(2,1)S(1)}, bf16[512,256]{1,0:T(8,128)(2,1)S(1)}, u32[]{:S(2)}, u32[]{:S(2)}) collective-permute-start(bf16[512,256]{1,0:T(8,128)(2,1)S(1)} %get-tuple-element.454), channel_id=1, source_target_pairs={{0,24},{8,16},{16,8},{24,0},{1,25},{9,17},{17,9},{25,1},{2,26},{10... | collective-permute-start | bytes 786440 | tf_op jit(solution)/shard_map/ppermute | solution.py:1088
  126.9 25.6 %collective-permute-start.29 = (bf16[512,1024]{1,0:T(8,128)(2,1)}, bf16[512,1024]{1,0:T(8,128)(2,1)S(1)}, u32[]{:S(2)}, u32[]{:S(2)}) collective-permute-start(bf16[512,1024]{1,0:T(8,128)(2,1)} %get-tuple-element.279.sa.refs_6_), channel_id=1, source_target_pairs={{0,16},{8,24},{16,0},{24,8},{1,17},{9,25},{17,1},{25,9},{2,18},{10... | collective-permute-start | bytes 3145736 | tf_op jit(solution)/shard_map/ppermute | solution.py:1100
  152.5 21.4 %collective-permute-start.32 = (bf16[512,1024]{1,0:T(8,128)(2,1)}, bf16[512,1024]{1,0:T(8,128)(2,1)S(1)}, u32[]{:S(2)}, u32[]{:S(2)}) collective-permute-start(bf16[512,1024]{1,0:T(8,128)(2,1)} %get-tuple-element.298), channel_id=1, source_target_pairs={{0,8},{8,0},{16,24},{24,16},{1,9},{9,1},{17,25},{25,17},{2,10},{10... | collective-permute-start | bytes 3145736 | tf_op jit(solution)/shard_map/ppermute | solution.py:1116
  153.0 21.0 %collective-permute-start.33 = (bf16[512,1024]{1,0:T(8,128)(2,1)}, bf16[512,1024]{1,0:T(8,128)(2,1)}, u32[]{:S(2)}, u32[]{:S(2)}) collective-permute-start(bf16[512,1024]{1,0:T(8,128)(2,1)} %get-tuple-element.299), channel_id=1, source_target_pairs={{0,8},{8,0},{16,24},{24,16},{1,9},{9,1},{17,25},{25,17},{2,10},{10... | collective-permute-start | bytes 3145736 | tf_op jit(solution)/shard_map/ppermute | solution.py:1117
  176.9 24.8 %collective-permute-start.36 = (bf16[512,1024]{1,0:T(8,128)(2,1)}, bf16[512,1024]{1,0:T(8,128)(2,1)S(1)}, u32[]{:S(2)}, u32[]{:S(2)}) collective-permute-start(bf16[512,1024]{1,0:T(8,128)(2,1)} %get-tuple-element.306), channel_id=1, source_target_pairs={{0,8},{8,0},{16,24},{24,16},{1,9},{9,1},{17,25},{25,17},{2,10},{10... | collective-permute-start | bytes 3145736 | tf_op jit(solution)/shard_map/ppermute | solution.py:1129
  179.5 25.7 %collective-permute-start.35 = (bf16[512,1024]{1,0:T(8,128)(2,1)}, bf16[512,1024]{1,0:T(8,128)(2,1)}, u32[]{:S(2)}, u32[]{:S(2)}) collective-permute-start(bf16[512,1024]{1,0:T(8,128)(2,1)} %add_pairs.8), channel_id=1, source_target_pairs={{0,16},{8,24},{16,0},{24,8},{1,17},{9,25},{17,1},{25,9},{2,18},{10... | collective-permute-start | bytes 3145736 | tf_op jit(solution)/shard_map/ppermute | solution.py:1128
  200.1 21.0 %collective-permute-start.31 = (bf16[256,1024]{1,0:T(8,128)(2,1)}, bf16[256,1024]{1,0:T(8,128)(2,1)S(1)}, u32[]{:S(2)}, u32[]{:S(2)}) collective-permute-start(bf16[256,1024]{1,0:T(8,128)(2,1)} %bitcast.119), channel_id=1, source_target_pairs={{0,2},{2,4},{4,6},{6,7},{7,5},{5,3},{3,1},{1,0},{8,10},{10,12},{12... | collective-permute-start | bytes 1572872 | tf_op jit(solution)/shard_map/ppermute | solution.py:116
  213.4 9.4 %collective-permute-start.38 = (bf16[512,256]{1,0:T(8,128)(2,1)}, bf16[512,256]{1,0:T(8,128)(2,1)S(1)}, u32[]{:S(2)}, u32[]{:S(2)}) collective-permute-start(bf16[512,256]{1,0:T(8,128)(2,1)} %get-tuple-element.318), channel_id=1, source_target_pairs={{0,16},{8,24},{16,0},{24,8},{1,17},{9,25},{17,1},{25,9},{2,18},{10... | collective-permute-start | bytes 786440 | tf_op jit(solution)/shard_map/ppermute | solution.py:1183
  214.9 12.5 %collective-permute-start.39 = (bf16[512,256]{1,0:T(8,128)(2,1)}, bf16[512,256]{1,0:T(8,128)(2,1)S(1)}, u32[]{:S(2)}, u32[]{:S(2)}) collective-permute-start(bf16[512,256]{1,0:T(8,128)(2,1)} %get-tuple-element.319), channel_id=1, source_target_pairs={{0,24},{8,16},{16,8},{24,0},{1,25},{9,17},{17,9},{25,1},{2,26},{10... | collective-permute-start | bytes 786440 | tf_op jit(solution)/shard_map/ppermute | solution.py:1183
  228.3 23.9 %collective-permute-start.42 = (bf16[2,1024,256]{2,1,0:T(8,128)(2,1)}, bf16[2,1024,256]{2,1,0:T(8,128)(2,1)}, u32[]{:S(2)}, u32[]{:S(2)}) collective-permute-start(bf16[2,1024,256]{2,1,0:T(8,128)(2,1)} %get-tuple-element.336), channel_id=1, source_target_pairs={{0,8},{8,0},{16,24},{24,16},{1,9},{9,1},{17,25},{25,17},{2,10},{10... | collective-permute-start | bytes 3145736 | tf_op jit(solution)/shard_map/ppermute | solution.py:1191
  228.6 23.5 %collective-permute-start.41 = (bf16[256,1024]{1,0:T(8,128)(2,1)}, bf16[256,1024]{1,0:T(8,128)(2,1)S(1)}, u32[]{:S(2)}, u32[]{:S(2)}) collective-permute-start(bf16[256,1024]{1,0:T(8,128)(2,1)} %bitcast.31), channel_id=1, source_target_pairs={{2,0},{4,2},{6,4},{7,6},{5,7},{3,5},{1,3},{0,1},{10,8},{12,10},{14... | collective-permute-start | bytes 1572872 | tf_op jit(solution)/shard_map/ppermute | solution.py:119
  229.6 22.5 %collective-permute-start.40 = (bf16[256,1024]{1,0:T(8,128)(2,1)S(1)}, bf16[256,1024]{1,0:T(8,128)(2,1)S(1)}, u32[]{:S(2)}, u32[]{:S(2)}) collective-permute-start(bf16[256,1024]{1,0:T(8,128)(2,1)S(1)} %add_pairs.10), channel_id=1, source_target_pairs={{0,2},{2,4},{4,6},{6,7},{7,5},{5,3},{3,1},{1,0},{8,10},{10,12},{12... | collective-permute-start | bytes 1572872 | tf_op jit(solution)/shard_map/ppermute | solution.py:116
  230.8 46.7 %collective-permute-start.46 = (bf16[512,1024]{1,0:T(8,128)(2,1)S(1)}, bf16[512,1024]{1,0:T(8,128)(2,1)}, u32[]{:S(2)}, u32[]{:S(2)}) collective-permute-start(bf16[512,1024]{1,0:T(8,128)(2,1)S(1)} %add_pairs.9), channel_id=1, source_target_pairs={{0,16},{8,24},{16,0},{24,8},{1,17},{9,25},{17,1},{25,9},{2,18},{10... | collective-permute-start | bytes 3145736 | tf_op jit(solution)/shard_map/ppermute | solution.py:1189
  255.3 22.2 %collective-permute-start.43 = (bf16[256,1024]{1,0:T(8,128)(2,1)}, bf16[256,1024]{1,0:T(8,128)(2,1)S(1)}, u32[]{:S(2)}, u32[]{:S(2)}) collective-permute-start(bf16[256,1024]{1,0:T(8,128)(2,1)} %get-tuple-element.346), channel_id=1, source_target_pairs={{0,2},{2,4},{4,6},{6,7},{7,5},{5,3},{3,1},{1,0},{8,10},{10,12},{12... | collective-permute-start | bytes 1572872 | tf_op jit(solution)/shard_map/ppermute | solution.py:116
  256.9 20.6 %collective-permute-start.44 = (bf16[256,1024]{1,0:T(8,128)(2,1)}, bf16[256,1024]{1,0:T(8,128)(2,1)S(1)}, u32[]{:S(2)}, u32[]{:S(2)}) collective-permute-start(bf16[256,1024]{1,0:T(8,128)(2,1)} %get-tuple-element.347), channel_id=1, source_target_pairs={{2,0},{4,2},{6,4},{7,6},{5,7},{3,5},{1,3},{0,1},{10,8},{12,10},{14... | collective-permute-start | bytes 1572872 | tf_op jit(solution)/shard_map/ppermute | solution.py:119
  257.4 20.2 %collective-permute-start.45 = (bf16[1024,256]{1,0:T(8,128)(2,1)}, bf16[1024,256]{1,0:T(8,128)(2,1)S(1)}, u32[]{:S(2)}, u32[]{:S(2)}) collective-permute-start(bf16[1024,256]{1,0:T(8,128)(2,1)} %fusion.1), channel_id=1, source_target_pairs={{0,16},{8,24},{16,0},{24,8},{1,17},{9,25},{17,1},{25,9},{2,18},{10... | collective-permute-start | bytes 1572872 | tf_op jit(solution)/shard_map/ppermute | solution.py:1203
  277.9 13.0 %collective-permute-start.47 = (bf16[256,1024]{1,0:T(8,128)(2,1)S(1)}, bf16[256,1024]{1,0:T(8,128)(2,1)S(1)}, u32[]{:S(2)}, u32[]{:S(2)}) collective-permute-start(bf16[256,1024]{1,0:T(8,128)(2,1)S(1)} %get-tuple-element.360), channel_id=1, source_target_pairs={{0,2},{2,4},{4,6},{6,7},{7,5},{5,3},{3,1},{1,0},{8,10},{10,12},{12... | collective-permute-start | bytes 1572872 | tf_op jit(solution)/shard_map/ppermute | solution.py:116
  279.5 12.1 %collective-permute-start.48 = (bf16[256,1024]{1,0:T(8,128)(2,1)S(1)}, bf16[256,1024]{1,0:T(8,128)(2,1)S(1)}, u32[]{:S(2)}, u32[]{:S(2)}) collective-permute-start(bf16[256,1024]{1,0:T(8,128)(2,1)S(1)} %get-tuple-element.361), channel_id=1, source_target_pairs={{2,0},{4,2},{6,4},{7,6},{5,7},{3,5},{1,3},{0,1},{10,8},{12,10},{14... | collective-permute-start | bytes 1572872 | tf_op jit(solution)/shard_map/ppermute | solution.py:119
  291.9 12.1 %collective-permute-start.50 = (bf16[256,1024]{1,0:T(8,128)(2,1)S(1)}, bf16[256,1024]{1,0:T(8,128)(2,1)S(1)}, u32[]{:S(2)}, u32[]{:S(2)}) collective-permute-start(bf16[256,1024]{1,0:T(8,128)(2,1)S(1)} %fusion.3.refs_0_), channel_id=1, source_target_pairs={{0,16},{8,24},{16,0},{24,8},{1,17},{9,25},{17,1},{25,9},{2,18},{10... | collective-permute-start | bytes 1572872 | tf_op jit(solution)/shard_map/ppermute | solution.py:1231
  293.5 10.5 %collective-permute-start.49 = (bf16[144,1024]{1,0:T(8,128)(2,1)S(1)}, bf16[144,1024]{1,0:T(8,128)(2,1)S(1)}, u32[]{:S(2)}, u32[]{:S(2)}) collective-permute-start(bf16[144,1024]{1,0:T(8,128)(2,1)S(1)} %bitcast.121), channel_id=1, source_target_pairs={{0,2},{2,4},{4,6},{6,7},{7,5},{5,3},{3,1},{1,0},{8,10},{10,12},{12... | collective-permute-start | bytes 884744 | tf_op jit(solution)/shard_map/ppermute | solution.py:116
  304.2 9.4 %collective-permute-start.52 = (bf16[144,1024]{1,0:T(8,128)(2,1)S(1)}, bf16[144,1024]{1,0:T(8,128)(2,1)S(1)}, u32[]{:S(2)}, u32[]{:S(2)}) collective-permute-start(bf16[144,1024]{1,0:T(8,128)(2,1)S(1)} %bitcast.120), channel_id=1, source_target_pairs={{2,0},{4,2},{6,4},{7,6},{5,7},{3,5},{1,3},{0,1},{10,8},{12,10},{14... | collective-permute-start | bytes 884744 | tf_op jit(solution)/shard_map/ppermute | solution.py:119
  310.3 25.3 %collective-permute-start.58 = (bf16[512,1024]{1,0:T(8,128)(2,1)S(1)}, bf16[512,1024]{1,0:T(8,128)(2,1)S(1)}, u32[]{:S(2)}, u32[]{:S(2)}) collective-permute-start(bf16[512,1024]{1,0:T(8,128)(2,1)S(1)} %fusion), channel_id=1, source_target_pairs={{0,16},{8,24},{16,0},{24,8},{1,17},{9,25},{17,1},{25,9},{2,18},{10... | collective-permute-start | bytes 3145736 | tf_op jit(solution)/shard_map/ppermute | solution.py:1247
  323.7 10.7 %collective-permute-start.59 = (bf16[256,1024]{1,0:T(8,128)(2,1)S(1)}, bf16[256,1024]{1,0:T(8,128)(2,1)S(1)}, u32[]{:S(2)}, u32[]{:S(2)}) collective-permute-start(bf16[256,1024]{1,0:T(8,128)(2,1)S(1)} %fusion.3.refs_0_), channel_id=1, source_target_pairs={{0,8},{8,0},{16,24},{24,16},{1,9},{9,1},{17,25},{25,17},{2,10},{10... | collective-permute-start | bytes 1572872 | tf_op jit(solution)/shard_map/ppermute | solution.py:1259
  323.8 10.6 %collective-permute-start.60 = (bf16[256,1024]{1,0:T(8,128)(2,1)S(1)}, bf16[256,1024]{1,0:T(8,128)(2,1)S(1)}, u32[]{:S(2)}, u32[]{:S(2)}) collective-permute-start(bf16[256,1024]{1,0:T(8,128)(2,1)S(1)} %collective-permute-done.50.refs_2_), channel_id=1, source_target_pairs={{0,8},{8,0},{16,24},{24,16},{1,9},{9,1},{17,25},{25,17},{2,10},{10... | collective-permute-start | bytes 1572872 | tf_op jit(solution)/shard_map/ppermute | solution.py:1260
  (78 other events, 809.9 us)

commit v7 on v6

--- a/solution.py
+++ b/solution.py
@@ -371,7 +371,7 @@
         ],
         input_output_aliases={3: 0, 4: 1} if extra else {},
         scratch_shapes=[pltpu.VMEM((2, count, 2 * HD), BF)],
-        compiler_params=params(60),
+        compiler_params=params(48),
         cost_estimate=cost(area * 1024, 20 * count * HD, area),
         name="attend",
     )(info, slopes, joined, *extra)
@@ -453,7 +453,7 @@
         out_shape=[jax.ShapeDtypeStruct((count, width), BF), jax.ShapeDtypeStruct((1, 6 * HD), F32)],
         input_output_aliases={5 + ns: 0} if extra else {},
         scratch_shapes=[pltpu.VMEM((2, count, 2 * HD), BF)] * 4 + [pltpu.VMEM((2, 2 * HD, count), F32)],
-        compiler_params=params(60),
+        compiler_params=params(48),
         cost_estimate=cost(area * 2560, 40 * count * HD, area),
         name="attend_back",
     )(info, slopes, joined, mixed, sums, *grads, *extra)

time: 356 us -> 349 us (0.980)
    unnamed x124 -> x114, local copies, waits for them, and re-layouts: 7.19 us -> 8.04 us
  transfers between devices with their start and end apart: 64 -> 64, of which waited for: 25 -> 26; matrix products, arithmetic and copies ran while one was open for 3% -> 2% of each run, Pallas kernels for 50% -> 50%
where the time goes in v7:
time: 349 us; the launch traced here: 343 us
  Pallas kernels  184 us (53%)
  waiting for transfers between devices  91.6 us (26%)
  starting transfers between devices  50 us (14%)
  local copies, waits for them, and re-layouts  8.89 us (3%)
  other arithmetic  6.13 us (2%)
    pallas_call x2, Pallas kernels, attend_back(): pl.pallas_call(kernel, grid=(1,), in_specs=[smem, smem, wide, narrow, nar...  38.4 us
    pallas_call x2, Pallas kernels, feed_call(): pl.pallas_call(functools.partial(feed_kernel, nt, nb, rows, units, live),...  32.4 us
    ppermute x16, waiting for transfers between devices, ahead(): return lax.ppermute(value, 'batch', self.forward)  21.2 us
    pallas_call x2, Pallas kernels, attend(): pl.pallas_call(kernel, grid=(1,), in_specs=[smem, smem, pl.BlockSpec((cou...  20.5 us
    pallas_call x1, Pallas kernels, feed_grad_call(): pl.pallas_call(functools.partial(feed_grad_kernel, ns, nb, rows, units, s...  18.8 us
    ppermute x6, waiting for transfers between devices, body(): lax.ppermute(block, 'seq', pairs(ns, rel))  18.3 us
    ppermute x12, starting transfers between devices, back(): return lax.ppermute(value, 'batch', self.backward)  15.6 us
    ppermute x16, starting transfers between devices, ahead(): return lax.ppermute(value, 'batch', self.forward)  14.3 us
  transfers between devices with their start and end apart: 64, of which 26 were waited for; matrix products, arithmetic and copies ran while one was open for 2% of the time, Pallas kernels for 50%

profile of v7, /device:TPU:0, one launch (start us, length us, event | category | flops | bytes accessed | tf_op | source)
XLA Modules:
  0.0 342.6 jit_solution(17348454526973668566)
XLA Ops:
  1.2 1.8 first_pack.1
  3.0 2.6 collective-permute-start
  5.6 2.2 second_pack.1
  7.8 5.6 %collective-permute-done = bf16[144,1024]{1,0:T(8,128)(2,1)S(1)} collective-permute-done((bf16[144,1024]{1,0:T(8,128)(2,1)}, bf16[144,1024]{1,0:T(8,128)(2,1)S(1)}, u32[]{:S(2)}, u32[]{:S(2)}) %collective-permute-start) | collective-permute-done | bytes 294944 | tf_op jit(solution)/shard_map/ppermute | solution.py:119
  14.9 1.6 collective-permute-start.6
  16.5 1.6 collective-permute-start.3
  19.2 10.6 %collective-permute-done.6.refs_2_ = bf16[256,1024]{1,0:T(8,128)(2,1)S(1)} collective-permute-done((bf16[256,1024]{1,0:T(8,128)(2,1)S(1)}, bf16[256,1024]{1,0:T(8,128)(2,1)S(1)}, u32[]{:S(2)}, u32[]{:S(2)}) %collective-permute-start.6) | collective-permute-done | bytes 524320 | tf_op jit(solution)/shard_map/ppermute | solution.py:1030
  29.9 1.6 collective-permute-start.7
  31.9 8.6 %collective-permute-done.9.refs_3_ = bf16[256,1024]{1,0:T(8,128)(2,1)S(1)} collective-permute-done((bf16[256,1024]{1,0:T(8,128)(2,1)S(1)}, bf16[256,1024]{1,0:T(8,128)(2,1)S(1)}, u32[]{:S(2)}, u32[]{:S(2)}) %collective-permute-start.9) | collective-permute-done | bytes 524320 | tf_op jit(solution)/shard_map/ppermute | solution.py:1035
  41.1 8.2 %collective-permute-done.12 = bf16[144,1024]{1,0:T(8,128)(2,1)S(1)} collective-permute-done((bf16[144,1024]{1,0:T(8,128)(2,1)S(1)}, bf16[144,1024]{1,0:T(8,128)(2,1)S(1)}, u32[]{:S(2)}, u32[]{:S(2)}) %collective-permute-start.12) | collective-permute-done | bytes 294944 | tf_op jit(solution)/shard_map/ppermute | solution.py:116
  49.3 1.6 collective-permute-start.13
  55.0 13.4 %first.1 = (bf16[2048,1024]{1,0:T(8,128)(2,1)}, bf16[2048,768]{1,0:T(8,128)(2,1)}, bf16[1024,768]{1,0:T(8,128)(2,1)}, bf16[1024,256]{1,0:T(8,128)(2,1)}, f32[16,1024]{1,0:T(8,128)}) custom-call(s32[18]{0:T(128)} %pad_add_fusion.info.refs_0_, bf16[512,1024]{1,0:T(8,128)(2,1)} %bitcast.69, bf16[512,1024]{1,0:T(8,128)(2,1)} %copy-done.28, ...), custom_call_target="tpu_custom_call" | custom-call | flops 3221225 | bytes 11534 | tf_op jit(solution)/shard_map/first/pallas_call | solution.py:264
  69.1 1.6 collective-permute-start.15
  71.6 10.3 %attend.2 = (bf16[2048,256]{1,0:T(8,128)(2,1)S(1)}, f32[2048,256]{1,0:T(8,128)S(1)}) custom-call(s32[18]{0:T(128)S(1)} %copy-done.19, f32[4]{0:T(128)S(1)} %multiply_power_fusion.refs_1_, bf16[2048,768]{1,0:T(8,128)(2,1)} %get-tuple-element.348.refs_2_), custom_call_target="tpu_custom_call" | custom-call | flops 4294967 | bytes 2621 | tf_op jit(solution)/shard_map/attend/pallas_call | solution.py:362
  81.8 4.3 %collective-permute-done.18.refs_6_ = bf16[1024,256]{1,0:T(8,128)(2,1)} collective-permute-done((bf16[1024,256]{1,0:T(8,128)(2,1)}, bf16[1024,256]{1,0:T(8,128)(2,1)}, u32[]{:S(2)}, u32[]{:S(2)}) %collective-permute-start.18) | collective-permute-done | bytes 524320 | tf_op jit(solution)/shard_map/ppermute | solution.py:73
  86.2 1.6 collective-permute-start.20
  88.4 10.3 %attend.3 = (bf16[2048,256]{1,0:T(8,128)(2,1)S(1)}, f32[2048,256]{1,0:T(8,128)S(1)}) custom-call(s32[18]{0:T(128)S(1)} %copy-done.19, f32[4]{0:T(128)S(1)} %multiply_power_fusion.refs_1_, bf16[2048,768]{1,0:T(8,128)(2,1)} %get-tuple-element.348.refs_2_, ...), custom_call_target="tpu_custom_call", output_to_operand_aliasing={{0}: (3, {}), {1}: (4, {})} | custom-call | flops 4294967 | bytes 2621 | tf_op jit(solution)/shard_map/attend/pallas_call | solution.py:362
  102.8 7.5 %collective-permute-done.26.refs_2_ = bf16[512,256]{1,0:T(8,128)(2,1)S(1)} collective-permute-done((bf16[512,256]{1,0:T(8,128)(2,1)S(1)}, bf16[512,256]{1,0:T(8,128)(2,1)S(1)}, u32[]{:S(2)}, u32[]{:S(2)}) %collective-permute-start.26) | collective-permute-done | bytes 262176 | tf_op jit(solution)/shard_map/ppermute | solution.py:1088
  110.3 4.3 %collective-permute-done.27.refs_3_ = bf16[512,256]{1,0:T(8,128)(2,1)S(1)} collective-permute-done((bf16[512,256]{1,0:T(8,128)(2,1)S(1)}, bf16[512,256]{1,0:T(8,128)(2,1)S(1)}, u32[]{:S(2)}, u32[]{:S(2)}) %collective-permute-start.27) | collective-permute-done | bytes 262176 | tf_op jit(solution)/shard_map/ppermute | solution.py:1088
  115.4 7.1 %middle.1 = (bf16[512,1024]{1,0:T(8,128)(2,1)}, f32[512,1024]{1,0:T(8,128)}, bf16[512,1024]{1,0:T(8,128)(2,1)}, bf16[1024,1024]{1,0:T(8,128)(2,1)}) custom-call(s32[18]{0:T(128)} %pad_add_fusion.info.refs_0_, bf16[512,1024]{1,0:T(8,128)(2,1)} %bitcast.70, f32[16,1024]{1,0:T(8,128)} %get-tuple-element.253.vecs.ebias, ...), custom_call_target="tpu_custom_call" | custom-call | flops 1073741 | bytes 10485 | tf_op jit(solution)/shard_map/middle/pallas_call | solution.py:489
  125.5 16.2 %feed.2 = (bf16[1024,1024]{1,0:T(8,128)(2,1)}, bf16[1024,1024]{1,0:T(8,128)(2,1)}, bf16[512,1024]{1,0:T(8,128)(2,1)}, bf16[512,1024]{1,0:T(8,128)(2,1)}, bf16[51...) custom-call(s32[18]{0:T(128)} %pad_add_fusion.info.refs_0_, ...), custom_call_target="tpu_custom_call" | custom-call | flops 8589934 | bytes 16777 | tf_op jit(solution)/shard_map/feed/pallas_call | solution.py:568
  141.7 6.6 %collective-permute-done.29.sa.refs_8_ = bf16[512,1024]{1,0:T(8,128)(2,1)} collective-permute-done((bf16[512,1024]{1,0:T(8,128)(2,1)}, bf16[512,1024]{1,0:T(8,128)(2,1)}, u32[]{:S(2)}, u32[]{:S(2)}) %collective-permute-start.29) | collective-permute-done | bytes 1048608 | tf_op jit(solution)/shard_map/ppermute | solution.py:1100
  148.9 2.5 collective-permute-done.30.sb.refs_9_
  151.3 16.2 %feed.3 = (bf16[1024,1024]{1,0:T(8,128)(2,1)}, bf16[1024,1024]{1,0:T(8,128)(2,1)}, bf16[512,1024]{1,0:T(8,128)(2,1)}, bf16[512,1024]{1,0:T(8,128)(2,1)}, bf16[51...) custom-call(s32[18]{0:T(128)} %pad_add_fusion.info.refs_0_, ...), custom_call_target="tpu_custom_call" | custom-call | flops 8589934 | bytes 16777 | tf_op jit(solution)/shard_map/feed/pallas_call | solution.py:568
  167.7 2.7 collective-permute-done.34.refs_1_
  173.0 1.5 collective-permute-start.35
  174.6 18.8 %feed_grad.1 = (bf16[1,256,1024]{2,1,0:T(8,128)(2,1)}, bf16[1,256,1024]{2,1,0:T(8,128)(2,1)}, bf16[1,256,1024]{2,1,0:T(8,128)(2,1)}, bf16[1,256,1024]{2,1,0:T(8,...) custom-call(s32[18]{0:T(128)} %pad_add_fusion.info.refs_0_, ...), custom_call_target="tpu_custom_call" | custom-call | flops 8589934 | bytes 20971 | tf_op jit(solution)/shard_map/feed_grad/pallas_call | solution.py:637
  198.8 7.9 %turn.1 = (f32[512,1024]{1,0:T(8,128)}, bf16[512,1024]{1,0:T(8,128)(2,1)}, bf16[512,256]{1,0:T(8,128)(2,1)}, bf16[512,256]{1,0:T(8,128)(2,1)}, bf16[512,256]{1,0...) custom-call(s32[18]{0:T(128)} %pad_add_fusion.info.refs_0_, bf16[512,1024]{1,0:T(8,128)(2,1)} %get-tuple-element.296.ga, ...), custom_call_target="tpu_custom_call" | custom-call | flops 1073741 | bytes 10485 | tf_op jit(solution)/shard_map/turn/pallas_call | solution.py:801
  206.8 1.6 collective-permute-start.38
  208.7 5.9 %split_grad.1 = (bf16[1024,256]{1,0:T(8,128)(2,1)}, bf16[1024,256]{1,0:T(8,128)(2,1)}, bf16[2,1024,256]{2,1,0:T(8,128)(2,1)}) custom-call(s32[18]{0:T(128)} %pad_add_fusion.info.refs_0_, bf16[512,1024]{1,0:T(8,128)(2,1)} %get-tuple-element.311.left, bf16[512,1024]{1,0:T(8,128)(2,1)} %get-tuple-element.312.right), custom_call_target="tpu_custom_call" | custom-call | flops 1073741 | bytes 6291 | tf_op jit(solution)/shard_map/split_grad/pallas_call | solution.py:683
  214.6 1.7 collective-permute-done.38.refs_7_
  216.2 4.8 %collective-permute-done.39.refs_8_ = bf16[512,256]{1,0:T(8,128)(2,1)} collective-permute-done((bf16[512,256]{1,0:T(8,128)(2,1)}, bf16[512,256]{1,0:T(8,128)(2,1)}, u32[]{:S(2)}, u32[]{:S(2)}) %collective-permute-start.39) | collective-permute-done | bytes 262176 | tf_op jit(solution)/shard_map/ppermute | solution.py:1183
  223.6 1.6 collective-permute-start.41
  227.3 19.4 %attend_back.2 = (bf16[2048,768]{1,0:T(8,128)(2,1)}, f32[1,384]{1,0:T(1,128)S(1)}) custom-call(s32[18]{0:T(128)S(1)} %copy-done.20, f32[4]{0:T(128)S(1)} %multiply_power_fusion.refs_1_, bf16[2048,768]{1,0:T(8,128)(2,1)} %get-tuple-element.348.refs_2_, bf16[2048,256]{1,0:T(8,128)(2,1)S(1)} %get-tuple-element.272.refs_3_, ...), custom_call_target="tpu_custom_call" | custom-call | flops 10737418 | bytes 5242 | tf_op jit(solution)/shard_map/attend_back/pallas_call | solution.py:446
  250.8 18.9 %attend_back.3 = (bf16[2048,768]{1,0:T(8,128)(2,1)}, f32[1,384]{1,0:T(1,128)S(1)}) custom-call(s32[18]{0:T(128)S(1)} %copy-done.20, f32[4]{0:T(128)S(1)} %multiply_power_fusion.refs_1_, bf16[2048,768]{1,0:T(8,128)(2,1)} %get-tuple-element.348.refs_2_, bf16[2048,256]{1,0:T(8,128)(2,1)S(1)} %get-tuple-element.272.refs_3_, ...), custom_call_target="tpu_custom_call", output_to_operand_aliasing={{0}: (9, {})} | custom-call | flops 10737418 | bytes 5242 | tf_op jit(solution)/shard_map/attend_back/pallas_call | solution.py:446
  272.3 11.0 %joined_grad.1 = (bf16[1,144,1024]{2,1,0:T(8,128)(2,1)}, bf16[1,144,1024]{2,1,0:T(8,128)(2,1)}, bf16[1,144,1024]{2,1,0:T(8,128)(2,1)}, bf16[1,144,1024]{2,1,0:T(...) custom-call(s32[18]{0:T(128)} %pad_add_fusion.info.refs_0_, ...), custom_call_target="tpu_custom_call" | custom-call | flops 3221225 | bytes 11534 | tf_op jit(solution)/shard_map/joined_grad/pallas_call | solution.py:754
  284.1 1.6 collective-permute-start.50
  285.7 1.6 collective-permute-start.49
  287.3 8.9 %last.1 = (bf16[512,1024]{1,0:T(8,128)(2,1)}, bf16[512,1024]{1,0:T(8,128)(2,1)}, bf16[2,512,1024]{2,1,0:T(8,128)(2,1)}) custom-call(s32[18]{0:T(128)} %pad_add_fusion.info.refs_0_, bf16[1024,768]{1,0:T(8,128)(2,1)} %get-tuple-element.363.weight, bf16[2048,768]{1,0:T(8,128)(2,1)} %get-tuple-element.395.refs_6_.right), custom_call_target="tpu_custom_call" | custom-call | flops 3221225 | bytes 11534 | tf_op jit(solution)/shard_map/last/pallas_call | solution.py:845
  298.5 2.3 collective-permute-done.53.gb
  300.8 1.8 fusion
  303.5 2.4 collective-permute-done.52.refs_3_
  308.7 3.1 add_convert_fusion
  311.8 3.0 collective-permute-done.54.refs_2_
  318.7 7.0 %collective-permute-done.56 = bf16[144,1024]{1,0:T(8,128)(2,1)S(1)} collective-permute-done((bf16[144,1024]{1,0:T(8,128)(2,1)S(1)}, bf16[144,1024]{1,0:T(8,128)(2,1)S(1)}, u32[]{:S(2)}, u32[]{:S(2)}) %collective-permute-start.56) | collective-permute-done | bytes 294944 | tf_op jit(solution)/shard_map/ppermute | solution.py:116
  328.9 3.0 end.1
  331.9 4.6 %feed_out.1 = (f32[128,4096]{1,0:T(8,128)}, f32[512,1024]{1,0:T(8,128)}) custom-call(s32[18]{0:T(128)} %pad_add_fusion.info.refs_0_, bf16[256,1024]{1,0:T(8,128)(2,1)} %copy-done.25, bf16[256,1024]{1,0:T(8,128)(2,1)} %copy-done.34, bf16[256,1024]{1,0:T(8,128)(2,1)} %copy-done.31, bf16[256,1024]{1,0:T(8,128)(2,1)} %copy-done.35), custom_call_target="tpu_custom_call" | custom-call | bytes 6291 | tf_op jit(solution)/shard_map/feed_out/pallas_call | solution.py:960
  339.1 3.4 joined_out.1
  (232 shorter events, 54.3 us)
Async XLA Ops:
  0.7 14.2 %collective-permute-start.2 = (bf16[512,1024]{1,0:T(8,128)(2,1)}, bf16[512,1024]{1,0:T(8,128)(2,1)S(1)}, u32[]{:S(2)}, u32[]{:S(2)}) collective-permute-start(bf16[512,1024]{1,0:T(8,128)(2,1)} %bitcast.68), channel_id=1, source_target_pairs={{0,8},{8,0},{16,24},{24,16},{1,9},{9,1},{17,25},{25,17},{2,10},{10... | collective-permute-start | bytes 3145736 | tf_op jit(solution)/shard_map/ppermute | solution.py:1029
  3.0 10.5 %collective-permute-start = (bf16[144,1024]{1,0:T(8,128)(2,1)}, bf16[144,1024]{1,0:T(8,128)(2,1)S(1)}, u32[]{:S(2)}, u32[]{:S(2)}) collective-permute-start(bf16[144,1024]{1,0:T(8,128)(2,1)} %first_pack.1), channel_id=1, source_target_pairs={{2,0},{4,2},{6,4},{7,6},{5,7},{3,5},{1,3},{0,1},{10,8},{12,10},{14... | collective-permute-start | bytes 884744 | tf_op jit(solution)/shard_map/ppermute | solution.py:119
  5.5 9.3 %collective-permute-start.1 = (bf16[144,1024]{1,0:T(8,128)(2,1)}, bf16[144,1024]{1,0:T(8,128)(2,1)S(1)}, u32[]{:S(2)}, u32[]{:S(2)}) collective-permute-start(bf16[144,1024]{1,0:T(8,128)(2,1)} %first_pack.1), channel_id=1, source_target_pairs={{0,2},{2,4},{4,6},{6,7},{7,5},{5,3},{3,1},{1,0},{8,10},{10,12},{12... | collective-permute-start | bytes 884744 | tf_op jit(solution)/shard_map/ppermute | solution.py:116
  14.8 14.9 %collective-permute-start.5 = (bf16[512,1024]{1,0:T(8,128)(2,1)}, bf16[512,1024]{1,0:T(8,128)(2,1)}, u32[]{:S(2)}, u32[]{:S(2)}) collective-permute-start(bf16[512,1024]{1,0:T(8,128)(2,1)} %bitcast.1.ca.refs_2_.cot), channel_id=1, source_target_pairs={{0,8},{8,0},{16,24},{24,16},{1,9},{9,1},{17,25},{25,17},{2,10},{10... | collective-permute-start | bytes 3145736 | tf_op jit(solution)/shard_map/ppermute | solution.py:1036
  14.9 14.8 %collective-permute-start.6 = (bf16[256,1024]{1,0:T(8,128)(2,1)S(1)}, bf16[256,1024]{1,0:T(8,128)(2,1)S(1)}, u32[]{:S(2)}, u32[]{:S(2)}) collective-permute-start(bf16[256,1024]{1,0:T(8,128)(2,1)S(1)} %slice_bitcast_fusion.1), channel_id=1, source_target_pairs={{0,16},{8,24},{16,0},{24,8},{1,17},{9,25},{17,1},{25,9},{2,18},{10... | collective-permute-start | bytes 1572872 | tf_op jit(solution)/shard_map/ppermute | solution.py:1030
  16.5 13.2 %collective-permute-start.3 = (bf16[144,1024]{1,0:T(8,128)(2,1)S(1)}, bf16[144,1024]{1,0:T(8,128)(2,1)S(1)}, u32[]{:S(2)}, u32[]{:S(2)}) collective-permute-start(bf16[144,1024]{1,0:T(8,128)(2,1)S(1)} %collective-permute-done), channel_id=1, source_target_pairs={{2,0},{4,2},{6,4},{7,6},{5,7},{3,5},{1,3},{0,1},{10,8},{12,10},{14... | collective-permute-start | bytes 884744 | tf_op jit(solution)/shard_map/ppermute | solution.py:119
  18.1 11.6 %collective-permute-start.4 = (bf16[144,1024]{1,0:T(8,128)(2,1)S(1)}, bf16[144,1024]{1,0:T(8,128)(2,1)S(1)}, u32[]{:S(2)}, u32[]{:S(2)}) collective-permute-start(bf16[144,1024]{1,0:T(8,128)(2,1)S(1)} %collective-permute-done.1), channel_id=1, source_target_pairs={{0,2},{2,4},{4,6},{6,7},{7,5},{5,3},{3,1},{1,0},{8,10},{10,12},{12... | collective-permute-start | bytes 884744 | tf_op jit(solution)/shard_map/ppermute | solution.py:116
  18.6 22.0 %collective-permute-start.9 = (bf16[256,1024]{1,0:T(8,128)(2,1)S(1)}, bf16[256,1024]{1,0:T(8,128)(2,1)S(1)}, u32[]{:S(2)}, u32[]{:S(2)}) collective-permute-start(bf16[256,1024]{1,0:T(8,128)(2,1)S(1)} %slice.20), channel_id=1, source_target_pairs={{0,16},{8,24},{16,0},{24,8},{1,17},{9,25},{17,1},{25,9},{2,18},{10... | collective-permute-start | bytes 1572872 | tf_op jit(solution)/shard_map/ppermute | solution.py:1035
  29.8 10.8 %collective-permute-start.10 = (bf16[256,1024]{1,0:T(8,128)(2,1)S(1)}, bf16[256,1024]{1,0:T(8,128)(2,1)S(1)}, u32[]{:S(2)}, u32[]{:S(2)}) collective-permute-start(bf16[256,1024]{1,0:T(8,128)(2,1)S(1)} %collective-permute-done.6.refs_2_), channel_id=1, source_target_pairs={{0,8},{8,0},{16,24},{24,16},{1,9},{9,1},{17,25},{25,17},{2,10},{10... | collective-permute-start | bytes 1572872 | tf_op jit(solution)/shard_map/ppermute | solution.py:1039
  29.9 10.7 %collective-permute-start.7 = (bf16[144,1024]{1,0:T(8,128)(2,1)S(1)}, bf16[144,1024]{1,0:T(8,128)(2,1)S(1)}, u32[]{:S(2)}, u32[]{:S(2)}) collective-permute-start(bf16[144,1024]{1,0:T(8,128)(2,1)S(1)} %collective-permute-done.3), channel_id=1, source_target_pairs={{2,0},{4,2},{6,4},{7,6},{5,7},{3,5},{1,3},{0,1},{10,8},{12,10},{14... | collective-permute-start | bytes 884744 | tf_op jit(solution)/shard_map/ppermute | solution.py:119
  41.1 13.1 %collective-permute-start.11 = (bf16[256,1024]{1,0:T(8,128)(2,1)S(1)}, bf16[256,1024]{1,0:T(8,128)(2,1)S(1)}, u32[]{:S(2)}, u32[]{:S(2)}) collective-permute-start(bf16[256,1024]{1,0:T(8,128)(2,1)S(1)} %collective-permute-done.9.refs_3_), channel_id=1, source_target_pairs={{0,8},{8,0},{16,24},{24,16},{1,9},{9,1},{17,25},{25,17},{2,10},{10... | collective-permute-start | bytes 1572872 | tf_op jit(solution)/shard_map/ppermute | solution.py:1042
  49.3 19.8 %collective-permute-start.13 = (bf16[256,1024]{1,0:T(8,128)(2,1)}, bf16[256,1024]{1,0:T(8,128)(2,1)}, u32[]{:S(2)}, u32[]{:S(2)}) collective-permute-start(bf16[256,1024]{1,0:T(8,128)(2,1)} %second_pack.1), channel_id=1, source_target_pairs={{2,0},{4,2},{6,4},{7,6},{5,7},{3,5},{1,3},{0,1},{10,8},{12,10},{14... | collective-permute-start | bytes 1572872 | tf_op jit(solution)/shard_map/ppermute | solution.py:119
  50.9 18.2 %collective-permute-start.14 = (bf16[256,1024]{1,0:T(8,128)(2,1)}, bf16[256,1024]{1,0:T(8,128)(2,1)}, u32[]{:S(2)}, u32[]{:S(2)}) collective-permute-start(bf16[256,1024]{1,0:T(8,128)(2,1)} %second_pack.1), channel_id=1, source_target_pairs={{0,2},{2,4},{4,6},{6,7},{7,5},{5,3},{3,1},{1,0},{8,10},{10,12},{12... | collective-permute-start | bytes 1572872 | tf_op jit(solution)/shard_map/ppermute | solution.py:116
  51.3 34.9 %collective-permute-start.19 = (bf16[512,1024]{1,0:T(8,128)(2,1)}, bf16[512,1024]{1,0:T(8,128)(2,1)}, u32[]{:S(2)}, u32[]{:S(2)}) collective-permute-start(bf16[512,1024]{1,0:T(8,128)(2,1)} %bitcast.1.ca.refs_2_.cot), channel_id=1, source_target_pairs={{0,16},{8,24},{16,0},{24,8},{1,17},{9,25},{17,1},{25,9},{2,18},{10... | collective-permute-start | bytes 3145736 | tf_op jit(solution)/shard_map/ppermute | solution.py:1043
  68.4 13.4 %collective-permute-start.17 = (bf16[1024,256]{1,0:T(8,128)(2,1)}, bf16[1024,256]{1,0:T(8,128)(2,1)}, u32[]{:S(2)}, u32[]{:S(2)}) collective-permute-start(bf16[1024,256]{1,0:T(8,128)(2,1)} %get-tuple-element.260.refs_4_), channel_id=1, source_target_pairs={{0,8},{8,0},{16,24},{24,16},{1,9},{9,1},{17,25},{25,17},{2,10},{10... | collective-permute-start | bytes 1572872 | tf_op jit(solution)/shard_map/ppermute | solution.py:73
  68.5 17.7 %collective-permute-start.18 = (bf16[1024,256]{1,0:T(8,128)(2,1)}, bf16[1024,256]{1,0:T(8,128)(2,1)}, u32[]{:S(2)}, u32[]{:S(2)}) collective-permute-start(bf16[1024,256]{1,0:T(8,128)(2,1)} %get-tuple-element.260.refs_4_), channel_id=1, source_target_pairs={{0,16},{8,24},{16,0},{24,8},{1,17},{9,25},{17,1},{25,9},{2,18},{10... | collective-permute-start | bytes 1572872 | tf_op jit(solution)/shard_map/ppermute | solution.py:73
  69.1 17.1 %collective-permute-start.15 = (bf16[256,1024]{1,0:T(8,128)(2,1)}, bf16[256,1024]{1,0:T(8,128)(2,1)}, u32[]{:S(2)}, u32[]{:S(2)}) collective-permute-start(bf16[256,1024]{1,0:T(8,128)(2,1)} %collective-permute-done.13), channel_id=1, source_target_pairs={{2,0},{4,2},{6,4},{7,6},{5,7},{3,5},{1,3},{0,1},{10,8},{12,10},{14... | collective-permute-start | bytes 1572872 | tf_op jit(solution)/shard_map/ppermute | solution.py:119
  70.6 15.5 %collective-permute-start.16 = (bf16[256,1024]{1,0:T(8,128)(2,1)}, bf16[256,1024]{1,0:T(8,128)(2,1)}, u32[]{:S(2)}, u32[]{:S(2)}) collective-permute-start(bf16[256,1024]{1,0:T(8,128)(2,1)} %collective-permute-done.14), channel_id=1, source_target_pairs={{0,2},{2,4},{4,6},{6,7},{7,5},{5,3},{3,1},{1,0},{8,10},{10,12},{12... | collective-permute-start | bytes 1572872 | tf_op jit(solution)/shard_map/ppermute | solution.py:116
  86.2 12.5 %collective-permute-start.20 = (bf16[256,1024]{1,0:T(8,128)(2,1)}, bf16[256,1024]{1,0:T(8,128)(2,1)}, u32[]{:S(2)}, u32[]{:S(2)}) collective-permute-start(bf16[256,1024]{1,0:T(8,128)(2,1)} %collective-permute-done.15), channel_id=1, source_target_pairs={{2,0},{4,2},{6,4},{7,6},{5,7},{3,5},{1,3},{0,1},{10,8},{12,10},{14... | collective-permute-start | bytes 1572872 | tf_op jit(solution)/shard_map/ppermute | solution.py:119
  87.8 11.9 %collective-permute-start.21 = (bf16[256,1024]{1,0:T(8,128)(2,1)}, bf16[256,1024]{1,0:T(8,128)(2,1)}, u32[]{:S(2)}, u32[]{:S(2)}) collective-permute-start(bf16[256,1024]{1,0:T(8,128)(2,1)} %collective-permute-done.16), channel_id=1, source_target_pairs={{0,2},{2,4},{4,6},{6,7},{7,5},{5,3},{3,1},{1,0},{8,10},{10,12},{12... | collective-permute-start | bytes 1572872 | tf_op jit(solution)/shard_map/ppermute | solution.py:116
  88.4 11.3 %collective-permute-start.22 = (bf16[1024,256]{1,0:T(8,128)(2,1)}, bf16[1024,256]{1,0:T(8,128)(2,1)}, u32[]{:S(2)}, u32[]{:S(2)}) collective-permute-start(bf16[1024,256]{1,0:T(8,128)(2,1)} %collective-permute-done.18.refs_6_), channel_id=1, source_target_pairs={{0,8},{8,0},{16,24},{24,16},{1,9},{9,1},{17,25},{25,17},{2,10},{10... | collective-permute-start | bytes 1572872 | tf_op jit(solution)/shard_map/ppermute | solution.py:1079
  99.7 14.9 %collective-permute-start.23 = (bf16[512,1024]{1,0:T(8,128)(2,1)}, bf16[512,1024]{1,0:T(8,128)(2,1)}, u32[]{:S(2)}, u32[]{:S(2)}) collective-permute-start(bf16[512,1024]{1,0:T(8,128)(2,1)} %collective-permute-done.19.ca.refs_4_), channel_id=1, source_target_pairs={{0,8},{8,0},{16,24},{24,16},{1,9},{9,1},{17,25},{25,17},{2,10},{10... | collective-permute-start | bytes 3145736 | tf_op jit(solution)/shard_map/ppermute | solution.py:1084
  99.7 14.9 %collective-permute-start.24 = (bf16[256,1024]{1,0:T(8,128)(2,1)}, bf16[256,1024]{1,0:T(8,128)(2,1)}, u32[]{:S(2)}, u32[]{:S(2)}) collective-permute-start(bf16[256,1024]{1,0:T(8,128)(2,1)} %collective-permute-done.21), channel_id=1, source_target_pairs={{0,2},{2,4},{4,6},{6,7},{7,5},{5,3},{3,1},{1,0},{8,10},{10,12},{12... | collective-permute-start | bytes 1572872 | tf_op jit(solution)/shard_map/ppermute | solution.py:116
  101.2 9.1 %collective-permute-start.26 = (bf16[512,256]{1,0:T(8,128)(2,1)S(1)}, bf16[512,256]{1,0:T(8,128)(2,1)S(1)}, u32[]{:S(2)}, u32[]{:S(2)}) collective-permute-start(bf16[512,256]{1,0:T(8,128)(2,1)S(1)} %get-tuple-element.455), channel_id=1, source_target_pairs={{0,16},{8,24},{16,0},{24,8},{1,17},{9,25},{17,1},{25,9},{2,18},{10... | collective-permute-start | bytes 786440 | tf_op jit(solution)/shard_map/ppermute | solution.py:1088
  102.7 11.9 %collective-permute-start.27 = (bf16[512,256]{1,0:T(8,128)(2,1)S(1)}, bf16[512,256]{1,0:T(8,128)(2,1)S(1)}, u32[]{:S(2)}, u32[]{:S(2)}) collective-permute-start(bf16[512,256]{1,0:T(8,128)(2,1)S(1)} %get-tuple-element.454), channel_id=1, source_target_pairs={{0,24},{8,16},{16,8},{24,0},{1,25},{9,17},{17,9},{25,1},{2,26},{10... | collective-permute-start | bytes 786440 | tf_op jit(solution)/shard_map/ppermute | solution.py:1088
  122.9 25.5 %collective-permute-start.29 = (bf16[512,1024]{1,0:T(8,128)(2,1)}, bf16[512,1024]{1,0:T(8,128)(2,1)}, u32[]{:S(2)}, u32[]{:S(2)}) collective-permute-start(bf16[512,1024]{1,0:T(8,128)(2,1)} %get-tuple-element.279.sa.refs_6_), channel_id=1, source_target_pairs={{0,16},{8,24},{16,0},{24,8},{1,17},{9,25},{17,1},{25,9},{2,18},{10... | collective-permute-start | bytes 3145736 | tf_op jit(solution)/shard_map/ppermute | solution.py:1100
  148.3 19.2 %collective-permute-start.32 = (bf16[512,1024]{1,0:T(8,128)(2,1)}, bf16[512,1024]{1,0:T(8,128)(2,1)}, u32[]{:S(2)}, u32[]{:S(2)}) collective-permute-start(bf16[512,1024]{1,0:T(8,128)(2,1)} %get-tuple-element.298), channel_id=1, source_target_pairs={{0,8},{8,0},{16,24},{24,16},{1,9},{9,1},{17,25},{25,17},{2,10},{10... | collective-permute-start | bytes 3145736 | tf_op jit(solution)/shard_map/ppermute | solution.py:1116
  148.9 18.7 %collective-permute-start.33 = (bf16[512,1024]{1,0:T(8,128)(2,1)}, bf16[512,1024]{1,0:T(8,128)(2,1)}, u32[]{:S(2)}, u32[]{:S(2)}) collective-permute-start(bf16[512,1024]{1,0:T(8,128)(2,1)} %get-tuple-element.299), channel_id=1, source_target_pairs={{0,8},{8,0},{16,24},{24,16},{1,9},{9,1},{17,25},{25,17},{2,10},{10... | collective-permute-start | bytes 3145736 | tf_op jit(solution)/shard_map/ppermute | solution.py:1117
  170.5 24.4 %collective-permute-start.36 = (bf16[512,1024]{1,0:T(8,128)(2,1)}, bf16[512,1024]{1,0:T(8,128)(2,1)}, u32[]{:S(2)}, u32[]{:S(2)}) collective-permute-start(bf16[512,1024]{1,0:T(8,128)(2,1)} %get-tuple-element.306), channel_id=1, source_target_pairs={{0,8},{8,0},{16,24},{24,16},{1,9},{9,1},{17,25},{25,17},{2,10},{10... | collective-permute-start | bytes 3145736 | tf_op jit(solution)/shard_map/ppermute | solution.py:1129
  173.0 25.8 %collective-permute-start.35 = (bf16[512,1024]{1,0:T(8,128)(2,1)}, bf16[512,1024]{1,0:T(8,128)(2,1)}, u32[]{:S(2)}, u32[]{:S(2)}) collective-permute-start(bf16[512,1024]{1,0:T(8,128)(2,1)} %add_pairs.8), channel_id=1, source_target_pairs={{0,16},{8,24},{16,0},{24,8},{1,17},{9,25},{17,1},{25,9},{2,18},{10... | collective-permute-start | bytes 3145736 | tf_op jit(solution)/shard_map/ppermute | solution.py:1128
  193.3 21.2 %collective-permute-start.31 = (bf16[256,1024]{1,0:T(8,128)(2,1)}, bf16[256,1024]{1,0:T(8,128)(2,1)}, u32[]{:S(2)}, u32[]{:S(2)}) collective-permute-start(bf16[256,1024]{1,0:T(8,128)(2,1)} %bitcast.105), channel_id=1, source_target_pairs={{0,2},{2,4},{4,6},{6,7},{7,5},{5,3},{3,1},{1,0},{8,10},{10,12},{12... | collective-permute-start | bytes 1572872 | tf_op jit(solution)/shard_map/ppermute | solution.py:116
  206.8 9.4 %collective-permute-start.38 = (bf16[512,256]{1,0:T(8,128)(2,1)}, bf16[512,256]{1,0:T(8,128)(2,1)S(1)}, u32[]{:S(2)}, u32[]{:S(2)}) collective-permute-start(bf16[512,256]{1,0:T(8,128)(2,1)} %get-tuple-element.318), channel_id=1, source_target_pairs={{0,16},{8,24},{16,0},{24,8},{1,17},{9,25},{17,1},{25,9},{2,18},{10... | collective-permute-start | bytes 786440 | tf_op jit(solution)/shard_map/ppermute | solution.py:1183
  208.4 12.6 %collective-permute-start.39 = (bf16[512,256]{1,0:T(8,128)(2,1)}, bf16[512,256]{1,0:T(8,128)(2,1)}, u32[]{:S(2)}, u32[]{:S(2)}) collective-permute-start(bf16[512,256]{1,0:T(8,128)(2,1)} %get-tuple-element.319), channel_id=1, source_target_pairs={{0,24},{8,16},{16,8},{24,0},{1,25},{9,17},{17,9},{25,1},{2,26},{10... | collective-permute-start | bytes 786440 | tf_op jit(solution)/shard_map/ppermute | solution.py:1183
  223.3 23.5 %collective-permute-start.42 = (bf16[2,1024,256]{2,1,0:T(8,128)(2,1)}, bf16[2,1024,256]{2,1,0:T(8,128)(2,1)S(1)}, u32[]{:S(2)}, u32[]{:S(2)}) collective-permute-start(bf16[2,1024,256]{2,1,0:T(8,128)(2,1)} %get-tuple-element.336), channel_id=1, source_target_pairs={{0,8},{8,0},{16,24},{24,16},{1,9},{9,1},{17,25},{25,17},{2,10},{10... | collective-permute-start | bytes 3145736 | tf_op jit(solution)/shard_map/ppermute | solution.py:1191
  223.6 23.2 %collective-permute-start.41 = (bf16[256,1024]{1,0:T(8,128)(2,1)}, bf16[256,1024]{1,0:T(8,128)(2,1)S(1)}, u32[]{:S(2)}, u32[]{:S(2)}) collective-permute-start(bf16[256,1024]{1,0:T(8,128)(2,1)} %bitcast.104), channel_id=1, source_target_pairs={{2,0},{4,2},{6,4},{7,6},{5,7},{3,5},{1,3},{0,1},{10,8},{12,10},{14... | collective-permute-start | bytes 1572872 | tf_op jit(solution)/shard_map/ppermute | solution.py:119
  225.2 21.6 %collective-permute-start.40 = (bf16[256,1024]{1,0:T(8,128)(2,1)S(1)}, bf16[256,1024]{1,0:T(8,128)(2,1)S(1)}, u32[]{:S(2)}, u32[]{:S(2)}) collective-permute-start(bf16[256,1024]{1,0:T(8,128)(2,1)S(1)} %add_pairs.10), channel_id=1, source_target_pairs={{0,2},{2,4},{4,6},{6,7},{7,5},{5,3},{3,1},{1,0},{8,10},{10,12},{12... | collective-permute-start | bytes 1572872 | tf_op jit(solution)/shard_map/ppermute | solution.py:116
  225.8 44.0 %collective-permute-start.46 = (bf16[512,1024]{1,0:T(8,128)(2,1)}, bf16[512,1024]{1,0:T(8,128)(2,1)S(1)}, u32[]{:S(2)}, u32[]{:S(2)}) collective-permute-start(bf16[512,1024]{1,0:T(8,128)(2,1)} %copy-done.5), channel_id=1, source_target_pairs={{0,16},{8,24},{16,0},{24,8},{1,17},{9,25},{17,1},{25,9},{2,18},{10... | collective-permute-start | bytes 3145736 | tf_op jit(solution)/shard_map/ppermute | solution.py:1189
  248.2 21.6 %collective-permute-start.43 = (bf16[256,1024]{1,0:T(8,128)(2,1)S(1)}, bf16[256,1024]{1,0:T(8,128)(2,1)S(1)}, u32[]{:S(2)}, u32[]{:S(2)}) collective-permute-start(bf16[256,1024]{1,0:T(8,128)(2,1)S(1)} %get-tuple-element.346), channel_id=1, source_target_pairs={{0,2},{2,4},{4,6},{6,7},{7,5},{5,3},{3,1},{1,0},{8,10},{10,12},{12... | collective-permute-start | bytes 1572872 | tf_op jit(solution)/shard_map/ppermute | solution.py:116
  249.7 20.1 %collective-permute-start.44 = (bf16[256,1024]{1,0:T(8,128)(2,1)S(1)}, bf16[256,1024]{1,0:T(8,128)(2,1)S(1)}, u32[]{:S(2)}, u32[]{:S(2)}) collective-permute-start(bf16[256,1024]{1,0:T(8,128)(2,1)S(1)} %get-tuple-element.347), channel_id=1, source_target_pairs={{2,0},{4,2},{6,4},{7,6},{5,7},{3,5},{1,3},{0,1},{10,8},{12,10},{14... | collective-permute-start | bytes 1572872 | tf_op jit(solution)/shard_map/ppermute | solution.py:119
  250.3 19.5 %collective-permute-start.45 = (bf16[1024,256]{1,0:T(8,128)(2,1)S(1)}, bf16[1024,256]{1,0:T(8,128)(2,1)S(1)}, u32[]{:S(2)}, u32[]{:S(2)}) collective-permute-start(bf16[1024,256]{1,0:T(8,128)(2,1)S(1)} %fusion.1), channel_id=1, source_target_pairs={{0,16},{8,24},{16,0},{24,8},{1,17},{9,25},{17,1},{25,9},{2,18},{10... | collective-permute-start | bytes 1572872 | tf_op jit(solution)/shard_map/ppermute | solution.py:1203
  270.3 13.1 %collective-permute-start.47 = (bf16[256,1024]{1,0:T(8,128)(2,1)S(1)}, bf16[256,1024]{1,0:T(8,128)(2,1)S(1)}, u32[]{:S(2)}, u32[]{:S(2)}) collective-permute-start(bf16[256,1024]{1,0:T(8,128)(2,1)S(1)} %get-tuple-element.360), channel_id=1, source_target_pairs={{0,2},{2,4},{4,6},{6,7},{7,5},{5,3},{3,1},{1,0},{8,10},{10,12},{12... | collective-permute-start | bytes 1572872 | tf_op jit(solution)/shard_map/ppermute | solution.py:116
  271.7 12.1 %collective-permute-start.48 = (bf16[256,1024]{1,0:T(8,128)(2,1)S(1)}, bf16[256,1024]{1,0:T(8,128)(2,1)S(1)}, u32[]{:S(2)}, u32[]{:S(2)}) collective-permute-start(bf16[256,1024]{1,0:T(8,128)(2,1)S(1)} %get-tuple-element.361), channel_id=1, source_target_pairs={{2,0},{4,2},{6,4},{7,6},{5,7},{3,5},{1,3},{0,1},{10,8},{12,10},{14... | collective-permute-start | bytes 1572872 | tf_op jit(solution)/shard_map/ppermute | solution.py:119
  284.1 12.1 %collective-permute-start.50 = (bf16[256,1024]{1,0:T(8,128)(2,1)S(1)}, bf16[256,1024]{1,0:T(8,128)(2,1)S(1)}, u32[]{:S(2)}, u32[]{:S(2)}) collective-permute-start(bf16[256,1024]{1,0:T(8,128)(2,1)S(1)} %fusion.3.refs_0_), channel_id=1, source_target_pairs={{0,16},{8,24},{16,0},{24,8},{1,17},{9,25},{17,1},{25,9},{2,18},{10... | collective-permute-start | bytes 1572872 | tf_op jit(solution)/shard_map/ppermute | solution.py:1231
  285.7 10.5 %collective-permute-start.49 = (bf16[144,1024]{1,0:T(8,128)(2,1)S(1)}, bf16[144,1024]{1,0:T(8,128)(2,1)S(1)}, u32[]{:S(2)}, u32[]{:S(2)}) collective-permute-start(bf16[144,1024]{1,0:T(8,128)(2,1)S(1)} %bitcast.107), channel_id=1, source_target_pairs={{0,2},{2,4},{4,6},{6,7},{7,5},{5,3},{3,1},{1,0},{8,10},{10,12},{12... | collective-permute-start | bytes 884744 | tf_op jit(solution)/shard_map/ppermute | solution.py:116
  296.5 9.4 %collective-permute-start.52 = (bf16[144,1024]{1,0:T(8,128)(2,1)S(1)}, bf16[144,1024]{1,0:T(8,128)(2,1)S(1)}, u32[]{:S(2)}, u32[]{:S(2)}) collective-permute-start(bf16[144,1024]{1,0:T(8,128)(2,1)S(1)} %bitcast.106), channel_id=1, source_target_pairs={{2,0},{4,2},{6,4},{7,6},{5,7},{3,5},{1,3},{0,1},{10,8},{12,10},{14... | collective-permute-start | bytes 884744 | tf_op jit(solution)/shard_map/ppermute | solution.py:119
  302.6 25.3 %collective-permute-start.58 = (bf16[512,1024]{1,0:T(8,128)(2,1)S(1)}, bf16[512,1024]{1,0:T(8,128)(2,1)S(1)}, u32[]{:S(2)}, u32[]{:S(2)}) collective-permute-start(bf16[512,1024]{1,0:T(8,128)(2,1)S(1)} %fusion), channel_id=1, source_target_pairs={{0,16},{8,24},{16,0},{24,8},{1,17},{9,25},{17,1},{25,9},{2,18},{10... | collective-permute-start | bytes 3145736 | tf_op jit(solution)/shard_map/ppermute | solution.py:1247
  316.1 10.8 %collective-permute-start.59 = (bf16[256,1024]{1,0:T(8,128)(2,1)S(1)}, bf16[256,1024]{1,0:T(8,128)(2,1)S(1)}, u32[]{:S(2)}, u32[]{:S(2)}) collective-permute-start(bf16[256,1024]{1,0:T(8,128)(2,1)S(1)} %fusion.3.refs_0_), channel_id=1, source_target_pairs={{0,8},{8,0},{16,24},{24,16},{1,9},{9,1},{17,25},{25,17},{2,10},{10... | collective-permute-start | bytes 1572872 | tf_op jit(solution)/shard_map/ppermute | solution.py:1259
  316.2 10.7 %collective-permute-start.60 = (bf16[256,1024]{1,0:T(8,128)(2,1)S(1)}, bf16[256,1024]{1,0:T(8,128)(2,1)S(1)}, u32[]{:S(2)}, u32[]{:S(2)}) collective-permute-start(bf16[256,1024]{1,0:T(8,128)(2,1)S(1)} %collective-permute-done.50.refs_2_), channel_id=1, source_target_pairs={{0,8},{8,0},{16,24},{24,16},{1,9},{9,1},{17,25},{25,17},{2,10},{10... | collective-permute-start | bytes 1572872 | tf_op jit(solution)/shard_map/ppermute | solution.py:1260
  (73 other events, 755.6 us)
